TPU v7x, 32 devices: a whole 2x2x4 slice. The times are simulated.
32 devices in a mesh: sector: 16 (over z, y, core), radial: 2 (over x).
Axes of the slice: x: 2, y: 2, z: 4, core: 2. Of those that a mesh axis runs over, the one named last changes fastest.
Arguments:
- fields: float32 [16, 2, 140, 1024], P('sector', 'radial'), may hold values from -6 to 6
- pattern: int32 [16, 2, 1024], P('sector', 'radial'), may hold values from 0 to 15
- tent_order: int32 [16, 2, 1024], P('sector', 'radial'), may hold values from 0 to 1023, each once within a row
- level_sizes: int32 [16, 2, 4], P('sector', 'radial'), may hold values from 1 to 384, 1024 in all within a row
- send_rows: int32 [16, 2, 4, 128], P('sector', 'radial'), may hold values from 0 to 1023
- neighbours: int32 [16, 2, 4, 1024], P('sector', 'radial'), may hold values from 0 to 1535, as said below
- operator: float32 [140, 140], replicated, may hold values from -2 to 2, as said below
- trace_map: float32 [60, 140], replicated, may hold values from -0.5 to 0.5
- lift_map: float32 [4, 140, 60], replicated, may hold values from -0.375 to 0.375
- tent_height: float32 [16], replicated, may hold values from 0.15 to 0.5
Outputs:
- advanced: float32 [16, 2, 140, 1024], P('sector', 'radial')
Inputs may be any that keep to these rules, and one draw needn't show every extreme that they name: `tent_order`: each block's entries are a permutation of 0 to 1023. `level_sizes`: each block's 4 sizes sum to 1024, and some level of every block has exactly 384 tents. `neighbours`: an entry below 1024 names an element of the same block; an entry 1024 + d * 128 + j names the j-th received trace of group d of extended; each of these 512 slots is named by face 0 of exactly one element of the block. `operator`: a skew-symmetric matrix minus a diagonal of positive damping rates.
All inputs are finite; a program needn't handle non-finite values.
Results may differ from a plain program's by a relative error of at most 0.0003.
Values sent between devices are 32-bit elements; how exact they have to be, the bound alone decides.
No kernel may reach another device: no remote copies, remote signals or barrier semaphores. Data moves between devices by JAX's collectives and lax.ppermute only.
A program may use at most 64 MiB of HBM per device.

v0:
```python
import functools
import math

import jax
import jax.numpy as jnp
from jax import lax
from jax.experimental import pallas as pl
from jax.experimental.pallas import tpu as pltpu
from jax.sharding import PartitionSpec as P

LEVELS = 4
SUBSTEPS = 2
TERMS = 4
BLOCK = 384
LANES = 128
NO_GROUP = 1 << 20

f32, bf16, i32 = jnp.float32, jnp.bfloat16, jnp.int32
precise = lax.Precision.HIGHEST


def rounded_up(size, unit):
    return -(-size // unit) * unit


def taylor_weights():
    once = [1.0 / math.factorial(k) for k in range(TERMS + 1)]
    whole = [1.0]
    for _ in range(SUBSTEPS):
        longer = [0.0] * (len(whole) + TERMS)
        for i, a in enumerate(whole):
            for j, b in enumerate(once):
                longer[i + j] += a * b
        whole = longer
    return whole


WEIGHTS = taylor_weights()
POWERS = len(WEIGHTS) - 1


def split(values):
    high = values.astype(bf16)
    return high, (values - high.astype(f32)).astype(bf16)


def stacked_columns(values):
    high, low = split(values)
    return jnp.concatenate([high, low, high], axis=0)


def stacked_matrix(values):
    high = values.astype(bf16).astype(f32)
    low = values - high
    return jnp.concatenate([high, high, low], axis=1).astype(bf16)


def product(matrix, columns):
    return jnp.dot(matrix, columns, preferred_element_type=f32)


def pad_rows(values, rows):
    short = rows - values.shape[0]
    if short == 0:
        return values
    return jnp.concatenate([values, jnp.zeros((short,) + values.shape[1:], values.dtype)], axis=0)


def pick(blocks, index, which, start=None):
    result = start
    for number, read in blocks:
        table = read()
        lane = jnp.broadcast_to(index & (LANES - 1), table.shape)
        got = jnp.take_along_axis(table, lane, axis=1, mode="promise_in_bounds")
        if result is None:
            result = got
        else:
            result = jnp.where(jnp.broadcast_to(which, table.shape) == number, got, result)
    return result


def ref_blocks(ref, count, rows=None):
    def reader(b):
        def read():
            values = ref[:, b * LANES:(b + 1) * LANES]
            return values if rows is None else pad_rows(values, rows)
        return read
    return [(b, reader(b)) for b in range(count)]


def value_blocks(values):
    return [
        (b, functools.partial(lambda b: values[:, b * LANES:(b + 1) * LANES], b))
        for b in range(values.shape[1] // LANES)
    ]


def first_kernel(fields_ref, trace_ref, send_ref, out_ref, *sends):
    rows = out_ref.shape[0]
    trace = pad_rows(trace_ref[...], rows)
    trace_high, trace_low = split(trace)
    both = jnp.concatenate([trace_high, trace_low], axis=0)
    high, low = split(fields_ref[...])
    upper = product(both, high)
    out_ref[...] = upper[:rows] + upper[rows:] + product(trace_high, low)
    count = out_ref.shape[1] // LANES
    for group, send in enumerate(sends):
        index = send_ref[group:group + 1, :]
        send[...] = pick(ref_blocks(out_ref, count), index, index >> 7)


def level_starts(sizes_ref):
    starts = [jnp.int32(0)]
    for level in range(LEVELS - 1):
        starts.append(starts[-1] + sizes_ref[level])
    return starts


def local_part(level, members_ref, joined_ref, fields_ref, out_ref, heights_ref, own_ref, faces_ref, weights_ref):
    faces = faces_in(joined_ref)
    count = fields_ref.shape[1] // LANES
    rows, trace_rows = own_ref.shape[0], out_ref.shape[0]
    for block in range(BLOCK // LANES):
        here = slice(block * LANES, (block + 1) * LANES)
        there = slice(level * BLOCK + block * LANES, level * BLOCK + (block + 1) * LANES)
        index = members_ref[0:1, there]
        own_ref[:, here] = pick(ref_blocks(fields_ref, count, rows), index, index >> 7)
        for face in range(faces):
            index = joined_ref[face:face + 1, there]
            faces_ref[face * trace_rows:(face + 1) * trace_rows, here] = pick(
                ref_blocks(out_ref, count), index, index >> 7)
        pattern = jnp.broadcast_to(joined_ref[faces:faces + 1, there], (8, LANES))
        height = jnp.take_along_axis(
            jnp.broadcast_to(heights_ref[...], (8, LANES)), pattern, axis=1, mode="promise_in_bounds")
        weight = jnp.ones((8, LANES), f32)
        for power in range(1, POWERS + 1):
            weight = weight * height
            weights_ref[power - 1:power, here] = weight[0:1] * WEIGHTS[power]


def faces_in(joined_ref):
    return joined_ref.shape[0] // 2


def matrix_powers(operator_ref, trace_ref, lift_ref, grow_ref, trace_grow_ref, lift_out_ref, rows, trace_rows):
    comp = operator_ref.shape[0]
    operator = pad_rows(operator_ref[...], rows)
    operator = jnp.concatenate([operator, jnp.zeros((rows, rows - comp), f32)], axis=1)
    trace = pad_rows(trace_ref[...], trace_rows)
    trace = jnp.concatenate([trace, jnp.zeros((trace_rows, rows - comp), f32)], axis=1)
    powers = operator
    have = 1
    while have < POWERS:
        take = min(have, POWERS - have)
        more = jnp.dot(powers[:take * rows], powers[(have - 1) * rows:have * rows],
                       precision=precise, preferred_element_type=f32)
        powers = jnp.concatenate([powers, more], axis=0)
        have += take
    grow_ref[...] = stacked_matrix(powers)
    traces = [trace]
    for power in range(POWERS):
        traces.append(jnp.dot(trace, powers[power * rows:(power + 1) * rows],
                              precision=precise, preferred_element_type=f32))
    trace_grow_ref[...] = stacked_matrix(jnp.concatenate(traces, axis=0))
    faces, tall, wide = lift_ref.shape
    lift = jnp.concatenate([
        jnp.concatenate([pad_rows(lift_ref[face], rows), jnp.zeros((rows, trace_rows - wide), f32)], axis=1)
        for face in range(faces)
    ], axis=1)
    lift_out_ref[...] = stacked_matrix(lift)


def plan_kernel(sizes_ref, fields_ref, order_ref, pattern_ref, neighbours_ref, send_ref, heights_ref,
                operator_ref, trace_ref, lift_ref, out_ref,
                members_ref, joined_ref, places_ref, send_places_ref, own_ref, faces_ref, weights_ref,
                grow_ref, trace_grow_ref, lift_out_ref, columns_ref):
    elements = fields_ref.shape[1]
    count = elements // LANES
    faces = neighbours_ref.shape[0]
    starts = level_starts(sizes_ref)
    order = order_ref[...]
    wide_order = jnp.broadcast_to(order, (8, elements))
    table = jnp.concatenate(
        [neighbours_ref[...], pattern_ref[...], jnp.zeros((faces - 1, elements), i32)], axis=0)
    for level in range(LEVELS):
        shift = jnp.where(starts[level] == 0, 0, elements - starts[level])
        members_ref[:, level * BLOCK:(level + 1) * BLOCK] = pltpu.roll(wide_order, shift, 1)[:, :BLOCK]
    for block in range(LEVELS * BLOCK // LANES):
        here = slice(block * LANES, (block + 1) * LANES)
        index = members_ref[:, here]
        joined_ref[:, here] = pick(value_blocks(table), index, index >> 7)
    for block in range(count):
        here = slice(block * LANES, (block + 1) * LANES)
        columns_ref[here, :] = jnp.transpose(jnp.broadcast_to(order[:, here], (LANES, LANES)))
    rank = lax.broadcasted_iota(i32, (elements, LANES), 0).astype(f32)
    for block in range(count):
        here = slice(block * LANES, (block + 1) * LANES)
        number = lax.broadcasted_iota(i32, (elements, LANES), 1) + block * LANES
        found = jnp.where(columns_ref[...] == number, rank, 0.0)
        place = jnp.sum(found, axis=0, keepdims=True).astype(i32)
        at = place
        for level in range(1, LEVELS):
            at = jnp.where(place >= starts[level], place - starts[level] + level * BLOCK, at)
        places_ref[:, here] = jnp.broadcast_to(at, (8, LANES))
    index = pad_rows(send_ref[...], 8)
    send_places_ref[...] = pick(ref_blocks(places_ref, count), index, index >> 7)
    matrix_powers(operator_ref, trace_ref, lift_ref, grow_ref, trace_grow_ref, lift_out_ref,
                  own_ref.shape[0], out_ref.shape[0])
    local_part(0, members_ref, joined_ref, fields_ref, out_ref, heights_ref, own_ref, faces_ref, weights_ref)


def grown(loaded, matrix_ref, weights_ref, rows, first):
    stacked = product(matrix_ref[...], stacked_columns(loaded))
    total = first if first is not None else stacked[:rows]
    skip = 0 if first is not None else 1
    for power in range(1, POWERS + 1):
        part = stacked[(power - 1 + skip) * rows:(power + skip) * rows]
        total = total + part * weights_ref[power - 1:power, :]
    return total


def settle(level, new_ref, places_ref, before, rows, block):
    here = slice(block * LANES, (block + 1) * LANES)
    index = places_ref[0:1, here]
    which = (index >> 7) - level * (BLOCK // LANES)
    return pick(ref_blocks(new_ref, BLOCK // LANES), index, which, before)


def between_kernel(level, members_ref, joined_ref, places_ref, fields_ref, old_out_ref, new_trace_ref,
                   heights_ref, loaded_ref, old_weights_ref, grow_ref, *rest):
    if level > 1:
        advanced_ref, rest = rest[0], rest[1:]
    out_ref, own_ref, faces_ref, weights_ref, new_advanced_ref, new_ref = rest
    elements = fields_ref.shape[1]
    for block in range(elements // LANES):
        here = slice(block * LANES, (block + 1) * LANES)
        out_ref[:, here] = settle(level - 1, new_trace_ref, places_ref, old_out_ref[:, here], None, block)
    local_part(level, members_ref, joined_ref, fields_ref, out_ref, heights_ref, own_ref, faces_ref, weights_ref)
    loaded = loaded_ref[...]
    new_ref[...] = grown(loaded, grow_ref, old_weights_ref, loaded.shape[0], loaded)
    for block in range(elements // LANES):
        here = slice(block * LANES, (block + 1) * LANES)
        before = advanced_ref[:, here] if level > 1 else None
        new_advanced_ref[:, here] = settle(level - 1, new_ref, places_ref, before, None, block)


def load(level, groups_ref, received, joined_ref, own_ref, faces_ref, lift_ref):
    faces = faces_in(joined_ref)
    trace_rows = faces_ref.shape[0] // faces
    own_groups = groups_ref[len(received)]
    parts = []
    for face in range(faces):
        across = []
        for block in range(BLOCK // LANES):
            here = slice(block * LANES, (block + 1) * LANES)
            there = slice(level * BLOCK + block * LANES, level * BLOCK + (block + 1) * LANES)
            index = joined_ref[face:face + 1, there]
            group = (index >> 7) - own_groups
            inner = faces_ref[face * trace_rows:(face + 1) * trace_rows, here]
            start = jnp.where(jnp.broadcast_to(group, inner.shape) >= 0, 0.0, inner)
            blocks = [(groups_ref[i], functools.partial(lambda ref: ref[...], ref))
                      for i, ref in enumerate(received)]
            across.append(pick(blocks, index, group, start))
        parts.append(jnp.concatenate(across, axis=1))
    return own_ref[...] + product(lift_ref[...], stacked_columns(jnp.concatenate(parts, axis=0)))


def level_kernel(level, messages, groups_ref, joined_ref, own_ref, faces_ref, weights_ref, lift_ref, trace_grow_ref,
                 send_places_ref, *rest):
    received, rest = rest[:messages], rest[messages:]
    sent, rest = rest[:messages], rest[messages:]
    loaded_ref, new_trace_ref, sends = rest[0], rest[1], rest[2:]
    loaded = load(level, groups_ref, received, joined_ref, own_ref, faces_ref, lift_ref)
    new_trace_ref[...] = grown(loaded, trace_grow_ref, weights_ref, new_trace_ref.shape[0], None)
    for group, (before, send) in enumerate(zip(sent, sends)):
        index = send_places_ref[group:group + 1, :]
        which = (index >> 7) - level * (BLOCK // LANES)
        send[...] = pick(ref_blocks(new_trace_ref, BLOCK // LANES), index, which, before[...])
    loaded_ref[...] = loaded


def last_kernel(level, messages, groups_ref, joined_ref, own_ref, faces_ref, weights_ref, lift_ref, grow_ref,
                places_ref, advanced_ref, *rest):
    received, (final_ref, new_ref) = rest[:messages], rest[messages:]
    loaded = load(level, groups_ref, received, joined_ref, own_ref, faces_ref, lift_ref)
    new_ref[...] = grown(loaded, grow_ref, weights_ref, loaded.shape[0], loaded)
    for block in range(final_ref.shape[1] // LANES):
        here = slice(block * LANES, (block + 1) * LANES)
        done = settle(level, new_ref, places_ref, advanced_ref[:, here], None, block)
        final_ref[:, here] = done[:final_ref.shape[0]]


def call(kernel, name, flops, scalars, vectors, outs, scratch=()):
    vmem, smem = pl.BlockSpec(memory_space=pltpu.VMEM), pl.BlockSpec(memory_space=pltpu.SMEM)
    return pl.pallas_call(
        kernel,
        out_shape=tuple(jax.ShapeDtypeStruct(shape, dtype) for shape, dtype in outs),
        in_specs=[smem] * len(scalars) + [vmem] * len(vectors),
        out_specs=tuple([vmem] * len(outs)),
        scratch_shapes=[pltpu.VMEM(shape, dtype) for shape, dtype in scratch],
        compiler_params=pltpu.CompilerParams(vmem_limit_bytes=16 * 1024 * 1024),
        cost_estimate=pl.CostEstimate(flops=flops, bytes_accessed=1 << 20, transcendentals=0),
        name=name,
    )(*scalars, *vectors)


def swap_plan(axis, periodic, low_group, high_group):
    count = lax.axis_size(axis)
    index = lax.axis_index(axis)
    odd = (index % 2) == 1
    first = [(i, i ^ 1) for i in range(count)]
    plan = [(first, jnp.where(odd, high_group, low_group), jnp.where(odd, low_group, high_group))]
    if count > 2 or periodic:
        second = [(i, (i + 1) % count if i % 2 else (i - 1) % count) for i in range(count)]
        came = jnp.where(odd, high_group, low_group)
        if not periodic:
            came = jnp.where((index == 0) | (index == count - 1), NO_GROUP, came)
        plan.append((second, jnp.where(odd, low_group, high_group), came))
    return plan


def body(fields, pattern, tent_order, level_sizes, send_rows, neighbours, operator, trace_map, lift_map, tent_height):
    fields, order, sizes = fields[0, 0], tent_order[0], level_sizes[0, 0]
    faces_of = neighbours[0, 0]
    comp, elements = fields.shape
    faces, trace = lift_map.shape[0], trace_map.shape[0]
    rows, trace_rows = rounded_up(comp, 16), rounded_up(trace, 16)
    padded = LEVELS * BLOCK
    bnd = send_rows.shape[-1]

    swaps = [("sector",) + one for one in swap_plan("sector", True, 0, 1)]
    swaps += [("radial",) + one for one in swap_plan("radial", False, 2, 3)]
    messages = len(swaps)
    send_list = jnp.concatenate([
        lax.dynamic_slice_in_dim(send_rows[0, 0], group, 1, axis=0) for _, _, group, _ in swaps])
    groups = jnp.stack([came for _, _, _, came in swaps] + [jnp.int32(elements // LANES)]).astype(i32)
    heights = jnp.pad(tent_height, (0, LANES - tent_height.shape[0]))[None]

    def exchange(sent):
        return [lax.ppermute(one, axis, pairs) for one, (axis, pairs, _, _) in zip(sent, swaps)]

    message = ((trace_rows, bnd), f32)
    own, face_stack = ((rows, BLOCK), f32), ((faces * trace_rows, BLOCK), f32)
    weight, table = ((POWERS, BLOCK), f32), ((trace_rows, elements), f32)
    whole = ((rows, elements), f32)

    out, *sent = call(first_kernel, "first", 10 ** 8, [], [fields, trace_map, send_list], [table] + [message] * messages)
    received = exchange(sent)
    members, joined, places, send_places, mine, inner, weights, grow, trace_grow, lift = call(
        plan_kernel, "plan", 2 * 10 ** 9, [sizes],
        [fields, order, pattern[0], faces_of, send_list, heights, operator, trace_map, lift_map, out],
        [((8, padded), i32), ((2 * faces, padded), i32), ((8, elements), i32), ((8, bnd), i32), own, face_stack, weight,
         ((POWERS * rows, 3 * rows), bf16), (((POWERS + 1) * trace_rows, 3 * rows), bf16),
         ((rows, 3 * faces * trace_rows), bf16)],
        [((elements, LANES), i32)])
    advanced = []
    for level in range(LEVELS):
        if level == LEVELS - 1:
            final, = call(
                functools.partial(last_kernel, level, messages), "last", 10 ** 9, [groups],
                [joined, mine, inner, weights, lift, grow, places] + advanced + received,
                [((comp, elements), f32)], [own])
            return final[None, None]
        loaded, new_trace, *sent = call(
            functools.partial(level_kernel, level, messages), "level", 10 ** 8, [groups],
            [joined, mine, inner, weights, lift, trace_grow, send_places] + received + sent,
            [own, ((trace_rows, BLOCK), f32)] + [message] * messages)
        received = exchange(sent)
        out, mine, inner, weights, *advanced = call(
            functools.partial(between_kernel, level + 1), "between", 2 * 10 ** 9, [],
            [members, joined, places, fields, out, new_trace, heights, loaded, weights, grow] + advanced,
            [table, own, face_stack, weight, whole], [own])


def solution(mesh):
    in_specs = (
        P("sector", "radial", None, None),
        P("sector", "radial", None),
        P("sector", "radial", None),
        P("sector", "radial", None),
        P("sector", "radial", None, None),
        P("sector", "radial", None, None),
        P(),
        P(),
        P(),
        P(),
    )
    out_specs = P("sector", "radial", None, None)
    return jax.shard_map(body, mesh=mesh, in_specs=in_specs, out_specs=out_specs, check_vma=False)
```

profile of v0, /device:TPU:0, one launch (start us, length us, event | category | flops | bytes accessed | tf_op | source)
XLA Modules:
  0.0 43.2 jit_solution(10934245103573143522)
XLA Ops:
  0.0 0.0 copy-start.7
  0.0 0.0 copy-start
  0.0 0.0 copy-start.8
  0.0 0.0 copy-start.6
  0.0 0.0 copy-start.1
  0.0 0.0 copy-start.2
  0.0 0.0 copy-start.3
  0.0 0.0 copy-start.4
  0.0 0.0 copy-start.5
  0.1 1.3 %copy.15 = f32[1,1,140,1024]{3,2,1,0:T(8,128)S(1)} copy(f32[1,1,140,1024]{3,1,2,0:T(1,128)} %param.10) | data formatting | bytes 1146880
  1.3 0.0 copy-done.7
  1.4 0.0 copy-done
  1.4 0.6 %first.1 = (f32[64,1024]{1,0:T(8,128)S(1)}, f32[64,128]{1,0:T(8,128)S(1)}, f32[64,128]{1,0:T(8,128)S(1)}, f32[64,128]{1,0:T(8,128)S(1)}) custom-call(f32[140,1024]{1,0:T(8,128)S(1)} %bitcast.19, f32[60,140]{1,0:T(8,128)S(1)} %copy-done, s32[3,128]{1,0:T(4,128)S(1)} %pad_add_fusion.send_ref), custom_call_target="tpu_custom_call" | custom-call | flops 100000000 | bytes 1048576 | tf_op jit(solution)/shard_map/first/pallas_call | solution.py:295
  2.0 0.6 %collective-permute-start = (f32[64,128]{1,0:T(8,128)S(1)}, f32[64,128]{1,0:T(8,128)S(1)}, u32[]{:S(2)}, u32[]{:S(2)}) collective-permute-start(f32[64,128]{1,0:T(8,128)S(1)} %get-tuple-element.58.rest_3_), channel_id=1, source_target_pairs={{0,2},{2,0},{4,6},{6,4},{8,10},{10,8},{12,14},{14,12},{16,18},{18,... | collective-permute-start | bytes 98312 | tf_op jit(solution)/shard_map/ppermute | solution.py:340
  2.6 5.7 %collective-permute-start.1 = (f32[64,128]{1,0:T(8,128)S(1)}, f32[64,128]{1,0:T(8,128)S(1)}, u32[]{:S(2)}, u32[]{:S(2)}) collective-permute-start(f32[64,128]{1,0:T(8,128)S(1)} %get-tuple-element.59.rest_4_), channel_id=1, source_target_pairs={{0,30},{2,4},{4,2},{6,8},{8,6},{10,12},{12,10},{14,16},{16,14},{18... | collective-permute-start | bytes 98312 | tf_op jit(solution)/shard_map/ppermute | solution.py:340
  8.3 1.5 %collective-permute-start.2 = (f32[64,128]{1,0:T(8,128)S(1)}, f32[64,128]{1,0:T(8,128)S(1)}, u32[]{:S(2)}, u32[]{:S(2)}) collective-permute-start(f32[64,128]{1,0:T(8,128)S(1)} %get-tuple-element.60.rest_5_), channel_id=1, source_target_pairs={{0,1},{1,0},{2,3},{3,2},{4,5},{5,4},{6,7},{7,6},{8,9},{9,8},{10,11... | collective-permute-start | bytes 98312 | tf_op jit(solution)/shard_map/ppermute | solution.py:340
  9.8 0.0 copy-done.8
  9.8 0.0 copy-done.6
  9.8 0.2 copy.11.lift_ref
  10.0 0.0 copy-done.1
  10.0 0.0 copy-done.2
  10.0 0.0 copy-done.3
  10.0 0.0 copy-done.4
  10.0 0.0 copy-done.5
  10.0 3.7 %plan.1 = (s32[8,1536]{1,0:T(8,128)S(1)}, s32[8,1536]{1,0:T(8,128)S(1)}, s32[8,1024]{1,0:T(8,128)S(1)}, s32[8,128]{1,0:T(8,128)S(1)}, f32[144,384]{1,0:T(8,128)S...) custom-call(s32[4]{0:T(128)S(1)} %bitcast.28, ...), custom_call_target="tpu_custom_call" | custom-call | flops 2000000000 | bytes 1048576 | tf_op jit(solution)/shard_map/plan/pallas_call | solution.py:295
  13.7 0.1 pad_add_fusion.1.groups_ref
  13.8 0.0 collective-permute-done.rest_0_
  13.8 0.0 collective-permute-done.1.rest_1_
  13.8 0.0 collective-permute-done.2.rest_2_
  13.8 2.2 %level.3 = (f32[144,384]{1,0:T(8,128)S(1)}, f32[64,384]{1,0:T(8,128)S(1)}, f32[64,128]{1,0:T(8,128)S(1)}, f32[64,128]{1,0:T(8,128)S(1)}, f32[64,128]{1,0:T(8,128)S(1)}) custom-call(s32[4]{0:T(128)S(1)} %pad_add_fusion.1.groups_ref, s32[8,1536]{1,0:T(8,128)S(1)} %get-tuple-element.49.joined_ref, f32[144,384]{1,0:T(8,128)S(1)} %get-tuple-element.52.own_ref, ...), custom_call_target="tpu_custom_call" | custom-call | flops 100000000 | bytes 1048576 | tf_op jit(solution)/shard_map/level/pallas_call | solution.py:295
  16.0 0.1 collective-permute-start.3
  16.1 0.6 %collective-permute-start.4 = (f32[64,128]{1,0:T(8,128)S(1)}, f32[64,128]{1,0:T(8,128)S(1)}, u32[]{:S(2)}, u32[]{:S(2)}) collective-permute-start(f32[64,128]{1,0:T(8,128)S(1)} %get-tuple-element.69.rest_4_), channel_id=1, source_target_pairs={{0,30},{2,4},{4,2},{6,8},{8,6},{10,12},{12,10},{14,16},{16,14},{18... | collective-permute-start | bytes 98312 | tf_op jit(solution)/shard_map/ppermute | solution.py:340
  16.7 1.4 %collective-permute-start.5 = (f32[64,128]{1,0:T(8,128)S(1)}, f32[64,128]{1,0:T(8,128)S(1)}, u32[]{:S(2)}, u32[]{:S(2)}) collective-permute-start(f32[64,128]{1,0:T(8,128)S(1)} %get-tuple-element.70.rest_5_), channel_id=1, source_target_pairs={{0,1},{1,0},{2,3},{3,2},{4,5},{5,4},{6,7},{7,6},{8,9},{9,8},{10,11... | collective-permute-start | bytes 98312 | tf_op jit(solution)/shard_map/ppermute | solution.py:340
  18.1 2.2 %between.3 = (f32[64,1024]{1,0:T(8,128)S(1)}, f32[144,384]{1,0:T(8,128)S(1)}, f32[256,384]{1,0:T(8,128)S(1)}, f32[8,384]{1,0:T(8,128)S(1)}, f32[144,1024]{1,0:T(8,128)S(1)}) custom-call(s32[8,1536]{1,0:T(8,128)S(1)} %get-tuple-element.50.members_ref, s32[8,1536]{1,0:T(8,128)S(1)} %get-tuple-element.49.joined_ref, ...), custom_call_target="tpu_custom_call" | custom-call | flops 2000000000 | bytes 1048576 | tf_op jit(solution)/shard_map/between/pallas_call | solution.py:295
  20.3 0.0 collective-permute-done.3.rest_0_
  20.3 1.9 %collective-permute-done.4.rest_1_ = f32[64,128]{1,0:T(8,128)S(1)} collective-permute-done((f32[64,128]{1,0:T(8,128)S(1)}, f32[64,128]{1,0:T(8,128)S(1)}, u32[]{:S(2)}, u32[]{:S(2)}) %collective-permute-start.4) | collective-permute-done | bytes 32800 | tf_op jit(solution)/shard_map/ppermute | solution.py:340
  22.2 0.0 collective-permute-done.5.rest_2_
  22.2 2.2 %level.4 = (f32[144,384]{1,0:T(8,128)S(1)}, f32[64,384]{1,0:T(8,128)S(1)}, f32[64,128]{1,0:T(8,128)S(1)}, f32[64,128]{1,0:T(8,128)S(1)}, f32[64,128]{1,0:T(8,128)S(1)}) custom-call(s32[4]{0:T(128)S(1)} %pad_add_fusion.1.groups_ref, s32[8,1536]{1,0:T(8,128)S(1)} %get-tuple-element.49.joined_ref, f32[144,384]{1,0:T(8,128)S(1)} %get-tuple-element.65.own_ref, ...), custom_call_target="tpu_custom_call" | custom-call | flops 100000000 | bytes 1048576 | tf_op jit(solution)/shard_map/level/pallas_call | solution.py:295
  24.4 0.1 collective-permute-start.6
  24.4 1.2 %collective-permute-start.7 = (f32[64,128]{1,0:T(8,128)S(1)}, f32[64,128]{1,0:T(8,128)S(1)}, u32[]{:S(2)}, u32[]{:S(2)}) collective-permute-start(f32[64,128]{1,0:T(8,128)S(1)} %get-tuple-element.79.rest_4_), channel_id=1, source_target_pairs={{0,30},{2,4},{4,2},{6,8},{8,6},{10,12},{12,10},{14,16},{16,14},{18... | collective-permute-start | bytes 98312 | tf_op jit(solution)/shard_map/ppermute | solution.py:340
  25.7 1.2 %collective-permute-start.8 = (f32[64,128]{1,0:T(8,128)S(1)}, f32[64,128]{1,0:T(8,128)S(1)}, u32[]{:S(2)}, u32[]{:S(2)}) collective-permute-start(f32[64,128]{1,0:T(8,128)S(1)} %get-tuple-element.80.rest_5_), channel_id=1, source_target_pairs={{0,1},{1,0},{2,3},{3,2},{4,5},{5,4},{6,7},{7,6},{8,9},{9,8},{10,11... | collective-permute-start | bytes 98312 | tf_op jit(solution)/shard_map/ppermute | solution.py:340
  26.9 2.2 %between.4 = (f32[64,1024]{1,0:T(8,128)S(1)}, f32[144,384]{1,0:T(8,128)S(1)}, f32[256,384]{1,0:T(8,128)S(1)}, f32[8,384]{1,0:T(8,128)S(1)}, f32[144,1024]{1,0:T(8,128)S(1)}) custom-call(s32[8,1536]{1,0:T(8,128)S(1)} %get-tuple-element.50.members_ref, s32[8,1536]{1,0:T(8,128)S(1)} %get-tuple-element.49.joined_ref, ...), custom_call_target="tpu_custom_call" | custom-call | flops 2000000000 | bytes 1048576 | tf_op jit(solution)/shard_map/between/pallas_call | solution.py:295
  29.1 0.0 collective-permute-done.6.rest_0_
  29.1 1.5 %collective-permute-done.7.rest_1_ = f32[64,128]{1,0:T(8,128)S(1)} collective-permute-done((f32[64,128]{1,0:T(8,128)S(1)}, f32[64,128]{1,0:T(8,128)S(1)}, u32[]{:S(2)}, u32[]{:S(2)}) %collective-permute-start.7) | collective-permute-done | bytes 32800 | tf_op jit(solution)/shard_map/ppermute | solution.py:340
  30.5 0.0 collective-permute-done.8.rest_2_
  30.5 2.2 %level.5 = (f32[144,384]{1,0:T(8,128)S(1)}, f32[64,384]{1,0:T(8,128)S(1)}, f32[64,128]{1,0:T(8,128)S(1)}, f32[64,128]{1,0:T(8,128)S(1)}, f32[64,128]{1,0:T(8,128)S(1)}) custom-call(s32[4]{0:T(128)S(1)} %pad_add_fusion.1.groups_ref, s32[8,1536]{1,0:T(8,128)S(1)} %get-tuple-element.49.joined_ref, f32[144,384]{1,0:T(8,128)S(1)} %get-tuple-element.75.own_ref, ...), custom_call_target="tpu_custom_call" | custom-call | flops 100000000 | bytes 1048576 | tf_op jit(solution)/shard_map/level/pallas_call | solution.py:295
  32.7 1.2 %collective-permute-start.10 = (f32[64,128]{1,0:T(8,128)S(1)}, f32[64,128]{1,0:T(8,128)S(1)}, u32[]{:S(2)}, u32[]{:S(2)}) collective-permute-start(f32[64,128]{1,0:T(8,128)S(1)} %get-tuple-element.89), channel_id=1, source_target_pairs={{0,30},{2,4},{4,2},{6,8},{8,6},{10,12},{12,10},{14,16},{16,14},{18... | collective-permute-start | bytes 98312 | tf_op jit(solution)/shard_map/ppermute | solution.py:340
  33.9 1.2 %collective-permute-start.11 = (f32[64,128]{1,0:T(8,128)S(1)}, f32[64,128]{1,0:T(8,128)S(1)}, u32[]{:S(2)}, u32[]{:S(2)}) collective-permute-start(f32[64,128]{1,0:T(8,128)S(1)} %get-tuple-element.90), channel_id=1, source_target_pairs={{0,1},{1,0},{2,3},{3,2},{4,5},{5,4},{6,7},{7,6},{8,9},{9,8},{10,11... | collective-permute-start | bytes 98312 | tf_op jit(solution)/shard_map/ppermute | solution.py:340
  35.2 0.0 collective-permute-start.9
  35.2 2.3 %between.5 = (f32[64,1024]{1,0:T(8,128)}, f32[144,384]{1,0:T(8,128)S(1)}, f32[256,384]{1,0:T(8,128)S(1)}, f32[8,384]{1,0:T(8,128)S(1)}, f32[144,1024]{1,0:T(8,128)S(1)}) custom-call(s32[8,1536]{1,0:T(8,128)S(1)} %get-tuple-element.50.members_ref, s32[8,1536]{1,0:T(8,128)S(1)} %get-tuple-element.49.joined_ref, s32[8,1024]{1,0:T(8,128)S(1)} %get-tuple-element.51.places_ref, ...), custom_call_target="tpu_custom_call" | custom-call | flops 2000000000 | bytes 1048576 | tf_op jit(solution)/shard_map/between/pallas_call | solution.py:295
  37.5 1.3 %collective-permute-done.10.rest_1_ = f32[64,128]{1,0:T(8,128)S(1)} collective-permute-done((f32[64,128]{1,0:T(8,128)S(1)}, f32[64,128]{1,0:T(8,128)S(1)}, u32[]{:S(2)}, u32[]{:S(2)}) %collective-permute-start.10) | collective-permute-done | bytes 32800 | tf_op jit(solution)/shard_map/ppermute | solution.py:340
  38.8 0.0 collective-permute-done.11.rest_2_
  38.8 0.0 collective-permute-done.9.rest_0_
  38.8 2.9 %last.1 = f32[140,1024]{1,0:T(8,128)S(1)} custom-call(s32[4]{0:T(128)S(1)} %pad_add_fusion.1.groups_ref, s32[8,1536]{1,0:T(8,128)S(1)} %get-tuple-element.49.joined_ref, f32[144,384]{1,0:T(8,128)S(1)} %get-tuple-element.84.own_ref, f32[256,384]{1,0:T(8,128)S(1)} %get-tuple-element.85.faces_ref, f32[8,384]{1,0:T(8,128)S(1)} %get-tuple-element.86.weights_ref, ...), custom_call_target="tpu_custom_call" | custom-call | flops 1000000000 | bytes 1048576 | tf_op jit(solution)/shard_map/last/pallas_call | solution.py:295
  41.8 1.4 %copy.12 = f32[1,1,140,1024]{3,1,2,0:T(1,128)} copy(f32[1,1,140,1024]{3,2,1,0:T(8,128)S(1)} %bitcast.24) | data formatting | bytes 1146880 | tf_op jit(solution)/shard_map/broadcast_in_dim | solution.py:363
  (3 shorter events, 0.0 us)
Async XLA Ops:
  0.0 1.3 %copy-start.7 = (s32[1,1,4,128]{3,2,1,0:T(4,128)S(1)}, s32[1,1,4,128]{3,2,1,0:T(4,128)}, u32[]{:S(2)}) copy-start(s32[1,1,4,128]{3,2,1,0:T(4,128)} %param.14) | copy-start | bytes 6148
  0.0 1.4 %copy-start = (f32[60,140]{1,0:T(8,128)S(1)}, f32[60,140]{1,0:T(8,128)}, u32[]{:S(2)}) copy-start(f32[60,140]{1,0:T(8,128)} %trace_ref.3) | copy-start | bytes 100804
  0.0 9.8 %copy-start.8 = (f32[16]{0:T(128)S(1)}, f32[16]{0:T(128)}, u32[]{:S(2)}) copy-start(f32[16]{0:T(128)} %param.19) | copy-start | bytes 196
  0.0 9.8 %copy-start.6 = (f32[4,140,60]{1,0,2:T(4,128)S(1)}, f32[4,140,60]{1,0,2:T(4,128)}, u32[]{:S(2)}) copy-start(f32[4,140,60]{1,0,2:T(4,128)} %param.18) | copy-start | bytes 403204
  0.0 10.0 %copy-start.1 = (f32[140,140]{1,0:T(8,128)S(1)}, f32[140,140]{1,0:T(8,128)}, u32[]{:S(2)}) copy-start(f32[140,140]{1,0:T(8,128)} %operator_ref.1) | copy-start | bytes 235204
  0.0 10.0 %copy-start.2 = (s32[1,1,4,1024]{3,2,1,0:T(4,128)S(1)}, s32[1,1,4,1024]{3,2,1,0:T(4,128)}, u32[]{:S(2)}) copy-start(s32[1,1,4,1024]{3,2,1,0:T(4,128)} %param.15) | copy-start | bytes 49156
  0.0 10.0 %copy-start.3 = (s32[1,1,1024]{2,1,0:T(1,128)S(1)}, s32[1,1,1024]{2,1,0:T(1,128)}, u32[]{:S(2)}) copy-start(s32[1,1,1024]{2,1,0:T(1,128)} %param.12) | copy-start | bytes 12292
  0.0 10.0 %copy-start.4 = (s32[1,1,1024]{2,1,0:T(1,128)S(1)}, s32[1,1,1024]{2,1,0:T(1,128)}, u32[]{:S(2)}) copy-start(s32[1,1,1024]{2,1,0:T(1,128)} %param.11) | copy-start | bytes 12292
  0.0 10.0 %copy-start.5 = (s32[1,1,4]{2,1,0:T(1,128)S(1)}, s32[1,1,4]{2,1,0:T(1,128)}, u32[]{:S(2)}) copy-start(s32[1,1,4]{2,1,0:T(1,128)} %param.13) | copy-start | bytes 52
  2.0 11.8 %collective-permute-start = (f32[64,128]{1,0:T(8,128)S(1)}, f32[64,128]{1,0:T(8,128)S(1)}, u32[]{:S(2)}, u32[]{:S(2)}) collective-permute-start(f32[64,128]{1,0:T(8,128)S(1)} %get-tuple-element.58.rest_3_), channel_id=1, source_target_pairs={{0,2},{2,0},{4,6},{6,4},{8,10},{10,8},{12,14},{14,12},{16,18},{18,... | collective-permute-start | bytes 98312 | tf_op jit(solution)/shard_map/ppermute | solution.py:340
  2.6 11.2 %collective-permute-start.1 = (f32[64,128]{1,0:T(8,128)S(1)}, f32[64,128]{1,0:T(8,128)S(1)}, u32[]{:S(2)}, u32[]{:S(2)}) collective-permute-start(f32[64,128]{1,0:T(8,128)S(1)} %get-tuple-element.59.rest_4_), channel_id=1, source_target_pairs={{0,30},{2,4},{4,2},{6,8},{8,6},{10,12},{12,10},{14,16},{16,14},{18... | collective-permute-start | bytes 98312 | tf_op jit(solution)/shard_map/ppermute | solution.py:340
  8.3 5.5 %collective-permute-start.2 = (f32[64,128]{1,0:T(8,128)S(1)}, f32[64,128]{1,0:T(8,128)S(1)}, u32[]{:S(2)}, u32[]{:S(2)}) collective-permute-start(f32[64,128]{1,0:T(8,128)S(1)} %get-tuple-element.60.rest_5_), channel_id=1, source_target_pairs={{0,1},{1,0},{2,3},{3,2},{4,5},{5,4},{6,7},{7,6},{8,9},{9,8},{10,11... | collective-permute-start | bytes 98312 | tf_op jit(solution)/shard_map/ppermute | solution.py:340
  16.0 4.3 %collective-permute-start.3 = (f32[64,128]{1,0:T(8,128)S(1)}, f32[64,128]{1,0:T(8,128)S(1)}, u32[]{:S(2)}, u32[]{:S(2)}) collective-permute-start(f32[64,128]{1,0:T(8,128)S(1)} %get-tuple-element.68.rest_3_), channel_id=1, source_target_pairs={{0,2},{2,0},{4,6},{6,4},{8,10},{10,8},{12,14},{14,12},{16,18},{18,... | collective-permute-start | bytes 98312 | tf_op jit(solution)/shard_map/ppermute | solution.py:340
  16.1 6.1 %collective-permute-start.4 = (f32[64,128]{1,0:T(8,128)S(1)}, f32[64,128]{1,0:T(8,128)S(1)}, u32[]{:S(2)}, u32[]{:S(2)}) collective-permute-start(f32[64,128]{1,0:T(8,128)S(1)} %get-tuple-element.69.rest_4_), channel_id=1, source_target_pairs={{0,30},{2,4},{4,2},{6,8},{8,6},{10,12},{12,10},{14,16},{16,14},{18... | collective-permute-start | bytes 98312 | tf_op jit(solution)/shard_map/ppermute | solution.py:340
  16.7 5.5 %collective-permute-start.5 = (f32[64,128]{1,0:T(8,128)S(1)}, f32[64,128]{1,0:T(8,128)S(1)}, u32[]{:S(2)}, u32[]{:S(2)}) collective-permute-start(f32[64,128]{1,0:T(8,128)S(1)} %get-tuple-element.70.rest_5_), channel_id=1, source_target_pairs={{0,1},{1,0},{2,3},{3,2},{4,5},{5,4},{6,7},{7,6},{8,9},{9,8},{10,11... | collective-permute-start | bytes 98312 | tf_op jit(solution)/shard_map/ppermute | solution.py:340
  24.4 4.7 %collective-permute-start.6 = (f32[64,128]{1,0:T(8,128)S(1)}, f32[64,128]{1,0:T(8,128)S(1)}, u32[]{:S(2)}, u32[]{:S(2)}) collective-permute-start(f32[64,128]{1,0:T(8,128)S(1)} %get-tuple-element.78.rest_3_), channel_id=1, source_target_pairs={{0,2},{2,0},{4,6},{6,4},{8,10},{10,8},{12,14},{14,12},{16,18},{18,... | collective-permute-start | bytes 98312 | tf_op jit(solution)/shard_map/ppermute | solution.py:340
  24.4 6.1 %collective-permute-start.7 = (f32[64,128]{1,0:T(8,128)S(1)}, f32[64,128]{1,0:T(8,128)S(1)}, u32[]{:S(2)}, u32[]{:S(2)}) collective-permute-start(f32[64,128]{1,0:T(8,128)S(1)} %get-tuple-element.79.rest_4_), channel_id=1, source_target_pairs={{0,30},{2,4},{4,2},{6,8},{8,6},{10,12},{12,10},{14,16},{16,14},{18... | collective-permute-start | bytes 98312 | tf_op jit(solution)/shard_map/ppermute | solution.py:340
  25.7 4.9 %collective-permute-start.8 = (f32[64,128]{1,0:T(8,128)S(1)}, f32[64,128]{1,0:T(8,128)S(1)}, u32[]{:S(2)}, u32[]{:S(2)}) collective-permute-start(f32[64,128]{1,0:T(8,128)S(1)} %get-tuple-element.80.rest_5_), channel_id=1, source_target_pairs={{0,1},{1,0},{2,3},{3,2},{4,5},{5,4},{6,7},{7,6},{8,9},{9,8},{10,11... | collective-permute-start | bytes 98312 | tf_op jit(solution)/shard_map/ppermute | solution.py:340
  32.7 6.1 %collective-permute-start.10 = (f32[64,128]{1,0:T(8,128)S(1)}, f32[64,128]{1,0:T(8,128)S(1)}, u32[]{:S(2)}, u32[]{:S(2)}) collective-permute-start(f32[64,128]{1,0:T(8,128)S(1)} %get-tuple-element.89), channel_id=1, source_target_pairs={{0,30},{2,4},{4,2},{6,8},{8,6},{10,12},{12,10},{14,16},{16,14},{18... | collective-permute-start | bytes 98312 | tf_op jit(solution)/shard_map/ppermute | solution.py:340
  33.9 4.9 %collective-permute-start.11 = (f32[64,128]{1,0:T(8,128)S(1)}, f32[64,128]{1,0:T(8,128)S(1)}, u32[]{:S(2)}, u32[]{:S(2)}) collective-permute-start(f32[64,128]{1,0:T(8,128)S(1)} %get-tuple-element.90), channel_id=1, source_target_pairs={{0,1},{1,0},{2,3},{3,2},{4,5},{5,4},{6,7},{7,6},{8,9},{9,8},{10,11... | collective-permute-start | bytes 98312 | tf_op jit(solution)/shard_map/ppermute | solution.py:340
  35.2 3.7 %collective-permute-start.9 = (f32[64,128]{1,0:T(8,128)S(1)}, f32[64,128]{1,0:T(8,128)S(1)}, u32[]{:S(2)}, u32[]{:S(2)}) collective-permute-start(f32[64,128]{1,0:T(8,128)S(1)} %get-tuple-element.88), channel_id=1, source_target_pairs={{0,2},{2,0},{4,6},{6,4},{8,10},{10,8},{12,14},{14,12},{16,18},{18,... | collective-permute-start | bytes 98312 | tf_op jit(solution)/shard_map/ppermute | solution.py:340
where the time goes:
time: 43.3 us; the launch traced here: 43.2 us
  Pallas kernels  20.4 us (47%)
  starting transfers between devices  14.9 us (34%)
  waiting for transfers between devices  4.68 us (11%)
  local copies, waits for them, and re-layouts  2.92 us (7%)
    pallas_call x9, Pallas kernels, call(): pl.pallas_call(kernel, out_shape=tuple((jax.ShapeDtypeStruct(shape, dtype...  20.4 us
    ppermute x12, starting transfers between devices, exchange(): lax.ppermute(one, axis, pairs)  14.9 us
    ppermute x12, waiting for transfers between devices, exchange(): lax.ppermute(one, axis, pairs)  4.68 us
    unnamed x20, local copies, waits for them, and re-layouts  1.5 us
    broadcast_in_dim x1, local copies, waits for them, and re-layouts, body(): return final[None, None]  1.41 us
  transfers between devices with their start and end apart: 12, of which 3 were waited for; matrix products, arithmetic and copies ran while one was open for 1% of the time, Pallas kernels for 24%

commit v1 on v0

v1 whole, which is shorter than its diff:
```python
import functools
import math

import jax
import jax.numpy as jnp
from jax import lax
from jax.experimental import pallas as pl
from jax.experimental.pallas import tpu as pltpu
from jax.sharding import PartitionSpec as P

LEVELS = 4
SUBSTEPS = 2
TERMS = 4
BLOCK = 384
LANES = 128
NO_GROUP = 1 << 20

f32, bf16, i32 = jnp.float32, jnp.bfloat16, jnp.int32
precise = lax.Precision.HIGHEST


def rounded_up(size, unit):
    return -(-size // unit) * unit


def taylor_weights():
    once = [1.0 / math.factorial(k) for k in range(TERMS + 1)]
    whole = [1.0]
    for _ in range(SUBSTEPS):
        longer = [0.0] * (len(whole) + TERMS)
        for i, a in enumerate(whole):
            for j, b in enumerate(once):
                longer[i + j] += a * b
        whole = longer
    return whole


WEIGHTS = taylor_weights()
POWERS = len(WEIGHTS) - 1


def split(values):
    high = values.astype(bf16)
    return high, (values - high.astype(f32)).astype(bf16)


def stacked_columns(values):
    high, low = split(values)
    return jnp.concatenate([high, low, high], axis=0)


def stacked_matrix(values):
    high = values.astype(bf16).astype(f32)
    low = values - high
    return jnp.concatenate([high, high, low], axis=1).astype(bf16)


def product(matrix, columns):
    return jnp.dot(matrix, columns, preferred_element_type=f32)


def pad_rows(values, rows):
    short = rows - values.shape[0]
    if short == 0:
        return values
    return jnp.concatenate([values, jnp.zeros((short,) + values.shape[1:], values.dtype)], axis=0)


def exact_product(left, right):
    left_high, left_low = split(left)
    right_high, right_low = split(right)
    rows = left.shape[0]
    both = product(jnp.concatenate([left_high, left_low], axis=0), right_high)
    return both[:rows] + both[rows:] + product(left_high, right_low)


def pick(blocks, index, which, start=None):
    result = start
    for number, read in blocks:
        table = read()
        lane = jnp.broadcast_to(index & (LANES - 1), table.shape)
        got = jnp.take_along_axis(table, lane, axis=1, mode="promise_in_bounds")
        if result is None:
            result = got
        else:
            result = jnp.where(jnp.broadcast_to(which, table.shape) == number, got, result)
    return result


def block_at(block):
    return slice(block * LANES, (block + 1) * LANES)


def ref_blocks(ref, count):
    return [(b, functools.partial(lambda b: ref[:, block_at(b)], b)) for b in range(count)]


def value_blocks(values):
    return [(b, functools.partial(lambda b: values[:, block_at(b)], b)) for b in range(values.shape[1] // LANES)]


def row_blocks(table, rows):
    return [
        (b, functools.partial(lambda b: jnp.broadcast_to(table[b:b + 1, :], (rows, LANES)), b))
        for b in range(table.shape[0])
    ]


def summed_powers(stacked, weights_ref, rows, total):
    for power in range(1, POWERS + 1):
        total = total + stacked[(power - 1) * rows:power * rows] * weights_ref[power - 1:power, :]
    return total


def first_kernel(fields_ref, trace_ref, send_ref, columns_ref, out_ref, *sends):
    rows = out_ref.shape[0]
    elements = out_ref.shape[1]
    count = elements // LANES
    comp = fields_ref.shape[0] // count
    trace = pad_rows(trace_ref[...], rows)
    trace_high, trace_low = split(trace)
    both = jnp.concatenate([trace_high, trace_low], axis=0)
    fields = jnp.concatenate([fields_ref[pl.ds(b, comp, stride=count), :] for b in range(count)], axis=1)
    high, low = split(fields)
    upper = product(both, high)
    out_ref[...] = upper[:rows] + upper[rows:] + product(trace_high, low)
    for group, send in enumerate(sends):
        index = send_ref[group:group + 1, :]
        send[...] = pick(ref_blocks(out_ref, count), index, index >> 7)
    columns_ref[...] = pad_rows(fields, columns_ref.shape[0])


def faces_in(joined_ref):
    return joined_ref.shape[0] // 2


def local_part(level, members_ref, joined_ref, columns_ref, out_ref, heights_ref, trace_grow_ref,
               own_ref, faces_ref, weights_ref, base_ref):
    faces = faces_in(joined_ref)
    count = columns_ref.shape[1] // LANES
    trace_rows = out_ref.shape[0]
    for block in range(BLOCK // LANES):
        here = block_at(block)
        there = block_at(level * (BLOCK // LANES) + block)
        index = members_ref[0:1, there]
        own_ref[:, here] = pick(ref_blocks(columns_ref, count), index, index >> 7)
        pattern = jnp.broadcast_to(joined_ref[faces:faces + 1, there], (8, LANES))
        height = jnp.take_along_axis(
            jnp.broadcast_to(heights_ref[...], (8, LANES)), pattern, axis=1, mode="promise_in_bounds")
        weight = jnp.ones((8, LANES), f32)
        for power in range(1, POWERS + 1):
            weight = weight * height
            weights_ref[power - 1:power, here] = weight[0:1] * WEIGHTS[power]
    stacked = product(trace_grow_ref[...], stacked_columns(own_ref[...]))
    for block in range(BLOCK // LANES):
        here = block_at(block)
        there = block_at(level * (BLOCK // LANES) + block)
        for face in range(faces):
            index = joined_ref[face:face + 1, there]
            faces_ref[face * trace_rows:(face + 1) * trace_rows, here] = pick(
                ref_blocks(out_ref, count), index, index >> 7, jnp.zeros((trace_rows, LANES), f32))
    base_ref[...] = summed_powers(stacked[trace_rows:], weights_ref, trace_rows, stacked[:trace_rows])


def matrix_powers(operator_ref, trace_ref, lift_ref, grow_ref, trace_grow_ref, mix_ref, lift_out_ref):
    comp = operator_ref.shape[0]
    faces, _, trace_comp = lift_ref.shape
    rows = lift_out_ref.shape[0]
    trace_rows = trace_grow_ref.shape[0] // (POWERS + 1)
    operator = pad_rows(operator_ref[...], rows)
    operator = jnp.concatenate([operator, jnp.zeros((rows, rows - comp), f32)], axis=1)
    traces = pad_rows(trace_ref[...], trace_rows)
    traces = jnp.concatenate([traces, jnp.zeros((trace_rows, rows - comp), f32)], axis=1)
    lift = jnp.concatenate([
        jnp.concatenate([pad_rows(lift_ref[face], rows), jnp.zeros((rows, trace_rows - trace_comp), f32)], axis=1)
        for face in range(faces)
    ], axis=1)
    powers, have = operator, 1
    while have < POWERS:
        more = exact_product(jnp.concatenate([traces, powers], axis=0), powers[(have - 1) * rows:have * rows])
        traces = jnp.concatenate([traces, more[:have * trace_rows]], axis=0)
        powers = jnp.concatenate([powers, more[have * trace_rows:]], axis=0)
        have *= 2
    traces = jnp.concatenate([traces, exact_product(traces[:trace_rows], powers[-rows:])], axis=0)
    mix_ref[...] = stacked_matrix(exact_product(traces, lift))
    trace_grow_ref[...] = stacked_matrix(traces)
    lift_out_ref[...] = stacked_matrix(lift)
    grow_ref[...] = stacked_matrix(powers)


def plan_kernel(sizes_ref, columns_ref, order_ref, pattern_ref, neighbours_ref, send_ref, heights_ref,
                operator_ref, trace_ref, lift_ref, out_ref,
                members_ref, joined_ref, places_ref, send_places_ref, own_ref, faces_ref, weights_ref, base_ref,
                grow_ref, trace_grow_ref, mix_ref, lift_out_ref):
    elements = columns_ref.shape[1]
    count = elements // LANES
    faces = neighbours_ref.shape[0]
    starts = [jnp.int32(0)]
    for level in range(LEVELS - 1):
        starts.append(starts[-1] + sizes_ref[level])
    wide_order = jnp.broadcast_to(order_ref[...], (8, elements))
    table = jnp.concatenate(
        [neighbours_ref[...], pattern_ref[...], jnp.zeros((faces - 1, elements), i32)], axis=0)
    for level in range(LEVELS):
        shift = jnp.where(starts[level] == 0, 0, elements - starts[level])
        members_ref[:, level * BLOCK:(level + 1) * BLOCK] = pltpu.roll(wide_order, shift, 1)[:, :BLOCK]
    for block in range(LEVELS * BLOCK // LANES):
        index = members_ref[:, block_at(block)]
        joined_ref[:, block_at(block)] = pick(value_blocks(table), index, index >> 7)
    ranks = lax.broadcasted_iota(i32, (count, elements), 1)
    in_block = (wide_order[:count] >> 7) == lax.broadcasted_iota(i32, (count, elements), 0)
    left = jnp.concatenate([
        jnp.where(in_block, ranks >> 5, 0).astype(f32), jnp.where(in_block, ranks & 31, 0).astype(f32)], axis=0)
    at_lane = jnp.broadcast_to(order_ref[...] & (LANES - 1), (LANES, elements)) == lax.broadcasted_iota(
        i32, (LANES, elements), 0)
    rank = lax.dot_general(left.astype(bf16), jnp.where(at_lane, 1.0, 0.0).astype(bf16), (((1,), (1,)), ((), ())),
                           preferred_element_type=f32)
    place = rank[:count].astype(i32) * 32 + rank[count:].astype(i32)
    at = place
    for level in range(1, LEVELS):
        at = jnp.where(place >= starts[level], place - starts[level] + level * BLOCK, at)
    places_ref[...] = at
    index = pad_rows(send_ref[...], 8)
    send_places_ref[...] = pick(row_blocks(at, 8), index, index >> 7)
    matrix_powers(operator_ref, trace_ref, lift_ref, grow_ref, trace_grow_ref, mix_ref, lift_out_ref)
    local_part(0, members_ref, joined_ref, columns_ref, out_ref, heights_ref, trace_grow_ref,
               own_ref, faces_ref, weights_ref, base_ref)


def advanced_columns(own_ref, inflow_ref, lift_ref, grow_ref, weights_ref):
    loaded = own_ref[...] + product(lift_ref[...], stacked_columns(inflow_ref[...]))
    stacked = product(grow_ref[...], stacked_columns(loaded))
    return summed_powers(stacked, weights_ref, loaded.shape[0], loaded)


def settle(level, new_ref, places_ref, before, block):
    index = places_ref[block:block + 1, :]
    which = (index >> 7) - level * (BLOCK // LANES)
    return pick(ref_blocks(new_ref, BLOCK // LANES), index, which, before)


def between_kernel(level, members_ref, joined_ref, places_ref, columns_ref, old_out_ref, new_trace_ref, heights_ref,
                   old_own_ref, inflow_ref, old_weights_ref, lift_ref, grow_ref, trace_grow_ref, *rest):
    if level > 1:
        advanced_ref, rest = rest[0], rest[1:]
    out_ref, own_ref, faces_ref, weights_ref, base_ref, new_advanced_ref, new_ref = rest
    elements = columns_ref.shape[1]
    for block in range(elements // LANES):
        here = block_at(block)
        out_ref[:, here] = settle(level - 1, new_trace_ref, places_ref, old_out_ref[:, here], block)
    local_part(level, members_ref, joined_ref, columns_ref, out_ref, heights_ref, trace_grow_ref,
               own_ref, faces_ref, weights_ref, base_ref)
    new_ref[...] = advanced_columns(old_own_ref, inflow_ref, lift_ref, grow_ref, old_weights_ref)
    for block in range(elements // LANES):
        here = block_at(block)
        before = advanced_ref[:, here] if level > 1 else None
        new_advanced_ref[:, here] = settle(level - 1, new_ref, places_ref, before, block)


def gather_inflow(level, groups_ref, received, joined_ref, faces_ref, inflow_ref):
    faces = faces_in(joined_ref)
    trace_rows = faces_ref.shape[0] // faces
    own_groups = groups_ref[len(received)]
    blocks = [(groups_ref[i], functools.partial(lambda ref: ref[...], ref)) for i, ref in enumerate(received)]
    for block in range(BLOCK // LANES):
        here = block_at(block)
        there = block_at(level * (BLOCK // LANES) + block)
        for face in range(faces):
            part = slice(face * trace_rows, (face + 1) * trace_rows)
            index = joined_ref[face:face + 1, there]
            inflow_ref[part, here] = pick(blocks, index, (index >> 7) - own_groups, faces_ref[part, here])


def level_kernel(level, messages, groups_ref, joined_ref, faces_ref, weights_ref, base_ref, mix_ref, send_places_ref,
                 *rest):
    received, rest = rest[:messages], rest[messages:]
    sent, rest = rest[:messages], rest[messages:]
    inflow_ref, new_trace_ref, sends = rest[0], rest[1], rest[2:]
    trace_rows = new_trace_ref.shape[0]
    gather_inflow(level, groups_ref, received, joined_ref, faces_ref, inflow_ref)
    stacked = product(mix_ref[...], stacked_columns(inflow_ref[...]))
    new_trace_ref[...] = summed_powers(
        stacked[trace_rows:], weights_ref, trace_rows, base_ref[...] + stacked[:trace_rows])
    for group, (before, send) in enumerate(zip(sent, sends)):
        index = send_places_ref[group:group + 1, :]
        which = (index >> 7) - level * (BLOCK // LANES)
        send[...] = pick(ref_blocks(new_trace_ref, BLOCK // LANES), index, which, before[...])


def last_kernel(level, messages, groups_ref, joined_ref, own_ref, faces_ref, weights_ref, lift_ref, grow_ref,
                places_ref, advanced_ref, *rest):
    received, (final_ref, inflow_ref, new_ref) = rest[:messages], rest[messages:]
    gather_inflow(level, groups_ref, received, joined_ref, faces_ref, inflow_ref)
    new_ref[...] = advanced_columns(own_ref, inflow_ref, lift_ref, grow_ref, weights_ref)
    count = places_ref.shape[0]
    comp = final_ref.shape[0] // count
    for block in range(count):
        done = settle(level, new_ref, places_ref, advanced_ref[:, block_at(block)], block)
        final_ref[pl.ds(block, comp, stride=count), :] = done[:comp]


def call(kernel, name, flops, scalars, vectors, outs, scratch=()):
    vmem, smem = pl.BlockSpec(memory_space=pltpu.VMEM), pl.BlockSpec(memory_space=pltpu.SMEM)
    return pl.pallas_call(
        kernel,
        out_shape=tuple(jax.ShapeDtypeStruct(shape, dtype) for shape, dtype in outs),
        in_specs=[smem] * len(scalars) + [vmem] * len(vectors),
        out_specs=tuple([vmem] * len(outs)),
        scratch_shapes=[pltpu.VMEM(shape, dtype) for shape, dtype in scratch],
        compiler_params=pltpu.CompilerParams(vmem_limit_bytes=16 * 1024 * 1024),
        cost_estimate=pl.CostEstimate(flops=flops, bytes_accessed=1 << 20, transcendentals=0),
        name=name,
    )(*scalars, *vectors)


def swap_plan(axis, periodic, low_group, high_group):
    count = lax.axis_size(axis)
    index = lax.axis_index(axis)
    odd = (index % 2) == 1
    first = [(i, i ^ 1) for i in range(count)]
    plan = [(first, jnp.where(odd, high_group, low_group), jnp.where(odd, low_group, high_group))]
    if count > 2 or periodic:
        second = [(i, (i + 1) % count if i % 2 else (i - 1) % count) for i in range(count)]
        came = jnp.where(odd, high_group, low_group)
        if not periodic:
            came = jnp.where((index == 0) | (index == count - 1), NO_GROUP, came)
        plan.append((second, jnp.where(odd, low_group, high_group), came))
    return plan


def body(fields, pattern, tent_order, level_sizes, send_rows, neighbours, operator, trace_map, lift_map, tent_height):
    fields, order, sizes = fields[0, 0], tent_order[0], level_sizes[0, 0]
    faces_of = neighbours[0, 0]
    comp, elements = fields.shape
    faces, trace = lift_map.shape[0], trace_map.shape[0]
    rows, trace_rows = rounded_up(comp, 16), rounded_up(trace, 16)
    padded = LEVELS * BLOCK
    bnd = send_rows.shape[-1]

    swaps = [("sector",) + one for one in swap_plan("sector", True, 0, 1)]
    swaps += [("radial",) + one for one in swap_plan("radial", False, 2, 3)]
    messages = len(swaps)
    send_list = jnp.concatenate([
        lax.dynamic_slice_in_dim(send_rows[0, 0], group, 1, axis=0) for _, _, group, _ in swaps])
    groups = jnp.stack([came for _, _, _, came in swaps] + [jnp.int32(elements // LANES)]).astype(i32)
    heights = jnp.pad(tent_height, (0, LANES - tent_height.shape[0]))[None]

    def exchange(sent):
        return [lax.ppermute(one, axis, pairs) for one, (axis, pairs, _, _) in zip(sent, swaps)]

    message = ((trace_rows, bnd), f32)
    own, face_stack = ((rows, BLOCK), f32), ((faces * trace_rows, BLOCK), f32)
    weight, table, traced = ((POWERS, BLOCK), f32), ((trace_rows, elements), f32), ((trace_rows, BLOCK), f32)
    whole = ((rows, elements), f32)
    flat = (comp * elements // LANES, LANES)

    columns, out, *sent = call(
        first_kernel, "first", 10 ** 8, [], [fields.reshape(flat), trace_map, send_list],
        [whole, table] + [message] * messages)
    received = exchange(sent)
    members, joined, places, send_places, mine, inner, weights, base, grow, trace_grow, mix, lift = call(
        plan_kernel, "plan", 2 * 10 ** 9, [sizes],
        [columns, order, pattern[0], faces_of, send_list, heights, operator, trace_map, lift_map, out],
        [((8, padded), i32), ((2 * faces, padded), i32), ((elements // LANES, LANES), i32), ((8, bnd), i32),
         own, face_stack, weight, traced,
         ((POWERS * rows, 3 * rows), bf16), (((POWERS + 1) * trace_rows, 3 * rows), bf16),
         (((POWERS + 1) * trace_rows, 3 * faces * trace_rows), bf16), ((rows, 3 * faces * trace_rows), bf16)])
    advanced = []
    for level in range(LEVELS):
        if level == LEVELS - 1:
            final, = call(
                functools.partial(last_kernel, level, messages), "last", 10 ** 9, [groups],
                [joined, mine, inner, weights, lift, grow, places] + advanced + received,
                [(flat, f32)], [face_stack, own])
            return final.reshape(1, 1, comp, elements)
        inflow, new_trace, *sent = call(
            functools.partial(level_kernel, level, messages), "level", 10 ** 8, [groups],
            [joined, inner, weights, base, mix, send_places] + received + sent,
            [face_stack, traced] + [message] * messages)
        received = exchange(sent)
        out, mine, inner, weights, base, *advanced = call(
            functools.partial(between_kernel, level + 1), "between", 2 * 10 ** 9, [],
            [members, joined, places, columns, out, new_trace, heights, mine, inflow, weights, lift, grow, trace_grow]
            + advanced,
            [table, own, face_stack, weight, traced, whole], [own])


def solution(mesh):
    in_specs = (
        P("sector", "radial", None, None),
        P("sector", "radial", None),
        P("sector", "radial", None),
        P("sector", "radial", None),
        P("sector", "radial", None, None),
        P("sector", "radial", None, None),
        P(),
        P(),
        P(),
        P(),
    )
    out_specs = P("sector", "radial", None, None)
    return jax.shard_map(body, mesh=mesh, in_specs=in_specs, out_specs=out_specs, check_vma=False)
```

time: 43.3 us -> 45.1 us (1.042)
  Pallas kernels: 20.4 us -> 22.4 us
  waiting for transfers between devices: 4.68 us -> 2.83 us
  local copies, waits for them, and re-layouts: 2.92 us -> 4.5 us
    pallas_call x9, Pallas kernels: 20.4 us -> 22.4 us  [call(): pl.pallas_call(kernel, out_shape=tuple((jax.ShapeDtypeStruct(shape, dtype...]
    ppermute x12, waiting for transfers between devices: 4.68 us -> 2.83 us  [exchange(): lax.ppermute(one, axis, pairs)]
    unnamed x20 -> x17, local copies, waits for them, and re-layouts: 1.5 us -> 3.04 us
    broadcast_in_dim x1 -> x0, local copies, waits for them, and re-layouts: 1.41 us -> none  [body(): return final[None, None]]
    dynamic_slice x1, local copies, waits for them, and re-layouts: 0.01 us -> 0.8 us  [body(): lax.dynamic_slice_in_dim(send_rows[0, 0], group, 1, axis=0)]
    broadcast_in_dim x1, local copies, waits for them, and re-layouts: 0.01 us -> 0.66 us  [body(): heights = jnp.pad(tent_height, (0, LANES - tent_height.shape[0]))[None]]
  transfers between devices with their start and end apart: 12 -> 12, of which waited for: 3 -> 2; matrix products, arithmetic and copies ran while one was open for 1% -> 4% of each run, Pallas kernels for 24% -> 26%
where the time goes in v1:
time: 45.1 us; the launch traced here: 44.8 us
  Pallas kernels  22.4 us (50%)
  starting transfers between devices  14.9 us (33%)
  local copies, waits for them, and re-layouts  4.5 us (10%)
  waiting for transfers between devices  2.83 us (6%)
    pallas_call x9, Pallas kernels, call(): pl.pallas_call(kernel, out_shape=tuple((jax.ShapeDtypeStruct(shape, dtype...  22.4 us
    ppermute x12, starting transfers between devices, exchange(): lax.ppermute(one, axis, pairs)  14.9 us
    unnamed x17, local copies, waits for them, and re-layouts  3.04 us
    ppermute x12, waiting for transfers between devices, exchange(): lax.ppermute(one, axis, pairs)  2.83 us
  transfers between devices with their start and end apart: 12, of which 2 were waited for; matrix products, arithmetic and copies ran while one was open for 4% of the time, Pallas kernels for 26%

profile of v1, /device:TPU:0, one launch (start us, length us, event | category | flops | bytes accessed | tf_op | source)
XLA Modules:
  0.0 44.8 jit_solution(327050750537452997)
XLA Ops:
  0.0 0.0 copy-start.2
  0.0 0.0 copy-start.7
  0.0 0.0 copy-start.5
  0.0 0.0 copy-start.6
  0.0 0.8 %fusion = (s32[1,128]{1,0:T(1,128)S(1)}, s32[1,128]{1,0:T(1,128)S(1)}, s32[1,128]{1,0:T(1,128)S(1)}) fusion(s32[1,1,4,128]{3,2,1,0:T(4,128)} %param.14, s32[]{:T(128)} %select_n.31, s32[]{:T(128)S(6)} %select_n.34, s32[]{:T(128)} %select_n.30), kind=kLoop, calls=%fused_computation.4 | loop fusion | bytes 3084 | tf_op jit(solution)/shard_map/dynamic_slice | solution.py:344
  0.8 0.0 copy-start
  0.8 1.1 %copy-done = f32[1,1,140,1024]{3,1,2,0:T(1,128)S(1)} copy-done((f32[1,1,140,1024]{3,1,2,0:T(1,128)S(1)}, f32[1,1,140,1024]{3,1,2,0:T(1,128)}, u32[]{:S(2)}) %copy-start) | copy-done | bytes 573464
  1.9 0.0 copy-start.1
  1.9 0.8 %copy-done.1 = f32[60,140]{1,0:T(8,128)S(1)} copy-done((f32[60,140]{1,0:T(8,128)S(1)}, f32[60,140]{1,0:T(8,128)}, u32[]{:S(2)}) %copy-start.1) | copy-done | bytes 33624
  2.7 0.0 copy-start.3
  2.7 0.0 copy-start.4
  2.7 0.7 %first.1 = (f32[144,1024]{1,0:T(8,128)S(1)}, f32[64,1024]{1,0:T(8,128)S(1)}, f32[64,128]{1,0:T(8,128)S(1)}, f32[64,128]{1,0:T(8,128)S(1)}, f32[64,128]{1,0:T(8,128)S(1)}) custom-call(f32[1120,128]{1,0:T(8,128)S(1)} %bitcast.17, f32[60,140]{1,0:T(8,128)S(1)} %copy-done.1, s32[3,128]{1,0:T(4,128)S(1)} %pad_add_fusion.send_ref), custom_call_target="tpu_custom_call" | custom-call | flops 100000000 | bytes 1048576 | tf_op jit(solution)/shard_map/first/pallas_call | solution.py:304
  3.4 0.6 %collective-permute-start = (f32[64,128]{1,0:T(8,128)S(1)}, f32[64,128]{1,0:T(8,128)S(1)}, u32[]{:S(2)}, u32[]{:S(2)}) collective-permute-start(f32[64,128]{1,0:T(8,128)S(1)} %get-tuple-element.63.rest_3_), channel_id=1, source_target_pairs={{0,2},{2,0},{4,6},{6,4},{8,10},{10,8},{12,14},{14,12},{16,18},{18,... | collective-permute-start | bytes 98312 | tf_op jit(solution)/shard_map/ppermute | solution.py:349
  4.0 5.7 %collective-permute-start.1 = (f32[64,128]{1,0:T(8,128)S(1)}, f32[64,128]{1,0:T(8,128)S(1)}, u32[]{:S(2)}, u32[]{:S(2)}) collective-permute-start(f32[64,128]{1,0:T(8,128)S(1)} %get-tuple-element.64.rest_4_), channel_id=1, source_target_pairs={{0,30},{2,4},{4,2},{6,8},{8,6},{10,12},{12,10},{14,16},{16,14},{18... | collective-permute-start | bytes 98312 | tf_op jit(solution)/shard_map/ppermute | solution.py:349
  9.6 1.5 %collective-permute-start.2 = (f32[64,128]{1,0:T(8,128)S(1)}, f32[64,128]{1,0:T(8,128)S(1)}, u32[]{:S(2)}, u32[]{:S(2)}) collective-permute-start(f32[64,128]{1,0:T(8,128)S(1)} %get-tuple-element.65.rest_5_), channel_id=1, source_target_pairs={{0,1},{1,0},{2,3},{3,2},{4,5},{5,4},{6,7},{7,6},{8,9},{9,8},{10,11... | collective-permute-start | bytes 98312 | tf_op jit(solution)/shard_map/ppermute | solution.py:349
  11.1 0.7 %pad_bitcast_fusion.heights_ref = f32[1,128]{1,0:T(1,128)S(1)} fusion(f32[16]{0:T(128)} %param.19), kind=kLoop, calls=%fused_computation.8 | loop fusion | bytes 576 | tf_op jit(solution)/shard_map/broadcast_in_dim | solution.py:346
  11.8 1.1 %copy.13.lift_ref = f32[4,140,60]{2,1,0:T(8,128)S(1)} copy(f32[4,140,60]{1,0,2:T(4,128)} %param.18) | data formatting | bytes 268800 | tf_op args[8]
  12.9 0.0 copy-done.2
  12.9 0.0 copy-done.7
  12.9 0.0 copy-done.5
  12.9 0.0 copy-done.6
  13.0 0.0 copy-done.3
  13.0 0.0 copy-done.4
  13.0 3.1 %plan.1 = (s32[8,1536]{1,0:T(8,128)S(1)}, s32[8,1536]{1,0:T(8,128)S(1)}, s32[8,128]{1,0:T(8,128)S(1)}, s32[8,128]{1,0:T(8,128)S(1)}, f32[144,384]{1,0:T(8,128)S(...) custom-call(s32[4]{0:T(128)S(1)} %bitcast.21, ...), custom_call_target="tpu_custom_call" | custom-call | flops 2000000000 | bytes 1048576 | tf_op jit(solution)/shard_map/plan/pallas_call | solution.py:304
  16.1 0.1 pad_add_fusion.1.groups_ref
  16.1 0.0 collective-permute-done.rest_0_
  16.1 0.0 collective-permute-done.1.rest_1_
  16.1 0.0 collective-permute-done.2.rest_2_
  16.2 2.1 %level.3 = (f32[256,384]{1,0:T(8,128)S(1)}, f32[64,384]{1,0:T(8,128)S(1)}, f32[64,128]{1,0:T(8,128)S(1)}, f32[64,128]{1,0:T(8,128)S(1)}, f32[64,128]{1,0:T(8,128)S(1)}) custom-call(s32[4]{0:T(128)S(1)} %pad_add_fusion.1.groups_ref, s32[8,1536]{1,0:T(8,128)S(1)} %get-tuple-element.55.joined_ref, f32[256,384]{1,0:T(8,128)S(1)} %get-tuple-element.58.faces_ref, ...), custom_call_target="tpu_custom_call" | custom-call | flops 100000000 | bytes 1048576 | tf_op jit(solution)/shard_map/level/pallas_call | solution.py:304
  18.2 0.1 collective-permute-start.3
  18.3 0.6 %collective-permute-start.4 = (f32[64,128]{1,0:T(8,128)S(1)}, f32[64,128]{1,0:T(8,128)S(1)}, u32[]{:S(2)}, u32[]{:S(2)}) collective-permute-start(f32[64,128]{1,0:T(8,128)S(1)} %get-tuple-element.77.rest_4_), channel_id=1, source_target_pairs={{0,30},{2,4},{4,2},{6,8},{8,6},{10,12},{12,10},{14,16},{16,14},{18... | collective-permute-start | bytes 98312 | tf_op jit(solution)/shard_map/ppermute | solution.py:349
  18.9 0.5 %collective-permute-start.5 = (f32[64,128]{1,0:T(8,128)S(1)}, f32[64,128]{1,0:T(8,128)S(1)}, u32[]{:S(2)}, u32[]{:S(2)}) collective-permute-start(f32[64,128]{1,0:T(8,128)S(1)} %get-tuple-element.78.rest_5_), channel_id=1, source_target_pairs={{0,1},{1,0},{2,3},{3,2},{4,5},{5,4},{6,7},{7,6},{8,9},{9,8},{10,11... | collective-permute-start | bytes 98312 | tf_op jit(solution)/shard_map/ppermute | solution.py:349
  19.4 2.7 %between.3 = (f32[64,1024]{1,0:T(8,128)S(1)}, f32[144,384]{1,0:T(8,128)S(1)}, f32[256,384]{1,0:T(8,128)S(1)}, f32[8,384]{1,0:T(8,128)S(1)}, f32[64,384]{1,0:T(8,128)S(1)}, /*index=5*/f32[144,1024]{1,0:T(8,128)S(1)}) custom-call(s32[8,1536]{1,0:T(8,128)S(1)} %get-tuple-element.56.members_ref, s32[8,1536]{1,0:T(8,128)S(1)} %get-tuple-element.55.joined_ref, ...), custom_call_target="tpu_custom_call" | custom-call | flops 2000000000 | bytes 1048576 | tf_op jit(solution)/shard_map/between/pallas_call | solution.py:304
  22.1 0.0 collective-permute-done.3.rest_0_
  22.1 2.3 %collective-permute-done.4.rest_1_ = f32[64,128]{1,0:T(8,128)S(1)} collective-permute-done((f32[64,128]{1,0:T(8,128)S(1)}, f32[64,128]{1,0:T(8,128)S(1)}, u32[]{:S(2)}, u32[]{:S(2)}) %collective-permute-start.4) | collective-permute-done | bytes 32800 | tf_op jit(solution)/shard_map/ppermute | solution.py:349
  24.4 0.0 collective-permute-done.5.rest_2_
  24.4 2.1 %level.4 = (f32[256,384]{1,0:T(8,128)S(1)}, f32[64,384]{1,0:T(8,128)S(1)}, f32[64,128]{1,0:T(8,128)S(1)}, f32[64,128]{1,0:T(8,128)S(1)}, f32[64,128]{1,0:T(8,128)S(1)}) custom-call(s32[4]{0:T(128)S(1)} %pad_add_fusion.1.groups_ref, s32[8,1536]{1,0:T(8,128)S(1)} %get-tuple-element.55.joined_ref, f32[256,384]{1,0:T(8,128)S(1)} %get-tuple-element.73.faces_ref, ...), custom_call_target="tpu_custom_call" | custom-call | flops 100000000 | bytes 1048576 | tf_op jit(solution)/shard_map/level/pallas_call | solution.py:304
  26.5 0.1 collective-permute-start.6
  26.6 1.4 %collective-permute-start.7 = (f32[64,128]{1,0:T(8,128)S(1)}, f32[64,128]{1,0:T(8,128)S(1)}, u32[]{:S(2)}, u32[]{:S(2)}) collective-permute-start(f32[64,128]{1,0:T(8,128)S(1)} %get-tuple-element.88.rest_4_), channel_id=1, source_target_pairs={{0,30},{2,4},{4,2},{6,8},{8,6},{10,12},{12,10},{14,16},{16,14},{18... | collective-permute-start | bytes 98312 | tf_op jit(solution)/shard_map/ppermute | solution.py:349
  28.0 1.5 %collective-permute-start.8 = (f32[64,128]{1,0:T(8,128)S(1)}, f32[64,128]{1,0:T(8,128)S(1)}, u32[]{:S(2)}, u32[]{:S(2)}) collective-permute-start(f32[64,128]{1,0:T(8,128)S(1)} %get-tuple-element.89.rest_5_), channel_id=1, source_target_pairs={{0,1},{1,0},{2,3},{3,2},{4,5},{5,4},{6,7},{7,6},{8,9},{9,8},{10,11... | collective-permute-start | bytes 98312 | tf_op jit(solution)/shard_map/ppermute | solution.py:349
  29.5 2.7 %between.4 = (f32[64,1024]{1,0:T(8,128)S(1)}, f32[144,384]{1,0:T(8,128)S(1)}, f32[256,384]{1,0:T(8,128)S(1)}, f32[8,384]{1,0:T(8,128)S(1)}, f32[64,384]{1,0:T(8,128)S(1)}, /*index=5*/f32[144,1024]{1,0:T(8,128)S(1)}) custom-call(s32[8,1536]{1,0:T(8,128)S(1)} %get-tuple-element.56.members_ref, s32[8,1536]{1,0:T(8,128)S(1)} %get-tuple-element.55.joined_ref, ...), custom_call_target="tpu_custom_call" | custom-call | flops 2000000000 | bytes 1048576 | tf_op jit(solution)/shard_map/between/pallas_call | solution.py:304
  32.1 0.0 collective-permute-done.6.rest_0_
  32.1 0.5 %collective-permute-done.7.rest_1_ = f32[64,128]{1,0:T(8,128)S(1)} collective-permute-done((f32[64,128]{1,0:T(8,128)S(1)}, f32[64,128]{1,0:T(8,128)S(1)}, u32[]{:S(2)}, u32[]{:S(2)}) %collective-permute-start.7) | collective-permute-done | bytes 32800 | tf_op jit(solution)/shard_map/ppermute | solution.py:349
  32.7 0.0 collective-permute-done.8.rest_2_
  32.7 2.1 %level.5 = (f32[256,384]{1,0:T(8,128)S(1)}, f32[64,384]{1,0:T(8,128)S(1)}, f32[64,128]{1,0:T(8,128)S(1)}, f32[64,128]{1,0:T(8,128)S(1)}, f32[64,128]{1,0:T(8,128)S(1)}) custom-call(s32[4]{0:T(128)S(1)} %pad_add_fusion.1.groups_ref, s32[8,1536]{1,0:T(8,128)S(1)} %get-tuple-element.55.joined_ref, f32[256,384]{1,0:T(8,128)S(1)} %get-tuple-element.84.faces_ref, ...), custom_call_target="tpu_custom_call" | custom-call | flops 100000000 | bytes 1048576 | tf_op jit(solution)/shard_map/level/pallas_call | solution.py:304
  34.7 0.1 collective-permute-start.9
  34.8 1.4 %collective-permute-start.10 = (f32[64,128]{1,0:T(8,128)S(1)}, f32[64,128]{1,0:T(8,128)S(1)}, u32[]{:S(2)}, u32[]{:S(2)}) collective-permute-start(f32[64,128]{1,0:T(8,128)S(1)} %get-tuple-element.99), channel_id=1, source_target_pairs={{0,30},{2,4},{4,2},{6,8},{8,6},{10,12},{12,10},{14,16},{16,14},{18... | collective-permute-start | bytes 98312 | tf_op jit(solution)/shard_map/ppermute | solution.py:349
  36.2 1.5 %collective-permute-start.11 = (f32[64,128]{1,0:T(8,128)S(1)}, f32[64,128]{1,0:T(8,128)S(1)}, u32[]{:S(2)}, u32[]{:S(2)}) collective-permute-start(f32[64,128]{1,0:T(8,128)S(1)} %get-tuple-element.100), channel_id=1, source_target_pairs={{0,1},{1,0},{2,3},{3,2},{4,5},{5,4},{6,7},{7,6},{8,9},{9,8},{10,11... | collective-permute-start | bytes 98312 | tf_op jit(solution)/shard_map/ppermute | solution.py:349
  37.7 3.4 %between.5 = (f32[64,1024]{1,0:T(8,128)}, f32[144,384]{1,0:T(8,128)S(1)}, f32[256,384]{1,0:T(8,128)S(1)}, f32[8,384]{1,0:T(8,128)S(1)}, f32[64,384]{1,0:T(8,128)}, /*index=5*/f32[144,1024]{1,0:T(8,128)S(1)}) custom-call(s32[8,1536]{1,0:T(8,128)S(1)} %get-tuple-element.56.members_ref, s32[8,1536]{1,0:T(8,128)S(1)} %get-tuple-element.55.joined_ref, ...), custom_call_target="tpu_custom_call" | custom-call | flops 2000000000 | bytes 1048576 | tf_op jit(solution)/shard_map/between/pallas_call | solution.py:304
  41.1 0.0 collective-permute-done.9.rest_0_
  41.1 0.0 collective-permute-done.10.rest_1_
  41.1 0.0 collective-permute-done.11.rest_2_
  41.1 3.8 %last.1 = f32[1120,128]{1,0:T(8,128)} custom-call(s32[4]{0:T(128)S(1)} %pad_add_fusion.1.groups_ref, s32[8,1536]{1,0:T(8,128)S(1)} %get-tuple-element.55.joined_ref, f32[144,384]{1,0:T(8,128)S(1)} %get-tuple-element.94.own_ref, f32[256,384]{1,0:T(8,128)S(1)} %get-tuple-element.95.faces_ref, f32[8,384]{1,0:T(8,128)S(1)} %get-tuple-element.96.weights_ref, ...), custom_call_target="tpu_custom_call" | custom-call | flops 1000000000 | bytes 1048576 | tf_op jit(solution)/shard_map/last/pallas_call | solution.py:304
  (1 shorter events, 0.0 us)
Async XLA Ops:
  0.0 12.9 %copy-start.2 = (f32[60,140]{1,0:T(8,128)S(1)}, f32[60,140]{1,0:T(8,128)}, u32[]{:S(2)}) copy-start(f32[60,140]{1,0:T(8,128)} %trace_ref.3) | copy-start | bytes 100804
  0.0 12.9 %copy-start.7 = (s32[1,1,4]{2,1,0:T(1,128)S(1)}, s32[1,1,4]{2,1,0:T(1,128)}, u32[]{:S(2)}) copy-start(s32[1,1,4]{2,1,0:T(1,128)} %param.13) | copy-start | bytes 52
  0.0 12.9 %copy-start.5 = (s32[1,1,1024]{2,1,0:T(1,128)S(1)}, s32[1,1,1024]{2,1,0:T(1,128)}, u32[]{:S(2)}) copy-start(s32[1,1,1024]{2,1,0:T(1,128)} %param.12) | copy-start | bytes 12292
  0.0 12.9 %copy-start.6 = (s32[1,1,1024]{2,1,0:T(1,128)S(1)}, s32[1,1,1024]{2,1,0:T(1,128)}, u32[]{:S(2)}) copy-start(s32[1,1,1024]{2,1,0:T(1,128)} %param.11) | copy-start | bytes 12292
  0.8 1.1 %copy-start = (f32[1,1,140,1024]{3,1,2,0:T(1,128)S(1)}, f32[1,1,140,1024]{3,1,2,0:T(1,128)}, u32[]{:S(2)}) copy-start(f32[1,1,140,1024]{3,1,2,0:T(1,128)} %param.10) | copy-start | bytes 1720324
  1.9 0.8 %copy-start.1 = (f32[60,140]{1,0:T(8,128)S(1)}, f32[60,140]{1,0:T(8,128)}, u32[]{:S(2)}) copy-start(f32[60,140]{1,0:T(8,128)} %trace_ref.3) | copy-start | bytes 100804
  2.7 10.2 %copy-start.3 = (f32[140,140]{1,0:T(8,128)S(1)}, f32[140,140]{1,0:T(8,128)}, u32[]{:S(2)}) copy-start(f32[140,140]{1,0:T(8,128)} %operator_ref.1) | copy-start | bytes 235204
  2.7 10.2 %copy-start.4 = (s32[1,1,4,1024]{3,2,1,0:T(4,128)S(1)}, s32[1,1,4,1024]{3,2,1,0:T(4,128)}, u32[]{:S(2)}) copy-start(s32[1,1,4,1024]{3,2,1,0:T(4,128)} %param.15) | copy-start | bytes 49156
  3.4 12.7 %collective-permute-start = (f32[64,128]{1,0:T(8,128)S(1)}, f32[64,128]{1,0:T(8,128)S(1)}, u32[]{:S(2)}, u32[]{:S(2)}) collective-permute-start(f32[64,128]{1,0:T(8,128)S(1)} %get-tuple-element.63.rest_3_), channel_id=1, source_target_pairs={{0,2},{2,0},{4,6},{6,4},{8,10},{10,8},{12,14},{14,12},{16,18},{18,... | collective-permute-start | bytes 98312 | tf_op jit(solution)/shard_map/ppermute | solution.py:349
  4.0 12.2 %collective-permute-start.1 = (f32[64,128]{1,0:T(8,128)S(1)}, f32[64,128]{1,0:T(8,128)S(1)}, u32[]{:S(2)}, u32[]{:S(2)}) collective-permute-start(f32[64,128]{1,0:T(8,128)S(1)} %get-tuple-element.64.rest_4_), channel_id=1, source_target_pairs={{0,30},{2,4},{4,2},{6,8},{8,6},{10,12},{12,10},{14,16},{16,14},{18... | collective-permute-start | bytes 98312 | tf_op jit(solution)/shard_map/ppermute | solution.py:349
  9.6 6.5 %collective-permute-start.2 = (f32[64,128]{1,0:T(8,128)S(1)}, f32[64,128]{1,0:T(8,128)S(1)}, u32[]{:S(2)}, u32[]{:S(2)}) collective-permute-start(f32[64,128]{1,0:T(8,128)S(1)} %get-tuple-element.65.rest_5_), channel_id=1, source_target_pairs={{0,1},{1,0},{2,3},{3,2},{4,5},{5,4},{6,7},{7,6},{8,9},{9,8},{10,11... | collective-permute-start | bytes 98312 | tf_op jit(solution)/shard_map/ppermute | solution.py:349
  18.2 3.9 %collective-permute-start.3 = (f32[64,128]{1,0:T(8,128)S(1)}, f32[64,128]{1,0:T(8,128)S(1)}, u32[]{:S(2)}, u32[]{:S(2)}) collective-permute-start(f32[64,128]{1,0:T(8,128)S(1)} %get-tuple-element.76.rest_3_), channel_id=1, source_target_pairs={{0,2},{2,0},{4,6},{6,4},{8,10},{10,8},{12,14},{14,12},{16,18},{18,... | collective-permute-start | bytes 98312 | tf_op jit(solution)/shard_map/ppermute | solution.py:349
  18.3 6.1 %collective-permute-start.4 = (f32[64,128]{1,0:T(8,128)S(1)}, f32[64,128]{1,0:T(8,128)S(1)}, u32[]{:S(2)}, u32[]{:S(2)}) collective-permute-start(f32[64,128]{1,0:T(8,128)S(1)} %get-tuple-element.77.rest_4_), channel_id=1, source_target_pairs={{0,30},{2,4},{4,2},{6,8},{8,6},{10,12},{12,10},{14,16},{16,14},{18... | collective-permute-start | bytes 98312 | tf_op jit(solution)/shard_map/ppermute | solution.py:349
  18.9 5.5 %collective-permute-start.5 = (f32[64,128]{1,0:T(8,128)S(1)}, f32[64,128]{1,0:T(8,128)S(1)}, u32[]{:S(2)}, u32[]{:S(2)}) collective-permute-start(f32[64,128]{1,0:T(8,128)S(1)} %get-tuple-element.78.rest_5_), channel_id=1, source_target_pairs={{0,1},{1,0},{2,3},{3,2},{4,5},{5,4},{6,7},{7,6},{8,9},{9,8},{10,11... | collective-permute-start | bytes 98312 | tf_op jit(solution)/shard_map/ppermute | solution.py:349
  26.5 5.7 %collective-permute-start.6 = (f32[64,128]{1,0:T(8,128)S(1)}, f32[64,128]{1,0:T(8,128)S(1)}, u32[]{:S(2)}, u32[]{:S(2)}) collective-permute-start(f32[64,128]{1,0:T(8,128)S(1)} %get-tuple-element.87.rest_3_), channel_id=1, source_target_pairs={{0,2},{2,0},{4,6},{6,4},{8,10},{10,8},{12,14},{14,12},{16,18},{18,... | collective-permute-start | bytes 98312 | tf_op jit(solution)/shard_map/ppermute | solution.py:349
  26.6 6.1 %collective-permute-start.7 = (f32[64,128]{1,0:T(8,128)S(1)}, f32[64,128]{1,0:T(8,128)S(1)}, u32[]{:S(2)}, u32[]{:S(2)}) collective-permute-start(f32[64,128]{1,0:T(8,128)S(1)} %get-tuple-element.88.rest_4_), channel_id=1, source_target_pairs={{0,30},{2,4},{4,2},{6,8},{8,6},{10,12},{12,10},{14,16},{16,14},{18... | collective-permute-start | bytes 98312 | tf_op jit(solution)/shard_map/ppermute | solution.py:349
  28.0 4.7 %collective-permute-start.8 = (f32[64,128]{1,0:T(8,128)S(1)}, f32[64,128]{1,0:T(8,128)S(1)}, u32[]{:S(2)}, u32[]{:S(2)}) collective-permute-start(f32[64,128]{1,0:T(8,128)S(1)} %get-tuple-element.89.rest_5_), channel_id=1, source_target_pairs={{0,1},{1,0},{2,3},{3,2},{4,5},{5,4},{6,7},{7,6},{8,9},{9,8},{10,11... | collective-permute-start | bytes 98312 | tf_op jit(solution)/shard_map/ppermute | solution.py:349
  34.7 6.4 %collective-permute-start.9 = (f32[64,128]{1,0:T(8,128)S(1)}, f32[64,128]{1,0:T(8,128)S(1)}, u32[]{:S(2)}, u32[]{:S(2)}) collective-permute-start(f32[64,128]{1,0:T(8,128)S(1)} %get-tuple-element.98), channel_id=1, source_target_pairs={{0,2},{2,0},{4,6},{6,4},{8,10},{10,8},{12,14},{14,12},{16,18},{18,... | collective-permute-start | bytes 98312 | tf_op jit(solution)/shard_map/ppermute | solution.py:349
  34.8 6.3 %collective-permute-start.10 = (f32[64,128]{1,0:T(8,128)S(1)}, f32[64,128]{1,0:T(8,128)S(1)}, u32[]{:S(2)}, u32[]{:S(2)}) collective-permute-start(f32[64,128]{1,0:T(8,128)S(1)} %get-tuple-element.99), channel_id=1, source_target_pairs={{0,30},{2,4},{4,2},{6,8},{8,6},{10,12},{12,10},{14,16},{16,14},{18... | collective-permute-start | bytes 98312 | tf_op jit(solution)/shard_map/ppermute | solution.py:349
  36.2 4.9 %collective-permute-start.11 = (f32[64,128]{1,0:T(8,128)S(1)}, f32[64,128]{1,0:T(8,128)S(1)}, u32[]{:S(2)}, u32[]{:S(2)}) collective-permute-start(f32[64,128]{1,0:T(8,128)S(1)} %get-tuple-element.100), channel_id=1, source_target_pairs={{0,1},{1,0},{2,3},{3,2},{4,5},{5,4},{6,7},{7,6},{8,9},{9,8},{10,11... | collective-permute-start | bytes 98312 | tf_op jit(solution)/shard_map/ppermute | solution.py:349

commit v2 on v1

--- a/solution.py
+++ b/solution.py
@@ -14,6 +14,7 @@
 BLOCK = 384
 LANES = 128
 NO_GROUP = 1 << 20
+ARGUMENTS = 10
 
 f32, bf16, i32 = jnp.float32, jnp.bfloat16, jnp.int32
 precise = lax.Precision.HIGHEST
@@ -112,7 +113,28 @@
     return total
 
 
-def first_kernel(fields_ref, trace_ref, send_ref, columns_ref, out_ref, *sends):
+def sent_rows(send_ref, swaps):
+    rows = []
+    for axis, _, low, high, _ in swaps:
+        odd, even = send_ref[high:high + 1, :], send_ref[low:low + 1, :]
+        rows.append(jnp.where(is_odd(axis), odd, even))
+    return rows
+
+
+def first_kernel(swaps, *refs):
+    (fields_hbm, *given), refs = refs[:ARGUMENTS], refs[ARGUMENTS:]
+    (columns_ref, out_ref), refs = refs[:2], refs[2:]
+    sends, refs = refs[:len(swaps)], refs[len(swaps):]
+    *held, fields_ref, arrived = refs
+    copies = [
+        pltpu.make_async_copy(source, target, arrived.at[i])
+        for i, (source, target) in enumerate(zip([fields_hbm] + given, [fields_ref] + held))
+    ]
+    for copy in copies:
+        copy.start()
+    for copy in copies[:3]:
+        copy.wait()
+    trace_ref, send_ref = held[:2]
     rows = out_ref.shape[0]
     elements = out_ref.shape[1]
     count = elements // LANES
@@ -124,10 +146,11 @@
     high, low = split(fields)
     upper = product(both, high)
     out_ref[...] = upper[:rows] + upper[rows:] + product(trace_high, low)
-    for group, send in enumerate(sends):
-        index = send_ref[group:group + 1, :]
+    for index, send in zip(sent_rows(send_ref, swaps), sends):
         send[...] = pick(ref_blocks(out_ref, count), index, index >> 7)
     columns_ref[...] = pad_rows(fields, columns_ref.shape[0])
+    for copy in copies[3:]:
+        copy.wait()
 
 
 def faces_in(joined_ref):
@@ -135,7 +158,7 @@
 
 
 def local_part(level, members_ref, joined_ref, columns_ref, out_ref, heights_ref, trace_grow_ref,
-               own_ref, faces_ref, weights_ref, base_ref):
+               own_ref, faces_ref, weights_ref, base_ref=None):
     faces = faces_in(joined_ref)
     count = columns_ref.shape[1] // LANES
     trace_rows = out_ref.shape[0]
@@ -151,7 +174,8 @@
         for power in range(1, POWERS + 1):
             weight = weight * height
             weights_ref[power - 1:power, here] = weight[0:1] * WEIGHTS[power]
-    stacked = product(trace_grow_ref[...], stacked_columns(own_ref[...]))
+    if base_ref is not None:
+        stacked = product(trace_grow_ref[...], stacked_columns(own_ref[...]))
     for block in range(BLOCK // LANES):
         here = block_at(block)
         there = block_at(level * (BLOCK // LANES) + block)
@@ -159,22 +183,21 @@
             index = joined_ref[face:face + 1, there]
             faces_ref[face * trace_rows:(face + 1) * trace_rows, here] = pick(
                 ref_blocks(out_ref, count), index, index >> 7, jnp.zeros((trace_rows, LANES), f32))
-    base_ref[...] = summed_powers(stacked[trace_rows:], weights_ref, trace_rows, stacked[:trace_rows])
+    if base_ref is not None:
+        base_ref[...] = summed_powers(stacked[trace_rows:], weights_ref, trace_rows, stacked[:trace_rows])
 
 
 def matrix_powers(operator_ref, trace_ref, lift_ref, grow_ref, trace_grow_ref, mix_ref, lift_out_ref):
     comp = operator_ref.shape[0]
-    faces, _, trace_comp = lift_ref.shape
+    trace_comp, faces, _ = lift_ref.shape
     rows = lift_out_ref.shape[0]
     trace_rows = trace_grow_ref.shape[0] // (POWERS + 1)
     operator = pad_rows(operator_ref[...], rows)
     operator = jnp.concatenate([operator, jnp.zeros((rows, rows - comp), f32)], axis=1)
     traces = pad_rows(trace_ref[...], trace_rows)
     traces = jnp.concatenate([traces, jnp.zeros((trace_rows, rows - comp), f32)], axis=1)
-    lift = jnp.concatenate([
-        jnp.concatenate([pad_rows(lift_ref[face], rows), jnp.zeros((rows, trace_rows - trace_comp), f32)], axis=1)
-        for face in range(faces)
-    ], axis=1)
+    lift = jnp.concatenate([pad_rows(lift_ref[:, face, :], trace_rows) for face in range(faces)], axis=0)
+    lift = pad_rows(jnp.transpose(lift), rows)
     powers, have = operator, 1
     while have < POWERS:
         more = exact_product(jnp.concatenate([traces, powers], axis=0), powers[(have - 1) * rows:have * rows])
@@ -188,19 +211,28 @@
     grow_ref[...] = stacked_matrix(powers)
 
 
-def plan_kernel(sizes_ref, columns_ref, order_ref, pattern_ref, neighbours_ref, send_ref, heights_ref,
-                operator_ref, trace_ref, lift_ref, out_ref,
+def plan_kernel(swaps, trace_ref, send_ref, order_ref, pattern_ref, sizes_ref, neighbours_ref, operator_ref,
+                lift_ref, heights_ref, columns_ref, out_ref,
                 members_ref, joined_ref, places_ref, send_places_ref, own_ref, faces_ref, weights_ref, base_ref,
-                grow_ref, trace_grow_ref, mix_ref, lift_out_ref):
+                grow_ref, trace_grow_ref, mix_ref, lift_out_ref, wide_heights_ref):
     elements = columns_ref.shape[1]
     count = elements // LANES
     faces = neighbours_ref.shape[0]
-    starts = [jnp.int32(0)]
-    for level in range(LEVELS - 1):
-        starts.append(starts[-1] + sizes_ref[level])
+    sizes = sizes_ref[...].astype(f32)
+    number = lax.broadcasted_iota(i32, sizes.shape, 1)
+    starts = [jnp.sum(jnp.where(number < level, sizes, 0.0)).astype(i32) for level in range(LEVELS)]
     wide_order = jnp.broadcast_to(order_ref[...], (8, elements))
+    neighbours = neighbours_ref[...]
+    group = (neighbours >> 7) - count
+    message = jnp.full(neighbours.shape, count + len(swaps), i32)
+    for number, swap in enumerate(swaps):
+        message = jnp.where(group == came_group(swap), count + number, message)
+    neighbours = jnp.where(group >= 0, message * LANES + (neighbours & (LANES - 1)), neighbours)
     table = jnp.concatenate(
-        [neighbours_ref[...], pattern_ref[...], jnp.zeros((faces - 1, elements), i32)], axis=0)
+        [neighbours, pattern_ref[...], jnp.zeros((faces - 1, elements), i32)], axis=0)
+    heights = heights_ref[...]
+    wide_heights_ref[...] = jnp.concatenate(
+        [heights, jnp.zeros((1, LANES - heights.shape[1]), f32)], axis=1)
     for level in range(LEVELS):
         shift = jnp.where(starts[level] == 0, 0, elements - starts[level])
         members_ref[:, level * BLOCK:(level + 1) * BLOCK] = pltpu.roll(wide_order, shift, 1)[:, :BLOCK]
@@ -220,10 +252,10 @@
     for level in range(1, LEVELS):
         at = jnp.where(place >= starts[level], place - starts[level] + level * BLOCK, at)
     places_ref[...] = at
-    index = pad_rows(send_ref[...], 8)
+    index = pad_rows(jnp.concatenate(sent_rows(send_ref, swaps), axis=0), 8)
     send_places_ref[...] = pick(row_blocks(at, 8), index, index >> 7)
     matrix_powers(operator_ref, trace_ref, lift_ref, grow_ref, trace_grow_ref, mix_ref, lift_out_ref)
-    local_part(0, members_ref, joined_ref, columns_ref, out_ref, heights_ref, trace_grow_ref,
+    local_part(0, members_ref, joined_ref, columns_ref, out_ref, wide_heights_ref, trace_grow_ref,
                own_ref, faces_ref, weights_ref, base_ref)
 
 
@@ -243,7 +275,11 @@
                    old_own_ref, inflow_ref, old_weights_ref, lift_ref, grow_ref, trace_grow_ref, *rest):
     if level > 1:
         advanced_ref, rest = rest[0], rest[1:]
-    out_ref, own_ref, faces_ref, weights_ref, base_ref, new_advanced_ref, new_ref = rest
+    if level == LEVELS - 1:
+        own_ref, faces_ref, weights_ref, new_advanced_ref, out_ref, new_ref = rest
+        base_ref = None
+    else:
+        out_ref, own_ref, faces_ref, weights_ref, base_ref, new_advanced_ref, new_ref = rest
     elements = columns_ref.shape[1]
     for block in range(elements // LANES):
         here = block_at(block)
@@ -257,27 +293,26 @@
         new_advanced_ref[:, here] = settle(level - 1, new_ref, places_ref, before, block)
 
 
-def gather_inflow(level, groups_ref, received, joined_ref, faces_ref, inflow_ref):
+def gather_inflow(level, received, joined_ref, faces_ref, inflow_ref, count):
     faces = faces_in(joined_ref)
     trace_rows = faces_ref.shape[0] // faces
-    own_groups = groups_ref[len(received)]
-    blocks = [(groups_ref[i], functools.partial(lambda ref: ref[...], ref)) for i, ref in enumerate(received)]
+    blocks = [(count + i, functools.partial(lambda ref: ref[...], ref)) for i, ref in enumerate(received)]
     for block in range(BLOCK // LANES):
         here = block_at(block)
         there = block_at(level * (BLOCK // LANES) + block)
         for face in range(faces):
             part = slice(face * trace_rows, (face + 1) * trace_rows)
             index = joined_ref[face:face + 1, there]
-            inflow_ref[part, here] = pick(blocks, index, (index >> 7) - own_groups, faces_ref[part, here])
-
-
-def level_kernel(level, messages, groups_ref, joined_ref, faces_ref, weights_ref, base_ref, mix_ref, send_places_ref,
+            inflow_ref[part, here] = pick(blocks, index, index >> 7, faces_ref[part, here])
+
+
+def level_kernel(level, messages, count, joined_ref, faces_ref, weights_ref, base_ref, mix_ref, send_places_ref,
                  *rest):
     received, rest = rest[:messages], rest[messages:]
     sent, rest = rest[:messages], rest[messages:]
     inflow_ref, new_trace_ref, sends = rest[0], rest[1], rest[2:]
     trace_rows = new_trace_ref.shape[0]
-    gather_inflow(level, groups_ref, received, joined_ref, faces_ref, inflow_ref)
+    gather_inflow(level, received, joined_ref, faces_ref, inflow_ref, count)
     stacked = product(mix_ref[...], stacked_columns(inflow_ref[...]))
     new_trace_ref[...] = summed_powers(
         stacked[trace_rows:], weights_ref, trace_rows, base_ref[...] + stacked[:trace_rows])
@@ -287,102 +322,114 @@
         send[...] = pick(ref_blocks(new_trace_ref, BLOCK // LANES), index, which, before[...])
 
 
-def last_kernel(level, messages, groups_ref, joined_ref, own_ref, faces_ref, weights_ref, lift_ref, grow_ref,
+def last_kernel(level, messages, joined_ref, own_ref, faces_ref, weights_ref, lift_ref, grow_ref,
                 places_ref, advanced_ref, *rest):
     received, (final_ref, inflow_ref, new_ref) = rest[:messages], rest[messages:]
-    gather_inflow(level, groups_ref, received, joined_ref, faces_ref, inflow_ref)
+    count = places_ref.shape[0]
+    gather_inflow(level, received, joined_ref, faces_ref, inflow_ref, count)
     new_ref[...] = advanced_columns(own_ref, inflow_ref, lift_ref, grow_ref, weights_ref)
-    count = places_ref.shape[0]
     comp = final_ref.shape[0] // count
     for block in range(count):
         done = settle(level, new_ref, places_ref, advanced_ref[:, block_at(block)], block)
         final_ref[pl.ds(block, comp, stride=count), :] = done[:comp]
 
 
-def call(kernel, name, flops, scalars, vectors, outs, scratch=()):
-    vmem, smem = pl.BlockSpec(memory_space=pltpu.VMEM), pl.BlockSpec(memory_space=pltpu.SMEM)
+def call(kernel, name, flops, operands, outs, scratch=(), hbm=False):
+    vmem = pl.BlockSpec(memory_space=pltpu.VMEM)
+    given = pl.BlockSpec(memory_space=pltpu.HBM) if hbm else vmem
+    if hbm:
+        operands = [pltpu.with_memory_space_constraint(one, pltpu.HBM) for one in operands]
     return pl.pallas_call(
         kernel,
         out_shape=tuple(jax.ShapeDtypeStruct(shape, dtype) for shape, dtype in outs),
-        in_specs=[smem] * len(scalars) + [vmem] * len(vectors),
+        in_specs=[given] * len(operands),
         out_specs=tuple([vmem] * len(outs)),
-        scratch_shapes=[pltpu.VMEM(shape, dtype) for shape, dtype in scratch],
+        scratch_shapes=[one if not isinstance(one, tuple) else pltpu.VMEM(*one) for one in scratch],
         compiler_params=pltpu.CompilerParams(vmem_limit_bytes=16 * 1024 * 1024),
         cost_estimate=pl.CostEstimate(flops=flops, bytes_accessed=1 << 20, transcendentals=0),
         name=name,
-    )(*scalars, *vectors)
-
-
-def swap_plan(axis, periodic, low_group, high_group):
+    )(*operands)
+
+
+def is_odd(axis):
+    return (lax.axis_index(axis) & 1) == 1
+
+
+def swap_plan(axis, periodic, low, high):
     count = lax.axis_size(axis)
-    index = lax.axis_index(axis)
-    odd = (index % 2) == 1
-    first = [(i, i ^ 1) for i in range(count)]
-    plan = [(first, jnp.where(odd, high_group, low_group), jnp.where(odd, low_group, high_group))]
+    plan = [(axis, [(i, i ^ 1) for i in range(count)], low, high, False)]
     if count > 2 or periodic:
-        second = [(i, (i + 1) % count if i % 2 else (i - 1) % count) for i in range(count)]
-        came = jnp.where(odd, high_group, low_group)
-        if not periodic:
-            came = jnp.where((index == 0) | (index == count - 1), NO_GROUP, came)
-        plan.append((second, jnp.where(odd, low_group, high_group), came))
+        pairs = [(i, (i + 1) % count if i % 2 else (i - 1) % count) for i in range(count)]
+        plan.append((axis, pairs, high, low, not periodic))
     return plan
 
 
+def came_group(swap):
+    axis, _, even, odd, is_open = swap
+    came = jnp.where(is_odd(axis), even, odd)
+    if is_open:
+        index = lax.axis_index(axis)
+        came = jnp.where((index == 0) | (index == lax.axis_size(axis) - 1), NO_GROUP, came)
+    return came
+
+
 def body(fields, pattern, tent_order, level_sizes, send_rows, neighbours, operator, trace_map, lift_map, tent_height):
-    fields, order, sizes = fields[0, 0], tent_order[0], level_sizes[0, 0]
-    faces_of = neighbours[0, 0]
+    fields, order, sizes = fields[0, 0], tent_order[0], level_sizes[0]
+    faces_of, send_list = neighbours[0, 0], send_rows[0, 0]
     comp, elements = fields.shape
     faces, trace = lift_map.shape[0], trace_map.shape[0]
     rows, trace_rows = rounded_up(comp, 16), rounded_up(trace, 16)
-    padded = LEVELS * BLOCK
-    bnd = send_rows.shape[-1]
-
-    swaps = [("sector",) + one for one in swap_plan("sector", True, 0, 1)]
-    swaps += [("radial",) + one for one in swap_plan("radial", False, 2, 3)]
+    padded, count = LEVELS * BLOCK, elements // LANES
+    bnd = send_list.shape[-1]
+
+    swaps = swap_plan("sector", True, 0, 1) + swap_plan("radial", False, 2, 3)
     messages = len(swaps)
-    send_list = jnp.concatenate([
-        lax.dynamic_slice_in_dim(send_rows[0, 0], group, 1, axis=0) for _, _, group, _ in swaps])
-    groups = jnp.stack([came for _, _, _, came in swaps] + [jnp.int32(elements // LANES)]).astype(i32)
-    heights = jnp.pad(tent_height, (0, LANES - tent_height.shape[0]))[None]
 
     def exchange(sent):
-        return [lax.ppermute(one, axis, pairs) for one, (axis, pairs, _, _) in zip(sent, swaps)]
+        return [lax.ppermute(one, swap[0], swap[1]) for one, swap in zip(sent, swaps)]
 
     message = ((trace_rows, bnd), f32)
     own, face_stack = ((rows, BLOCK), f32), ((faces * trace_rows, BLOCK), f32)
     weight, table, traced = ((POWERS, BLOCK), f32), ((trace_rows, elements), f32), ((trace_rows, BLOCK), f32)
     whole = ((rows, elements), f32)
-    flat = (comp * elements // LANES, LANES)
-
-    columns, out, *sent = call(
-        first_kernel, "first", 10 ** 8, [], [fields.reshape(flat), trace_map, send_list],
-        [whole, table] + [message] * messages)
+    flat = (comp * count, LANES)
+
+    arguments = [trace_map, send_list, order, pattern[0], sizes, faces_of, operator,
+                 jnp.transpose(lift_map, (2, 0, 1)), tent_height[None]]
+    columns, out, *rest = call(
+        functools.partial(first_kernel, swaps), "first", 10 ** 8, [fields.reshape(flat)] + arguments,
+        [whole, table] + [message] * messages + [(one.shape, one.dtype) for one in arguments],
+        [(flat, f32), pltpu.SemaphoreType.DMA((ARGUMENTS,))], hbm=True)
+    sent, held = rest[:messages], rest[messages:]
     received = exchange(sent)
-    members, joined, places, send_places, mine, inner, weights, base, grow, trace_grow, mix, lift = call(
-        plan_kernel, "plan", 2 * 10 ** 9, [sizes],
-        [columns, order, pattern[0], faces_of, send_list, heights, operator, trace_map, lift_map, out],
-        [((8, padded), i32), ((2 * faces, padded), i32), ((elements // LANES, LANES), i32), ((8, bnd), i32),
+    members, joined, places, send_places, mine, inner, weights, base, grow, trace_grow, mix, lift, heights = call(
+        functools.partial(plan_kernel, swaps), "plan", 2 * 10 ** 9, held + [columns, out],
+        [((8, padded), i32), ((2 * faces, padded), i32), ((count, LANES), i32), ((8, bnd), i32),
          own, face_stack, weight, traced,
          ((POWERS * rows, 3 * rows), bf16), (((POWERS + 1) * trace_rows, 3 * rows), bf16),
-         (((POWERS + 1) * trace_rows, 3 * faces * trace_rows), bf16), ((rows, 3 * faces * trace_rows), bf16)])
+         (((POWERS + 1) * trace_rows, 3 * faces * trace_rows), bf16), ((rows, 3 * faces * trace_rows), bf16),
+         ((1, LANES), f32)])
     advanced = []
-    for level in range(LEVELS):
-        if level == LEVELS - 1:
-            final, = call(
-                functools.partial(last_kernel, level, messages), "last", 10 ** 9, [groups],
-                [joined, mine, inner, weights, lift, grow, places] + advanced + received,
-                [(flat, f32)], [face_stack, own])
-            return final.reshape(1, 1, comp, elements)
+    for level in range(LEVELS - 1):
         inflow, new_trace, *sent = call(
-            functools.partial(level_kernel, level, messages), "level", 10 ** 8, [groups],
+            functools.partial(level_kernel, level, messages, count), "level", 10 ** 8,
             [joined, inner, weights, base, mix, send_places] + received + sent,
             [face_stack, traced] + [message] * messages)
         received = exchange(sent)
-        out, mine, inner, weights, base, *advanced = call(
-            functools.partial(between_kernel, level + 1), "between", 2 * 10 ** 9, [],
-            [members, joined, places, columns, out, new_trace, heights, mine, inflow, weights, lift, grow, trace_grow]
-            + advanced,
-            [table, own, face_stack, weight, traced, whole], [own])
+        beside = functools.partial(between_kernel, level + 1)
+        operands = [members, joined, places, columns, out, new_trace, heights, mine, inflow, weights, lift, grow,
+                    trace_grow] + advanced
+        if level + 1 < LEVELS - 1:
+            out, mine, inner, weights, base, *advanced = call(
+                beside, "between", 2 * 10 ** 9, operands, [table, own, face_stack, weight, traced, whole], [own])
+        else:
+            mine, inner, weights, *advanced = call(
+                beside, "between", 2 * 10 ** 9, operands, [own, face_stack, weight, whole], [table, own])
+    final, = call(
+        functools.partial(last_kernel, LEVELS - 1, messages), "last", 10 ** 9,
+        [joined, mine, inner, weights, lift, grow, places] + advanced + received,
+        [(flat, f32)], [face_stack, own])
+    return final.reshape(1, 1, comp, elements)
 
 
 def solution(mesh):

time: 45.1 us -> 38.6 us (0.86)
  local copies, waits for them, and re-layouts: 4.5 us -> 0 us
  starting transfers between devices: 14.9 us -> 18.3 us
  Pallas kernels: 22.4 us -> 19.8 us
  waiting for transfers between devices: 2.83 us -> 0.3 us
    ppermute x12, starting transfers between devices: 14.9 us -> 18.3 us  [exchange(): lax.ppermute(one, swap[0], swap[1])]
    unnamed x17 -> x0, local copies, waits for them, and re-layouts: 3.04 us -> none
    pallas_call x9, Pallas kernels: 22.4 us -> 19.8 us  [call(): pl.pallas_call(kernel, out_shape=tuple((jax.ShapeDtypeStruct(shape, dtype...]
    ppermute x12, waiting for transfers between devices: 2.83 us -> 0.3 us  [exchange(): lax.ppermute(one, swap[0], swap[1])]
    dynamic_slice x1 -> x0, local copies, waits for them, and re-layouts: 0.8 us -> none  [body(): lax.dynamic_slice_in_dim(send_rows[0, 0], group, 1, axis=0)]
    broadcast_in_dim x1 -> x0, local copies, waits for them, and re-layouts: 0.66 us -> none  [body(): heights = jnp.pad(tent_height, (0, LANES - tent_height.shape[0]))[None]]
  transfers between devices with their start and end apart: 12 -> 12, of which waited for: 2 -> 1; matrix products, arithmetic and copies ran while one was open for 4% -> 0% of each run, Pallas kernels for 26% -> 26%
where the time goes in v2:
time: 38.6 us; the launch traced here: 38.5 us
  Pallas kernels  19.8 us (51%)
  starting transfers between devices  18.3 us (47%)
    pallas_call x9, Pallas kernels, call(): pl.pallas_call(kernel, out_shape=tuple((jax.ShapeDtypeStruct(shape, dtype...  19.8 us
    ppermute x12, starting transfers between devices, exchange(): lax.ppermute(one, swap[0], swap[1])  18.3 us
  transfers between devices with their start and end apart: 12, of which 1 were waited for; matrix products, arithmetic and copies ran while one was open for 0% of the time, Pallas kernels for 26%

profile of v2, /device:TPU:0, one launch (start us, length us, event | category | flops | bytes accessed | tf_op | source)
XLA Modules:
  0.0 38.5 jit_solution(16210080702090947282)
XLA Ops:
  0.0 1.8 %first.1 = (f32[144,1024]{1,0:T(8,128)S(1)}, f32[64,1024]{1,0:T(8,128)S(1)}, f32[64,128]{1,0:T(8,128)S(1)}, f32[64,128]{1,0:T(8,128)S(1)}, f32[64,128]{1,0:T(8,1...) custom-call(f32[1120,128]{1,0:T(8,128)} %bitcast.9, ...), custom_call_target="tpu_custom_call" | custom-call | flops 100000000 | bytes 1048576 | tf_op jit(solution)/shard_map/first/pallas_call | solution.py:342
  1.8 0.5 %collective-permute-start = (f32[64,128]{1,0:T(8,128)S(1)}, f32[64,128]{1,0:T(8,128)S(1)}, u32[]{:S(2)}, u32[]{:S(2)}) collective-permute-start(f32[64,128]{1,0:T(8,128)S(1)} %get-tuple-element.82.rest_3_), channel_id=1, source_target_pairs={{0,2},{2,0},{4,6},{6,4},{8,10},{10,8},{12,14},{14,12},{16,18},{18,... | collective-permute-start | bytes 98312 | tf_op jit(solution)/shard_map/ppermute | solution.py:389
  2.4 5.7 %collective-permute-start.1 = (f32[64,128]{1,0:T(8,128)S(1)}, f32[64,128]{1,0:T(8,128)S(1)}, u32[]{:S(2)}, u32[]{:S(2)}) collective-permute-start(f32[64,128]{1,0:T(8,128)S(1)} %get-tuple-element.83.rest_4_), channel_id=1, source_target_pairs={{0,30},{2,4},{4,2},{6,8},{8,6},{10,12},{12,10},{14,16},{16,14},{18... | collective-permute-start | bytes 98312 | tf_op jit(solution)/shard_map/ppermute | solution.py:389
  8.0 1.5 %collective-permute-start.2 = (f32[64,128]{1,0:T(8,128)S(1)}, f32[64,128]{1,0:T(8,128)S(1)}, u32[]{:S(2)}, u32[]{:S(2)}) collective-permute-start(f32[64,128]{1,0:T(8,128)S(1)} %get-tuple-element.84.rest_5_), channel_id=1, source_target_pairs={{0,1},{1,0},{2,3},{3,2},{4,5},{5,4},{6,7},{7,6},{8,9},{9,8},{10,11... | collective-permute-start | bytes 98312 | tf_op jit(solution)/shard_map/ppermute | solution.py:389
  9.5 2.5 %plan.1 = (s32[8,1536]{1,0:T(8,128)S(1)}, s32[8,1536]{1,0:T(8,128)S(1)}, s32[8,128]{1,0:T(8,128)S(1)}, s32[8,128]{1,0:T(8,128)S(1)}, f32[144,384]{1,0:T(8,128)S(...) custom-call(f32[60,140]{1,0:T(8,128)S(1)} %get-tuple-element.63.trac, ...), custom_call_target="tpu_custom_call" | custom-call | flops 2000000000 | bytes 1048576 | tf_op jit(solution)/shard_map/plan/pallas_call | solution.py:342
  12.0 0.0 collective-permute-done.rest_0_
  12.1 0.0 collective-permute-done.1.rest_1_
  12.1 0.0 collective-permute-done.2.rest_2_
  12.1 1.5 %level.3 = (f32[256,384]{1,0:T(8,128)S(1)}, f32[64,384]{1,0:T(8,128)S(1)}, f32[64,128]{1,0:T(8,128)S(1)}, f32[64,128]{1,0:T(8,128)S(1)}, f32[64,128]{1,0:T(8,128)S(1)}) custom-call(s32[8,1536]{1,0:T(8,128)S(1)} %get-tuple-element.74.joined_ref, f32[256,384]{1,0:T(8,128)S(1)} %get-tuple-element.77.faces_ref, ...), custom_call_target="tpu_custom_call" | custom-call | flops 100000000 | bytes 1048576 | tf_op jit(solution)/shard_map/level/pallas_call | solution.py:342
  13.6 0.1 collective-permute-start.3
  13.7 2.1 %collective-permute-start.4 = (f32[64,128]{1,0:T(8,128)S(1)}, f32[64,128]{1,0:T(8,128)S(1)}, u32[]{:S(2)}, u32[]{:S(2)}) collective-permute-start(f32[64,128]{1,0:T(8,128)S(1)} %get-tuple-element.97.rest_4_), channel_id=1, source_target_pairs={{0,30},{2,4},{4,2},{6,8},{8,6},{10,12},{12,10},{14,16},{16,14},{18... | collective-permute-start | bytes 98312 | tf_op jit(solution)/shard_map/ppermute | solution.py:389
  15.7 1.5 %collective-permute-start.5 = (f32[64,128]{1,0:T(8,128)S(1)}, f32[64,128]{1,0:T(8,128)S(1)}, u32[]{:S(2)}, u32[]{:S(2)}) collective-permute-start(f32[64,128]{1,0:T(8,128)S(1)} %get-tuple-element.98.rest_5_), channel_id=1, source_target_pairs={{0,1},{1,0},{2,3},{3,2},{4,5},{5,4},{6,7},{7,6},{8,9},{9,8},{10,11... | collective-permute-start | bytes 98312 | tf_op jit(solution)/shard_map/ppermute | solution.py:389
  17.2 2.6 %between.3 = (f32[64,1024]{1,0:T(8,128)S(1)}, f32[144,384]{1,0:T(8,128)S(1)}, f32[256,384]{1,0:T(8,128)S(1)}, f32[8,384]{1,0:T(8,128)S(1)}, f32[64,384]{1,0:T(8,128)S(1)}, /*index=5*/f32[144,1024]{1,0:T(8,128)S(1)}) custom-call(s32[8,1536]{1,0:T(8,128)S(1)} %get-tuple-element.75.members_ref, s32[8,1536]{1,0:T(8,128)S(1)} %get-tuple-element.74.joined_ref, ...), custom_call_target="tpu_custom_call" | custom-call | flops 2000000000 | bytes 1048576 | tf_op jit(solution)/shard_map/between/pallas_call | solution.py:342
  19.9 0.0 collective-permute-done.3.rest_0_
  19.9 0.0 collective-permute-done.4.rest_1_
  19.9 0.0 collective-permute-done.5.rest_2_
  19.9 1.5 %level.4 = (f32[256,384]{1,0:T(8,128)S(1)}, f32[64,384]{1,0:T(8,128)S(1)}, f32[64,128]{1,0:T(8,128)S(1)}, f32[64,128]{1,0:T(8,128)S(1)}, f32[64,128]{1,0:T(8,128)S(1)}) custom-call(s32[8,1536]{1,0:T(8,128)S(1)} %get-tuple-element.74.joined_ref, f32[256,384]{1,0:T(8,128)S(1)} %get-tuple-element.93.faces_ref, ...), custom_call_target="tpu_custom_call" | custom-call | flops 100000000 | bytes 1048576 | tf_op jit(solution)/shard_map/level/pallas_call | solution.py:342
  21.4 0.1 collective-permute-start.6
  21.5 2.1 %collective-permute-start.7 = (f32[64,128]{1,0:T(8,128)S(1)}, f32[64,128]{1,0:T(8,128)S(1)}, u32[]{:S(2)}, u32[]{:S(2)}) collective-permute-start(f32[64,128]{1,0:T(8,128)S(1)} %get-tuple-element.108.rest_4_), channel_id=1, source_target_pairs={{0,30},{2,4},{4,2},{6,8},{8,6},{10,12},{12,10},{14,16},{16,14},{18... | collective-permute-start | bytes 98312 | tf_op jit(solution)/shard_map/ppermute | solution.py:389
  23.6 1.3 %collective-permute-start.8 = (f32[64,128]{1,0:T(8,128)S(1)}, f32[64,128]{1,0:T(8,128)S(1)}, u32[]{:S(2)}, u32[]{:S(2)}) collective-permute-start(f32[64,128]{1,0:T(8,128)S(1)} %get-tuple-element.109.rest_5_), channel_id=1, source_target_pairs={{0,1},{1,0},{2,3},{3,2},{4,5},{5,4},{6,7},{7,6},{8,9},{9,8},{10,11... | collective-permute-start | bytes 98312 | tf_op jit(solution)/shard_map/ppermute | solution.py:389
  24.9 2.6 %between.4 = (f32[64,1024]{1,0:T(8,128)S(1)}, f32[144,384]{1,0:T(8,128)S(1)}, f32[256,384]{1,0:T(8,128)S(1)}, f32[8,384]{1,0:T(8,128)S(1)}, f32[64,384]{1,0:T(8,128)S(1)}, /*index=5*/f32[144,1024]{1,0:T(8,128)S(1)}) custom-call(s32[8,1536]{1,0:T(8,128)S(1)} %get-tuple-element.75.members_ref, s32[8,1536]{1,0:T(8,128)S(1)} %get-tuple-element.74.joined_ref, ...), custom_call_target="tpu_custom_call" | custom-call | flops 2000000000 | bytes 1048576 | tf_op jit(solution)/shard_map/between/pallas_call | solution.py:342
  27.6 0.0 collective-permute-done.6.rest_0_
  27.6 0.0 collective-permute-done.7.rest_1_
  27.6 0.0 collective-permute-done.8.rest_2_
  27.6 1.5 %level.5 = (f32[256,384]{1,0:T(8,128)S(1)}, f32[64,384]{1,0:T(8,128)S(1)}, f32[64,128]{1,0:T(8,128)S(1)}, f32[64,128]{1,0:T(8,128)S(1)}, f32[64,128]{1,0:T(8,128)S(1)}) custom-call(s32[8,1536]{1,0:T(8,128)S(1)} %get-tuple-element.74.joined_ref, f32[256,384]{1,0:T(8,128)S(1)} %get-tuple-element.104.faces_ref, ...), custom_call_target="tpu_custom_call" | custom-call | flops 100000000 | bytes 1048576 | tf_op jit(solution)/shard_map/level/pallas_call | solution.py:342
  29.1 0.1 collective-permute-start.9
  29.2 2.1 %collective-permute-start.10 = (f32[64,128]{1,0:T(8,128)S(1)}, f32[64,128]{1,0:T(8,128)S(1)}, u32[]{:S(2)}, u32[]{:S(2)}) collective-permute-start(f32[64,128]{1,0:T(8,128)S(1)} %get-tuple-element.119), channel_id=1, source_target_pairs={{0,30},{2,4},{4,2},{6,8},{8,6},{10,12},{12,10},{14,16},{16,14},{18... | collective-permute-start | bytes 98312 | tf_op jit(solution)/shard_map/ppermute | solution.py:389
  31.3 1.3 %collective-permute-start.11 = (f32[64,128]{1,0:T(8,128)S(1)}, f32[64,128]{1,0:T(8,128)S(1)}, u32[]{:S(2)}, u32[]{:S(2)}) collective-permute-start(f32[64,128]{1,0:T(8,128)S(1)} %get-tuple-element.120), channel_id=1, source_target_pairs={{0,1},{1,0},{2,3},{3,2},{4,5},{5,4},{6,7},{7,6},{8,9},{9,8},{10,11... | collective-permute-start | bytes 98312 | tf_op jit(solution)/shard_map/ppermute | solution.py:389
  32.6 2.4 %between.5 = (f32[144,384]{1,0:T(8,128)S(1)}, f32[256,384]{1,0:T(8,128)S(1)}, f32[8,384]{1,0:T(8,128)S(1)}, f32[144,1024]{1,0:T(8,128)S(1)}) custom-call(s32[8,1536]{1,0:T(8,128)S(1)} %get-tuple-element.75.members_ref, s32[8,1536]{1,0:T(8,128)S(1)} %get-tuple-element.74.joined_ref, s32[8,128]{1,0:T(8,128)S(1)} %get-tuple-element.76.places_ref, ...), custom_call_target="tpu_custom_call" | custom-call | flops 2000000000 | bytes 1048576 | tf_op jit(solution)/shard_map/between/pallas_call | solution.py:342
  35.0 0.0 collective-permute-done.9.rest_0_
  35.1 0.2 collective-permute-done.10.rest_1_
  35.3 0.0 collective-permute-done.11.rest_2_
  35.3 3.2 %last.1 = f32[1120,128]{1,0:T(8,128)} custom-call(s32[8,1536]{1,0:T(8,128)S(1)} %get-tuple-element.74.joined_ref, f32[144,384]{1,0:T(8,128)S(1)} %get-tuple-element.114.own_ref, f32[256,384]{1,0:T(8,128)S(1)} %get-tuple-element.115.faces_ref, f32[8,384]{1,0:T(8,128)S(1)} %get-tuple-element.116.weights_ref, bf16[144,768]{1,0:T(8,128)(2,1)S(1)} %get-tuple-element.89.lift_ref, ...), custom_call_target="tpu_custom_call" | custom-call | flops 1000000000 | bytes 1048576 | tf_op jit(solution)/shard_map/last/pallas_call | solution.py:342
Async XLA Ops:
  1.8 10.2 %collective-permute-start = (f32[64,128]{1,0:T(8,128)S(1)}, f32[64,128]{1,0:T(8,128)S(1)}, u32[]{:S(2)}, u32[]{:S(2)}) collective-permute-start(f32[64,128]{1,0:T(8,128)S(1)} %get-tuple-element.82.rest_3_), channel_id=1, source_target_pairs={{0,2},{2,0},{4,6},{6,4},{8,10},{10,8},{12,14},{14,12},{16,18},{18,... | collective-permute-start | bytes 98312 | tf_op jit(solution)/shard_map/ppermute | solution.py:389
  2.4 9.7 %collective-permute-start.1 = (f32[64,128]{1,0:T(8,128)S(1)}, f32[64,128]{1,0:T(8,128)S(1)}, u32[]{:S(2)}, u32[]{:S(2)}) collective-permute-start(f32[64,128]{1,0:T(8,128)S(1)} %get-tuple-element.83.rest_4_), channel_id=1, source_target_pairs={{0,30},{2,4},{4,2},{6,8},{8,6},{10,12},{12,10},{14,16},{16,14},{18... | collective-permute-start | bytes 98312 | tf_op jit(solution)/shard_map/ppermute | solution.py:389
  8.0 4.0 %collective-permute-start.2 = (f32[64,128]{1,0:T(8,128)S(1)}, f32[64,128]{1,0:T(8,128)S(1)}, u32[]{:S(2)}, u32[]{:S(2)}) collective-permute-start(f32[64,128]{1,0:T(8,128)S(1)} %get-tuple-element.84.rest_5_), channel_id=1, source_target_pairs={{0,1},{1,0},{2,3},{3,2},{4,5},{5,4},{6,7},{7,6},{8,9},{9,8},{10,11... | collective-permute-start | bytes 98312 | tf_op jit(solution)/shard_map/ppermute | solution.py:389
  13.6 6.3 %collective-permute-start.3 = (f32[64,128]{1,0:T(8,128)S(1)}, f32[64,128]{1,0:T(8,128)S(1)}, u32[]{:S(2)}, u32[]{:S(2)}) collective-permute-start(f32[64,128]{1,0:T(8,128)S(1)} %get-tuple-element.96.rest_3_), channel_id=1, source_target_pairs={{0,2},{2,0},{4,6},{6,4},{8,10},{10,8},{12,14},{14,12},{16,18},{18,... | collective-permute-start | bytes 98312 | tf_op jit(solution)/shard_map/ppermute | solution.py:389
  13.7 6.2 %collective-permute-start.4 = (f32[64,128]{1,0:T(8,128)S(1)}, f32[64,128]{1,0:T(8,128)S(1)}, u32[]{:S(2)}, u32[]{:S(2)}) collective-permute-start(f32[64,128]{1,0:T(8,128)S(1)} %get-tuple-element.97.rest_4_), channel_id=1, source_target_pairs={{0,30},{2,4},{4,2},{6,8},{8,6},{10,12},{12,10},{14,16},{16,14},{18... | collective-permute-start | bytes 98312 | tf_op jit(solution)/shard_map/ppermute | solution.py:389
  15.7 4.2 %collective-permute-start.5 = (f32[64,128]{1,0:T(8,128)S(1)}, f32[64,128]{1,0:T(8,128)S(1)}, u32[]{:S(2)}, u32[]{:S(2)}) collective-permute-start(f32[64,128]{1,0:T(8,128)S(1)} %get-tuple-element.98.rest_5_), channel_id=1, source_target_pairs={{0,1},{1,0},{2,3},{3,2},{4,5},{5,4},{6,7},{7,6},{8,9},{9,8},{10,11... | collective-permute-start | bytes 98312 | tf_op jit(solution)/shard_map/ppermute | solution.py:389
  21.4 6.1 %collective-permute-start.6 = (f32[64,128]{1,0:T(8,128)S(1)}, f32[64,128]{1,0:T(8,128)S(1)}, u32[]{:S(2)}, u32[]{:S(2)}) collective-permute-start(f32[64,128]{1,0:T(8,128)S(1)} %get-tuple-element.107.rest_3_), channel_id=1, source_target_pairs={{0,2},{2,0},{4,6},{6,4},{8,10},{10,8},{12,14},{14,12},{16,18},{18,... | collective-permute-start | bytes 98312 | tf_op jit(solution)/shard_map/ppermute | solution.py:389
  21.5 6.1 %collective-permute-start.7 = (f32[64,128]{1,0:T(8,128)S(1)}, f32[64,128]{1,0:T(8,128)S(1)}, u32[]{:S(2)}, u32[]{:S(2)}) collective-permute-start(f32[64,128]{1,0:T(8,128)S(1)} %get-tuple-element.108.rest_4_), channel_id=1, source_target_pairs={{0,30},{2,4},{4,2},{6,8},{8,6},{10,12},{12,10},{14,16},{16,14},{18... | collective-permute-start | bytes 98312 | tf_op jit(solution)/shard_map/ppermute | solution.py:389
  23.6 4.0 %collective-permute-start.8 = (f32[64,128]{1,0:T(8,128)S(1)}, f32[64,128]{1,0:T(8,128)S(1)}, u32[]{:S(2)}, u32[]{:S(2)}) collective-permute-start(f32[64,128]{1,0:T(8,128)S(1)} %get-tuple-element.109.rest_5_), channel_id=1, source_target_pairs={{0,1},{1,0},{2,3},{3,2},{4,5},{5,4},{6,7},{7,6},{8,9},{9,8},{10,11... | collective-permute-start | bytes 98312 | tf_op jit(solution)/shard_map/ppermute | solution.py:389
  29.1 5.9 %collective-permute-start.9 = (f32[64,128]{1,0:T(8,128)S(1)}, f32[64,128]{1,0:T(8,128)S(1)}, u32[]{:S(2)}, u32[]{:S(2)}) collective-permute-start(f32[64,128]{1,0:T(8,128)S(1)} %get-tuple-element.118), channel_id=1, source_target_pairs={{0,2},{2,0},{4,6},{6,4},{8,10},{10,8},{12,14},{14,12},{16,18},{18,... | collective-permute-start | bytes 98312 | tf_op jit(solution)/shard_map/ppermute | solution.py:389
  29.2 6.1 %collective-permute-start.10 = (f32[64,128]{1,0:T(8,128)S(1)}, f32[64,128]{1,0:T(8,128)S(1)}, u32[]{:S(2)}, u32[]{:S(2)}) collective-permute-start(f32[64,128]{1,0:T(8,128)S(1)} %get-tuple-element.119), channel_id=1, source_target_pairs={{0,30},{2,4},{4,2},{6,8},{8,6},{10,12},{12,10},{14,16},{16,14},{18... | collective-permute-start | bytes 98312 | tf_op jit(solution)/shard_map/ppermute | solution.py:389
  31.3 4.0 %collective-permute-start.11 = (f32[64,128]{1,0:T(8,128)S(1)}, f32[64,128]{1,0:T(8,128)S(1)}, u32[]{:S(2)}, u32[]{:S(2)}) collective-permute-start(f32[64,128]{1,0:T(8,128)S(1)} %get-tuple-element.120), channel_id=1, source_target_pairs={{0,1},{1,0},{2,3},{3,2},{4,5},{5,4},{6,7},{7,6},{8,9},{9,8},{10,11... | collective-permute-start | bytes 98312 | tf_op jit(solution)/shard_map/ppermute | solution.py:389

commit v3 on v2

--- a/solution.py
+++ b/solution.py
@@ -15,6 +15,8 @@
 LANES = 128
 NO_GROUP = 1 << 20
 ARGUMENTS = 10
+FIELD_COPIES = 4
+ROW_CHUNK = 48
 
 f32, bf16, i32 = jnp.float32, jnp.bfloat16, jnp.int32
 precise = lax.Precision.HIGHEST
@@ -126,13 +128,16 @@
     (columns_ref, out_ref), refs = refs[:2], refs[2:]
     sends, refs = refs[:len(swaps)], refs[len(swaps):]
     *held, fields_ref, arrived = refs
-    copies = [
-        pltpu.make_async_copy(source, target, arrived.at[i])
-        for i, (source, target) in enumerate(zip([fields_hbm] + given, [fields_ref] + held))
-    ]
+    share = fields_ref.shape[0] // FIELD_COPIES
+    pairs = list(zip(given[:2], held[:2]))
+    pairs += [(fields_hbm.at[pl.ds(i * share, share)], fields_ref.at[pl.ds(i * share, share)])
+              for i in range(FIELD_COPIES)]
+    needed = len(pairs)
+    pairs += list(zip(given[2:], held[2:]))
+    copies = [pltpu.make_async_copy(source, target, arrived.at[i]) for i, (source, target) in enumerate(pairs)]
     for copy in copies:
         copy.start()
-    for copy in copies[:3]:
+    for copy in copies[:needed]:
         copy.wait()
     trace_ref, send_ref = held[:2]
     rows = out_ref.shape[0]
@@ -149,7 +154,7 @@
     for index, send in zip(sent_rows(send_ref, swaps), sends):
         send[...] = pick(ref_blocks(out_ref, count), index, index >> 7)
     columns_ref[...] = pad_rows(fields, columns_ref.shape[0])
-    for copy in copies[3:]:
+    for copy in copies[needed:]:
         copy.wait()
 
 
@@ -157,34 +162,43 @@
     return joined_ref.shape[0] // 2
 
 
-def local_part(level, members_ref, joined_ref, columns_ref, out_ref, heights_ref, trace_grow_ref,
-               own_ref, faces_ref, weights_ref, base_ref=None):
+def own_block(level, block, members_ref, joined_ref, columns_ref, heights_ref, own_ref, weights_ref):
     faces = faces_in(joined_ref)
-    count = columns_ref.shape[1] // LANES
+    here, there = block_at(block), block_at(level * (BLOCK // LANES) + block)
+    index = members_ref[0:1, there]
+    own_ref[:, here] = pick(ref_blocks(columns_ref, columns_ref.shape[1] // LANES), index, index >> 7)
+    pattern = jnp.broadcast_to(joined_ref[faces:faces + 1, there], (8, LANES))
+    height = jnp.take_along_axis(
+        jnp.broadcast_to(heights_ref[...], (8, LANES)), pattern, axis=1, mode="promise_in_bounds")
+    weight = jnp.ones((8, LANES), f32)
+    for power in range(1, POWERS + 1):
+        weight = weight * height
+        weights_ref[power - 1:power, here] = weight[0:1] * WEIGHTS[power]
+
+
+def face_block(level, block, joined_ref, out_ref, faces_ref):
     trace_rows = out_ref.shape[0]
-    for block in range(BLOCK // LANES):
-        here = block_at(block)
-        there = block_at(level * (BLOCK // LANES) + block)
-        index = members_ref[0:1, there]
-        own_ref[:, here] = pick(ref_blocks(columns_ref, count), index, index >> 7)
-        pattern = jnp.broadcast_to(joined_ref[faces:faces + 1, there], (8, LANES))
-        height = jnp.take_along_axis(
-            jnp.broadcast_to(heights_ref[...], (8, LANES)), pattern, axis=1, mode="promise_in_bounds")
-        weight = jnp.ones((8, LANES), f32)
-        for power in range(1, POWERS + 1):
-            weight = weight * height
-            weights_ref[power - 1:power, here] = weight[0:1] * WEIGHTS[power]
-    if base_ref is not None:
-        stacked = product(trace_grow_ref[...], stacked_columns(own_ref[...]))
-    for block in range(BLOCK // LANES):
-        here = block_at(block)
-        there = block_at(level * (BLOCK // LANES) + block)
-        for face in range(faces):
-            index = joined_ref[face:face + 1, there]
-            faces_ref[face * trace_rows:(face + 1) * trace_rows, here] = pick(
-                ref_blocks(out_ref, count), index, index >> 7, jnp.zeros((trace_rows, LANES), f32))
-    if base_ref is not None:
-        base_ref[...] = summed_powers(stacked[trace_rows:], weights_ref, trace_rows, stacked[:trace_rows])
+    here, there = block_at(block), block_at(level * (BLOCK // LANES) + block)
+    for face in range(faces_in(joined_ref)):
+        index = joined_ref[face:face + 1, there]
+        faces_ref[face * trace_rows:(face + 1) * trace_rows, here] = pick(
+            ref_blocks(out_ref, out_ref.shape[1] // LANES), index, index >> 7, jnp.zeros((trace_rows, LANES), f32))
+
+
+def base_traces(own_ref, trace_grow_ref, weights_ref, rows):
+    stacked = product(trace_grow_ref[...], stacked_columns(own_ref[...]))
+    return summed_powers(stacked[rows:], weights_ref, rows, stacked[:rows])
+
+
+def row_chunks(rows):
+    return [slice(low, low + ROW_CHUNK) for low in range(0, rows, ROW_CHUNK)]
+
+
+def grown_rows(chunk, stacked, loaded, grow_ref, weights_ref):
+    rows = loaded.shape[0]
+    matrix = jnp.concatenate(
+        [grow_ref[power * rows + chunk.start:power * rows + chunk.stop, :] for power in range(POWERS)], axis=0)
+    return summed_powers(product(matrix, stacked), weights_ref, ROW_CHUNK, loaded[chunk])
 
 
 def matrix_powers(operator_ref, trace_ref, lift_ref, grow_ref, trace_grow_ref, mix_ref, lift_out_ref):
@@ -255,20 +269,17 @@
     index = pad_rows(jnp.concatenate(sent_rows(send_ref, swaps), axis=0), 8)
     send_places_ref[...] = pick(row_blocks(at, 8), index, index >> 7)
     matrix_powers(operator_ref, trace_ref, lift_ref, grow_ref, trace_grow_ref, mix_ref, lift_out_ref)
-    local_part(0, members_ref, joined_ref, columns_ref, out_ref, wide_heights_ref, trace_grow_ref,
-               own_ref, faces_ref, weights_ref, base_ref)
-
-
-def advanced_columns(own_ref, inflow_ref, lift_ref, grow_ref, weights_ref):
-    loaded = own_ref[...] + product(lift_ref[...], stacked_columns(inflow_ref[...]))
-    stacked = product(grow_ref[...], stacked_columns(loaded))
-    return summed_powers(stacked, weights_ref, loaded.shape[0], loaded)
-
-
-def settle(level, new_ref, places_ref, before, block):
+    for block in range(BLOCK // LANES):
+        own_block(0, block, members_ref, joined_ref, columns_ref, wide_heights_ref, own_ref, weights_ref)
+    base_ref[...] = base_traces(own_ref, trace_grow_ref, weights_ref, out_ref.shape[0])
+    for block in range(BLOCK // LANES):
+        face_block(0, block, joined_ref, out_ref, faces_ref)
+
+
+def settle(level, blocks, places_ref, before, block):
     index = places_ref[block:block + 1, :]
     which = (index >> 7) - level * (BLOCK // LANES)
-    return pick(ref_blocks(new_ref, BLOCK // LANES), index, which, before)
+    return pick(blocks, index, which, before)
 
 
 def between_kernel(level, members_ref, joined_ref, places_ref, columns_ref, old_out_ref, new_trace_ref, heights_ref,
@@ -276,34 +287,42 @@
     if level > 1:
         advanced_ref, rest = rest[0], rest[1:]
     if level == LEVELS - 1:
-        own_ref, faces_ref, weights_ref, new_advanced_ref, out_ref, new_ref = rest
-        base_ref = None
+        own_ref, faces_ref, weights_ref, new_advanced_ref, out_ref = rest
     else:
-        out_ref, own_ref, faces_ref, weights_ref, base_ref, new_advanced_ref, new_ref = rest
-    elements = columns_ref.shape[1]
-    for block in range(elements // LANES):
+        out_ref, own_ref, faces_ref, weights_ref, base_ref, new_advanced_ref = rest
+    count = places_ref.shape[0]
+    done = level - 1
+    loaded = old_own_ref[...] + product(lift_ref[...], stacked_columns(inflow_ref[...]))
+    for block in range(count):
         here = block_at(block)
-        out_ref[:, here] = settle(level - 1, new_trace_ref, places_ref, old_out_ref[:, here], block)
-    local_part(level, members_ref, joined_ref, columns_ref, out_ref, heights_ref, trace_grow_ref,
-               own_ref, faces_ref, weights_ref, base_ref)
-    new_ref[...] = advanced_columns(old_own_ref, inflow_ref, lift_ref, grow_ref, old_weights_ref)
-    for block in range(elements // LANES):
-        here = block_at(block)
-        before = advanced_ref[:, here] if level > 1 else None
-        new_advanced_ref[:, here] = settle(level - 1, new_ref, places_ref, before, block)
-
-
-def gather_inflow(level, received, joined_ref, faces_ref, inflow_ref, count):
+        out_ref[:, here] = settle(
+            done, ref_blocks(new_trace_ref, BLOCK // LANES), places_ref, old_out_ref[:, here], block)
+    stacked = stacked_columns(loaded)
+    chunks = row_chunks(loaded.shape[0])
+    pieces = BLOCK // LANES
+    for number, chunk in enumerate(chunks):
+        new = grown_rows(chunk, stacked, loaded, grow_ref, old_weights_ref)
+        for block in range(number * pieces // len(chunks), (number + 1) * pieces // len(chunks)):
+            own_block(level, block, members_ref, joined_ref, columns_ref, heights_ref, own_ref, weights_ref)
+            face_block(level, block, joined_ref, out_ref, faces_ref)
+        for block in range(count):
+            here = block_at(block)
+            before = advanced_ref[chunk, here] if level > 1 else None
+            new_advanced_ref[chunk, here] = settle(done, value_blocks(new), places_ref, before, block)
+    if level < LEVELS - 1:
+        base_ref[...] = base_traces(own_ref, trace_grow_ref, weights_ref, out_ref.shape[0])
+
+
+def inflow_block(level, block, received, joined_ref, faces_ref, count):
     faces = faces_in(joined_ref)
     trace_rows = faces_ref.shape[0] // faces
     blocks = [(count + i, functools.partial(lambda ref: ref[...], ref)) for i, ref in enumerate(received)]
-    for block in range(BLOCK // LANES):
-        here = block_at(block)
-        there = block_at(level * (BLOCK // LANES) + block)
-        for face in range(faces):
-            part = slice(face * trace_rows, (face + 1) * trace_rows)
-            index = joined_ref[face:face + 1, there]
-            inflow_ref[part, here] = pick(blocks, index, index >> 7, faces_ref[part, here])
+    here, there = block_at(block), block_at(level * (BLOCK // LANES) + block)
+    parts = []
+    for face in range(faces):
+        index = joined_ref[face:face + 1, there]
+        parts.append(pick(blocks, index, index >> 7, faces_ref[face * trace_rows:(face + 1) * trace_rows, here]))
+    return jnp.concatenate(parts, axis=0)
 
 
 def level_kernel(level, messages, count, joined_ref, faces_ref, weights_ref, base_ref, mix_ref, send_places_ref,
@@ -312,10 +331,17 @@
     sent, rest = rest[:messages], rest[messages:]
     inflow_ref, new_trace_ref, sends = rest[0], rest[1], rest[2:]
     trace_rows = new_trace_ref.shape[0]
-    gather_inflow(level, received, joined_ref, faces_ref, inflow_ref, count)
-    stacked = product(mix_ref[...], stacked_columns(inflow_ref[...]))
-    new_trace_ref[...] = summed_powers(
-        stacked[trace_rows:], weights_ref, trace_rows, base_ref[...] + stacked[:trace_rows])
+    blocks = range(BLOCK // LANES)
+    for tile in (blocks[:2], blocks[2:]):
+        across = slice(tile[0] * LANES, (tile[-1] + 1) * LANES)
+        inflow = jnp.concatenate(
+            [inflow_block(level, block, received, joined_ref, faces_ref, count) for block in tile], axis=1)
+        inflow_ref[:, across] = inflow
+        stacked = product(mix_ref[...], stacked_columns(inflow))
+        total = base_ref[:, across] + stacked[:trace_rows]
+        for power in range(1, POWERS + 1):
+            total = total + stacked[power * trace_rows:(power + 1) * trace_rows] * weights_ref[power - 1:power, across]
+        new_trace_ref[:, across] = total
     for group, (before, send) in enumerate(zip(sent, sends)):
         index = send_places_ref[group:group + 1, :]
         which = (index >> 7) - level * (BLOCK // LANES)
@@ -324,17 +350,28 @@
 
 def last_kernel(level, messages, joined_ref, own_ref, faces_ref, weights_ref, lift_ref, grow_ref,
                 places_ref, advanced_ref, *rest):
-    received, (final_ref, inflow_ref, new_ref) = rest[:messages], rest[messages:]
+    received, (final_hbm, final_ref, sent) = rest[:messages], rest[messages:]
     count = places_ref.shape[0]
-    gather_inflow(level, received, joined_ref, faces_ref, inflow_ref, count)
-    new_ref[...] = advanced_columns(own_ref, inflow_ref, lift_ref, grow_ref, weights_ref)
     comp = final_ref.shape[0] // count
-    for block in range(count):
-        done = settle(level, new_ref, places_ref, advanced_ref[:, block_at(block)], block)
-        final_ref[pl.ds(block, comp, stride=count), :] = done[:comp]
-
-
-def call(kernel, name, flops, operands, outs, scratch=(), hbm=False):
+    inflow = jnp.concatenate(
+        [inflow_block(level, block, received, joined_ref, faces_ref, count) for block in range(BLOCK // LANES)], axis=1)
+    loaded = own_ref[...] + product(lift_ref[...], stacked_columns(inflow))
+    stacked = stacked_columns(loaded)
+    copies = []
+    for number, chunk in enumerate(row_chunks(loaded.shape[0])):
+        new = grown_rows(chunk, stacked, loaded, grow_ref, weights_ref)
+        height = min(chunk.stop, comp) - chunk.start
+        for block in range(count):
+            done = settle(level, value_blocks(new), places_ref, advanced_ref[chunk, block_at(block)], block)
+            final_ref[pl.ds(chunk.start * count + block, height, stride=count), :] = done[:height]
+        part = pl.ds(chunk.start * count, height * count)
+        copies.append(pltpu.make_async_copy(final_ref.at[part], final_hbm.at[part], sent.at[number]))
+        copies[-1].start()
+    for copy in copies:
+        copy.wait()
+
+
+def call(kernel, name, flops, operands, outs, scratch=(), hbm=False, out_hbm=False):
     vmem = pl.BlockSpec(memory_space=pltpu.VMEM)
     given = pl.BlockSpec(memory_space=pltpu.HBM) if hbm else vmem
     if hbm:
@@ -343,7 +380,7 @@
         kernel,
         out_shape=tuple(jax.ShapeDtypeStruct(shape, dtype) for shape, dtype in outs),
         in_specs=[given] * len(operands),
-        out_specs=tuple([vmem] * len(outs)),
+        out_specs=tuple([pl.BlockSpec(memory_space=pltpu.HBM) if out_hbm else vmem] * len(outs)),
         scratch_shapes=[one if not isinstance(one, tuple) else pltpu.VMEM(*one) for one in scratch],
         compiler_params=pltpu.CompilerParams(vmem_limit_bytes=16 * 1024 * 1024),
         cost_estimate=pl.CostEstimate(flops=flops, bytes_accessed=1 << 20, transcendentals=0),
@@ -382,7 +419,8 @@
     padded, count = LEVELS * BLOCK, elements // LANES
     bnd = send_list.shape[-1]
 
-    swaps = swap_plan("sector", True, 0, 1) + swap_plan("radial", False, 2, 3)
+    near, *far = swap_plan("sector", True, 0, 1)
+    swaps = far + swap_plan("radial", False, 2, 3) + [near]
     messages = len(swaps)
 
     def exchange(sent):
@@ -399,7 +437,7 @@
     columns, out, *rest = call(
         functools.partial(first_kernel, swaps), "first", 10 ** 8, [fields.reshape(flat)] + arguments,
         [whole, table] + [message] * messages + [(one.shape, one.dtype) for one in arguments],
-        [(flat, f32), pltpu.SemaphoreType.DMA((ARGUMENTS,))], hbm=True)
+        [(flat, f32), pltpu.SemaphoreType.DMA((ARGUMENTS - 1 + FIELD_COPIES,))], hbm=True)
     sent, held = rest[:messages], rest[messages:]
     received = exchange(sent)
     members, joined, places, send_places, mine, inner, weights, base, grow, trace_grow, mix, lift, heights = call(
@@ -421,14 +459,14 @@
                     trace_grow] + advanced
         if level + 1 < LEVELS - 1:
             out, mine, inner, weights, base, *advanced = call(
-                beside, "between", 2 * 10 ** 9, operands, [table, own, face_stack, weight, traced, whole], [own])
+                beside, "between", 2 * 10 ** 9, operands, [table, own, face_stack, weight, traced, whole])
         else:
             mine, inner, weights, *advanced = call(
-                beside, "between", 2 * 10 ** 9, operands, [own, face_stack, weight, whole], [table, own])
+                beside, "between", 2 * 10 ** 9, operands, [own, face_stack, weight, whole], [table])
     final, = call(
         functools.partial(last_kernel, LEVELS - 1, messages), "last", 10 ** 9,
         [joined, mine, inner, weights, lift, grow, places] + advanced + received,
-        [(flat, f32)], [face_stack, own])
+        [(flat, f32)], [(flat, f32), pltpu.SemaphoreType.DMA((-(-rows // ROW_CHUNK),))], out_hbm=True)
     return final.reshape(1, 1, comp, elements)
 
 

time: 38.6 us -> 37.4 us (0.969)
  Pallas kernels: 19.8 us -> 18.6 us
  starting transfers between devices: 18.3 us -> 17.7 us
  waiting for transfers between devices: 0.3 us -> 0.71 us
    pallas_call x9, Pallas kernels: 19.8 us -> 18.6 us  [call(): pl.pallas_call(kernel, out_shape=tuple((jax.ShapeDtypeStruct(shape, dtype...]
    ppermute x12, starting transfers between devices: 18.3 us -> 17.7 us  [exchange(): lax.ppermute(one, swap[0], swap[1])]
    ppermute x12, waiting for transfers between devices: 0.3 us -> 0.71 us  [exchange(): lax.ppermute(one, swap[0], swap[1])]
  transfers between devices with their start and end apart: 12 -> 12, of which waited for: 1 -> 3; matrix products, arithmetic and copies ran while one was open for 0% -> 0% of each run, Pallas kernels for 26% -> 25%
where the time goes in v3:
time: 37.4 us; the launch traced here: 37.3 us
  Pallas kernels  18.6 us (50%)
  starting transfers between devices  17.7 us (47%)
  waiting for transfers between devices  0.71 us (2%)
    pallas_call x9, Pallas kernels, call(): pl.pallas_call(kernel, out_shape=tuple((jax.ShapeDtypeStruct(shape, dtype...  18.6 us
    ppermute x12, starting transfers between devices, exchange(): lax.ppermute(one, swap[0], swap[1])  17.7 us
  transfers between devices with their start and end apart: 12, of which 3 were waited for; matrix products, arithmetic and copies ran while one was open for 0% of the time, Pallas kernels for 25%

profile of v3, /device:TPU:0, one launch (start us, length us, event | category | flops | bytes accessed | tf_op | source)
XLA Modules:
  0.0 37.3 jit_solution(16865105193635779866)
XLA Ops:
  0.0 2.0 %first.1 = (f32[144,1024]{1,0:T(8,128)S(1)}, f32[64,1024]{1,0:T(8,128)S(1)}, f32[64,128]{1,0:T(8,128)S(1)}, f32[64,128]{1,0:T(8,128)S(1)}, f32[64,128]{1,0:T(8,1...) custom-call(f32[1120,128]{1,0:T(8,128)} %bitcast.9, ...), custom_call_target="tpu_custom_call" | custom-call | flops 100000000 | bytes 1048576 | tf_op jit(solution)/shard_map/first/pallas_call | solution.py:379
  2.0 5.5 %collective-permute-start = (f32[64,128]{1,0:T(8,128)S(1)}, f32[64,128]{1,0:T(8,128)S(1)}, u32[]{:S(2)}, u32[]{:S(2)}) collective-permute-start(f32[64,128]{1,0:T(8,128)S(1)} %get-tuple-element.82.rest_3_), channel_id=1, source_target_pairs={{0,30},{2,4},{4,2},{6,8},{8,6},{10,12},{12,10},{14,16},{16,14},{18... | collective-permute-start | bytes 98312 | tf_op jit(solution)/shard_map/ppermute | solution.py:427
  7.5 1.5 %collective-permute-start.1 = (f32[64,128]{1,0:T(8,128)S(1)}, f32[64,128]{1,0:T(8,128)S(1)}, u32[]{:S(2)}, u32[]{:S(2)}) collective-permute-start(f32[64,128]{1,0:T(8,128)S(1)} %get-tuple-element.83.rest_4_), channel_id=1, source_target_pairs={{0,1},{1,0},{2,3},{3,2},{4,5},{5,4},{6,7},{7,6},{8,9},{9,8},{10,11... | collective-permute-start | bytes 98312 | tf_op jit(solution)/shard_map/ppermute | solution.py:427
  9.0 0.0 collective-permute-start.2
  9.0 2.5 %plan.1 = (s32[8,1536]{1,0:T(8,128)S(1)}, s32[8,1536]{1,0:T(8,128)S(1)}, s32[8,128]{1,0:T(8,128)S(1)}, s32[8,128]{1,0:T(8,128)S(1)}, f32[144,384]{1,0:T(8,128)S(...) custom-call(f32[60,140]{1,0:T(8,128)S(1)} %get-tuple-element.63.trac, ...), custom_call_target="tpu_custom_call" | custom-call | flops 2000000000 | bytes 1048576 | tf_op jit(solution)/shard_map/plan/pallas_call | solution.py:379
  11.5 0.0 collective-permute-done.rest_0_
  11.5 0.0 collective-permute-done.1.rest_1_
  11.5 0.0 collective-permute-done.2.rest_2_
  11.5 1.5 %level.3 = (f32[256,384]{1,0:T(8,128)S(1)}, f32[64,384]{1,0:T(8,128)S(1)}, f32[64,128]{1,0:T(8,128)S(1)}, f32[64,128]{1,0:T(8,128)S(1)}, f32[64,128]{1,0:T(8,128)S(1)}) custom-call(s32[8,1536]{1,0:T(8,128)S(1)} %get-tuple-element.74.joined_ref, f32[256,384]{1,0:T(8,128)S(1)} %get-tuple-element.77.faces_ref, ...), custom_call_target="tpu_custom_call" | custom-call | flops 100000000 | bytes 1048576 | tf_op jit(solution)/shard_map/level/pallas_call | solution.py:379
  13.0 2.1 %collective-permute-start.3 = (f32[64,128]{1,0:T(8,128)S(1)}, f32[64,128]{1,0:T(8,128)S(1)}, u32[]{:S(2)}, u32[]{:S(2)}) collective-permute-start(f32[64,128]{1,0:T(8,128)S(1)} %get-tuple-element.96.rest_3_), channel_id=1, source_target_pairs={{0,30},{2,4},{4,2},{6,8},{8,6},{10,12},{12,10},{14,16},{16,14},{18... | collective-permute-start | bytes 98312 | tf_op jit(solution)/shard_map/ppermute | solution.py:427
  15.1 1.5 %collective-permute-start.4 = (f32[64,128]{1,0:T(8,128)S(1)}, f32[64,128]{1,0:T(8,128)S(1)}, u32[]{:S(2)}, u32[]{:S(2)}) collective-permute-start(f32[64,128]{1,0:T(8,128)S(1)} %get-tuple-element.97.rest_4_), channel_id=1, source_target_pairs={{0,1},{1,0},{2,3},{3,2},{4,5},{5,4},{6,7},{7,6},{8,9},{9,8},{10,11... | collective-permute-start | bytes 98312 | tf_op jit(solution)/shard_map/ppermute | solution.py:427
  16.6 0.0 collective-permute-start.5
  16.6 2.2 %between.3 = (f32[64,1024]{1,0:T(8,128)S(1)}, f32[144,384]{1,0:T(8,128)S(1)}, f32[256,384]{1,0:T(8,128)S(1)}, f32[8,384]{1,0:T(8,128)S(1)}, f32[64,384]{1,0:T(8,128)S(1)}, /*index=5*/f32[144,1024]{1,0:T(8,128)S(1)}) custom-call(s32[8,1536]{1,0:T(8,128)S(1)} %get-tuple-element.75.members_ref, s32[8,1536]{1,0:T(8,128)S(1)} %get-tuple-element.74.joined_ref, ...), custom_call_target="tpu_custom_call" | custom-call | flops 2000000000 | bytes 1048576 | tf_op jit(solution)/shard_map/between/pallas_call | solution.py:379
  18.8 0.3 collective-permute-done.3.rest_0_
  19.1 0.0 collective-permute-done.4.rest_1_
  19.1 0.0 collective-permute-done.5.rest_2_
  19.1 1.5 %level.4 = (f32[256,384]{1,0:T(8,128)S(1)}, f32[64,384]{1,0:T(8,128)S(1)}, f32[64,128]{1,0:T(8,128)S(1)}, f32[64,128]{1,0:T(8,128)S(1)}, f32[64,128]{1,0:T(8,128)S(1)}) custom-call(s32[8,1536]{1,0:T(8,128)S(1)} %get-tuple-element.74.joined_ref, f32[256,384]{1,0:T(8,128)S(1)} %get-tuple-element.93.faces_ref, ...), custom_call_target="tpu_custom_call" | custom-call | flops 100000000 | bytes 1048576 | tf_op jit(solution)/shard_map/level/pallas_call | solution.py:379
  20.7 2.1 %collective-permute-start.6 = (f32[64,128]{1,0:T(8,128)S(1)}, f32[64,128]{1,0:T(8,128)S(1)}, u32[]{:S(2)}, u32[]{:S(2)}) collective-permute-start(f32[64,128]{1,0:T(8,128)S(1)} %get-tuple-element.107.rest_3_), channel_id=1, source_target_pairs={{0,30},{2,4},{4,2},{6,8},{8,6},{10,12},{12,10},{14,16},{16,14},{18... | collective-permute-start | bytes 98312 | tf_op jit(solution)/shard_map/ppermute | solution.py:427
  22.7 1.5 %collective-permute-start.7 = (f32[64,128]{1,0:T(8,128)S(1)}, f32[64,128]{1,0:T(8,128)S(1)}, u32[]{:S(2)}, u32[]{:S(2)}) collective-permute-start(f32[64,128]{1,0:T(8,128)S(1)} %get-tuple-element.108.rest_4_), channel_id=1, source_target_pairs={{0,1},{1,0},{2,3},{3,2},{4,5},{5,4},{6,7},{7,6},{8,9},{9,8},{10,11... | collective-permute-start | bytes 98312 | tf_op jit(solution)/shard_map/ppermute | solution.py:427
  24.2 0.0 collective-permute-start.8
  24.2 2.2 %between.4 = (f32[64,1024]{1,0:T(8,128)S(1)}, f32[144,384]{1,0:T(8,128)S(1)}, f32[256,384]{1,0:T(8,128)S(1)}, f32[8,384]{1,0:T(8,128)S(1)}, f32[64,384]{1,0:T(8,128)S(1)}, /*index=5*/f32[144,1024]{1,0:T(8,128)S(1)}) custom-call(s32[8,1536]{1,0:T(8,128)S(1)} %get-tuple-element.75.members_ref, s32[8,1536]{1,0:T(8,128)S(1)} %get-tuple-element.74.joined_ref, ...), custom_call_target="tpu_custom_call" | custom-call | flops 2000000000 | bytes 1048576 | tf_op jit(solution)/shard_map/between/pallas_call | solution.py:379
  26.5 0.3 collective-permute-done.6.rest_0_
  26.8 0.0 collective-permute-done.7.rest_1_
  26.8 0.0 collective-permute-done.8.rest_2_
  26.8 1.5 %level.5 = (f32[256,384]{1,0:T(8,128)S(1)}, f32[64,384]{1,0:T(8,128)S(1)}, f32[64,128]{1,0:T(8,128)S(1)}, f32[64,128]{1,0:T(8,128)S(1)}, f32[64,128]{1,0:T(8,128)S(1)}) custom-call(s32[8,1536]{1,0:T(8,128)S(1)} %get-tuple-element.74.joined_ref, f32[256,384]{1,0:T(8,128)S(1)} %get-tuple-element.104.faces_ref, ...), custom_call_target="tpu_custom_call" | custom-call | flops 100000000 | bytes 1048576 | tf_op jit(solution)/shard_map/level/pallas_call | solution.py:379
  28.3 2.1 %collective-permute-start.9 = (f32[64,128]{1,0:T(8,128)S(1)}, f32[64,128]{1,0:T(8,128)S(1)}, u32[]{:S(2)}, u32[]{:S(2)}) collective-permute-start(f32[64,128]{1,0:T(8,128)S(1)} %get-tuple-element.118), channel_id=1, source_target_pairs={{0,30},{2,4},{4,2},{6,8},{8,6},{10,12},{12,10},{14,16},{16,14},{18... | collective-permute-start | bytes 98312 | tf_op jit(solution)/shard_map/ppermute | solution.py:427
  30.3 1.5 %collective-permute-start.10 = (f32[64,128]{1,0:T(8,128)S(1)}, f32[64,128]{1,0:T(8,128)S(1)}, u32[]{:S(2)}, u32[]{:S(2)}) collective-permute-start(f32[64,128]{1,0:T(8,128)S(1)} %get-tuple-element.119), channel_id=1, source_target_pairs={{0,1},{1,0},{2,3},{3,2},{4,5},{5,4},{6,7},{7,6},{8,9},{9,8},{10,11... | collective-permute-start | bytes 98312 | tf_op jit(solution)/shard_map/ppermute | solution.py:427
  31.8 0.0 collective-permute-start.11
  31.9 2.4 %between.5 = (f32[144,384]{1,0:T(8,128)S(1)}, f32[256,384]{1,0:T(8,128)S(1)}, f32[8,384]{1,0:T(8,128)S(1)}, f32[144,1024]{1,0:T(8,128)S(1)}) custom-call(s32[8,1536]{1,0:T(8,128)S(1)} %get-tuple-element.75.members_ref, s32[8,1536]{1,0:T(8,128)S(1)} %get-tuple-element.74.joined_ref, s32[8,128]{1,0:T(8,128)S(1)} %get-tuple-element.76.places_ref, ...), custom_call_target="tpu_custom_call" | custom-call | flops 2000000000 | bytes 1048576 | tf_op jit(solution)/shard_map/between/pallas_call | solution.py:379
  34.3 0.1 collective-permute-done.9.rest_0_
  34.4 0.0 collective-permute-done.10.rest_1_
  34.4 0.0 collective-permute-done.11.rest_2_
  34.4 2.8 %last.1 = f32[1120,128]{1,0:T(8,128)} custom-call(s32[8,1536]{1,0:T(8,128)S(1)} %get-tuple-element.74.joined_ref, f32[144,384]{1,0:T(8,128)S(1)} %get-tuple-element.114.own_ref, f32[256,384]{1,0:T(8,128)S(1)} %get-tuple-element.115.faces_ref, f32[8,384]{1,0:T(8,128)S(1)} %get-tuple-element.116.weights_ref, bf16[144,768]{1,0:T(8,128)(2,1)S(1)} %get-tuple-element.89.lift_ref, ...), custom_call_target="tpu_custom_call" | custom-call | flops 1000000000 | bytes 1048576 | tf_op jit(solution)/shard_map/last/pallas_call | solution.py:379
Async XLA Ops:
  2.0 9.5 %collective-permute-start = (f32[64,128]{1,0:T(8,128)S(1)}, f32[64,128]{1,0:T(8,128)S(1)}, u32[]{:S(2)}, u32[]{:S(2)}) collective-permute-start(f32[64,128]{1,0:T(8,128)S(1)} %get-tuple-element.82.rest_3_), channel_id=1, source_target_pairs={{0,30},{2,4},{4,2},{6,8},{8,6},{10,12},{12,10},{14,16},{16,14},{18... | collective-permute-start | bytes 98312 | tf_op jit(solution)/shard_map/ppermute | solution.py:427
  7.5 4.0 %collective-permute-start.1 = (f32[64,128]{1,0:T(8,128)S(1)}, f32[64,128]{1,0:T(8,128)S(1)}, u32[]{:S(2)}, u32[]{:S(2)}) collective-permute-start(f32[64,128]{1,0:T(8,128)S(1)} %get-tuple-element.83.rest_4_), channel_id=1, source_target_pairs={{0,1},{1,0},{2,3},{3,2},{4,5},{5,4},{6,7},{7,6},{8,9},{9,8},{10,11... | collective-permute-start | bytes 98312 | tf_op jit(solution)/shard_map/ppermute | solution.py:427
  9.0 2.5 %collective-permute-start.2 = (f32[64,128]{1,0:T(8,128)S(1)}, f32[64,128]{1,0:T(8,128)S(1)}, u32[]{:S(2)}, u32[]{:S(2)}) collective-permute-start(f32[64,128]{1,0:T(8,128)S(1)} %get-tuple-element.84.rest_5_), channel_id=1, source_target_pairs={{0,2},{2,0},{4,6},{6,4},{8,10},{10,8},{12,14},{14,12},{16,18},{18,... | collective-permute-start | bytes 98312 | tf_op jit(solution)/shard_map/ppermute | solution.py:427
  13.0 6.1 %collective-permute-start.3 = (f32[64,128]{1,0:T(8,128)S(1)}, f32[64,128]{1,0:T(8,128)S(1)}, u32[]{:S(2)}, u32[]{:S(2)}) collective-permute-start(f32[64,128]{1,0:T(8,128)S(1)} %get-tuple-element.96.rest_3_), channel_id=1, source_target_pairs={{0,30},{2,4},{4,2},{6,8},{8,6},{10,12},{12,10},{14,16},{16,14},{18... | collective-permute-start | bytes 98312 | tf_op jit(solution)/shard_map/ppermute | solution.py:427
  15.1 4.0 %collective-permute-start.4 = (f32[64,128]{1,0:T(8,128)S(1)}, f32[64,128]{1,0:T(8,128)S(1)}, u32[]{:S(2)}, u32[]{:S(2)}) collective-permute-start(f32[64,128]{1,0:T(8,128)S(1)} %get-tuple-element.97.rest_4_), channel_id=1, source_target_pairs={{0,1},{1,0},{2,3},{3,2},{4,5},{5,4},{6,7},{7,6},{8,9},{9,8},{10,11... | collective-permute-start | bytes 98312 | tf_op jit(solution)/shard_map/ppermute | solution.py:427
  16.6 2.5 %collective-permute-start.5 = (f32[64,128]{1,0:T(8,128)S(1)}, f32[64,128]{1,0:T(8,128)S(1)}, u32[]{:S(2)}, u32[]{:S(2)}) collective-permute-start(f32[64,128]{1,0:T(8,128)S(1)} %get-tuple-element.98.rest_5_), channel_id=1, source_target_pairs={{0,2},{2,0},{4,6},{6,4},{8,10},{10,8},{12,14},{14,12},{16,18},{18,... | collective-permute-start | bytes 98312 | tf_op jit(solution)/shard_map/ppermute | solution.py:427
  20.7 6.1 %collective-permute-start.6 = (f32[64,128]{1,0:T(8,128)S(1)}, f32[64,128]{1,0:T(8,128)S(1)}, u32[]{:S(2)}, u32[]{:S(2)}) collective-permute-start(f32[64,128]{1,0:T(8,128)S(1)} %get-tuple-element.107.rest_3_), channel_id=1, source_target_pairs={{0,30},{2,4},{4,2},{6,8},{8,6},{10,12},{12,10},{14,16},{16,14},{18... | collective-permute-start | bytes 98312 | tf_op jit(solution)/shard_map/ppermute | solution.py:427
  22.7 4.0 %collective-permute-start.7 = (f32[64,128]{1,0:T(8,128)S(1)}, f32[64,128]{1,0:T(8,128)S(1)}, u32[]{:S(2)}, u32[]{:S(2)}) collective-permute-start(f32[64,128]{1,0:T(8,128)S(1)} %get-tuple-element.108.rest_4_), channel_id=1, source_target_pairs={{0,1},{1,0},{2,3},{3,2},{4,5},{5,4},{6,7},{7,6},{8,9},{9,8},{10,11... | collective-permute-start | bytes 98312 | tf_op jit(solution)/shard_map/ppermute | solution.py:427
  24.2 2.5 %collective-permute-start.8 = (f32[64,128]{1,0:T(8,128)S(1)}, f32[64,128]{1,0:T(8,128)S(1)}, u32[]{:S(2)}, u32[]{:S(2)}) collective-permute-start(f32[64,128]{1,0:T(8,128)S(1)} %get-tuple-element.109.rest_5_), channel_id=1, source_target_pairs={{0,2},{2,0},{4,6},{6,4},{8,10},{10,8},{12,14},{14,12},{16,18},{18,... | collective-permute-start | bytes 98312 | tf_op jit(solution)/shard_map/ppermute | solution.py:427
  28.3 6.1 %collective-permute-start.9 = (f32[64,128]{1,0:T(8,128)S(1)}, f32[64,128]{1,0:T(8,128)S(1)}, u32[]{:S(2)}, u32[]{:S(2)}) collective-permute-start(f32[64,128]{1,0:T(8,128)S(1)} %get-tuple-element.118), channel_id=1, source_target_pairs={{0,30},{2,4},{4,2},{6,8},{8,6},{10,12},{12,10},{14,16},{16,14},{18... | collective-permute-start | bytes 98312 | tf_op jit(solution)/shard_map/ppermute | solution.py:427
  30.3 4.0 %collective-permute-start.10 = (f32[64,128]{1,0:T(8,128)S(1)}, f32[64,128]{1,0:T(8,128)S(1)}, u32[]{:S(2)}, u32[]{:S(2)}) collective-permute-start(f32[64,128]{1,0:T(8,128)S(1)} %get-tuple-element.119), channel_id=1, source_target_pairs={{0,1},{1,0},{2,3},{3,2},{4,5},{5,4},{6,7},{7,6},{8,9},{9,8},{10,11... | collective-permute-start | bytes 98312 | tf_op jit(solution)/shard_map/ppermute | solution.py:427
  31.8 2.5 %collective-permute-start.11 = (f32[64,128]{1,0:T(8,128)S(1)}, f32[64,128]{1,0:T(8,128)S(1)}, u32[]{:S(2)}, u32[]{:S(2)}) collective-permute-start(f32[64,128]{1,0:T(8,128)S(1)} %get-tuple-element.120), channel_id=1, source_target_pairs={{0,2},{2,0},{4,6},{6,4},{8,10},{10,8},{12,14},{14,12},{16,18},{18,... | collective-permute-start | bytes 98312 | tf_op jit(solution)/shard_map/ppermute | solution.py:427

commit v4 on v3

--- a/solution.py
+++ b/solution.py
@@ -424,7 +424,18 @@
     messages = len(swaps)
 
     def exchange(sent):
-        return [lax.ppermute(one, swap[0], swap[1]) for one, swap in zip(sent, swaps)]
+        got = []
+        for one, (axis, pairs, *_) in zip(sent, swaps):
+            if one is sent[0]:
+                groups = [pair for pair in pairs if pair[0] < pair[1]]
+                both = lax.all_gather(one, axis, axis_index_groups=groups)
+                index = lax.axis_index(axis)
+                partner_first = (index & 1) == 0
+                partner_first = partner_first & (index > 0) | (index == lax.axis_size(axis) - 1)
+                got.append(jnp.where(partner_first, both[0], both[1]))
+            else:
+                got.append(lax.ppermute(one, axis, pairs))
+        return got
 
     message = ((trace_rows, bnd), f32)
     own, face_stack = ((rows, BLOCK), f32), ((faces * trace_rows, BLOCK), f32)

time: 37.4 us -> 51.8 us (1.39)
  blocking collectives: 0 us -> 27.2 us
  starting transfers between devices: 17.7 us -> 5.75 us
  waiting for transfers between devices: 0.71 us -> 0.02 us
    all_gather x0 -> x4, blocking collectives: none -> 27.2 us  [exchange(): both = lax.all_gather(one, axis, axis_index_groups=groups)]
    ppermute x12 -> x8, starting transfers between devices: 17.7 us -> 5.75 us  [exchange(): got.append(lax.ppermute(one, axis, pairs))]
    ppermute x12 -> x8, waiting for transfers between devices: 0.71 us -> 0.02 us  [exchange(): got.append(lax.ppermute(one, axis, pairs))]
  transfers between devices with their start and end apart: 12 -> 8, of which waited for: 3 -> 0; matrix products, arithmetic and copies ran while one was open for 0% -> 0% of each run, Pallas kernels for 25% -> 18%
where the time goes in v4:
time: 51.8 us; the launch traced here: 51.7 us
  blocking collectives  27.2 us (53%)
  Pallas kernels  18.4 us (36%)
  starting transfers between devices  5.75 us (11%)
    all_gather x4, blocking collectives, exchange(): both = lax.all_gather(one, axis, axis_index_groups=groups)  27.2 us
    pallas_call x9, Pallas kernels, call(): pl.pallas_call(kernel, out_shape=tuple((jax.ShapeDtypeStruct(shape, dtype...  18.4 us
    ppermute x8, starting transfers between devices, exchange(): got.append(lax.ppermute(one, axis, pairs))  5.75 us
  transfers between devices with their start and end apart: 8, of which 0 were waited for; matrix products, arithmetic and copies ran while one was open for 0% of the time, Pallas kernels for 18%

profile of v4, /device:TPU:0, one launch (start us, length us, event | category | flops | bytes accessed | tf_op | source)
XLA Modules:
  0.0 51.7 jit_solution(7674260735734735179)
XLA Ops:
  0.0 2.0 %first.1 = (f32[144,1024]{1,0:T(8,128)S(1)}, f32[64,1024]{1,0:T(8,128)S(1)}, f32[64,128]{1,0:T(8,128)S(1)}, f32[64,128]{1,0:T(8,128)S(1)}, f32[64,128]{1,0:T(8,1...) custom-call(f32[1120,128]{1,0:T(8,128)} %bitcast.9, ...), custom_call_target="tpu_custom_call" | custom-call | flops 100000000 | bytes 1048576 | tf_op jit(solution)/shard_map/first/pallas_call | solution.py:379
  2.0 3.0 %collective-permute-start = (f32[64,128]{1,0:T(8,128)S(1)}, f32[64,128]{1,0:T(8,128)S(1)}, u32[]{:S(2)}, u32[]{:S(2)}) collective-permute-start(f32[64,128]{1,0:T(8,128)S(1)} %get-tuple-element.83.rest_4_), channel_id=1, source_target_pairs={{0,1},{1,0},{2,3},{3,2},{4,5},{5,4},{6,7},{7,6},{8,9},{9,8},{10,11... | collective-permute-start | bytes 98312 | tf_op jit(solution)/shard_map/ppermute | solution.py:437
  5.0 0.0 collective-permute-start.1
  5.0 6.9 %all-gather = f32[128,128]{1,0:T(8,128)S(1)} all-gather(f32[64,128]{1,0:T(8,128)S(1)} %get-tuple-element.82.rest_3_), channel_id=2, replica_groups={{0,30},{2,4},{6,8},{10,12},{14,16},{18,20},{22,24},{26,28},{1,31},{3,5}..., dimensions={0}, use_global_device_ids=true | all-gather | bytes 98304 | tf_op jit(solution)/shard_map/all_gather | solution.py:431
  11.9 2.5 %plan.1 = (s32[8,1536]{1,0:T(8,128)S(1)}, s32[8,1536]{1,0:T(8,128)S(1)}, s32[8,128]{1,0:T(8,128)S(1)}, s32[8,128]{1,0:T(8,128)S(1)}, f32[144,384]{1,0:T(8,128)S(...) custom-call(f32[60,140]{1,0:T(8,128)S(1)} %get-tuple-element.63.trac, ...), custom_call_target="tpu_custom_call" | custom-call | flops 2000000000 | bytes 1048576 | tf_op jit(solution)/shard_map/plan/pallas_call | solution.py:379
  14.4 0.0 collective-permute-done.rest_1_
  14.4 0.0 collective-permute-done.1.rest_2_
  14.4 1.5 %level.3 = (f32[256,384]{1,0:T(8,128)S(1)}, f32[64,384]{1,0:T(8,128)S(1)}, f32[64,128]{1,0:T(8,128)S(1)}, f32[64,128]{1,0:T(8,128)S(1)}, f32[64,128]{1,0:T(8,128)S(1)}) custom-call(s32[8,1536]{1,0:T(8,128)S(1)} %get-tuple-element.74.joined_ref, f32[256,384]{1,0:T(8,128)S(1)} %get-tuple-element.77.faces_ref, ...), custom_call_target="tpu_custom_call" | custom-call | flops 100000000 | bytes 1048576 | tf_op jit(solution)/shard_map/level/pallas_call | solution.py:379
  15.9 0.6 %collective-permute-start.2 = (f32[64,128]{1,0:T(8,128)S(1)}, f32[64,128]{1,0:T(8,128)S(1)}, u32[]{:S(2)}, u32[]{:S(2)}) collective-permute-start(f32[64,128]{1,0:T(8,128)S(1)} %get-tuple-element.97.rest_4_), channel_id=1, source_target_pairs={{0,1},{1,0},{2,3},{3,2},{4,5},{5,4},{6,7},{7,6},{8,9},{9,8},{10,11... | collective-permute-start | bytes 98312 | tf_op jit(solution)/shard_map/ppermute | solution.py:437
  16.5 0.0 collective-permute-start.3
  16.5 6.7 %all-gather.1 = f32[128,128]{1,0:T(8,128)S(1)} all-gather(f32[64,128]{1,0:T(8,128)S(1)} %get-tuple-element.96.rest_3_), channel_id=3, replica_groups={{0,30},{2,4},{6,8},{10,12},{14,16},{18,20},{22,24},{26,28},{1,31},{3,5}..., dimensions={0}, use_global_device_ids=true | all-gather | bytes 98304 | tf_op jit(solution)/shard_map/all_gather | solution.py:431
  23.2 2.2 %between.3 = (f32[64,1024]{1,0:T(8,128)S(1)}, f32[144,384]{1,0:T(8,128)S(1)}, f32[256,384]{1,0:T(8,128)S(1)}, f32[8,384]{1,0:T(8,128)S(1)}, f32[64,384]{1,0:T(8,128)S(1)}, /*index=5*/f32[144,1024]{1,0:T(8,128)S(1)}) custom-call(s32[8,1536]{1,0:T(8,128)S(1)} %get-tuple-element.75.members_ref, s32[8,1536]{1,0:T(8,128)S(1)} %get-tuple-element.74.joined_ref, ...), custom_call_target="tpu_custom_call" | custom-call | flops 2000000000 | bytes 1048576 | tf_op jit(solution)/shard_map/between/pallas_call | solution.py:379
  25.5 0.0 collective-permute-done.2.rest_1_
  25.5 0.0 collective-permute-done.3.rest_2_
  25.5 1.5 %level.4 = (f32[256,384]{1,0:T(8,128)S(1)}, f32[64,384]{1,0:T(8,128)S(1)}, f32[64,128]{1,0:T(8,128)S(1)}, f32[64,128]{1,0:T(8,128)S(1)}, f32[64,128]{1,0:T(8,128)S(1)}) custom-call(s32[8,1536]{1,0:T(8,128)S(1)} %get-tuple-element.74.joined_ref, f32[256,384]{1,0:T(8,128)S(1)} %get-tuple-element.93.faces_ref, ...), custom_call_target="tpu_custom_call" | custom-call | flops 100000000 | bytes 1048576 | tf_op jit(solution)/shard_map/level/pallas_call | solution.py:379
  27.0 1.6 %collective-permute-start.4 = (f32[64,128]{1,0:T(8,128)S(1)}, f32[64,128]{1,0:T(8,128)S(1)}, u32[]{:S(2)}, u32[]{:S(2)}) collective-permute-start(f32[64,128]{1,0:T(8,128)S(1)} %get-tuple-element.108.rest_4_), channel_id=1, source_target_pairs={{0,1},{1,0},{2,3},{3,2},{4,5},{5,4},{6,7},{7,6},{8,9},{9,8},{10,11... | collective-permute-start | bytes 98312 | tf_op jit(solution)/shard_map/ppermute | solution.py:437
  28.6 0.0 collective-permute-start.5
  28.6 6.7 %all-gather.2 = f32[128,128]{1,0:T(8,128)S(1)} all-gather(f32[64,128]{1,0:T(8,128)S(1)} %get-tuple-element.107.rest_3_), channel_id=4, replica_groups={{0,30},{2,4},{6,8},{10,12},{14,16},{18,20},{22,24},{26,28},{1,31},{3,5}..., dimensions={0}, use_global_device_ids=true | all-gather | bytes 98304 | tf_op jit(solution)/shard_map/all_gather | solution.py:431
  35.3 2.2 %between.4 = (f32[64,1024]{1,0:T(8,128)S(1)}, f32[144,384]{1,0:T(8,128)S(1)}, f32[256,384]{1,0:T(8,128)S(1)}, f32[8,384]{1,0:T(8,128)S(1)}, f32[64,384]{1,0:T(8,128)S(1)}, /*index=5*/f32[144,1024]{1,0:T(8,128)S(1)}) custom-call(s32[8,1536]{1,0:T(8,128)S(1)} %get-tuple-element.75.members_ref, s32[8,1536]{1,0:T(8,128)S(1)} %get-tuple-element.74.joined_ref, ...), custom_call_target="tpu_custom_call" | custom-call | flops 2000000000 | bytes 1048576 | tf_op jit(solution)/shard_map/between/pallas_call | solution.py:379
  37.5 0.0 collective-permute-done.4.rest_1_
  37.5 0.0 collective-permute-done.5.rest_2_
  37.5 1.5 %level.5 = (f32[256,384]{1,0:T(8,128)S(1)}, f32[64,384]{1,0:T(8,128)S(1)}, f32[64,128]{1,0:T(8,128)S(1)}, f32[64,128]{1,0:T(8,128)S(1)}, f32[64,128]{1,0:T(8,128)S(1)}) custom-call(s32[8,1536]{1,0:T(8,128)S(1)} %get-tuple-element.74.joined_ref, f32[256,384]{1,0:T(8,128)S(1)} %get-tuple-element.104.faces_ref, ...), custom_call_target="tpu_custom_call" | custom-call | flops 100000000 | bytes 1048576 | tf_op jit(solution)/shard_map/level/pallas_call | solution.py:379
  39.0 0.6 %collective-permute-start.6 = (f32[64,128]{1,0:T(8,128)S(1)}, f32[64,128]{1,0:T(8,128)S(1)}, u32[]{:S(2)}, u32[]{:S(2)}) collective-permute-start(f32[64,128]{1,0:T(8,128)S(1)} %get-tuple-element.119), channel_id=1, source_target_pairs={{0,1},{1,0},{2,3},{3,2},{4,5},{5,4},{6,7},{7,6},{8,9},{9,8},{10,11... | collective-permute-start | bytes 98312 | tf_op jit(solution)/shard_map/ppermute | solution.py:437
  39.6 0.0 collective-permute-start.7
  39.6 6.9 %all-gather.3 = f32[128,128]{1,0:T(8,128)S(1)} all-gather(f32[64,128]{1,0:T(8,128)S(1)} %get-tuple-element.118), channel_id=5, replica_groups={{0,30},{2,4},{6,8},{10,12},{14,16},{18,20},{22,24},{26,28},{1,31},{3,5}..., dimensions={0}, use_global_device_ids=true | all-gather | bytes 98304 | tf_op jit(solution)/shard_map/all_gather | solution.py:431
  46.5 2.2 %between.5 = (f32[144,384]{1,0:T(8,128)S(1)}, f32[256,384]{1,0:T(8,128)S(1)}, f32[8,384]{1,0:T(8,128)S(1)}, f32[144,1024]{1,0:T(8,128)S(1)}) custom-call(s32[8,1536]{1,0:T(8,128)S(1)} %get-tuple-element.75.members_ref, s32[8,1536]{1,0:T(8,128)S(1)} %get-tuple-element.74.joined_ref, s32[8,128]{1,0:T(8,128)S(1)} %get-tuple-element.76.places_ref, ...), custom_call_target="tpu_custom_call" | custom-call | flops 2000000000 | bytes 1048576 | tf_op jit(solution)/shard_map/between/pallas_call | solution.py:379
  48.7 0.0 collective-permute-done.6.rest_1_
  48.7 0.0 collective-permute-done.7.rest_2_
  48.7 2.8 %last.1 = f32[1120,128]{1,0:T(8,128)} custom-call(s32[8,1536]{1,0:T(8,128)S(1)} %get-tuple-element.74.joined_ref, f32[144,384]{1,0:T(8,128)S(1)} %get-tuple-element.114.own_ref, f32[256,384]{1,0:T(8,128)S(1)} %get-tuple-element.115.faces_ref, f32[8,384]{1,0:T(8,128)S(1)} %get-tuple-element.116.weights_ref, bf16[144,768]{1,0:T(8,128)(2,1)S(1)} %get-tuple-element.89.lift_ref, ...), custom_call_target="tpu_custom_call" | custom-call | flops 1000000000 | bytes 1048576 | tf_op jit(solution)/shard_map/last/pallas_call | solution.py:379
  (4 shorter events, 0.0 us)
Async XLA Ops:
  2.0 12.4 %collective-permute-start = (f32[64,128]{1,0:T(8,128)S(1)}, f32[64,128]{1,0:T(8,128)S(1)}, u32[]{:S(2)}, u32[]{:S(2)}) collective-permute-start(f32[64,128]{1,0:T(8,128)S(1)} %get-tuple-element.83.rest_4_), channel_id=1, source_target_pairs={{0,1},{1,0},{2,3},{3,2},{4,5},{5,4},{6,7},{7,6},{8,9},{9,8},{10,11... | collective-permute-start | bytes 98312 | tf_op jit(solution)/shard_map/ppermute | solution.py:437
  5.0 9.4 %collective-permute-start.1 = (f32[64,128]{1,0:T(8,128)S(1)}, f32[64,128]{1,0:T(8,128)S(1)}, u32[]{:S(2)}, u32[]{:S(2)}) collective-permute-start(f32[64,128]{1,0:T(8,128)S(1)} %get-tuple-element.84.rest_5_), channel_id=1, source_target_pairs={{0,2},{2,0},{4,6},{6,4},{8,10},{10,8},{12,14},{14,12},{16,18},{18,... | collective-permute-start | bytes 98312 | tf_op jit(solution)/shard_map/ppermute | solution.py:437
  15.9 9.5 %collective-permute-start.2 = (f32[64,128]{1,0:T(8,128)S(1)}, f32[64,128]{1,0:T(8,128)S(1)}, u32[]{:S(2)}, u32[]{:S(2)}) collective-permute-start(f32[64,128]{1,0:T(8,128)S(1)} %get-tuple-element.97.rest_4_), channel_id=1, source_target_pairs={{0,1},{1,0},{2,3},{3,2},{4,5},{5,4},{6,7},{7,6},{8,9},{9,8},{10,11... | collective-permute-start | bytes 98312 | tf_op jit(solution)/shard_map/ppermute | solution.py:437
  16.5 8.9 %collective-permute-start.3 = (f32[64,128]{1,0:T(8,128)S(1)}, f32[64,128]{1,0:T(8,128)S(1)}, u32[]{:S(2)}, u32[]{:S(2)}) collective-permute-start(f32[64,128]{1,0:T(8,128)S(1)} %get-tuple-element.98.rest_5_), channel_id=1, source_target_pairs={{0,2},{2,0},{4,6},{6,4},{8,10},{10,8},{12,14},{14,12},{16,18},{18,... | collective-permute-start | bytes 98312 | tf_op jit(solution)/shard_map/ppermute | solution.py:437
  27.0 10.5 %collective-permute-start.4 = (f32[64,128]{1,0:T(8,128)S(1)}, f32[64,128]{1,0:T(8,128)S(1)}, u32[]{:S(2)}, u32[]{:S(2)}) collective-permute-start(f32[64,128]{1,0:T(8,128)S(1)} %get-tuple-element.108.rest_4_), channel_id=1, source_target_pairs={{0,1},{1,0},{2,3},{3,2},{4,5},{5,4},{6,7},{7,6},{8,9},{9,8},{10,11... | collective-permute-start | bytes 98312 | tf_op jit(solution)/shard_map/ppermute | solution.py:437
  28.6 8.9 %collective-permute-start.5 = (f32[64,128]{1,0:T(8,128)S(1)}, f32[64,128]{1,0:T(8,128)S(1)}, u32[]{:S(2)}, u32[]{:S(2)}) collective-permute-start(f32[64,128]{1,0:T(8,128)S(1)} %get-tuple-element.109.rest_5_), channel_id=1, source_target_pairs={{0,2},{2,0},{4,6},{6,4},{8,10},{10,8},{12,14},{14,12},{16,18},{18,... | collective-permute-start | bytes 98312 | tf_op jit(solution)/shard_map/ppermute | solution.py:437
  39.0 9.7 %collective-permute-start.6 = (f32[64,128]{1,0:T(8,128)S(1)}, f32[64,128]{1,0:T(8,128)S(1)}, u32[]{:S(2)}, u32[]{:S(2)}) collective-permute-start(f32[64,128]{1,0:T(8,128)S(1)} %get-tuple-element.119), channel_id=1, source_target_pairs={{0,1},{1,0},{2,3},{3,2},{4,5},{5,4},{6,7},{7,6},{8,9},{9,8},{10,11... | collective-permute-start | bytes 98312 | tf_op jit(solution)/shard_map/ppermute | solution.py:437
  39.6 9.1 %collective-permute-start.7 = (f32[64,128]{1,0:T(8,128)S(1)}, f32[64,128]{1,0:T(8,128)S(1)}, u32[]{:S(2)}, u32[]{:S(2)}) collective-permute-start(f32[64,128]{1,0:T(8,128)S(1)} %get-tuple-element.120), channel_id=1, source_target_pairs={{0,2},{2,0},{4,6},{6,4},{8,10},{10,8},{12,14},{14,12},{16,18},{18,... | collective-permute-start | bytes 98312 | tf_op jit(solution)/shard_map/ppermute | solution.py:437

commit v5 on v3

--- a/solution.py
+++ b/solution.py
@@ -15,7 +15,6 @@
 LANES = 128
 NO_GROUP = 1 << 20
 ARGUMENTS = 10
-FIELD_COPIES = 4
 ROW_CHUNK = 48
 
 f32, bf16, i32 = jnp.float32, jnp.bfloat16, jnp.int32
@@ -109,6 +108,13 @@
     ]
 
 
+def row_blocks_of(row, rows):
+    return [
+        (b, functools.partial(lambda b: jnp.broadcast_to(row[:, block_at(b)], (rows, LANES)), b))
+        for b in range(row.shape[1] // LANES)
+    ]
+
+
 def summed_powers(stacked, weights_ref, rows, total):
     for power in range(1, POWERS + 1):
         total = total + stacked[(power - 1) * rows:power * rows] * weights_ref[power - 1:power, :]
@@ -128,15 +134,13 @@
     (columns_ref, out_ref), refs = refs[:2], refs[2:]
     sends, refs = refs[:len(swaps)], refs[len(swaps):]
     *held, fields_ref, arrived = refs
-    share = fields_ref.shape[0] // FIELD_COPIES
-    pairs = list(zip(given[:2], held[:2]))
-    pairs += [(fields_hbm.at[pl.ds(i * share, share)], fields_ref.at[pl.ds(i * share, share)])
-              for i in range(FIELD_COPIES)]
-    needed = len(pairs)
-    pairs += list(zip(given[2:], held[2:]))
-    copies = [pltpu.make_async_copy(source, target, arrived.at[i]) for i, (source, target) in enumerate(pairs)]
+    copies = [
+        pltpu.make_async_copy(source, target, arrived.at[i])
+        for i, (source, target) in enumerate(zip([fields_hbm] + given, [fields_ref] + held))
+    ]
     for copy in copies:
         copy.start()
+    needed = 3
     for copy in copies[:needed]:
         copy.wait()
     trace_ref, send_ref = held[:2]
@@ -185,9 +189,24 @@
             ref_blocks(out_ref, out_ref.shape[1] // LANES), index, index >> 7, jnp.zeros((trace_rows, LANES), f32))
 
 
-def base_traces(own_ref, trace_grow_ref, weights_ref, rows):
-    stacked = product(trace_grow_ref[...], stacked_columns(own_ref[...]))
+def local_part(level, members_ref, joined_ref, columns_ref, out_ref, heights_ref, lift_ref,
+               loaded_ref, weights_ref, faces_ref):
+    for block in range(BLOCK // LANES):
+        own_block(level, block, members_ref, joined_ref, columns_ref, heights_ref, loaded_ref, weights_ref)
+        face_block(level, block, joined_ref, out_ref, faces_ref)
+    loaded_ref[...] = loaded_ref[...] + product(lift_ref[...], stacked_columns(faces_ref[...]))
+
+
+def advanced_traces(loaded, matrix_ref, weights_ref, rows):
+    stacked = product(matrix_ref[...], stacked_columns(loaded))
     return summed_powers(stacked[rows:], weights_ref, rows, stacked[:rows])
+
+
+def local_messages(level, trace_ref, send_places_ref, sent, messages):
+    for group, (before, message) in enumerate(zip(sent, messages)):
+        index = send_places_ref[group:group + 1, :]
+        which = (index >> 7) - level * (BLOCK // LANES)
+        message[...] = pick(ref_blocks(trace_ref, BLOCK // LANES), index, which, before[...])
 
 
 def row_chunks(rows):
@@ -201,7 +220,8 @@
     return summed_powers(product(matrix, stacked), weights_ref, ROW_CHUNK, loaded[chunk])
 
 
-def matrix_powers(operator_ref, trace_ref, lift_ref, grow_ref, trace_grow_ref, mix_ref, lift_out_ref):
+def matrix_powers(operator_ref, trace_ref, lift_ref, grow_ref, trace_grow_ref, mix_ref, mix_first_ref,
+                  lift_out_ref, lift_first_ref):
     comp = operator_ref.shape[0]
     trace_comp, faces, _ = lift_ref.shape
     rows = lift_out_ref.shape[0]
@@ -219,16 +239,24 @@
         powers = jnp.concatenate([powers, more[have * trace_rows:]], axis=0)
         have *= 2
     traces = jnp.concatenate([traces, exact_product(traces[:trace_rows], powers[-rows:])], axis=0)
-    mix_ref[...] = stacked_matrix(exact_product(traces, lift))
+    mix = exact_product(traces, lift)
+    mix_ref[...] = stacked_matrix(mix)
+    mix_first_ref[...] = stacked_matrix(mix[:, :trace_rows])
+    lift_first_ref[...] = stacked_matrix(lift[:, :trace_rows])
     trace_grow_ref[...] = stacked_matrix(traces)
     lift_out_ref[...] = stacked_matrix(lift)
     grow_ref[...] = stacked_matrix(powers)
 
 
-def plan_kernel(swaps, trace_ref, send_ref, order_ref, pattern_ref, sizes_ref, neighbours_ref, operator_ref,
-                lift_ref, heights_ref, columns_ref, out_ref,
-                members_ref, joined_ref, places_ref, send_places_ref, own_ref, faces_ref, weights_ref, base_ref,
-                grow_ref, trace_grow_ref, mix_ref, lift_out_ref, wide_heights_ref):
+def plan_kernel(swaps, *refs):
+    (trace_ref, send_ref, order_ref, pattern_ref, sizes_ref, neighbours_ref, operator_ref, lift_ref, heights_ref,
+     columns_ref, out_ref), refs = refs[:11], refs[11:]
+    messages = len(swaps)
+    sent, refs = refs[:messages], refs[messages:]
+    (members_ref, joined_ref, places_ref, send_places_ref, send_codes_ref, slot_weights_ref, flags_ref, loaded_ref,
+     weights_ref, new_trace_ref, grow_ref, trace_grow_ref, mix_ref, mix_first_ref, lift_out_ref, lift_first_ref,
+     wide_heights_ref), refs = refs[:17], refs[17:]
+    prepared, (faces_ref,) = refs[:messages], refs[messages:]
     elements = columns_ref.shape[1]
     count = elements // LANES
     faces = neighbours_ref.shape[0]
@@ -268,12 +296,34 @@
     places_ref[...] = at
     index = pad_rows(jnp.concatenate(sent_rows(send_ref, swaps), axis=0), 8)
     send_places_ref[...] = pick(row_blocks(at, 8), index, index >> 7)
-    matrix_powers(operator_ref, trace_ref, lift_ref, grow_ref, trace_grow_ref, mix_ref, lift_out_ref)
-    for block in range(BLOCK // LANES):
-        own_block(0, block, members_ref, joined_ref, columns_ref, wide_heights_ref, own_ref, weights_ref)
-    base_ref[...] = base_traces(own_ref, trace_grow_ref, weights_ref, out_ref.shape[0])
-    for block in range(BLOCK // LANES):
-        face_block(0, block, joined_ref, out_ref, faces_ref)
+    send_codes_ref[...] = pick(row_blocks_of(neighbours[:1], 8), index, index >> 7)
+    block = jnp.broadcast_to(neighbours[:1] >> 7, (8, elements)) - count
+    named = jnp.where(block == lax.broadcasted_iota(i32, (8, elements), 0),
+                      jnp.broadcast_to(pattern_ref[...], (8, elements)), 0).astype(f32).astype(bf16)
+    slot_lane = jnp.broadcast_to(neighbours[:1] & (LANES - 1), (LANES, elements)) == lax.broadcasted_iota(
+        i32, (LANES, elements), 0)
+    slot_pattern = lax.dot_general(named, jnp.where(slot_lane, 1.0, 0.0).astype(bf16), (((1,), (1,)), ((), ())),
+                                   preferred_element_type=f32).astype(i32)
+    height = jnp.take_along_axis(jnp.broadcast_to(wide_heights_ref[...], (8, LANES)), slot_pattern & (LANES - 1),
+                                 axis=1, mode="promise_in_bounds")
+    weight = jnp.ones((8, LANES), f32)
+    for power in range(1, POWERS + 1):
+        weight = weight * height
+        for number in range(messages):
+            slot_weights_ref[power - 1:power, block_at(number)] = weight[number:number + 1] * WEIGHTS[power]
+    for level in range(LEVELS):
+        code = joined_ref[1:faces, level * BLOCK:(level + 1) * BLOCK]
+        code = jnp.max(jnp.where(code >= elements, 1.0, 0.0), axis=0, keepdims=True)
+        row = code[:, block_at(0)]
+        for number in range(1, BLOCK // LANES):
+            row = jnp.maximum(row, code[:, block_at(number)])
+        flags_ref[level:level + 1, :] = row
+    matrix_powers(operator_ref, trace_ref, lift_ref, grow_ref, trace_grow_ref, mix_ref, mix_first_ref,
+                  lift_out_ref, lift_first_ref)
+    local_part(0, members_ref, joined_ref, columns_ref, out_ref, wide_heights_ref, lift_out_ref,
+               loaded_ref, weights_ref, faces_ref)
+    new_trace_ref[...] = advanced_traces(loaded_ref[...], trace_grow_ref, weights_ref, out_ref.shape[0])
+    local_messages(0, new_trace_ref, send_places_ref, sent, prepared)
 
 
 def settle(level, blocks, places_ref, before, block):
@@ -282,84 +332,125 @@
     return pick(blocks, index, which, before)
 
 
-def between_kernel(level, members_ref, joined_ref, places_ref, columns_ref, old_out_ref, new_trace_ref, heights_ref,
-                   old_own_ref, inflow_ref, old_weights_ref, lift_ref, grow_ref, trace_grow_ref, *rest):
+def received_blocks(received, count):
+    return [(count + i, functools.partial(lambda ref: ref[...], ref)) for i, ref in enumerate(received)]
+
+
+def received_traces(level, face, received, joined_ref, count):
+    parts = []
+    for block in range(BLOCK // LANES):
+        index = joined_ref[face:face + 1, block_at(level * (BLOCK // LANES) + block)]
+        zeros = jnp.zeros(received[0].shape, f32)
+        parts.append(pick(received_blocks(received, count), index, index >> 7, zeros))
+    return jnp.concatenate(parts, axis=1)
+
+
+def other_traces(level, received, joined_ref, count):
+    parts = [received_traces(level, face, received, joined_ref, count) for face in range(1, faces_in(joined_ref))]
+    return jnp.concatenate([jnp.zeros_like(parts[0])] + parts, axis=0)
+
+
+def any_other(level, flags_ref):
+    return jnp.max(flags_ref[level:level + 1, :]) > 0.0
+
+
+def add_received(level, received, joined_ref, count, flags_ref, local_ref, lift_ref, lift_first_ref, loaded_ref):
+    first = received_traces(level, 0, received, joined_ref, count)
+    loaded_ref[...] = local_ref[...] + product(lift_first_ref[...], stacked_columns(first))
+
+    @pl.when(any_other(level, flags_ref))
+    def _():
+        others = other_traces(level, received, joined_ref, count)
+        loaded_ref[...] = loaded_ref[...] + product(lift_ref[...], stacked_columns(others))
+
+
+def between_kernel(level, messages, members_ref, joined_ref, places_ref, columns_ref, old_out_ref, old_trace_ref,
+                   moved_ref, extra_ref, heights_ref, local_ref, old_weights_ref, lift_ref, lift_first_ref, grow_ref,
+                   trace_grow_ref, flags_ref, send_places_ref, *rest):
+    received, rest = rest[:messages], rest[messages:]
+    final = level == LEVELS - 1
+    if not final:
+        sent, rest = rest[:messages], rest[messages:]
     if level > 1:
         advanced_ref, rest = rest[0], rest[1:]
-    if level == LEVELS - 1:
-        own_ref, faces_ref, weights_ref, new_advanced_ref, out_ref = rest
+    if final:
+        loaded_ref, weights_ref, new_advanced_ref, out_ref, faces_ref, trace_ref, whole_ref = rest
     else:
-        out_ref, own_ref, faces_ref, weights_ref, base_ref, new_advanced_ref = rest
+        out_ref, loaded_ref, weights_ref, new_trace_ref, new_advanced_ref = rest[:5]
+        prepared, (faces_ref, trace_ref, whole_ref) = rest[5:5 + messages], rest[5 + messages:]
     count = places_ref.shape[0]
     done = level - 1
-    loaded = old_own_ref[...] + product(lift_ref[...], stacked_columns(inflow_ref[...]))
+    add_received(done, received, joined_ref, count, flags_ref, local_ref, lift_ref, lift_first_ref, whole_ref)
+    for block in range(BLOCK // LANES):
+        here = block_at(block)
+        index = joined_ref[0:1, block_at(done * (BLOCK // LANES) + block)]
+        moved = [(count + i, read) for i, read in ref_blocks(moved_ref, messages)]
+        trace_ref[:, here] = old_trace_ref[:, here] + extra_ref[:, here] + pick(
+            moved, index, index >> 7, jnp.zeros((old_trace_ref.shape[0], LANES), f32))
     for block in range(count):
         here = block_at(block)
         out_ref[:, here] = settle(
-            done, ref_blocks(new_trace_ref, BLOCK // LANES), places_ref, old_out_ref[:, here], block)
-    stacked = stacked_columns(loaded)
-    chunks = row_chunks(loaded.shape[0])
+            done, ref_blocks(trace_ref, BLOCK // LANES), places_ref, old_out_ref[:, here], block)
+    whole = whole_ref[...]
+    stacked = stacked_columns(whole)
+    chunks = row_chunks(whole.shape[0])
     pieces = BLOCK // LANES
     for number, chunk in enumerate(chunks):
-        new = grown_rows(chunk, stacked, loaded, grow_ref, old_weights_ref)
+        new = grown_rows(chunk, stacked, whole, grow_ref, old_weights_ref)
         for block in range(number * pieces // len(chunks), (number + 1) * pieces // len(chunks)):
-            own_block(level, block, members_ref, joined_ref, columns_ref, heights_ref, own_ref, weights_ref)
+            own_block(level, block, members_ref, joined_ref, columns_ref, heights_ref, loaded_ref, weights_ref)
             face_block(level, block, joined_ref, out_ref, faces_ref)
         for block in range(count):
             here = block_at(block)
             before = advanced_ref[chunk, here] if level > 1 else None
             new_advanced_ref[chunk, here] = settle(done, value_blocks(new), places_ref, before, block)
-    if level < LEVELS - 1:
-        base_ref[...] = base_traces(own_ref, trace_grow_ref, weights_ref, out_ref.shape[0])
-
-
-def inflow_block(level, block, received, joined_ref, faces_ref, count):
-    faces = faces_in(joined_ref)
-    trace_rows = faces_ref.shape[0] // faces
-    blocks = [(count + i, functools.partial(lambda ref: ref[...], ref)) for i, ref in enumerate(received)]
-    here, there = block_at(block), block_at(level * (BLOCK // LANES) + block)
-    parts = []
-    for face in range(faces):
-        index = joined_ref[face:face + 1, there]
-        parts.append(pick(blocks, index, index >> 7, faces_ref[face * trace_rows:(face + 1) * trace_rows, here]))
-    return jnp.concatenate(parts, axis=0)
-
-
-def level_kernel(level, messages, count, joined_ref, faces_ref, weights_ref, base_ref, mix_ref, send_places_ref,
-                 *rest):
+    loaded = loaded_ref[...] + product(lift_ref[...], stacked_columns(faces_ref[...]))
+    loaded_ref[...] = loaded
+    if not final:
+        new_trace_ref[...] = advanced_traces(loaded, trace_grow_ref, weights_ref, out_ref.shape[0])
+        local_messages(level, new_trace_ref, send_places_ref, sent, prepared)
+
+
+def level_kernel(level, messages, count, flags_ref, joined_ref, weights_ref, slot_weights_ref, mix_ref, mix_first_ref,
+                 send_places_ref, send_codes_ref, *rest):
     received, rest = rest[:messages], rest[messages:]
-    sent, rest = rest[:messages], rest[messages:]
-    inflow_ref, new_trace_ref, sends = rest[0], rest[1], rest[2:]
-    trace_rows = new_trace_ref.shape[0]
-    blocks = range(BLOCK // LANES)
-    for tile in (blocks[:2], blocks[2:]):
-        across = slice(tile[0] * LANES, (tile[-1] + 1) * LANES)
-        inflow = jnp.concatenate(
-            [inflow_block(level, block, received, joined_ref, faces_ref, count) for block in tile], axis=1)
-        inflow_ref[:, across] = inflow
-        stacked = product(mix_ref[...], stacked_columns(inflow))
-        total = base_ref[:, across] + stacked[:trace_rows]
-        for power in range(1, POWERS + 1):
-            total = total + stacked[power * trace_rows:(power + 1) * trace_rows] * weights_ref[power - 1:power, across]
-        new_trace_ref[:, across] = total
-    for group, (before, send) in enumerate(zip(sent, sends)):
-        index = send_places_ref[group:group + 1, :]
-        which = (index >> 7) - level * (BLOCK // LANES)
-        send[...] = pick(ref_blocks(new_trace_ref, BLOCK // LANES), index, which, before[...])
-
-
-def last_kernel(level, messages, joined_ref, own_ref, faces_ref, weights_ref, lift_ref, grow_ref,
+    prepared, rest = rest[:messages], rest[messages:]
+    moved_ref, extra_ref, sends = rest[0], rest[1], rest[2:]
+    rows = moved_ref.shape[0]
+    pieces = BLOCK // LANES
+    arrived = jnp.concatenate([ref[...] for ref in received], axis=1)
+    stacked = product(mix_first_ref[...], stacked_columns(arrived))
+    moved_ref[...] = summed_powers(stacked[rows:], slot_weights_ref, rows, stacked[:rows])
+    extra_ref[...] = jnp.zeros(extra_ref.shape, f32)
+    moved = [(count + i, read) for i, read in ref_blocks(moved_ref, messages)]
+    for group, (before, send) in enumerate(zip(prepared, sends)):
+        place, code = send_places_ref[group:group + 1, :], send_codes_ref[group:group + 1, :]
+        here = ((place >> 7) >= level * pieces) & ((place >> 7) < (level + 1) * pieces)
+        send[...] = before[...] + pick(
+            moved, code, jnp.where(here, code >> 7, 0), jnp.zeros(before.shape, f32))
+
+    @pl.when(any_other(level, flags_ref))
+    def _():
+        others = other_traces(level, received, joined_ref, count)
+        stacked = product(mix_ref[...], stacked_columns(others))
+        extra_ref[...] = summed_powers(stacked[rows:], weights_ref, rows, stacked[:rows])
+        for group, send in enumerate(sends):
+            place = send_places_ref[group:group + 1, :]
+            send[...] = send[...] + pick(
+                ref_blocks(extra_ref, pieces), place, (place >> 7) - level * pieces, jnp.zeros(send.shape, f32))
+
+
+def last_kernel(level, messages, flags_ref, joined_ref, local_ref, weights_ref, lift_ref, lift_first_ref, grow_ref,
                 places_ref, advanced_ref, *rest):
-    received, (final_hbm, final_ref, sent) = rest[:messages], rest[messages:]
+    received, (final_hbm, final_ref, whole_ref, sent) = rest[:messages], rest[messages:]
     count = places_ref.shape[0]
     comp = final_ref.shape[0] // count
-    inflow = jnp.concatenate(
-        [inflow_block(level, block, received, joined_ref, faces_ref, count) for block in range(BLOCK // LANES)], axis=1)
-    loaded = own_ref[...] + product(lift_ref[...], stacked_columns(inflow))
-    stacked = stacked_columns(loaded)
+    add_received(level, received, joined_ref, count, flags_ref, local_ref, lift_ref, lift_first_ref, whole_ref)
+    whole = whole_ref[...]
+    stacked = stacked_columns(whole)
     copies = []
-    for number, chunk in enumerate(row_chunks(loaded.shape[0])):
-        new = grown_rows(chunk, stacked, loaded, grow_ref, weights_ref)
+    for number, chunk in enumerate(row_chunks(whole.shape[0])):
+        new = grown_rows(chunk, stacked, whole, grow_ref, weights_ref)
         height = min(chunk.stop, comp) - chunk.start
         for block in range(count):
             done = settle(level, value_blocks(new), places_ref, advanced_ref[chunk, block_at(block)], block)
@@ -437,36 +528,42 @@
     columns, out, *rest = call(
         functools.partial(first_kernel, swaps), "first", 10 ** 8, [fields.reshape(flat)] + arguments,
         [whole, table] + [message] * messages + [(one.shape, one.dtype) for one in arguments],
-        [(flat, f32), pltpu.SemaphoreType.DMA((ARGUMENTS - 1 + FIELD_COPIES,))], hbm=True)
+        [(flat, f32), pltpu.SemaphoreType.DMA((ARGUMENTS,))], hbm=True)
     sent, held = rest[:messages], rest[messages:]
     received = exchange(sent)
-    members, joined, places, send_places, mine, inner, weights, base, grow, trace_grow, mix, lift, heights = call(
-        functools.partial(plan_kernel, swaps), "plan", 2 * 10 ** 9, held + [columns, out],
-        [((8, padded), i32), ((2 * faces, padded), i32), ((count, LANES), i32), ((8, bnd), i32),
-         own, face_stack, weight, traced,
+    slots = ((trace_rows, messages * LANES), f32)
+    (members, joined, places, send_places, send_codes, slot_weights, flags, loaded, weights, new_trace, grow,
+     trace_grow, mix, mix_first, lift, lift_first, heights, *prepared) = call(
+        functools.partial(plan_kernel, swaps), "plan", 2 * 10 ** 9, held + [columns, out] + sent,
+        [((8, padded), i32), ((2 * faces, padded), i32), ((count, LANES), i32), ((8, bnd), i32), ((8, bnd), i32),
+         ((POWERS, messages * LANES), f32), ((LEVELS, LANES), f32), own, weight, traced,
          ((POWERS * rows, 3 * rows), bf16), (((POWERS + 1) * trace_rows, 3 * rows), bf16),
-         (((POWERS + 1) * trace_rows, 3 * faces * trace_rows), bf16), ((rows, 3 * faces * trace_rows), bf16),
-         ((1, LANES), f32)])
+         (((POWERS + 1) * trace_rows, 3 * faces * trace_rows), bf16), (((POWERS + 1) * trace_rows, 3 * trace_rows), bf16),
+         ((rows, 3 * faces * trace_rows), bf16), ((rows, 3 * trace_rows), bf16), ((1, LANES), f32)]
+        + [message] * messages, [face_stack])
     advanced = []
     for level in range(LEVELS - 1):
-        inflow, new_trace, *sent = call(
+        moved, extra, *sent = call(
             functools.partial(level_kernel, level, messages, count), "level", 10 ** 8,
-            [joined, inner, weights, base, mix, send_places] + received + sent,
-            [face_stack, traced] + [message] * messages)
-        received = exchange(sent)
-        beside = functools.partial(between_kernel, level + 1)
-        operands = [members, joined, places, columns, out, new_trace, heights, mine, inflow, weights, lift, grow,
-                    trace_grow] + advanced
+            [flags, joined, weights, slot_weights, mix, mix_first, send_places, send_codes] + received + prepared,
+            [slots, traced] + [message] * messages)
+        arrived, received = received, exchange(sent)
+        beside = functools.partial(between_kernel, level + 1, messages)
+        operands = [members, joined, places, columns, out, new_trace, moved, extra, heights, loaded, weights, lift,
+                    lift_first, grow, trace_grow, flags, send_places] + arrived
+        scratch = [face_stack, traced, own]
         if level + 1 < LEVELS - 1:
-            out, mine, inner, weights, base, *advanced = call(
-                beside, "between", 2 * 10 ** 9, operands, [table, own, face_stack, weight, traced, whole])
+            out, loaded, weights, new_trace, *rest = call(
+                beside, "between", 2 * 10 ** 9, operands + sent + advanced,
+                [table, own, weight, traced, whole] + [message] * messages, scratch)
+            advanced, prepared = rest[:1], rest[1:]
         else:
-            mine, inner, weights, *advanced = call(
-                beside, "between", 2 * 10 ** 9, operands, [own, face_stack, weight, whole], [table])
+            loaded, weights, *advanced = call(
+                beside, "between", 2 * 10 ** 9, operands + advanced, [own, weight, whole], [table] + scratch)
     final, = call(
         functools.partial(last_kernel, LEVELS - 1, messages), "last", 10 ** 9,
-        [joined, mine, inner, weights, lift, grow, places] + advanced + received,
-        [(flat, f32)], [(flat, f32), pltpu.SemaphoreType.DMA((-(-rows // ROW_CHUNK),))], out_hbm=True)
+        [flags, joined, loaded, weights, lift, lift_first, grow, places] + advanced + received,
+        [(flat, f32)], [(flat, f32), own, pltpu.SemaphoreType.DMA((-(-rows // ROW_CHUNK),))], out_hbm=True)
     return final.reshape(1, 1, comp, elements)
 
 

time: 37.4 us -> 36.6 us (0.979)
  starting transfers between devices: 17.7 us -> 15.9 us
  Pallas kernels: 18.6 us -> 19.6 us
    ppermute x12, starting transfers between devices: 17.7 us -> 15.9 us  [exchange(): lax.ppermute(one, swap[0], swap[1])]
    pallas_call x9, Pallas kernels: 18.6 us -> 19.6 us  [call(): pl.pallas_call(kernel, out_shape=tuple((jax.ShapeDtypeStruct(shape, dtype...]
  transfers between devices with their start and end apart: 12 -> 12, of which waited for: 3 -> 1; matrix products, arithmetic and copies ran while one was open for 0% -> 0% of each run, Pallas kernels for 25% -> 37%
where the time goes in v5:
time: 36.6 us; the launch traced here: 36.5 us
  Pallas kernels  19.6 us (54%)
  starting transfers between devices  15.9 us (43%)
  waiting for transfers between devices  0.6 us (2%)
    pallas_call x9, Pallas kernels, call(): pl.pallas_call(kernel, out_shape=tuple((jax.ShapeDtypeStruct(shape, dtype...  19.6 us
    ppermute x12, starting transfers between devices, exchange(): lax.ppermute(one, swap[0], swap[1])  15.9 us
  transfers between devices with their start and end apart: 12, of which 1 were waited for; matrix products, arithmetic and copies ran while one was open for 0% of the time, Pallas kernels for 37%

profile of v5, /device:TPU:0, one launch (start us, length us, event | category | flops | bytes accessed | tf_op | source)
XLA Modules:
  0.0 36.5 jit_solution(17669904650692407055)
XLA Ops:
  0.0 1.8 %first.1 = (f32[144,1024]{1,0:T(8,128)S(1)}, f32[64,1024]{1,0:T(8,128)S(1)}, f32[64,128]{1,0:T(8,128)S(1)}, f32[64,128]{1,0:T(8,128)S(1)}, f32[64,128]{1,0:T(8,1...) custom-call(f32[1120,128]{1,0:T(8,128)} %bitcast.9, ...), custom_call_target="tpu_custom_call" | custom-call | flops 100000000 | bytes 1048576 | tf_op jit(solution)/shard_map/first/pallas_call | solution.py:470
  1.8 5.5 %collective-permute-start = (f32[64,128]{1,0:T(8,128)S(1)}, f32[64,128]{1,0:T(8,128)S(1)}, u32[]{:S(2)}, u32[]{:S(2)}) collective-permute-start(f32[64,128]{1,0:T(8,128)S(1)} %get-tuple-element.84.refs_11_), channel_id=1, source_target_pairs={{0,30},{2,4},{4,2},{6,8},{8,6},{10,12},{12,10},{14,16},{16,14},{18... | collective-permute-start | bytes 98312 | tf_op jit(solution)/shard_map/ppermute | solution.py:518
  7.4 1.5 %collective-permute-start.1 = (f32[64,128]{1,0:T(8,128)S(1)}, f32[64,128]{1,0:T(8,128)S(1)}, u32[]{:S(2)}, u32[]{:S(2)}) collective-permute-start(f32[64,128]{1,0:T(8,128)S(1)} %get-tuple-element.85.refs_12_), channel_id=1, source_target_pairs={{0,1},{1,0},{2,3},{3,2},{4,5},{5,4},{6,7},{7,6},{8,9},{9,8},{10,11... | collective-permute-start | bytes 98312 | tf_op jit(solution)/shard_map/ppermute | solution.py:518
  8.8 0.0 collective-permute-start.2
  8.9 3.5 %plan.1 = (s32[8,1536]{1,0:T(8,128)S(1)}, s32[8,1536]{1,0:T(8,128)S(1)}, s32[8,128]{1,0:T(8,128)S(1)}, s32[8,128]{1,0:T(8,128)S(1)}, s32[8,128]{1,0:T(8,128)S(1)...) custom-call(f32[60,140]{1,0:T(8,128)S(1)} %get-tuple-element.73.refs, ...), custom_call_target="tpu_custom_call" | custom-call | flops 2000000000 | bytes 1048576 | tf_op jit(solution)/shard_map/plan/pallas_call | solution.py:470
  12.3 0.0 collective-permute-done.rest_0_
  12.4 0.0 collective-permute-done.1.rest_1_
  12.4 0.0 collective-permute-done.2.rest_2_
  12.4 0.5 %level.3 = (f32[64,384]{1,0:T(8,128)S(1)}, f32[64,384]{1,0:T(8,128)S(1)}, f32[64,128]{1,0:T(8,128)S(1)}, f32[64,128]{1,0:T(8,128)S(1)}, f32[64,128]{1,0:T(8,128)S(1)}) custom-call(f32[4,128]{1,0:T(4,128)S(1)} %get-tuple-element.87.flags_ref, s32[8,1536]{1,0:T(8,128)S(1)} %get-tuple-element.88.joined_ref, ...), custom_call_target="tpu_custom_call" | custom-call | flops 100000000 | bytes 1048576 | tf_op jit(solution)/shard_map/level/pallas_call | solution.py:470
  12.9 1.1 %collective-permute-start.3 = (f32[64,128]{1,0:T(8,128)S(1)}, f32[64,128]{1,0:T(8,128)S(1)}, u32[]{:S(2)}, u32[]{:S(2)}) collective-permute-start(f32[64,128]{1,0:T(8,128)S(1)} %get-tuple-element.109.rest_3_), channel_id=1, source_target_pairs={{0,30},{2,4},{4,2},{6,8},{8,6},{10,12},{12,10},{14,16},{16,14},{18... | collective-permute-start | bytes 98312 | tf_op jit(solution)/shard_map/ppermute | solution.py:518
  14.0 1.5 %collective-permute-start.4 = (f32[64,128]{1,0:T(8,128)S(1)}, f32[64,128]{1,0:T(8,128)S(1)}, u32[]{:S(2)}, u32[]{:S(2)}) collective-permute-start(f32[64,128]{1,0:T(8,128)S(1)} %get-tuple-element.110.rest_4_), channel_id=1, source_target_pairs={{0,1},{1,0},{2,3},{3,2},{4,5},{5,4},{6,7},{7,6},{8,9},{9,8},{10,11... | collective-permute-start | bytes 98312 | tf_op jit(solution)/shard_map/ppermute | solution.py:518
  15.5 0.0 collective-permute-start.5
  15.5 3.5 %between.3 = (f32[64,1024]{1,0:T(8,128)S(1)}, f32[144,384]{1,0:T(8,128)S(1)}, f32[8,384]{1,0:T(8,128)S(1)}, f32[64,384]{1,0:T(8,128)S(1)}, f32[144,1024]{1,0:T(8...) custom-call(s32[8,1536]{1,0:T(8,128)S(1)} %get-tuple-element.89.members_ref, ...), custom_call_target="tpu_custom_call" | custom-call | flops 2000000000 | bytes 1048576 | tf_op jit(solution)/shard_map/between/pallas_call | solution.py:470
  19.1 0.0 collective-permute-done.3.rest_0_
  19.1 0.0 collective-permute-done.4.rest_1_
  19.1 0.0 collective-permute-done.5.rest_2_
  19.1 0.5 %level.4 = (f32[64,384]{1,0:T(8,128)S(1)}, f32[64,384]{1,0:T(8,128)S(1)}, f32[64,128]{1,0:T(8,128)S(1)}, f32[64,128]{1,0:T(8,128)S(1)}, f32[64,128]{1,0:T(8,128)S(1)}) custom-call(f32[4,128]{1,0:T(4,128)S(1)} %get-tuple-element.87.flags_ref, s32[8,1536]{1,0:T(8,128)S(1)} %get-tuple-element.88.joined_ref, ...), custom_call_target="tpu_custom_call" | custom-call | flops 100000000 | bytes 1048576 | tf_op jit(solution)/shard_map/level/pallas_call | solution.py:470
  19.6 2.3 %collective-permute-start.6 = (f32[64,128]{1,0:T(8,128)S(1)}, f32[64,128]{1,0:T(8,128)S(1)}, u32[]{:S(2)}, u32[]{:S(2)}) collective-permute-start(f32[64,128]{1,0:T(8,128)S(1)} %get-tuple-element.121.rest_3_), channel_id=1, source_target_pairs={{0,30},{2,4},{4,2},{6,8},{8,6},{10,12},{12,10},{14,16},{16,14},{18... | collective-permute-start | bytes 98312 | tf_op jit(solution)/shard_map/ppermute | solution.py:518
  21.9 1.5 %collective-permute-start.7 = (f32[64,128]{1,0:T(8,128)S(1)}, f32[64,128]{1,0:T(8,128)S(1)}, u32[]{:S(2)}, u32[]{:S(2)}) collective-permute-start(f32[64,128]{1,0:T(8,128)S(1)} %get-tuple-element.122.rest_4_), channel_id=1, source_target_pairs={{0,1},{1,0},{2,3},{3,2},{4,5},{5,4},{6,7},{7,6},{8,9},{9,8},{10,11... | collective-permute-start | bytes 98312 | tf_op jit(solution)/shard_map/ppermute | solution.py:518
  23.4 0.0 collective-permute-start.8
  23.4 3.7 %between.4 = (f32[64,1024]{1,0:T(8,128)S(1)}, f32[144,384]{1,0:T(8,128)S(1)}, f32[8,384]{1,0:T(8,128)S(1)}, f32[64,384]{1,0:T(8,128)S(1)}, f32[144,1024]{1,0:T(8...) custom-call(s32[8,1536]{1,0:T(8,128)S(1)} %get-tuple-element.89.members_ref, ...), custom_call_target="tpu_custom_call" | custom-call | flops 2000000000 | bytes 1048576 | tf_op jit(solution)/shard_map/between/pallas_call | solution.py:470
  27.1 0.0 collective-permute-done.6.rest_0_
  27.1 0.0 collective-permute-done.7.rest_1_
  27.1 0.0 collective-permute-done.8.rest_2_
  27.1 0.5 %level.5 = (f32[64,384]{1,0:T(8,128)S(1)}, f32[64,384]{1,0:T(8,128)S(1)}, f32[64,128]{1,0:T(8,128)S(1)}, f32[64,128]{1,0:T(8,128)S(1)}, f32[64,128]{1,0:T(8,128)S(1)}) custom-call(f32[4,128]{1,0:T(4,128)S(1)} %get-tuple-element.87.flags_ref, s32[8,1536]{1,0:T(8,128)S(1)} %get-tuple-element.88.joined_ref, ...), custom_call_target="tpu_custom_call" | custom-call | flops 100000000 | bytes 1048576 | tf_op jit(solution)/shard_map/level/pallas_call | solution.py:470
  27.7 1.1 %collective-permute-start.9 = (f32[64,128]{1,0:T(8,128)S(1)}, f32[64,128]{1,0:T(8,128)S(1)}, u32[]{:S(2)}, u32[]{:S(2)}) collective-permute-start(f32[64,128]{1,0:T(8,128)S(1)} %get-tuple-element.138), channel_id=1, source_target_pairs={{0,30},{2,4},{4,2},{6,8},{8,6},{10,12},{12,10},{14,16},{16,14},{18... | collective-permute-start | bytes 98312 | tf_op jit(solution)/shard_map/ppermute | solution.py:518
  28.8 1.5 %collective-permute-start.10 = (f32[64,128]{1,0:T(8,128)S(1)}, f32[64,128]{1,0:T(8,128)S(1)}, u32[]{:S(2)}, u32[]{:S(2)}) collective-permute-start(f32[64,128]{1,0:T(8,128)S(1)} %get-tuple-element.139), channel_id=1, source_target_pairs={{0,1},{1,0},{2,3},{3,2},{4,5},{5,4},{6,7},{7,6},{8,9},{9,8},{10,11... | collective-permute-start | bytes 98312 | tf_op jit(solution)/shard_map/ppermute | solution.py:518
  30.3 0.0 collective-permute-start.11
  30.3 2.9 %between.5 = (f32[144,384]{1,0:T(8,128)S(1)}, f32[8,384]{1,0:T(8,128)S(1)}, f32[144,1024]{1,0:T(8,128)S(1)}) custom-call(s32[8,1536]{1,0:T(8,128)S(1)} %get-tuple-element.89.members_ref, s32[8,1536]{1,0:T(8,128)S(1)} %get-tuple-element.88.joined_ref, s32[8,128]{1,0:T(8,128)S(1)} %get-tuple-element.90.places_ref, ...), custom_call_target="tpu_custom_call" | custom-call | flops 2000000000 | bytes 1048576 | tf_op jit(solution)/shard_map/between/pallas_call | solution.py:470
  33.2 0.6 %collective-permute-done.9.rest_0_ = f32[64,128]{1,0:T(8,128)S(1)} collective-permute-done((f32[64,128]{1,0:T(8,128)S(1)}, f32[64,128]{1,0:T(8,128)S(1)}, u32[]{:S(2)}, u32[]{:S(2)}) %collective-permute-start.9) | collective-permute-done | bytes 32800 | tf_op jit(solution)/shard_map/ppermute | solution.py:518
  33.8 0.0 collective-permute-done.10.rest_1_
  33.8 0.0 collective-permute-done.11.rest_2_
  33.8 2.5 %last.1 = f32[1120,128]{1,0:T(8,128)} custom-call(f32[4,128]{1,0:T(4,128)S(1)} %get-tuple-element.87.flags_ref, s32[8,1536]{1,0:T(8,128)S(1)} %get-tuple-element.88.joined_ref, f32[144,384]{1,0:T(8,128)S(1)} %get-tuple-element.135.local_ref, f32[8,384]{1,0:T(8,128)S(1)} %get-tuple-element.136.weights_ref, bf16[144,768]{1,0:T(8,128)(2,1)S(1)} %get-tuple-element.105.lift_ref, ...), custom_call_target="tpu_custom_call" | custom-call | flops 1000000000 | bytes 1048576 | tf_op jit(solution)/shard_map/last/pallas_call | solution.py:470
Async XLA Ops:
  1.8 10.5 %collective-permute-start = (f32[64,128]{1,0:T(8,128)S(1)}, f32[64,128]{1,0:T(8,128)S(1)}, u32[]{:S(2)}, u32[]{:S(2)}) collective-permute-start(f32[64,128]{1,0:T(8,128)S(1)} %get-tuple-element.84.refs_11_), channel_id=1, source_target_pairs={{0,30},{2,4},{4,2},{6,8},{8,6},{10,12},{12,10},{14,16},{16,14},{18... | collective-permute-start | bytes 98312 | tf_op jit(solution)/shard_map/ppermute | solution.py:518
  7.4 5.0 %collective-permute-start.1 = (f32[64,128]{1,0:T(8,128)S(1)}, f32[64,128]{1,0:T(8,128)S(1)}, u32[]{:S(2)}, u32[]{:S(2)}) collective-permute-start(f32[64,128]{1,0:T(8,128)S(1)} %get-tuple-element.85.refs_12_), channel_id=1, source_target_pairs={{0,1},{1,0},{2,3},{3,2},{4,5},{5,4},{6,7},{7,6},{8,9},{9,8},{10,11... | collective-permute-start | bytes 98312 | tf_op jit(solution)/shard_map/ppermute | solution.py:518
  8.8 3.5 %collective-permute-start.2 = (f32[64,128]{1,0:T(8,128)S(1)}, f32[64,128]{1,0:T(8,128)S(1)}, u32[]{:S(2)}, u32[]{:S(2)}) collective-permute-start(f32[64,128]{1,0:T(8,128)S(1)} %get-tuple-element.86.refs_13_), channel_id=1, source_target_pairs={{0,2},{2,0},{4,6},{6,4},{8,10},{10,8},{12,14},{14,12},{16,18},{18,... | collective-permute-start | bytes 98312 | tf_op jit(solution)/shard_map/ppermute | solution.py:518
  12.9 6.1 %collective-permute-start.3 = (f32[64,128]{1,0:T(8,128)S(1)}, f32[64,128]{1,0:T(8,128)S(1)}, u32[]{:S(2)}, u32[]{:S(2)}) collective-permute-start(f32[64,128]{1,0:T(8,128)S(1)} %get-tuple-element.109.rest_3_), channel_id=1, source_target_pairs={{0,30},{2,4},{4,2},{6,8},{8,6},{10,12},{12,10},{14,16},{16,14},{18... | collective-permute-start | bytes 98312 | tf_op jit(solution)/shard_map/ppermute | solution.py:518
  14.0 5.1 %collective-permute-start.4 = (f32[64,128]{1,0:T(8,128)S(1)}, f32[64,128]{1,0:T(8,128)S(1)}, u32[]{:S(2)}, u32[]{:S(2)}) collective-permute-start(f32[64,128]{1,0:T(8,128)S(1)} %get-tuple-element.110.rest_4_), channel_id=1, source_target_pairs={{0,1},{1,0},{2,3},{3,2},{4,5},{5,4},{6,7},{7,6},{8,9},{9,8},{10,11... | collective-permute-start | bytes 98312 | tf_op jit(solution)/shard_map/ppermute | solution.py:518
  15.5 3.6 %collective-permute-start.5 = (f32[64,128]{1,0:T(8,128)S(1)}, f32[64,128]{1,0:T(8,128)S(1)}, u32[]{:S(2)}, u32[]{:S(2)}) collective-permute-start(f32[64,128]{1,0:T(8,128)S(1)} %get-tuple-element.111.rest_5_), channel_id=1, source_target_pairs={{0,2},{2,0},{4,6},{6,4},{8,10},{10,8},{12,14},{14,12},{16,18},{18,... | collective-permute-start | bytes 98312 | tf_op jit(solution)/shard_map/ppermute | solution.py:518
  19.6 7.5 %collective-permute-start.6 = (f32[64,128]{1,0:T(8,128)S(1)}, f32[64,128]{1,0:T(8,128)S(1)}, u32[]{:S(2)}, u32[]{:S(2)}) collective-permute-start(f32[64,128]{1,0:T(8,128)S(1)} %get-tuple-element.121.rest_3_), channel_id=1, source_target_pairs={{0,30},{2,4},{4,2},{6,8},{8,6},{10,12},{12,10},{14,16},{16,14},{18... | collective-permute-start | bytes 98312 | tf_op jit(solution)/shard_map/ppermute | solution.py:518
  21.9 5.2 %collective-permute-start.7 = (f32[64,128]{1,0:T(8,128)S(1)}, f32[64,128]{1,0:T(8,128)S(1)}, u32[]{:S(2)}, u32[]{:S(2)}) collective-permute-start(f32[64,128]{1,0:T(8,128)S(1)} %get-tuple-element.122.rest_4_), channel_id=1, source_target_pairs={{0,1},{1,0},{2,3},{3,2},{4,5},{5,4},{6,7},{7,6},{8,9},{9,8},{10,11... | collective-permute-start | bytes 98312 | tf_op jit(solution)/shard_map/ppermute | solution.py:518
  23.4 3.8 %collective-permute-start.8 = (f32[64,128]{1,0:T(8,128)S(1)}, f32[64,128]{1,0:T(8,128)S(1)}, u32[]{:S(2)}, u32[]{:S(2)}) collective-permute-start(f32[64,128]{1,0:T(8,128)S(1)} %get-tuple-element.123.rest_5_), channel_id=1, source_target_pairs={{0,2},{2,0},{4,6},{6,4},{8,10},{10,8},{12,14},{14,12},{16,18},{18,... | collective-permute-start | bytes 98312 | tf_op jit(solution)/shard_map/ppermute | solution.py:518
  27.7 6.1 %collective-permute-start.9 = (f32[64,128]{1,0:T(8,128)S(1)}, f32[64,128]{1,0:T(8,128)S(1)}, u32[]{:S(2)}, u32[]{:S(2)}) collective-permute-start(f32[64,128]{1,0:T(8,128)S(1)} %get-tuple-element.138), channel_id=1, source_target_pairs={{0,30},{2,4},{4,2},{6,8},{8,6},{10,12},{12,10},{14,16},{16,14},{18... | collective-permute-start | bytes 98312 | tf_op jit(solution)/shard_map/ppermute | solution.py:518
  28.8 5.0 %collective-permute-start.10 = (f32[64,128]{1,0:T(8,128)S(1)}, f32[64,128]{1,0:T(8,128)S(1)}, u32[]{:S(2)}, u32[]{:S(2)}) collective-permute-start(f32[64,128]{1,0:T(8,128)S(1)} %get-tuple-element.139), channel_id=1, source_target_pairs={{0,1},{1,0},{2,3},{3,2},{4,5},{5,4},{6,7},{7,6},{8,9},{9,8},{10,11... | collective-permute-start | bytes 98312 | tf_op jit(solution)/shard_map/ppermute | solution.py:518
  30.3 3.5 %collective-permute-start.11 = (f32[64,128]{1,0:T(8,128)S(1)}, f32[64,128]{1,0:T(8,128)S(1)}, u32[]{:S(2)}, u32[]{:S(2)}) collective-permute-start(f32[64,128]{1,0:T(8,128)S(1)} %get-tuple-element.140), channel_id=1, source_target_pairs={{0,2},{2,0},{4,6},{6,4},{8,10},{10,8},{12,14},{14,12},{16,18},{18,... | collective-permute-start | bytes 98312 | tf_op jit(solution)/shard_map/ppermute | solution.py:518

commit v6 on v5

--- a/solution.py
+++ b/solution.py
@@ -46,15 +46,23 @@
     return high, (values - high.astype(f32)).astype(bf16)
 
 
+def whole_lanes(size):
+    return size // LANES * LANES
+
+
 def stacked_columns(values):
     high, low = split(values)
-    return jnp.concatenate([high, low, high], axis=0)
+    main = whole_lanes(values.shape[0])
+    parts = [high[:main], low[:main], high[:main], high[main:], low[main:], high[main:]]
+    return jnp.concatenate([part for part in parts if part.shape[0]], axis=0)
 
 
 def stacked_matrix(values):
     high = values.astype(bf16).astype(f32)
     low = values - high
-    return jnp.concatenate([high, high, low], axis=1).astype(bf16)
+    main = whole_lanes(values.shape[1])
+    parts = [high[:, :main], high[:, :main], low[:, :main], high[:, main:], high[:, main:], low[:, main:]]
+    return jnp.concatenate([part for part in parts if part.shape[1]], axis=1).astype(bf16)
 
 
 def product(matrix, columns):
@@ -189,14 +197,6 @@
             ref_blocks(out_ref, out_ref.shape[1] // LANES), index, index >> 7, jnp.zeros((trace_rows, LANES), f32))
 
 
-def local_part(level, members_ref, joined_ref, columns_ref, out_ref, heights_ref, lift_ref,
-               loaded_ref, weights_ref, faces_ref):
-    for block in range(BLOCK // LANES):
-        own_block(level, block, members_ref, joined_ref, columns_ref, heights_ref, loaded_ref, weights_ref)
-        face_block(level, block, joined_ref, out_ref, faces_ref)
-    loaded_ref[...] = loaded_ref[...] + product(lift_ref[...], stacked_columns(faces_ref[...]))
-
-
 def advanced_traces(loaded, matrix_ref, weights_ref, rows):
     stacked = product(matrix_ref[...], stacked_columns(loaded))
     return summed_powers(stacked[rows:], weights_ref, rows, stacked[:rows])
@@ -220,8 +220,8 @@
     return summed_powers(product(matrix, stacked), weights_ref, ROW_CHUNK, loaded[chunk])
 
 
-def matrix_powers(operator_ref, trace_ref, lift_ref, grow_ref, trace_grow_ref, mix_ref, mix_first_ref,
-                  lift_out_ref, lift_first_ref):
+def matrix_powers(operator_ref, trace_ref, lift_ref, grow_ref, trace_grow_ref, mix_ref, lift_out_ref,
+                  lift_first_ref):
     comp = operator_ref.shape[0]
     trace_comp, faces, _ = lift_ref.shape
     rows = lift_out_ref.shape[0]
@@ -232,20 +232,21 @@
     traces = jnp.concatenate([traces, jnp.zeros((trace_rows, rows - comp), f32)], axis=1)
     lift = jnp.concatenate([pad_rows(lift_ref[:, face, :], trace_rows) for face in range(faces)], axis=0)
     lift = pad_rows(jnp.transpose(lift), rows)
+    lift_out_ref[...] = stacked_matrix(lift)
+    lift_first_ref[...] = stacked_matrix(lift[:, :trace_rows])
     powers, have = operator, 1
     while have < POWERS:
         more = exact_product(jnp.concatenate([traces, powers], axis=0), powers[(have - 1) * rows:have * rows])
         traces = jnp.concatenate([traces, more[:have * trace_rows]], axis=0)
         powers = jnp.concatenate([powers, more[have * trace_rows:]], axis=0)
         have *= 2
+        yield
     traces = jnp.concatenate([traces, exact_product(traces[:trace_rows], powers[-rows:])], axis=0)
-    mix = exact_product(traces, lift)
-    mix_ref[...] = stacked_matrix(mix)
-    mix_first_ref[...] = stacked_matrix(mix[:, :trace_rows])
-    lift_first_ref[...] = stacked_matrix(lift[:, :trace_rows])
     trace_grow_ref[...] = stacked_matrix(traces)
-    lift_out_ref[...] = stacked_matrix(lift)
+    yield
+    mix_ref[...] = stacked_matrix(exact_product(traces, lift[:, :trace_rows]))
     grow_ref[...] = stacked_matrix(powers)
+    yield
 
 
 def plan_kernel(swaps, *refs):
@@ -254,12 +255,15 @@
     messages = len(swaps)
     sent, refs = refs[:messages], refs[messages:]
     (members_ref, joined_ref, places_ref, send_places_ref, send_codes_ref, slot_weights_ref, flags_ref, loaded_ref,
-     weights_ref, new_trace_ref, grow_ref, trace_grow_ref, mix_ref, mix_first_ref, lift_out_ref, lift_first_ref,
-     wide_heights_ref), refs = refs[:17], refs[17:]
+     weights_ref, new_trace_ref, grow_ref, trace_grow_ref, mix_ref, lift_out_ref, lift_first_ref,
+     wide_heights_ref), refs = refs[:16], refs[16:]
     prepared, (faces_ref,) = refs[:messages], refs[messages:]
     elements = columns_ref.shape[1]
     count = elements // LANES
     faces = neighbours_ref.shape[0]
+    steps = matrix_powers(operator_ref, trace_ref, lift_ref, grow_ref, trace_grow_ref, mix_ref, lift_out_ref,
+                          lift_first_ref)
+    next(steps)
     sizes = sizes_ref[...].astype(f32)
     number = lax.broadcasted_iota(i32, sizes.shape, 1)
     starts = [jnp.sum(jnp.where(number < level, sizes, 0.0)).astype(i32) for level in range(LEVELS)]
@@ -318,11 +322,14 @@
         for number in range(1, BLOCK // LANES):
             row = jnp.maximum(row, code[:, block_at(number)])
         flags_ref[level:level + 1, :] = row
-    matrix_powers(operator_ref, trace_ref, lift_ref, grow_ref, trace_grow_ref, mix_ref, mix_first_ref,
-                  lift_out_ref, lift_first_ref)
-    local_part(0, members_ref, joined_ref, columns_ref, out_ref, wide_heights_ref, lift_out_ref,
-               loaded_ref, weights_ref, faces_ref)
-    new_trace_ref[...] = advanced_traces(loaded_ref[...], trace_grow_ref, weights_ref, out_ref.shape[0])
+    next(steps)
+    for block in range(BLOCK // LANES):
+        own_block(0, block, members_ref, joined_ref, columns_ref, wide_heights_ref, loaded_ref, weights_ref)
+        face_block(0, block, joined_ref, out_ref, faces_ref)
+        next(steps)
+    loaded = loaded_ref[...] + product(lift_out_ref[...], stacked_columns(faces_ref[...]))
+    loaded_ref[...] = loaded
+    new_trace_ref[...] = advanced_traces(loaded, trace_grow_ref, weights_ref, out_ref.shape[0])
     local_messages(0, new_trace_ref, send_places_ref, sent, prepared)
 
 
@@ -365,8 +372,8 @@
 
 
 def between_kernel(level, messages, members_ref, joined_ref, places_ref, columns_ref, old_out_ref, old_trace_ref,
-                   moved_ref, extra_ref, heights_ref, local_ref, old_weights_ref, lift_ref, lift_first_ref, grow_ref,
-                   trace_grow_ref, flags_ref, send_places_ref, *rest):
+                   moved_ref, extra_ref, extra_trace_ref, heights_ref, local_ref, old_weights_ref, lift_ref,
+                   lift_first_ref, grow_ref, trace_grow_ref, send_places_ref, *rest):
     received, rest = rest[:messages], rest[messages:]
     final = level == LEVELS - 1
     if not final:
@@ -380,48 +387,71 @@
         prepared, (faces_ref, trace_ref, whole_ref) = rest[5:5 + messages], rest[5 + messages:]
     count = places_ref.shape[0]
     done = level - 1
-    add_received(done, received, joined_ref, count, flags_ref, local_ref, lift_ref, lift_first_ref, whole_ref)
+    first = received_traces(done, 0, received, joined_ref, count)
+    inflow = product(lift_first_ref[...], stacked_columns(first))
     for block in range(BLOCK // LANES):
         here = block_at(block)
         index = joined_ref[0:1, block_at(done * (BLOCK // LANES) + block)]
         moved = [(count + i, read) for i, read in ref_blocks(moved_ref, messages)]
-        trace_ref[:, here] = old_trace_ref[:, here] + extra_ref[:, here] + pick(
+        trace_ref[:, here] = old_trace_ref[:, here] + extra_trace_ref[:, here] + pick(
             moved, index, index >> 7, jnp.zeros((old_trace_ref.shape[0], LANES), f32))
-    for block in range(count):
-        here = block_at(block)
-        out_ref[:, here] = settle(
-            done, ref_blocks(trace_ref, BLOCK // LANES), places_ref, old_out_ref[:, here], block)
-    whole = whole_ref[...]
+    whole = local_ref[...] + inflow + extra_ref[...]
     stacked = stacked_columns(whole)
     chunks = row_chunks(whole.shape[0])
     pieces = BLOCK // LANES
-    for number, chunk in enumerate(chunks):
-        new = grown_rows(chunk, stacked, whole, grow_ref, old_weights_ref)
-        for block in range(number * pieces // len(chunks), (number + 1) * pieces // len(chunks)):
+
+    def gather_own(part):
+        for block in range(part * pieces // len(chunks), (part + 1) * pieces // len(chunks)):
             own_block(level, block, members_ref, joined_ref, columns_ref, heights_ref, loaded_ref, weights_ref)
+
+    def gather_faces(part):
+        for block in range(part * pieces // len(chunks), (part + 1) * pieces // len(chunks)):
             face_block(level, block, joined_ref, out_ref, faces_ref)
+
+    def put_out(part):
+        for block in range(part * count // len(chunks), (part + 1) * count // len(chunks)):
+            here = block_at(block)
+            out_ref[:, here] = settle(
+                done, ref_blocks(trace_ref, pieces), places_ref, old_out_ref[:, here], block)
+
+    def put_columns(chunk):
         for block in range(count):
             here = block_at(block)
             before = advanced_ref[chunk, here] if level > 1 else None
-            new_advanced_ref[chunk, here] = settle(done, value_blocks(new), places_ref, before, block)
+            new_advanced_ref[chunk, here] = settle(
+                done, [(b, functools.partial(lambda b: whole_ref[chunk, block_at(b)], b)) for b in range(pieces)],
+                places_ref, before, block)
+
+    for part in range(len(chunks)):
+        put_out(part)
+    for part, chunk in enumerate(chunks):
+        whole_ref[chunk, :] = grown_rows(chunk, stacked, whole, grow_ref, old_weights_ref)
+        gather_own(part)
+        gather_faces(part)
     loaded = loaded_ref[...] + product(lift_ref[...], stacked_columns(faces_ref[...]))
+    put_columns(chunks[0])
     loaded_ref[...] = loaded
     if not final:
-        new_trace_ref[...] = advanced_traces(loaded, trace_grow_ref, weights_ref, out_ref.shape[0])
+        traces = advanced_traces(loaded, trace_grow_ref, weights_ref, out_ref.shape[0])
+    for chunk in chunks[1:]:
+        put_columns(chunk)
+    if not final:
+        new_trace_ref[...] = traces
         local_messages(level, new_trace_ref, send_places_ref, sent, prepared)
 
 
-def level_kernel(level, messages, count, flags_ref, joined_ref, weights_ref, slot_weights_ref, mix_ref, mix_first_ref,
-                 send_places_ref, send_codes_ref, *rest):
+def level_kernel(level, messages, count, flags_ref, joined_ref, weights_ref, slot_weights_ref, mix_ref, lift_ref,
+                 trace_grow_ref, send_places_ref, send_codes_ref, *rest):
     received, rest = rest[:messages], rest[messages:]
     prepared, rest = rest[:messages], rest[messages:]
-    moved_ref, extra_ref, sends = rest[0], rest[1], rest[2:]
+    moved_ref, extra_ref, extra_trace_ref, sends = rest[0], rest[1], rest[2], rest[3:]
     rows = moved_ref.shape[0]
     pieces = BLOCK // LANES
     arrived = jnp.concatenate([ref[...] for ref in received], axis=1)
-    stacked = product(mix_first_ref[...], stacked_columns(arrived))
+    stacked = product(mix_ref[...], stacked_columns(arrived))
     moved_ref[...] = summed_powers(stacked[rows:], slot_weights_ref, rows, stacked[:rows])
     extra_ref[...] = jnp.zeros(extra_ref.shape, f32)
+    extra_trace_ref[...] = jnp.zeros(extra_trace_ref.shape, f32)
     moved = [(count + i, read) for i, read in ref_blocks(moved_ref, messages)]
     for group, (before, send) in enumerate(zip(prepared, sends)):
         place, code = send_places_ref[group:group + 1, :], send_codes_ref[group:group + 1, :]
@@ -432,12 +462,13 @@
     @pl.when(any_other(level, flags_ref))
     def _():
         others = other_traces(level, received, joined_ref, count)
-        stacked = product(mix_ref[...], stacked_columns(others))
-        extra_ref[...] = summed_powers(stacked[rows:], weights_ref, rows, stacked[:rows])
+        extra = product(lift_ref[...], stacked_columns(others))
+        extra_ref[...] = extra
+        extra_trace_ref[...] = advanced_traces(extra, trace_grow_ref, weights_ref, rows)
         for group, send in enumerate(sends):
             place = send_places_ref[group:group + 1, :]
             send[...] = send[...] + pick(
-                ref_blocks(extra_ref, pieces), place, (place >> 7) - level * pieces, jnp.zeros(send.shape, f32))
+                ref_blocks(extra_trace_ref, pieces), place, (place >> 7) - level * pieces, jnp.zeros(send.shape, f32))
 
 
 def last_kernel(level, messages, flags_ref, joined_ref, local_ref, weights_ref, lift_ref, lift_first_ref, grow_ref,
@@ -533,24 +564,23 @@
     received = exchange(sent)
     slots = ((trace_rows, messages * LANES), f32)
     (members, joined, places, send_places, send_codes, slot_weights, flags, loaded, weights, new_trace, grow,
-     trace_grow, mix, mix_first, lift, lift_first, heights, *prepared) = call(
+     trace_grow, mix, lift, lift_first, heights, *prepared) = call(
         functools.partial(plan_kernel, swaps), "plan", 2 * 10 ** 9, held + [columns, out] + sent,
         [((8, padded), i32), ((2 * faces, padded), i32), ((count, LANES), i32), ((8, bnd), i32), ((8, bnd), i32),
          ((POWERS, messages * LANES), f32), ((LEVELS, LANES), f32), own, weight, traced,
          ((POWERS * rows, 3 * rows), bf16), (((POWERS + 1) * trace_rows, 3 * rows), bf16),
-         (((POWERS + 1) * trace_rows, 3 * faces * trace_rows), bf16), (((POWERS + 1) * trace_rows, 3 * trace_rows), bf16),
-         ((rows, 3 * faces * trace_rows), bf16), ((rows, 3 * trace_rows), bf16), ((1, LANES), f32)]
+         (((POWERS + 1) * trace_rows, 3 * trace_rows), bf16), ((rows, 3 * faces * trace_rows), bf16), ((rows, 3 * trace_rows), bf16), ((1, LANES), f32)]
         + [message] * messages, [face_stack])
     advanced = []
     for level in range(LEVELS - 1):
-        moved, extra, *sent = call(
+        moved, extra, extra_trace, *sent = call(
             functools.partial(level_kernel, level, messages, count), "level", 10 ** 8,
-            [flags, joined, weights, slot_weights, mix, mix_first, send_places, send_codes] + received + prepared,
-            [slots, traced] + [message] * messages)
+            [flags, joined, weights, slot_weights, mix, lift, trace_grow, send_places, send_codes] + received + prepared,
+            [slots, own, traced] + [message] * messages)
         arrived, received = received, exchange(sent)
         beside = functools.partial(between_kernel, level + 1, messages)
-        operands = [members, joined, places, columns, out, new_trace, moved, extra, heights, loaded, weights, lift,
-                    lift_first, grow, trace_grow, flags, send_places] + arrived
+        operands = [members, joined, places, columns, out, new_trace, moved, extra, extra_trace, heights, loaded,
+                    weights, lift, lift_first, grow, trace_grow, send_places] + arrived
         scratch = [face_stack, traced, own]
         if level + 1 < LEVELS - 1:
             out, loaded, weights, new_trace, *rest = call(

time: 36.6 us -> 34.7 us (0.948)
  Pallas kernels: 19.6 us -> 17.1 us
  starting transfers between devices: 15.9 us -> 16.5 us
    pallas_call x9, Pallas kernels: 19.6 us -> 17.1 us  [call(): pl.pallas_call(kernel, out_shape=tuple((jax.ShapeDtypeStruct(shape, dtype...]
    ppermute x12, starting transfers between devices: 15.9 us -> 16.5 us  [exchange(): lax.ppermute(one, swap[0], swap[1])]
  transfers between devices with their start and end apart: 12 -> 12, of which waited for: 1 -> 3; matrix products, arithmetic and copies ran while one was open for 0% -> 0% of each run, Pallas kernels for 37% -> 32%
where the time goes in v6:
time: 34.7 us; the launch traced here: 34.6 us
  Pallas kernels  17.1 us (49%)
  starting transfers between devices  16.5 us (48%)
  waiting for transfers between devices  0.7 us (2%)
    pallas_call x9, Pallas kernels, call(): pl.pallas_call(kernel, out_shape=tuple((jax.ShapeDtypeStruct(shape, dtype...  17.1 us
    ppermute x12, starting transfers between devices, exchange(): lax.ppermute(one, swap[0], swap[1])  16.5 us
    ppermute x12, waiting for transfers between devices, exchange(): lax.ppermute(one, swap[0], swap[1])  0.7 us
  transfers between devices with their start and end apart: 12, of which 3 were waited for; matrix products, arithmetic and copies ran while one was open for 0% of the time, Pallas kernels for 32%

profile of v6, /device:TPU:0, one launch (start us, length us, event | category | flops | bytes accessed | tf_op | source)
XLA Modules:
  0.0 34.6 jit_solution(108610257540926325)
XLA Ops:
  0.0 1.8 %first.1 = (f32[144,1024]{1,0:T(8,128)S(1)}, f32[64,1024]{1,0:T(8,128)S(1)}, f32[64,128]{1,0:T(8,128)S(1)}, f32[64,128]{1,0:T(8,128)S(1)}, f32[64,128]{1,0:T(8,1...) custom-call(f32[1120,128]{1,0:T(8,128)} %bitcast.9, ...), custom_call_target="tpu_custom_call" | custom-call | flops 100000000 | bytes 1048576 | tf_op jit(solution)/shard_map/first/pallas_call | solution.py:501
  1.8 5.5 %collective-permute-start = (f32[64,128]{1,0:T(8,128)S(1)}, f32[64,128]{1,0:T(8,128)S(1)}, u32[]{:S(2)}, u32[]{:S(2)}) collective-permute-start(f32[64,128]{1,0:T(8,128)S(1)} %get-tuple-element.86.refs_11_), channel_id=1, source_target_pairs={{0,30},{2,4},{4,2},{6,8},{8,6},{10,12},{12,10},{14,16},{16,14},{18... | collective-permute-start | bytes 98312 | tf_op jit(solution)/shard_map/ppermute | solution.py:549
  7.4 1.5 %collective-permute-start.1 = (f32[64,128]{1,0:T(8,128)S(1)}, f32[64,128]{1,0:T(8,128)S(1)}, u32[]{:S(2)}, u32[]{:S(2)}) collective-permute-start(f32[64,128]{1,0:T(8,128)S(1)} %get-tuple-element.87.refs_12_), channel_id=1, source_target_pairs={{0,1},{1,0},{2,3},{3,2},{4,5},{5,4},{6,7},{7,6},{8,9},{9,8},{10,11... | collective-permute-start | bytes 98312 | tf_op jit(solution)/shard_map/ppermute | solution.py:549
  8.8 0.0 collective-permute-start.2
  8.9 2.9 %plan.1 = (s32[8,1536]{1,0:T(8,128)S(1)}, s32[8,1536]{1,0:T(8,128)S(1)}, s32[8,128]{1,0:T(8,128)S(1)}, s32[8,128]{1,0:T(8,128)S(1)}, s32[8,128]{1,0:T(8,128)S(1)...) custom-call(f32[60,140]{1,0:T(8,128)S(1)} %get-tuple-element.75.refs, ...), custom_call_target="tpu_custom_call" | custom-call | flops 2000000000 | bytes 1048576 | tf_op jit(solution)/shard_map/plan/pallas_call | solution.py:501
  11.7 0.0 collective-permute-done.rest_0_
  11.8 0.0 collective-permute-done.1.rest_1_
  11.8 0.0 collective-permute-done.2.rest_2_
  11.8 0.5 %level.3 = (f32[64,384]{1,0:T(8,128)S(1)}, f32[144,384]{1,0:T(8,128)S(1)}, f32[64,384]{1,0:T(8,128)S(1)}, f32[64,128]{1,0:T(8,128)S(1)}, f32[64,128]{1,0:T(8,128)S(1)}, /*index=5*/f32[64,128]{1,0:T(8,128)S(1)}) custom-call(f32[4,128]{1,0:T(4,128)S(1)} %get-tuple-element.89.flags_ref, s32[8,1536]{1,0:T(8,128)S(1)} %get-tuple-element.90.joined_ref, ...), custom_call_target="tpu_custom_call" | custom-call | flops 100000000 | bytes 1048576 | tf_op jit(solution)/shard_map/level/pallas_call | solution.py:501
  12.3 1.7 %collective-permute-start.3 = (f32[64,128]{1,0:T(8,128)S(1)}, f32[64,128]{1,0:T(8,128)S(1)}, u32[]{:S(2)}, u32[]{:S(2)}) collective-permute-start(f32[64,128]{1,0:T(8,128)S(1)} %get-tuple-element.111.rest_3_), channel_id=1, source_target_pairs={{0,30},{2,4},{4,2},{6,8},{8,6},{10,12},{12,10},{14,16},{16,14},{18... | collective-permute-start | bytes 98312 | tf_op jit(solution)/shard_map/ppermute | solution.py:549
  14.0 1.5 %collective-permute-start.4 = (f32[64,128]{1,0:T(8,128)S(1)}, f32[64,128]{1,0:T(8,128)S(1)}, u32[]{:S(2)}, u32[]{:S(2)}) collective-permute-start(f32[64,128]{1,0:T(8,128)S(1)} %get-tuple-element.112.rest_4_), channel_id=1, source_target_pairs={{0,1},{1,0},{2,3},{3,2},{4,5},{5,4},{6,7},{7,6},{8,9},{9,8},{10,11... | collective-permute-start | bytes 98312 | tf_op jit(solution)/shard_map/ppermute | solution.py:549
  15.5 0.0 collective-permute-start.5
  15.5 2.8 %between.3 = (f32[64,1024]{1,0:T(8,128)S(1)}, f32[144,384]{1,0:T(8,128)S(1)}, f32[8,384]{1,0:T(8,128)S(1)}, f32[64,384]{1,0:T(8,128)S(1)}, f32[144,1024]{1,0:T(8...) custom-call(s32[8,1536]{1,0:T(8,128)S(1)} %get-tuple-element.91.members_ref, ...), custom_call_target="tpu_custom_call" | custom-call | flops 2000000000 | bytes 1048576 | tf_op jit(solution)/shard_map/between/pallas_call | solution.py:501
  18.3 0.1 collective-permute-done.3.rest_0_
  18.4 0.0 collective-permute-done.4.rest_1_
  18.4 0.0 collective-permute-done.5.rest_2_
  18.4 0.5 %level.4 = (f32[64,384]{1,0:T(8,128)S(1)}, f32[144,384]{1,0:T(8,128)S(1)}, f32[64,384]{1,0:T(8,128)S(1)}, f32[64,128]{1,0:T(8,128)S(1)}, f32[64,128]{1,0:T(8,128)S(1)}, /*index=5*/f32[64,128]{1,0:T(8,128)S(1)}) custom-call(f32[4,128]{1,0:T(4,128)S(1)} %get-tuple-element.89.flags_ref, s32[8,1536]{1,0:T(8,128)S(1)} %get-tuple-element.90.joined_ref, ...), custom_call_target="tpu_custom_call" | custom-call | flops 100000000 | bytes 1048576 | tf_op jit(solution)/shard_map/level/pallas_call | solution.py:501
  19.0 2.0 %collective-permute-start.6 = (f32[64,128]{1,0:T(8,128)S(1)}, f32[64,128]{1,0:T(8,128)S(1)}, u32[]{:S(2)}, u32[]{:S(2)}) collective-permute-start(f32[64,128]{1,0:T(8,128)S(1)} %get-tuple-element.124.rest_3_), channel_id=1, source_target_pairs={{0,30},{2,4},{4,2},{6,8},{8,6},{10,12},{12,10},{14,16},{16,14},{18... | collective-permute-start | bytes 98312 | tf_op jit(solution)/shard_map/ppermute | solution.py:549
  21.0 1.2 %collective-permute-start.7 = (f32[64,128]{1,0:T(8,128)S(1)}, f32[64,128]{1,0:T(8,128)S(1)}, u32[]{:S(2)}, u32[]{:S(2)}) collective-permute-start(f32[64,128]{1,0:T(8,128)S(1)} %get-tuple-element.125.rest_4_), channel_id=1, source_target_pairs={{0,1},{1,0},{2,3},{3,2},{4,5},{5,4},{6,7},{7,6},{8,9},{9,8},{10,11... | collective-permute-start | bytes 98312 | tf_op jit(solution)/shard_map/ppermute | solution.py:549
  22.2 0.0 collective-permute-start.8
  22.2 2.8 %between.4 = (f32[64,1024]{1,0:T(8,128)S(1)}, f32[144,384]{1,0:T(8,128)S(1)}, f32[8,384]{1,0:T(8,128)S(1)}, f32[64,384]{1,0:T(8,128)S(1)}, f32[144,1024]{1,0:T(8...) custom-call(s32[8,1536]{1,0:T(8,128)S(1)} %get-tuple-element.91.members_ref, ...), custom_call_target="tpu_custom_call" | custom-call | flops 2000000000 | bytes 1048576 | tf_op jit(solution)/shard_map/between/pallas_call | solution.py:501
  24.9 0.1 collective-permute-done.6.rest_0_
  25.1 0.0 collective-permute-done.7.rest_1_
  25.1 0.0 collective-permute-done.8.rest_2_
  25.1 0.7 %level.5 = (f32[64,384]{1,0:T(8,128)S(1)}, f32[144,384]{1,0:T(8,128)S(1)}, f32[64,384]{1,0:T(8,128)S(1)}, f32[64,128]{1,0:T(8,128)S(1)}, f32[64,128]{1,0:T(8,128)S(1)}, /*index=5*/f32[64,128]{1,0:T(8,128)S(1)}) custom-call(f32[4,128]{1,0:T(4,128)S(1)} %get-tuple-element.89.flags_ref, s32[8,1536]{1,0:T(8,128)S(1)} %get-tuple-element.90.joined_ref, ...), custom_call_target="tpu_custom_call" | custom-call | flops 100000000 | bytes 1048576 | tf_op jit(solution)/shard_map/level/pallas_call | solution.py:501
  25.8 2.0 %collective-permute-start.9 = (f32[64,128]{1,0:T(8,128)S(1)}, f32[64,128]{1,0:T(8,128)S(1)}, u32[]{:S(2)}, u32[]{:S(2)}) collective-permute-start(f32[64,128]{1,0:T(8,128)S(1)} %get-tuple-element.142), channel_id=1, source_target_pairs={{0,30},{2,4},{4,2},{6,8},{8,6},{10,12},{12,10},{14,16},{16,14},{18... | collective-permute-start | bytes 98312 | tf_op jit(solution)/shard_map/ppermute | solution.py:549
  27.8 1.2 %collective-permute-start.10 = (f32[64,128]{1,0:T(8,128)S(1)}, f32[64,128]{1,0:T(8,128)S(1)}, u32[]{:S(2)}, u32[]{:S(2)}) collective-permute-start(f32[64,128]{1,0:T(8,128)S(1)} %get-tuple-element.143), channel_id=1, source_target_pairs={{0,1},{1,0},{2,3},{3,2},{4,5},{5,4},{6,7},{7,6},{8,9},{9,8},{10,11... | collective-permute-start | bytes 98312 | tf_op jit(solution)/shard_map/ppermute | solution.py:549
  29.0 0.0 collective-permute-start.11
  29.0 2.5 %between.5 = (f32[144,384]{1,0:T(8,128)S(1)}, f32[8,384]{1,0:T(8,128)S(1)}, f32[144,1024]{1,0:T(8,128)S(1)}) custom-call(s32[8,1536]{1,0:T(8,128)S(1)} %get-tuple-element.91.members_ref, s32[8,1536]{1,0:T(8,128)S(1)} %get-tuple-element.90.joined_ref, s32[8,128]{1,0:T(8,128)S(1)} %get-tuple-element.92.places_ref, ...), custom_call_target="tpu_custom_call" | custom-call | flops 2000000000 | bytes 1048576 | tf_op jit(solution)/shard_map/between/pallas_call | solution.py:501
  31.5 0.4 %collective-permute-done.9.rest_0_ = f32[64,128]{1,0:T(8,128)S(1)} collective-permute-done((f32[64,128]{1,0:T(8,128)S(1)}, f32[64,128]{1,0:T(8,128)S(1)}, u32[]{:S(2)}, u32[]{:S(2)}) %collective-permute-start.9) | collective-permute-done | bytes 32800 | tf_op jit(solution)/shard_map/ppermute | solution.py:549
  31.9 0.0 collective-permute-done.10.rest_1_
  31.9 0.0 collective-permute-done.11.rest_2_
  31.9 2.5 %last.1 = f32[1120,128]{1,0:T(8,128)} custom-call(f32[4,128]{1,0:T(4,128)S(1)} %get-tuple-element.89.flags_ref, s32[8,1536]{1,0:T(8,128)S(1)} %get-tuple-element.90.joined_ref, f32[144,384]{1,0:T(8,128)S(1)} %get-tuple-element.139.local_ref, f32[8,384]{1,0:T(8,128)S(1)} %get-tuple-element.140.weights_ref, bf16[144,768]{1,0:T(8,128)(2,1)S(1)} %get-tuple-element.97.lift_ref, ...), custom_call_target="tpu_custom_call" | custom-call | flops 1000000000 | bytes 1048576 | tf_op jit(solution)/shard_map/last/pallas_call | solution.py:501
Async XLA Ops:
  1.8 9.9 %collective-permute-start = (f32[64,128]{1,0:T(8,128)S(1)}, f32[64,128]{1,0:T(8,128)S(1)}, u32[]{:S(2)}, u32[]{:S(2)}) collective-permute-start(f32[64,128]{1,0:T(8,128)S(1)} %get-tuple-element.86.refs_11_), channel_id=1, source_target_pairs={{0,30},{2,4},{4,2},{6,8},{8,6},{10,12},{12,10},{14,16},{16,14},{18... | collective-permute-start | bytes 98312 | tf_op jit(solution)/shard_map/ppermute | solution.py:549
  7.4 4.4 %collective-permute-start.1 = (f32[64,128]{1,0:T(8,128)S(1)}, f32[64,128]{1,0:T(8,128)S(1)}, u32[]{:S(2)}, u32[]{:S(2)}) collective-permute-start(f32[64,128]{1,0:T(8,128)S(1)} %get-tuple-element.87.refs_12_), channel_id=1, source_target_pairs={{0,1},{1,0},{2,3},{3,2},{4,5},{5,4},{6,7},{7,6},{8,9},{9,8},{10,11... | collective-permute-start | bytes 98312 | tf_op jit(solution)/shard_map/ppermute | solution.py:549
  8.8 2.9 %collective-permute-start.2 = (f32[64,128]{1,0:T(8,128)S(1)}, f32[64,128]{1,0:T(8,128)S(1)}, u32[]{:S(2)}, u32[]{:S(2)}) collective-permute-start(f32[64,128]{1,0:T(8,128)S(1)} %get-tuple-element.88.refs_13_), channel_id=1, source_target_pairs={{0,2},{2,0},{4,6},{6,4},{8,10},{10,8},{12,14},{14,12},{16,18},{18,... | collective-permute-start | bytes 98312 | tf_op jit(solution)/shard_map/ppermute | solution.py:549
  12.3 6.1 %collective-permute-start.3 = (f32[64,128]{1,0:T(8,128)S(1)}, f32[64,128]{1,0:T(8,128)S(1)}, u32[]{:S(2)}, u32[]{:S(2)}) collective-permute-start(f32[64,128]{1,0:T(8,128)S(1)} %get-tuple-element.111.rest_3_), channel_id=1, source_target_pairs={{0,30},{2,4},{4,2},{6,8},{8,6},{10,12},{12,10},{14,16},{16,14},{18... | collective-permute-start | bytes 98312 | tf_op jit(solution)/shard_map/ppermute | solution.py:549
  14.0 4.4 %collective-permute-start.4 = (f32[64,128]{1,0:T(8,128)S(1)}, f32[64,128]{1,0:T(8,128)S(1)}, u32[]{:S(2)}, u32[]{:S(2)}) collective-permute-start(f32[64,128]{1,0:T(8,128)S(1)} %get-tuple-element.112.rest_4_), channel_id=1, source_target_pairs={{0,1},{1,0},{2,3},{3,2},{4,5},{5,4},{6,7},{7,6},{8,9},{9,8},{10,11... | collective-permute-start | bytes 98312 | tf_op jit(solution)/shard_map/ppermute | solution.py:549
  15.5 2.9 %collective-permute-start.5 = (f32[64,128]{1,0:T(8,128)S(1)}, f32[64,128]{1,0:T(8,128)S(1)}, u32[]{:S(2)}, u32[]{:S(2)}) collective-permute-start(f32[64,128]{1,0:T(8,128)S(1)} %get-tuple-element.113.rest_5_), channel_id=1, source_target_pairs={{0,2},{2,0},{4,6},{6,4},{8,10},{10,8},{12,14},{14,12},{16,18},{18,... | collective-permute-start | bytes 98312 | tf_op jit(solution)/shard_map/ppermute | solution.py:549
  19.0 6.1 %collective-permute-start.6 = (f32[64,128]{1,0:T(8,128)S(1)}, f32[64,128]{1,0:T(8,128)S(1)}, u32[]{:S(2)}, u32[]{:S(2)}) collective-permute-start(f32[64,128]{1,0:T(8,128)S(1)} %get-tuple-element.124.rest_3_), channel_id=1, source_target_pairs={{0,30},{2,4},{4,2},{6,8},{8,6},{10,12},{12,10},{14,16},{16,14},{18... | collective-permute-start | bytes 98312 | tf_op jit(solution)/shard_map/ppermute | solution.py:549
  21.0 4.1 %collective-permute-start.7 = (f32[64,128]{1,0:T(8,128)S(1)}, f32[64,128]{1,0:T(8,128)S(1)}, u32[]{:S(2)}, u32[]{:S(2)}) collective-permute-start(f32[64,128]{1,0:T(8,128)S(1)} %get-tuple-element.125.rest_4_), channel_id=1, source_target_pairs={{0,1},{1,0},{2,3},{3,2},{4,5},{5,4},{6,7},{7,6},{8,9},{9,8},{10,11... | collective-permute-start | bytes 98312 | tf_op jit(solution)/shard_map/ppermute | solution.py:549
  22.2 2.9 %collective-permute-start.8 = (f32[64,128]{1,0:T(8,128)S(1)}, f32[64,128]{1,0:T(8,128)S(1)}, u32[]{:S(2)}, u32[]{:S(2)}) collective-permute-start(f32[64,128]{1,0:T(8,128)S(1)} %get-tuple-element.126.rest_5_), channel_id=1, source_target_pairs={{0,2},{2,0},{4,6},{6,4},{8,10},{10,8},{12,14},{14,12},{16,18},{18,... | collective-permute-start | bytes 98312 | tf_op jit(solution)/shard_map/ppermute | solution.py:549
  25.8 6.1 %collective-permute-start.9 = (f32[64,128]{1,0:T(8,128)S(1)}, f32[64,128]{1,0:T(8,128)S(1)}, u32[]{:S(2)}, u32[]{:S(2)}) collective-permute-start(f32[64,128]{1,0:T(8,128)S(1)} %get-tuple-element.142), channel_id=1, source_target_pairs={{0,30},{2,4},{4,2},{6,8},{8,6},{10,12},{12,10},{14,16},{16,14},{18... | collective-permute-start | bytes 98312 | tf_op jit(solution)/shard_map/ppermute | solution.py:549
  27.8 4.1 %collective-permute-start.10 = (f32[64,128]{1,0:T(8,128)S(1)}, f32[64,128]{1,0:T(8,128)S(1)}, u32[]{:S(2)}, u32[]{:S(2)}) collective-permute-start(f32[64,128]{1,0:T(8,128)S(1)} %get-tuple-element.143), channel_id=1, source_target_pairs={{0,1},{1,0},{2,3},{3,2},{4,5},{5,4},{6,7},{7,6},{8,9},{9,8},{10,11... | collective-permute-start | bytes 98312 | tf_op jit(solution)/shard_map/ppermute | solution.py:549
  29.0 2.9 %collective-permute-start.11 = (f32[64,128]{1,0:T(8,128)S(1)}, f32[64,128]{1,0:T(8,128)S(1)}, u32[]{:S(2)}, u32[]{:S(2)}) collective-permute-start(f32[64,128]{1,0:T(8,128)S(1)} %get-tuple-element.144), channel_id=1, source_target_pairs={{0,2},{2,0},{4,6},{6,4},{8,10},{10,8},{12,14},{14,12},{16,18},{18,... | collective-permute-start | bytes 98312 | tf_op jit(solution)/shard_map/ppermute | solution.py:549

commit v7 on v6

--- a/solution.py
+++ b/solution.py
@@ -146,11 +146,13 @@
         pltpu.make_async_copy(source, target, arrived.at[i])
         for i, (source, target) in enumerate(zip([fields_hbm] + given, [fields_ref] + held))
     ]
-    for copy in copies:
-        copy.start()
     needed = 3
     for copy in copies[:needed]:
+        copy.start()
+    for copy in copies[:needed]:
         copy.wait()
+    for copy in copies[needed:]:
+        copy.start()
     trace_ref, send_ref = held[:2]
     rows = out_ref.shape[0]
     elements = out_ref.shape[1]
@@ -217,7 +219,7 @@
     rows = loaded.shape[0]
     matrix = jnp.concatenate(
         [grow_ref[power * rows + chunk.start:power * rows + chunk.stop, :] for power in range(POWERS)], axis=0)
-    return summed_powers(product(matrix, stacked), weights_ref, ROW_CHUNK, loaded[chunk])
+    return summed_powers(product(matrix, stacked), weights_ref, chunk.stop - chunk.start, loaded[chunk])
 
 
 def matrix_powers(operator_ref, trace_ref, lift_ref, grow_ref, trace_grow_ref, mix_ref, lift_out_ref,
@@ -361,16 +363,6 @@
     return jnp.max(flags_ref[level:level + 1, :]) > 0.0
 
 
-def add_received(level, received, joined_ref, count, flags_ref, local_ref, lift_ref, lift_first_ref, loaded_ref):
-    first = received_traces(level, 0, received, joined_ref, count)
-    loaded_ref[...] = local_ref[...] + product(lift_first_ref[...], stacked_columns(first))
-
-    @pl.when(any_other(level, flags_ref))
-    def _():
-        others = other_traces(level, received, joined_ref, count)
-        loaded_ref[...] = loaded_ref[...] + product(lift_ref[...], stacked_columns(others))
-
-
 def between_kernel(level, messages, members_ref, joined_ref, places_ref, columns_ref, old_out_ref, old_trace_ref,
                    moved_ref, extra_ref, extra_trace_ref, heights_ref, local_ref, old_weights_ref, lift_ref,
                    lift_first_ref, grow_ref, trace_grow_ref, send_places_ref, *rest):
@@ -471,26 +463,46 @@
                 ref_blocks(extra_trace_ref, pieces), place, (place >> 7) - level * pieces, jnp.zeros(send.shape, f32))
 
 
+def last_chunks(rows):
+    units = rows // 16
+    first = -(-units * 4 // 9)
+    second = -(-(units - first) * 3 // 5)
+    bounds = [0, first * 16, (first + second) * 16, rows]
+    return [slice(low, high) for low, high in zip(bounds, bounds[1:]) if high > low]
+
+
 def last_kernel(level, messages, flags_ref, joined_ref, local_ref, weights_ref, lift_ref, lift_first_ref, grow_ref,
                 places_ref, advanced_ref, *rest):
-    received, (final_hbm, final_ref, whole_ref, sent) = rest[:messages], rest[messages:]
+    received, (final_hbm, final_ref, sent) = rest[:messages], rest[messages:]
     count = places_ref.shape[0]
     comp = final_ref.shape[0] // count
-    add_received(level, received, joined_ref, count, flags_ref, local_ref, lift_ref, lift_first_ref, whole_ref)
-    whole = whole_ref[...]
-    stacked = stacked_columns(whole)
-    copies = []
-    for number, chunk in enumerate(row_chunks(whole.shape[0])):
-        new = grown_rows(chunk, stacked, whole, grow_ref, weights_ref)
-        height = min(chunk.stop, comp) - chunk.start
-        for block in range(count):
-            done = settle(level, value_blocks(new), places_ref, advanced_ref[chunk, block_at(block)], block)
-            final_ref[pl.ds(chunk.start * count + block, height, stride=count), :] = done[:height]
-        part = pl.ds(chunk.start * count, height * count)
-        copies.append(pltpu.make_async_copy(final_ref.at[part], final_hbm.at[part], sent.at[number]))
-        copies[-1].start()
-    for copy in copies:
-        copy.wait()
+
+    def finish(whole):
+        stacked = stacked_columns(whole)
+        copies = []
+        for number, chunk in enumerate(last_chunks(whole.shape[0])):
+            new = grown_rows(chunk, stacked, whole, grow_ref, weights_ref)
+            height = min(chunk.stop, comp) - chunk.start
+            for block in range(count):
+                done = settle(level, value_blocks(new), places_ref, advanced_ref[chunk, block_at(block)], block)
+                final_ref[pl.ds(chunk.start * count + block, height, stride=count), :] = done[:height]
+            part = pl.ds(chunk.start * count, height * count)
+            copies.append(pltpu.make_async_copy(final_ref.at[part], final_hbm.at[part], sent.at[number]))
+            copies[-1].start()
+        for copy in copies:
+            copy.wait()
+
+    def whole_of(others):
+        first = received_traces(level, 0, received, joined_ref, count)
+        whole = local_ref[...] + product(lift_first_ref[...], stacked_columns(first))
+        return whole if others is None else whole + product(lift_ref[...], stacked_columns(others))
+
+    other = any_other(level, flags_ref)
+    finish(whole_of(None))
+
+    @pl.when(other)
+    def _():
+        finish(whole_of(other_traces(level, received, joined_ref, count)))
 
 
 def call(kernel, name, flops, operands, outs, scratch=(), hbm=False, out_hbm=False):
@@ -593,7 +605,7 @@
     final, = call(
         functools.partial(last_kernel, LEVELS - 1, messages), "last", 10 ** 9,
         [flags, joined, loaded, weights, lift, lift_first, grow, places] + advanced + received,
-        [(flat, f32)], [(flat, f32), own, pltpu.SemaphoreType.DMA((-(-rows // ROW_CHUNK),))], out_hbm=True)
+        [(flat, f32)], [(flat, f32), pltpu.SemaphoreType.DMA((len(last_chunks(rows)),))], out_hbm=True)
     return final.reshape(1, 1, comp, elements)
 
 

time: 34.7 us -> 35.4 us (1.020)
  Pallas kernels: 17.1 us -> 17.7 us
    pallas_call x9, Pallas kernels: 17.1 us -> 17.7 us  [call(): pl.pallas_call(kernel, out_shape=tuple((jax.ShapeDtypeStruct(shape, dtype...]
  transfers between devices with their start and end apart: 12 -> 12, of which waited for: 3 -> 3; matrix products, arithmetic and copies ran while one was open for 0% -> 0% of each run, Pallas kernels for 32% -> 31%
where the time goes in v7:
time: 35.4 us; the launch traced here: 35.2 us
  Pallas kernels  17.7 us (50%)
  starting transfers between devices  16.5 us (47%)
  waiting for transfers between devices  0.69 us (2%)
    pallas_call x9, Pallas kernels, call(): pl.pallas_call(kernel, out_shape=tuple((jax.ShapeDtypeStruct(shape, dtype...  17.7 us
    ppermute x12, starting transfers between devices, exchange(): lax.ppermute(one, swap[0], swap[1])  16.5 us
  transfers between devices with their start and end apart: 12, of which 3 were waited for; matrix products, arithmetic and copies ran while one was open for 0% of the time, Pallas kernels for 31%

profile of v7, /device:TPU:0, one launch (start us, length us, event | category | flops | bytes accessed | tf_op | source)
XLA Modules:
  0.0 35.2 jit_solution(17638352037327643825)
XLA Ops:
  0.0 2.4 %first.1 = (f32[144,1024]{1,0:T(8,128)S(1)}, f32[64,1024]{1,0:T(8,128)S(1)}, f32[64,128]{1,0:T(8,128)S(1)}, f32[64,128]{1,0:T(8,128)S(1)}, f32[64,128]{1,0:T(8,1...) custom-call(f32[1120,128]{1,0:T(8,128)} %bitcast.9, ...), custom_call_target="tpu_custom_call" | custom-call | flops 100000000 | bytes 1048576 | tf_op jit(solution)/shard_map/first/pallas_call | solution.py:513
  2.4 5.5 %collective-permute-start = (f32[64,128]{1,0:T(8,128)S(1)}, f32[64,128]{1,0:T(8,128)S(1)}, u32[]{:S(2)}, u32[]{:S(2)}) collective-permute-start(f32[64,128]{1,0:T(8,128)S(1)} %get-tuple-element.86.refs_11_), channel_id=1, source_target_pairs={{0,30},{2,4},{4,2},{6,8},{8,6},{10,12},{12,10},{14,16},{16,14},{18... | collective-permute-start | bytes 98312 | tf_op jit(solution)/shard_map/ppermute | solution.py:561
  8.0 1.5 %collective-permute-start.1 = (f32[64,128]{1,0:T(8,128)S(1)}, f32[64,128]{1,0:T(8,128)S(1)}, u32[]{:S(2)}, u32[]{:S(2)}) collective-permute-start(f32[64,128]{1,0:T(8,128)S(1)} %get-tuple-element.87.refs_12_), channel_id=1, source_target_pairs={{0,1},{1,0},{2,3},{3,2},{4,5},{5,4},{6,7},{7,6},{8,9},{9,8},{10,11... | collective-permute-start | bytes 98312 | tf_op jit(solution)/shard_map/ppermute | solution.py:561
  9.4 0.0 collective-permute-start.2
  9.5 2.9 %plan.1 = (s32[8,1536]{1,0:T(8,128)S(1)}, s32[8,1536]{1,0:T(8,128)S(1)}, s32[8,128]{1,0:T(8,128)S(1)}, s32[8,128]{1,0:T(8,128)S(1)}, s32[8,128]{1,0:T(8,128)S(1)...) custom-call(f32[60,140]{1,0:T(8,128)S(1)} %get-tuple-element.75.refs, ...), custom_call_target="tpu_custom_call" | custom-call | flops 2000000000 | bytes 1048576 | tf_op jit(solution)/shard_map/plan/pallas_call | solution.py:513
  12.3 0.0 collective-permute-done.rest_0_
  12.4 0.0 collective-permute-done.1.rest_1_
  12.4 0.0 collective-permute-done.2.rest_2_
  12.4 0.5 %level.3 = (f32[64,384]{1,0:T(8,128)S(1)}, f32[144,384]{1,0:T(8,128)S(1)}, f32[64,384]{1,0:T(8,128)S(1)}, f32[64,128]{1,0:T(8,128)S(1)}, f32[64,128]{1,0:T(8,128)S(1)}, /*index=5*/f32[64,128]{1,0:T(8,128)S(1)}) custom-call(f32[4,128]{1,0:T(4,128)S(1)} %get-tuple-element.89.flags_ref, s32[8,1536]{1,0:T(8,128)S(1)} %get-tuple-element.90.joined_ref, ...), custom_call_target="tpu_custom_call" | custom-call | flops 100000000 | bytes 1048576 | tf_op jit(solution)/shard_map/level/pallas_call | solution.py:513
  12.9 1.7 %collective-permute-start.3 = (f32[64,128]{1,0:T(8,128)S(1)}, f32[64,128]{1,0:T(8,128)S(1)}, u32[]{:S(2)}, u32[]{:S(2)}) collective-permute-start(f32[64,128]{1,0:T(8,128)S(1)} %get-tuple-element.111.rest_3_), channel_id=1, source_target_pairs={{0,30},{2,4},{4,2},{6,8},{8,6},{10,12},{12,10},{14,16},{16,14},{18... | collective-permute-start | bytes 98312 | tf_op jit(solution)/shard_map/ppermute | solution.py:561
  14.6 1.5 %collective-permute-start.4 = (f32[64,128]{1,0:T(8,128)S(1)}, f32[64,128]{1,0:T(8,128)S(1)}, u32[]{:S(2)}, u32[]{:S(2)}) collective-permute-start(f32[64,128]{1,0:T(8,128)S(1)} %get-tuple-element.112.rest_4_), channel_id=1, source_target_pairs={{0,1},{1,0},{2,3},{3,2},{4,5},{5,4},{6,7},{7,6},{8,9},{9,8},{10,11... | collective-permute-start | bytes 98312 | tf_op jit(solution)/shard_map/ppermute | solution.py:561
  16.1 0.0 collective-permute-start.5
  16.1 2.8 %between.3 = (f32[64,1024]{1,0:T(8,128)S(1)}, f32[144,384]{1,0:T(8,128)S(1)}, f32[8,384]{1,0:T(8,128)S(1)}, f32[64,384]{1,0:T(8,128)S(1)}, f32[144,1024]{1,0:T(8...) custom-call(s32[8,1536]{1,0:T(8,128)S(1)} %get-tuple-element.91.members_ref, ...), custom_call_target="tpu_custom_call" | custom-call | flops 2000000000 | bytes 1048576 | tf_op jit(solution)/shard_map/between/pallas_call | solution.py:513
  18.9 0.1 collective-permute-done.3.rest_0_
  19.0 0.0 collective-permute-done.4.rest_1_
  19.0 0.0 collective-permute-done.5.rest_2_
  19.0 0.5 %level.4 = (f32[64,384]{1,0:T(8,128)S(1)}, f32[144,384]{1,0:T(8,128)S(1)}, f32[64,384]{1,0:T(8,128)S(1)}, f32[64,128]{1,0:T(8,128)S(1)}, f32[64,128]{1,0:T(8,128)S(1)}, /*index=5*/f32[64,128]{1,0:T(8,128)S(1)}) custom-call(f32[4,128]{1,0:T(4,128)S(1)} %get-tuple-element.89.flags_ref, s32[8,1536]{1,0:T(8,128)S(1)} %get-tuple-element.90.joined_ref, ...), custom_call_target="tpu_custom_call" | custom-call | flops 100000000 | bytes 1048576 | tf_op jit(solution)/shard_map/level/pallas_call | solution.py:513
  19.6 2.0 %collective-permute-start.6 = (f32[64,128]{1,0:T(8,128)S(1)}, f32[64,128]{1,0:T(8,128)S(1)}, u32[]{:S(2)}, u32[]{:S(2)}) collective-permute-start(f32[64,128]{1,0:T(8,128)S(1)} %get-tuple-element.124.rest_3_), channel_id=1, source_target_pairs={{0,30},{2,4},{4,2},{6,8},{8,6},{10,12},{12,10},{14,16},{16,14},{18... | collective-permute-start | bytes 98312 | tf_op jit(solution)/shard_map/ppermute | solution.py:561
  21.6 1.2 %collective-permute-start.7 = (f32[64,128]{1,0:T(8,128)S(1)}, f32[64,128]{1,0:T(8,128)S(1)}, u32[]{:S(2)}, u32[]{:S(2)}) collective-permute-start(f32[64,128]{1,0:T(8,128)S(1)} %get-tuple-element.125.rest_4_), channel_id=1, source_target_pairs={{0,1},{1,0},{2,3},{3,2},{4,5},{5,4},{6,7},{7,6},{8,9},{9,8},{10,11... | collective-permute-start | bytes 98312 | tf_op jit(solution)/shard_map/ppermute | solution.py:561
  22.8 0.0 collective-permute-start.8
  22.8 2.8 %between.4 = (f32[64,1024]{1,0:T(8,128)S(1)}, f32[144,384]{1,0:T(8,128)S(1)}, f32[8,384]{1,0:T(8,128)S(1)}, f32[64,384]{1,0:T(8,128)S(1)}, f32[144,1024]{1,0:T(8...) custom-call(s32[8,1536]{1,0:T(8,128)S(1)} %get-tuple-element.91.members_ref, ...), custom_call_target="tpu_custom_call" | custom-call | flops 2000000000 | bytes 1048576 | tf_op jit(solution)/shard_map/between/pallas_call | solution.py:513
  25.5 0.1 collective-permute-done.6.rest_0_
  25.7 0.0 collective-permute-done.7.rest_1_
  25.7 0.0 collective-permute-done.8.rest_2_
  25.7 0.7 %level.5 = (f32[64,384]{1,0:T(8,128)S(1)}, f32[144,384]{1,0:T(8,128)S(1)}, f32[64,384]{1,0:T(8,128)S(1)}, f32[64,128]{1,0:T(8,128)S(1)}, f32[64,128]{1,0:T(8,128)S(1)}, /*index=5*/f32[64,128]{1,0:T(8,128)S(1)}) custom-call(f32[4,128]{1,0:T(4,128)S(1)} %get-tuple-element.89.flags_ref, s32[8,1536]{1,0:T(8,128)S(1)} %get-tuple-element.90.joined_ref, ...), custom_call_target="tpu_custom_call" | custom-call | flops 100000000 | bytes 1048576 | tf_op jit(solution)/shard_map/level/pallas_call | solution.py:513
  26.4 2.0 %collective-permute-start.9 = (f32[64,128]{1,0:T(8,128)S(1)}, f32[64,128]{1,0:T(8,128)S(1)}, u32[]{:S(2)}, u32[]{:S(2)}) collective-permute-start(f32[64,128]{1,0:T(8,128)S(1)} %get-tuple-element.142), channel_id=1, source_target_pairs={{0,30},{2,4},{4,2},{6,8},{8,6},{10,12},{12,10},{14,16},{16,14},{18... | collective-permute-start | bytes 98312 | tf_op jit(solution)/shard_map/ppermute | solution.py:561
  28.4 1.2 %collective-permute-start.10 = (f32[64,128]{1,0:T(8,128)S(1)}, f32[64,128]{1,0:T(8,128)S(1)}, u32[]{:S(2)}, u32[]{:S(2)}) collective-permute-start(f32[64,128]{1,0:T(8,128)S(1)} %get-tuple-element.143), channel_id=1, source_target_pairs={{0,1},{1,0},{2,3},{3,2},{4,5},{5,4},{6,7},{7,6},{8,9},{9,8},{10,11... | collective-permute-start | bytes 98312 | tf_op jit(solution)/shard_map/ppermute | solution.py:561
  29.6 0.0 collective-permute-start.11
  29.6 2.5 %between.5 = (f32[144,384]{1,0:T(8,128)S(1)}, f32[8,384]{1,0:T(8,128)S(1)}, f32[144,1024]{1,0:T(8,128)S(1)}) custom-call(s32[8,1536]{1,0:T(8,128)S(1)} %get-tuple-element.91.members_ref, s32[8,1536]{1,0:T(8,128)S(1)} %get-tuple-element.90.joined_ref, s32[8,128]{1,0:T(8,128)S(1)} %get-tuple-element.92.places_ref, ...), custom_call_target="tpu_custom_call" | custom-call | flops 2000000000 | bytes 1048576 | tf_op jit(solution)/shard_map/between/pallas_call | solution.py:513
  32.1 0.4 %collective-permute-done.9.rest_0_ = f32[64,128]{1,0:T(8,128)S(1)} collective-permute-done((f32[64,128]{1,0:T(8,128)S(1)}, f32[64,128]{1,0:T(8,128)S(1)}, u32[]{:S(2)}, u32[]{:S(2)}) %collective-permute-start.9) | collective-permute-done | bytes 32800 | tf_op jit(solution)/shard_map/ppermute | solution.py:561
  32.5 0.0 collective-permute-done.10.rest_1_
  32.5 0.0 collective-permute-done.11.rest_2_
  32.5 2.5 %last.1 = f32[1120,128]{1,0:T(8,128)} custom-call(f32[4,128]{1,0:T(4,128)S(1)} %get-tuple-element.89.flags_ref, s32[8,1536]{1,0:T(8,128)S(1)} %get-tuple-element.90.joined_ref, f32[144,384]{1,0:T(8,128)S(1)} %get-tuple-element.139.local_ref, f32[8,384]{1,0:T(8,128)S(1)} %get-tuple-element.140.weights_ref, bf16[144,768]{1,0:T(8,128)(2,1)S(1)} %get-tuple-element.97.lift_ref, ...), custom_call_target="tpu_custom_call" | custom-call | flops 1000000000 | bytes 1048576 | tf_op jit(solution)/shard_map/last/pallas_call | solution.py:513
Async XLA Ops:
  2.4 9.9 %collective-permute-start = (f32[64,128]{1,0:T(8,128)S(1)}, f32[64,128]{1,0:T(8,128)S(1)}, u32[]{:S(2)}, u32[]{:S(2)}) collective-permute-start(f32[64,128]{1,0:T(8,128)S(1)} %get-tuple-element.86.refs_11_), channel_id=1, source_target_pairs={{0,30},{2,4},{4,2},{6,8},{8,6},{10,12},{12,10},{14,16},{16,14},{18... | collective-permute-start | bytes 98312 | tf_op jit(solution)/shard_map/ppermute | solution.py:561
  8.0 4.4 %collective-permute-start.1 = (f32[64,128]{1,0:T(8,128)S(1)}, f32[64,128]{1,0:T(8,128)S(1)}, u32[]{:S(2)}, u32[]{:S(2)}) collective-permute-start(f32[64,128]{1,0:T(8,128)S(1)} %get-tuple-element.87.refs_12_), channel_id=1, source_target_pairs={{0,1},{1,0},{2,3},{3,2},{4,5},{5,4},{6,7},{7,6},{8,9},{9,8},{10,11... | collective-permute-start | bytes 98312 | tf_op jit(solution)/shard_map/ppermute | solution.py:561
  9.4 2.9 %collective-permute-start.2 = (f32[64,128]{1,0:T(8,128)S(1)}, f32[64,128]{1,0:T(8,128)S(1)}, u32[]{:S(2)}, u32[]{:S(2)}) collective-permute-start(f32[64,128]{1,0:T(8,128)S(1)} %get-tuple-element.88.refs_13_), channel_id=1, source_target_pairs={{0,2},{2,0},{4,6},{6,4},{8,10},{10,8},{12,14},{14,12},{16,18},{18,... | collective-permute-start | bytes 98312 | tf_op jit(solution)/shard_map/ppermute | solution.py:561
  12.9 6.1 %collective-permute-start.3 = (f32[64,128]{1,0:T(8,128)S(1)}, f32[64,128]{1,0:T(8,128)S(1)}, u32[]{:S(2)}, u32[]{:S(2)}) collective-permute-start(f32[64,128]{1,0:T(8,128)S(1)} %get-tuple-element.111.rest_3_), channel_id=1, source_target_pairs={{0,30},{2,4},{4,2},{6,8},{8,6},{10,12},{12,10},{14,16},{16,14},{18... | collective-permute-start | bytes 98312 | tf_op jit(solution)/shard_map/ppermute | solution.py:561
  14.6 4.4 %collective-permute-start.4 = (f32[64,128]{1,0:T(8,128)S(1)}, f32[64,128]{1,0:T(8,128)S(1)}, u32[]{:S(2)}, u32[]{:S(2)}) collective-permute-start(f32[64,128]{1,0:T(8,128)S(1)} %get-tuple-element.112.rest_4_), channel_id=1, source_target_pairs={{0,1},{1,0},{2,3},{3,2},{4,5},{5,4},{6,7},{7,6},{8,9},{9,8},{10,11... | collective-permute-start | bytes 98312 | tf_op jit(solution)/shard_map/ppermute | solution.py:561
  16.1 2.9 %collective-permute-start.5 = (f32[64,128]{1,0:T(8,128)S(1)}, f32[64,128]{1,0:T(8,128)S(1)}, u32[]{:S(2)}, u32[]{:S(2)}) collective-permute-start(f32[64,128]{1,0:T(8,128)S(1)} %get-tuple-element.113.rest_5_), channel_id=1, source_target_pairs={{0,2},{2,0},{4,6},{6,4},{8,10},{10,8},{12,14},{14,12},{16,18},{18,... | collective-permute-start | bytes 98312 | tf_op jit(solution)/shard_map/ppermute | solution.py:561
  19.6 6.1 %collective-permute-start.6 = (f32[64,128]{1,0:T(8,128)S(1)}, f32[64,128]{1,0:T(8,128)S(1)}, u32[]{:S(2)}, u32[]{:S(2)}) collective-permute-start(f32[64,128]{1,0:T(8,128)S(1)} %get-tuple-element.124.rest_3_), channel_id=1, source_target_pairs={{0,30},{2,4},{4,2},{6,8},{8,6},{10,12},{12,10},{14,16},{16,14},{18... | collective-permute-start | bytes 98312 | tf_op jit(solution)/shard_map/ppermute | solution.py:561
  21.6 4.1 %collective-permute-start.7 = (f32[64,128]{1,0:T(8,128)S(1)}, f32[64,128]{1,0:T(8,128)S(1)}, u32[]{:S(2)}, u32[]{:S(2)}) collective-permute-start(f32[64,128]{1,0:T(8,128)S(1)} %get-tuple-element.125.rest_4_), channel_id=1, source_target_pairs={{0,1},{1,0},{2,3},{3,2},{4,5},{5,4},{6,7},{7,6},{8,9},{9,8},{10,11... | collective-permute-start | bytes 98312 | tf_op jit(solution)/shard_map/ppermute | solution.py:561
  22.8 2.9 %collective-permute-start.8 = (f32[64,128]{1,0:T(8,128)S(1)}, f32[64,128]{1,0:T(8,128)S(1)}, u32[]{:S(2)}, u32[]{:S(2)}) collective-permute-start(f32[64,128]{1,0:T(8,128)S(1)} %get-tuple-element.126.rest_5_), channel_id=1, source_target_pairs={{0,2},{2,0},{4,6},{6,4},{8,10},{10,8},{12,14},{14,12},{16,18},{18,... | collective-permute-start | bytes 98312 | tf_op jit(solution)/shard_map/ppermute | solution.py:561
  26.4 6.1 %collective-permute-start.9 = (f32[64,128]{1,0:T(8,128)S(1)}, f32[64,128]{1,0:T(8,128)S(1)}, u32[]{:S(2)}, u32[]{:S(2)}) collective-permute-start(f32[64,128]{1,0:T(8,128)S(1)} %get-tuple-element.142), channel_id=1, source_target_pairs={{0,30},{2,4},{4,2},{6,8},{8,6},{10,12},{12,10},{14,16},{16,14},{18... | collective-permute-start | bytes 98312 | tf_op jit(solution)/shard_map/ppermute | solution.py:561
  28.4 4.1 %collective-permute-start.10 = (f32[64,128]{1,0:T(8,128)S(1)}, f32[64,128]{1,0:T(8,128)S(1)}, u32[]{:S(2)}, u32[]{:S(2)}) collective-permute-start(f32[64,128]{1,0:T(8,128)S(1)} %get-tuple-element.143), channel_id=1, source_target_pairs={{0,1},{1,0},{2,3},{3,2},{4,5},{5,4},{6,7},{7,6},{8,9},{9,8},{10,11... | collective-permute-start | bytes 98312 | tf_op jit(solution)/shard_map/ppermute | solution.py:561
  29.6 2.9 %collective-permute-start.11 = (f32[64,128]{1,0:T(8,128)S(1)}, f32[64,128]{1,0:T(8,128)S(1)}, u32[]{:S(2)}, u32[]{:S(2)}) collective-permute-start(f32[64,128]{1,0:T(8,128)S(1)} %get-tuple-element.144), channel_id=1, source_target_pairs={{0,2},{2,0},{4,6},{6,4},{8,10},{10,8},{12,14},{14,12},{16,18},{18,... | collective-permute-start | bytes 98312 | tf_op jit(solution)/shard_map/ppermute | solution.py:561

commit v8 on v7

--- a/solution.py
+++ b/solution.py
@@ -142,33 +142,43 @@
     (columns_ref, out_ref), refs = refs[:2], refs[2:]
     sends, refs = refs[:len(swaps)], refs[len(swaps):]
     *held, fields_ref, arrived = refs
-    copies = [
-        pltpu.make_async_copy(source, target, arrived.at[i])
-        for i, (source, target) in enumerate(zip([fields_hbm] + given, [fields_ref] + held))
-    ]
-    needed = 3
-    for copy in copies[:needed]:
-        copy.start()
-    for copy in copies[:needed]:
-        copy.wait()
-    for copy in copies[needed:]:
-        copy.start()
-    trace_ref, send_ref = held[:2]
     rows = out_ref.shape[0]
     elements = out_ref.shape[1]
     count = elements // LANES
     comp = fields_ref.shape[0] // count
-    trace = pad_rows(trace_ref[...], rows)
-    trace_high, trace_low = split(trace)
-    both = jnp.concatenate([trace_high, trace_low], axis=0)
-    fields = jnp.concatenate([fields_ref[pl.ds(b, comp, stride=count), :] for b in range(count)], axis=1)
-    high, low = split(fields)
-    upper = product(both, high)
-    out_ref[...] = upper[:rows] + upper[rows:] + product(trace_high, low)
+    cuts = [slice(0, rounded_up(comp // 2, 16)), slice(rounded_up(comp // 2, 16), comp)]
+    parts = [pl.ds(cut.start * count, (cut.stop - cut.start) * count) for cut in cuts]
+    trace_hbm, send_hbm, *others = given
+    trace_ref, send_ref, *others_held = held
+    pairs = [(fields_hbm.at[parts[0]], fields_ref.at[parts[0]]), (trace_hbm, trace_ref),
+             (fields_hbm.at[parts[1]], fields_ref.at[parts[1]]), (send_hbm, send_ref)]
+    pairs += list(zip(others, others_held))
+    copies = [pltpu.make_async_copy(source, target, arrived.at[i]) for i, (source, target) in enumerate(pairs)]
+    for copy in copies:
+        copy.start()
+    total = None
+    for number, cut in enumerate(cuts):
+        if number == 0:
+            copies[0].wait()
+            copies[1].wait()
+            trace = pad_rows(trace_ref[...], rows)
+        else:
+            copies[2].wait()
+        height = cut.stop - cut.start
+        fields = jnp.concatenate(
+            [fields_ref[pl.ds(cut.start * count + b, height, stride=count), :] for b in range(count)], axis=1)
+        trace_high, trace_low = split(trace[:, cut])
+        high, low = split(fields)
+        upper = product(jnp.concatenate([trace_high, trace_low], axis=0), high)
+        part = upper[:rows] + upper[rows:] + product(trace_high, low)
+        total = part if total is None else total + part
+        columns_ref[cut, :] = fields
+    out_ref[...] = total
+    copies[3].wait()
     for index, send in zip(sent_rows(send_ref, swaps), sends):
         send[...] = pick(ref_blocks(out_ref, count), index, index >> 7)
-    columns_ref[...] = pad_rows(fields, columns_ref.shape[0])
-    for copy in copies[needed:]:
+    columns_ref[comp:, :] = jnp.zeros((columns_ref.shape[0] - comp, elements), f32)
+    for copy in copies[4:]:
         copy.wait()
 
 
@@ -439,6 +449,7 @@
     moved_ref, extra_ref, extra_trace_ref, sends = rest[0], rest[1], rest[2], rest[3:]
     rows = moved_ref.shape[0]
     pieces = BLOCK // LANES
+    other = any_other(level, flags_ref)
     arrived = jnp.concatenate([ref[...] for ref in received], axis=1)
     stacked = product(mix_ref[...], stacked_columns(arrived))
     moved_ref[...] = summed_powers(stacked[rows:], slot_weights_ref, rows, stacked[:rows])
@@ -451,7 +462,7 @@
         send[...] = before[...] + pick(
             moved, code, jnp.where(here, code >> 7, 0), jnp.zeros(before.shape, f32))
 
-    @pl.when(any_other(level, flags_ref))
+    @pl.when(other)
     def _():
         others = other_traces(level, received, joined_ref, count)
         extra = product(lift_ref[...], stacked_columns(others))
@@ -480,8 +491,8 @@
     def finish(whole):
         stacked = stacked_columns(whole)
         copies = []
-        for number, chunk in enumerate(last_chunks(whole.shape[0])):
-            new = grown_rows(chunk, stacked, whole, grow_ref, weights_ref)
+
+        def put(number, chunk, new):
             height = min(chunk.stop, comp) - chunk.start
             for block in range(count):
                 done = settle(level, value_blocks(new), places_ref, advanced_ref[chunk, block_at(block)], block)
@@ -489,6 +500,14 @@
             part = pl.ds(chunk.start * count, height * count)
             copies.append(pltpu.make_async_copy(final_ref.at[part], final_hbm.at[part], sent.at[number]))
             copies[-1].start()
+
+        ahead = None
+        for number, chunk in enumerate(last_chunks(whole.shape[0])):
+            new = grown_rows(chunk, stacked, whole, grow_ref, weights_ref)
+            if ahead is not None:
+                put(*ahead)
+            ahead = (number, chunk, new)
+        put(*ahead)
         for copy in copies:
             copy.wait()
 
@@ -571,7 +590,7 @@
     columns, out, *rest = call(
         functools.partial(first_kernel, swaps), "first", 10 ** 8, [fields.reshape(flat)] + arguments,
         [whole, table] + [message] * messages + [(one.shape, one.dtype) for one in arguments],
-        [(flat, f32), pltpu.SemaphoreType.DMA((ARGUMENTS,))], hbm=True)
+        [(flat, f32), pltpu.SemaphoreType.DMA((ARGUMENTS + 1,))], hbm=True)
     sent, held = rest[:messages], rest[messages:]
     received = exchange(sent)
     slots = ((trace_rows, messages * LANES), f32)

time: 35.4 us -> 34.7 us (0.980)
  Pallas kernels: 17.7 us -> 17.1 us
    pallas_call x9, Pallas kernels: 17.7 us -> 17.1 us  [call(): pl.pallas_call(kernel, out_shape=tuple((jax.ShapeDtypeStruct(shape, dtype...]
  transfers between devices with their start and end apart: 12 -> 12, of which waited for: 3 -> 3; matrix products, arithmetic and copies ran while one was open for 0% -> 0% of each run, Pallas kernels for 31% -> 32%
where the time goes in v8:
time: 34.7 us; the launch traced here: 34.6 us
  Pallas kernels  17.1 us (49%)
  starting transfers between devices  16.5 us (48%)
  waiting for transfers between devices  0.71 us (2%)
    pallas_call x9, Pallas kernels, call(): pl.pallas_call(kernel, out_shape=tuple((jax.ShapeDtypeStruct(shape, dtype...  17.1 us
    ppermute x12, starting transfers between devices, exchange(): lax.ppermute(one, swap[0], swap[1])  16.5 us
    ppermute x12, waiting for transfers between devices, exchange(): lax.ppermute(one, swap[0], swap[1])  0.71 us
  transfers between devices with their start and end apart: 12, of which 3 were waited for; matrix products, arithmetic and copies ran while one was open for 0% of the time, Pallas kernels for 32%

profile of v8, /device:TPU:0, one launch (start us, length us, event | category | flops | bytes accessed | tf_op | source)
XLA Modules:
  0.0 34.6 jit_solution(7004711523399516916)
XLA Ops:
  0.0 1.9 %first.1 = (f32[144,1024]{1,0:T(8,128)S(1)}, f32[64,1024]{1,0:T(8,128)S(1)}, f32[64,128]{1,0:T(8,128)S(1)}, f32[64,128]{1,0:T(8,128)S(1)}, f32[64,128]{1,0:T(8,1...) custom-call(f32[1120,128]{1,0:T(8,128)} %bitcast.9, ...), custom_call_target="tpu_custom_call" | custom-call | flops 100000000 | bytes 1048576 | tf_op jit(solution)/shard_map/first/pallas_call | solution.py:532
  1.9 5.5 %collective-permute-start = (f32[64,128]{1,0:T(8,128)S(1)}, f32[64,128]{1,0:T(8,128)S(1)}, u32[]{:S(2)}, u32[]{:S(2)}) collective-permute-start(f32[64,128]{1,0:T(8,128)S(1)} %get-tuple-element.86.refs_11_), channel_id=1, source_target_pairs={{0,30},{2,4},{4,2},{6,8},{8,6},{10,12},{12,10},{14,16},{16,14},{18... | collective-permute-start | bytes 98312 | tf_op jit(solution)/shard_map/ppermute | solution.py:580
  7.4 1.5 %collective-permute-start.1 = (f32[64,128]{1,0:T(8,128)S(1)}, f32[64,128]{1,0:T(8,128)S(1)}, u32[]{:S(2)}, u32[]{:S(2)}) collective-permute-start(f32[64,128]{1,0:T(8,128)S(1)} %get-tuple-element.87.refs_12_), channel_id=1, source_target_pairs={{0,1},{1,0},{2,3},{3,2},{4,5},{5,4},{6,7},{7,6},{8,9},{9,8},{10,11... | collective-permute-start | bytes 98312 | tf_op jit(solution)/shard_map/ppermute | solution.py:580
  8.9 0.0 collective-permute-start.2
  8.9 2.9 %plan.1 = (s32[8,1536]{1,0:T(8,128)S(1)}, s32[8,1536]{1,0:T(8,128)S(1)}, s32[8,128]{1,0:T(8,128)S(1)}, s32[8,128]{1,0:T(8,128)S(1)}, s32[8,128]{1,0:T(8,128)S(1)...) custom-call(f32[60,140]{1,0:T(8,128)S(1)} %get-tuple-element.75.refs, ...), custom_call_target="tpu_custom_call" | custom-call | flops 2000000000 | bytes 1048576 | tf_op jit(solution)/shard_map/plan/pallas_call | solution.py:532
  11.8 0.0 collective-permute-done.rest_0_
  11.8 0.0 collective-permute-done.1.rest_1_
  11.8 0.0 collective-permute-done.2.rest_2_
  11.8 0.5 %level.3 = (f32[64,384]{1,0:T(8,128)S(1)}, f32[144,384]{1,0:T(8,128)S(1)}, f32[64,384]{1,0:T(8,128)S(1)}, f32[64,128]{1,0:T(8,128)S(1)}, f32[64,128]{1,0:T(8,128)S(1)}, /*index=5*/f32[64,128]{1,0:T(8,128)S(1)}) custom-call(f32[4,128]{1,0:T(4,128)S(1)} %get-tuple-element.89.flags_ref, s32[8,1536]{1,0:T(8,128)S(1)} %get-tuple-element.90.joined_ref, ...), custom_call_target="tpu_custom_call" | custom-call | flops 100000000 | bytes 1048576 | tf_op jit(solution)/shard_map/level/pallas_call | solution.py:532
  12.3 1.7 %collective-permute-start.3 = (f32[64,128]{1,0:T(8,128)S(1)}, f32[64,128]{1,0:T(8,128)S(1)}, u32[]{:S(2)}, u32[]{:S(2)}) collective-permute-start(f32[64,128]{1,0:T(8,128)S(1)} %get-tuple-element.111.rest_3_), channel_id=1, source_target_pairs={{0,30},{2,4},{4,2},{6,8},{8,6},{10,12},{12,10},{14,16},{16,14},{18... | collective-permute-start | bytes 98312 | tf_op jit(solution)/shard_map/ppermute | solution.py:580
  14.0 1.5 %collective-permute-start.4 = (f32[64,128]{1,0:T(8,128)S(1)}, f32[64,128]{1,0:T(8,128)S(1)}, u32[]{:S(2)}, u32[]{:S(2)}) collective-permute-start(f32[64,128]{1,0:T(8,128)S(1)} %get-tuple-element.112.rest_4_), channel_id=1, source_target_pairs={{0,1},{1,0},{2,3},{3,2},{4,5},{5,4},{6,7},{7,6},{8,9},{9,8},{10,11... | collective-permute-start | bytes 98312 | tf_op jit(solution)/shard_map/ppermute | solution.py:580
  15.5 0.0 collective-permute-start.5
  15.5 2.8 %between.3 = (f32[64,1024]{1,0:T(8,128)S(1)}, f32[144,384]{1,0:T(8,128)S(1)}, f32[8,384]{1,0:T(8,128)S(1)}, f32[64,384]{1,0:T(8,128)S(1)}, f32[144,1024]{1,0:T(8...) custom-call(s32[8,1536]{1,0:T(8,128)S(1)} %get-tuple-element.91.members_ref, ...), custom_call_target="tpu_custom_call" | custom-call | flops 2000000000 | bytes 1048576 | tf_op jit(solution)/shard_map/between/pallas_call | solution.py:532
  18.3 0.1 collective-permute-done.3.rest_0_
  18.4 0.0 collective-permute-done.4.rest_1_
  18.4 0.0 collective-permute-done.5.rest_2_
  18.4 0.7 %level.4 = (f32[64,384]{1,0:T(8,128)S(1)}, f32[144,384]{1,0:T(8,128)S(1)}, f32[64,384]{1,0:T(8,128)S(1)}, f32[64,128]{1,0:T(8,128)S(1)}, f32[64,128]{1,0:T(8,128)S(1)}, /*index=5*/f32[64,128]{1,0:T(8,128)S(1)}) custom-call(f32[4,128]{1,0:T(4,128)S(1)} %get-tuple-element.89.flags_ref, s32[8,1536]{1,0:T(8,128)S(1)} %get-tuple-element.90.joined_ref, ...), custom_call_target="tpu_custom_call" | custom-call | flops 100000000 | bytes 1048576 | tf_op jit(solution)/shard_map/level/pallas_call | solution.py:532
  19.2 2.0 %collective-permute-start.6 = (f32[64,128]{1,0:T(8,128)S(1)}, f32[64,128]{1,0:T(8,128)S(1)}, u32[]{:S(2)}, u32[]{:S(2)}) collective-permute-start(f32[64,128]{1,0:T(8,128)S(1)} %get-tuple-element.124.rest_3_), channel_id=1, source_target_pairs={{0,30},{2,4},{4,2},{6,8},{8,6},{10,12},{12,10},{14,16},{16,14},{18... | collective-permute-start | bytes 98312 | tf_op jit(solution)/shard_map/ppermute | solution.py:580
  21.2 1.2 %collective-permute-start.7 = (f32[64,128]{1,0:T(8,128)S(1)}, f32[64,128]{1,0:T(8,128)S(1)}, u32[]{:S(2)}, u32[]{:S(2)}) collective-permute-start(f32[64,128]{1,0:T(8,128)S(1)} %get-tuple-element.125.rest_4_), channel_id=1, source_target_pairs={{0,1},{1,0},{2,3},{3,2},{4,5},{5,4},{6,7},{7,6},{8,9},{9,8},{10,11... | collective-permute-start | bytes 98312 | tf_op jit(solution)/shard_map/ppermute | solution.py:580
  22.3 0.0 collective-permute-start.8
  22.3 2.8 %between.4 = (f32[64,1024]{1,0:T(8,128)S(1)}, f32[144,384]{1,0:T(8,128)S(1)}, f32[8,384]{1,0:T(8,128)S(1)}, f32[64,384]{1,0:T(8,128)S(1)}, f32[144,1024]{1,0:T(8...) custom-call(s32[8,1536]{1,0:T(8,128)S(1)} %get-tuple-element.91.members_ref, ...), custom_call_target="tpu_custom_call" | custom-call | flops 2000000000 | bytes 1048576 | tf_op jit(solution)/shard_map/between/pallas_call | solution.py:532
  25.1 0.1 collective-permute-done.6.rest_0_
  25.3 0.0 collective-permute-done.7.rest_1_
  25.3 0.0 collective-permute-done.8.rest_2_
  25.3 0.5 %level.5 = (f32[64,384]{1,0:T(8,128)S(1)}, f32[144,384]{1,0:T(8,128)S(1)}, f32[64,384]{1,0:T(8,128)S(1)}, f32[64,128]{1,0:T(8,128)S(1)}, f32[64,128]{1,0:T(8,128)S(1)}, /*index=5*/f32[64,128]{1,0:T(8,128)S(1)}) custom-call(f32[4,128]{1,0:T(4,128)S(1)} %get-tuple-element.89.flags_ref, s32[8,1536]{1,0:T(8,128)S(1)} %get-tuple-element.90.joined_ref, ...), custom_call_target="tpu_custom_call" | custom-call | flops 100000000 | bytes 1048576 | tf_op jit(solution)/shard_map/level/pallas_call | solution.py:532
  25.8 2.0 %collective-permute-start.9 = (f32[64,128]{1,0:T(8,128)S(1)}, f32[64,128]{1,0:T(8,128)S(1)}, u32[]{:S(2)}, u32[]{:S(2)}) collective-permute-start(f32[64,128]{1,0:T(8,128)S(1)} %get-tuple-element.142), channel_id=1, source_target_pairs={{0,30},{2,4},{4,2},{6,8},{8,6},{10,12},{12,10},{14,16},{16,14},{18... | collective-permute-start | bytes 98312 | tf_op jit(solution)/shard_map/ppermute | solution.py:580
  27.8 1.2 %collective-permute-start.10 = (f32[64,128]{1,0:T(8,128)S(1)}, f32[64,128]{1,0:T(8,128)S(1)}, u32[]{:S(2)}, u32[]{:S(2)}) collective-permute-start(f32[64,128]{1,0:T(8,128)S(1)} %get-tuple-element.143), channel_id=1, source_target_pairs={{0,1},{1,0},{2,3},{3,2},{4,5},{5,4},{6,7},{7,6},{8,9},{9,8},{10,11... | collective-permute-start | bytes 98312 | tf_op jit(solution)/shard_map/ppermute | solution.py:580
  29.0 0.0 collective-permute-start.11
  29.0 2.5 %between.5 = (f32[144,384]{1,0:T(8,128)S(1)}, f32[8,384]{1,0:T(8,128)S(1)}, f32[144,1024]{1,0:T(8,128)S(1)}) custom-call(s32[8,1536]{1,0:T(8,128)S(1)} %get-tuple-element.91.members_ref, s32[8,1536]{1,0:T(8,128)S(1)} %get-tuple-element.90.joined_ref, s32[8,128]{1,0:T(8,128)S(1)} %get-tuple-element.92.places_ref, ...), custom_call_target="tpu_custom_call" | custom-call | flops 2000000000 | bytes 1048576 | tf_op jit(solution)/shard_map/between/pallas_call | solution.py:532
  31.5 0.4 %collective-permute-done.9.rest_0_ = f32[64,128]{1,0:T(8,128)S(1)} collective-permute-done((f32[64,128]{1,0:T(8,128)S(1)}, f32[64,128]{1,0:T(8,128)S(1)}, u32[]{:S(2)}, u32[]{:S(2)}) %collective-permute-start.9) | collective-permute-done | bytes 32800 | tf_op jit(solution)/shard_map/ppermute | solution.py:580
  31.9 0.0 collective-permute-done.10.rest_1_
  31.9 0.0 collective-permute-done.11.rest_2_
  31.9 2.5 %last.1 = f32[1120,128]{1,0:T(8,128)} custom-call(f32[4,128]{1,0:T(4,128)S(1)} %get-tuple-element.89.flags_ref, s32[8,1536]{1,0:T(8,128)S(1)} %get-tuple-element.90.joined_ref, f32[144,384]{1,0:T(8,128)S(1)} %get-tuple-element.139.local_ref, f32[8,384]{1,0:T(8,128)S(1)} %get-tuple-element.140.weights_ref, bf16[144,768]{1,0:T(8,128)(2,1)S(1)} %get-tuple-element.97.lift_ref, ...), custom_call_target="tpu_custom_call" | custom-call | flops 1000000000 | bytes 1048576 | tf_op jit(solution)/shard_map/last/pallas_call | solution.py:532
Async XLA Ops:
  1.9 9.9 %collective-permute-start = (f32[64,128]{1,0:T(8,128)S(1)}, f32[64,128]{1,0:T(8,128)S(1)}, u32[]{:S(2)}, u32[]{:S(2)}) collective-permute-start(f32[64,128]{1,0:T(8,128)S(1)} %get-tuple-element.86.refs_11_), channel_id=1, source_target_pairs={{0,30},{2,4},{4,2},{6,8},{8,6},{10,12},{12,10},{14,16},{16,14},{18... | collective-permute-start | bytes 98312 | tf_op jit(solution)/shard_map/ppermute | solution.py:580
  7.4 4.4 %collective-permute-start.1 = (f32[64,128]{1,0:T(8,128)S(1)}, f32[64,128]{1,0:T(8,128)S(1)}, u32[]{:S(2)}, u32[]{:S(2)}) collective-permute-start(f32[64,128]{1,0:T(8,128)S(1)} %get-tuple-element.87.refs_12_), channel_id=1, source_target_pairs={{0,1},{1,0},{2,3},{3,2},{4,5},{5,4},{6,7},{7,6},{8,9},{9,8},{10,11... | collective-permute-start | bytes 98312 | tf_op jit(solution)/shard_map/ppermute | solution.py:580
  8.9 2.9 %collective-permute-start.2 = (f32[64,128]{1,0:T(8,128)S(1)}, f32[64,128]{1,0:T(8,128)S(1)}, u32[]{:S(2)}, u32[]{:S(2)}) collective-permute-start(f32[64,128]{1,0:T(8,128)S(1)} %get-tuple-element.88.refs_13_), channel_id=1, source_target_pairs={{0,2},{2,0},{4,6},{6,4},{8,10},{10,8},{12,14},{14,12},{16,18},{18,... | collective-permute-start | bytes 98312 | tf_op jit(solution)/shard_map/ppermute | solution.py:580
  12.3 6.1 %collective-permute-start.3 = (f32[64,128]{1,0:T(8,128)S(1)}, f32[64,128]{1,0:T(8,128)S(1)}, u32[]{:S(2)}, u32[]{:S(2)}) collective-permute-start(f32[64,128]{1,0:T(8,128)S(1)} %get-tuple-element.111.rest_3_), channel_id=1, source_target_pairs={{0,30},{2,4},{4,2},{6,8},{8,6},{10,12},{12,10},{14,16},{16,14},{18... | collective-permute-start | bytes 98312 | tf_op jit(solution)/shard_map/ppermute | solution.py:580
  14.0 4.4 %collective-permute-start.4 = (f32[64,128]{1,0:T(8,128)S(1)}, f32[64,128]{1,0:T(8,128)S(1)}, u32[]{:S(2)}, u32[]{:S(2)}) collective-permute-start(f32[64,128]{1,0:T(8,128)S(1)} %get-tuple-element.112.rest_4_), channel_id=1, source_target_pairs={{0,1},{1,0},{2,3},{3,2},{4,5},{5,4},{6,7},{7,6},{8,9},{9,8},{10,11... | collective-permute-start | bytes 98312 | tf_op jit(solution)/shard_map/ppermute | solution.py:580
  15.5 2.9 %collective-permute-start.5 = (f32[64,128]{1,0:T(8,128)S(1)}, f32[64,128]{1,0:T(8,128)S(1)}, u32[]{:S(2)}, u32[]{:S(2)}) collective-permute-start(f32[64,128]{1,0:T(8,128)S(1)} %get-tuple-element.113.rest_5_), channel_id=1, source_target_pairs={{0,2},{2,0},{4,6},{6,4},{8,10},{10,8},{12,14},{14,12},{16,18},{18,... | collective-permute-start | bytes 98312 | tf_op jit(solution)/shard_map/ppermute | solution.py:580
  19.2 6.1 %collective-permute-start.6 = (f32[64,128]{1,0:T(8,128)S(1)}, f32[64,128]{1,0:T(8,128)S(1)}, u32[]{:S(2)}, u32[]{:S(2)}) collective-permute-start(f32[64,128]{1,0:T(8,128)S(1)} %get-tuple-element.124.rest_3_), channel_id=1, source_target_pairs={{0,30},{2,4},{4,2},{6,8},{8,6},{10,12},{12,10},{14,16},{16,14},{18... | collective-permute-start | bytes 98312 | tf_op jit(solution)/shard_map/ppermute | solution.py:580
  21.2 4.1 %collective-permute-start.7 = (f32[64,128]{1,0:T(8,128)S(1)}, f32[64,128]{1,0:T(8,128)S(1)}, u32[]{:S(2)}, u32[]{:S(2)}) collective-permute-start(f32[64,128]{1,0:T(8,128)S(1)} %get-tuple-element.125.rest_4_), channel_id=1, source_target_pairs={{0,1},{1,0},{2,3},{3,2},{4,5},{5,4},{6,7},{7,6},{8,9},{9,8},{10,11... | collective-permute-start | bytes 98312 | tf_op jit(solution)/shard_map/ppermute | solution.py:580
  22.3 2.9 %collective-permute-start.8 = (f32[64,128]{1,0:T(8,128)S(1)}, f32[64,128]{1,0:T(8,128)S(1)}, u32[]{:S(2)}, u32[]{:S(2)}) collective-permute-start(f32[64,128]{1,0:T(8,128)S(1)} %get-tuple-element.126.rest_5_), channel_id=1, source_target_pairs={{0,2},{2,0},{4,6},{6,4},{8,10},{10,8},{12,14},{14,12},{16,18},{18,... | collective-permute-start | bytes 98312 | tf_op jit(solution)/shard_map/ppermute | solution.py:580
  25.8 6.1 %collective-permute-start.9 = (f32[64,128]{1,0:T(8,128)S(1)}, f32[64,128]{1,0:T(8,128)S(1)}, u32[]{:S(2)}, u32[]{:S(2)}) collective-permute-start(f32[64,128]{1,0:T(8,128)S(1)} %get-tuple-element.142), channel_id=1, source_target_pairs={{0,30},{2,4},{4,2},{6,8},{8,6},{10,12},{12,10},{14,16},{16,14},{18... | collective-permute-start | bytes 98312 | tf_op jit(solution)/shard_map/ppermute | solution.py:580
  27.8 4.1 %collective-permute-start.10 = (f32[64,128]{1,0:T(8,128)S(1)}, f32[64,128]{1,0:T(8,128)S(1)}, u32[]{:S(2)}, u32[]{:S(2)}) collective-permute-start(f32[64,128]{1,0:T(8,128)S(1)} %get-tuple-element.143), channel_id=1, source_target_pairs={{0,1},{1,0},{2,3},{3,2},{4,5},{5,4},{6,7},{7,6},{8,9},{9,8},{10,11... | collective-permute-start | bytes 98312 | tf_op jit(solution)/shard_map/ppermute | solution.py:580
  29.0 2.9 %collective-permute-start.11 = (f32[64,128]{1,0:T(8,128)S(1)}, f32[64,128]{1,0:T(8,128)S(1)}, u32[]{:S(2)}, u32[]{:S(2)}) collective-permute-start(f32[64,128]{1,0:T(8,128)S(1)} %get-tuple-element.144), channel_id=1, source_target_pairs={{0,2},{2,0},{4,6},{6,4},{8,10},{10,8},{12,14},{14,12},{16,18},{18,... | collective-permute-start | bytes 98312 | tf_op jit(solution)/shard_map/ppermute | solution.py:580

commit v9 on v8

--- a/solution.py
+++ b/solution.py
@@ -176,7 +176,7 @@
     out_ref[...] = total
     copies[3].wait()
     for index, send in zip(sent_rows(send_ref, swaps), sends):
-        send[...] = pick(ref_blocks(out_ref, count), index, index >> 7)
+        send[...] = pick(ref_blocks(out_ref, count), index, index >> 7)[:send.shape[0]]
     columns_ref[comp:, :] = jnp.zeros((columns_ref.shape[0] - comp, elements), f32)
     for copy in copies[4:]:
         copy.wait()
@@ -218,7 +218,8 @@
     for group, (before, message) in enumerate(zip(sent, messages)):
         index = send_places_ref[group:group + 1, :]
         which = (index >> 7) - level * (BLOCK // LANES)
-        message[...] = pick(ref_blocks(trace_ref, BLOCK // LANES), index, which, before[...])
+        message[...] = pick(
+            ref_blocks(trace_ref, BLOCK // LANES), index, which, pad_rows(before[...], message.shape[0]))
 
 
 def row_chunks(rows):
@@ -351,16 +352,17 @@
     return pick(blocks, index, which, before)
 
 
-def received_blocks(received, count):
-    return [(count + i, functools.partial(lambda ref: ref[...], ref)) for i, ref in enumerate(received)]
+def received_blocks(received, count, rows):
+    return [(count + i, functools.partial(lambda ref: pad_rows(ref[...], rows), ref)) for i, ref in enumerate(received)]
 
 
 def received_traces(level, face, received, joined_ref, count):
     parts = []
     for block in range(BLOCK // LANES):
         index = joined_ref[face:face + 1, block_at(level * (BLOCK // LANES) + block)]
-        zeros = jnp.zeros(received[0].shape, f32)
-        parts.append(pick(received_blocks(received, count), index, index >> 7, zeros))
+        rows = rounded_up(received[0].shape[0], 16)
+        zeros = jnp.zeros((rows, LANES), f32)
+        parts.append(pick(received_blocks(received, count, rows), index, index >> 7, zeros))
     return jnp.concatenate(parts, axis=1)
 
 
@@ -450,7 +452,7 @@
     rows = moved_ref.shape[0]
     pieces = BLOCK // LANES
     other = any_other(level, flags_ref)
-    arrived = jnp.concatenate([ref[...] for ref in received], axis=1)
+    arrived = jnp.concatenate([pad_rows(ref[...], rows) for ref in received], axis=1)
     stacked = product(mix_ref[...], stacked_columns(arrived))
     moved_ref[...] = summed_powers(stacked[rows:], slot_weights_ref, rows, stacked[:rows])
     extra_ref[...] = jnp.zeros(extra_ref.shape, f32)
@@ -459,8 +461,8 @@
     for group, (before, send) in enumerate(zip(prepared, sends)):
         place, code = send_places_ref[group:group + 1, :], send_codes_ref[group:group + 1, :]
         here = ((place >> 7) >= level * pieces) & ((place >> 7) < (level + 1) * pieces)
-        send[...] = before[...] + pick(
-            moved, code, jnp.where(here, code >> 7, 0), jnp.zeros(before.shape, f32))
+        total = before[...] + pick(moved, code, jnp.where(here, code >> 7, 0), jnp.zeros(before.shape, f32))
+        send[...] = total[:send.shape[0]]
 
     @pl.when(other)
     def _():
@@ -470,8 +472,9 @@
         extra_trace_ref[...] = advanced_traces(extra, trace_grow_ref, weights_ref, rows)
         for group, send in enumerate(sends):
             place = send_places_ref[group:group + 1, :]
-            send[...] = send[...] + pick(
-                ref_blocks(extra_trace_ref, pieces), place, (place >> 7) - level * pieces, jnp.zeros(send.shape, f32))
+            more = pick(
+                ref_blocks(extra_trace_ref, pieces), place, (place >> 7) - level * pieces, jnp.zeros((rows, LANES), f32))
+            send[...] = send[...] + more[:send.shape[0]]
 
 
 def last_chunks(rows):
@@ -573,13 +576,13 @@
     bnd = send_list.shape[-1]
 
     near, *far = swap_plan("sector", True, 0, 1)
-    swaps = far + swap_plan("radial", False, 2, 3) + [near]
+    swaps = far + [near] + swap_plan("radial", False, 2, 3)
     messages = len(swaps)
 
     def exchange(sent):
         return [lax.ppermute(one, swap[0], swap[1]) for one, swap in zip(sent, swaps)]
 
-    message = ((trace_rows, bnd), f32)
+    message, prepared_message = ((trace, bnd), f32), ((trace_rows, bnd), f32)
     own, face_stack = ((rows, BLOCK), f32), ((faces * trace_rows, BLOCK), f32)
     weight, table, traced = ((POWERS, BLOCK), f32), ((trace_rows, elements), f32), ((trace_rows, BLOCK), f32)
     whole = ((rows, elements), f32)
@@ -601,7 +604,7 @@
          ((POWERS, messages * LANES), f32), ((LEVELS, LANES), f32), own, weight, traced,
          ((POWERS * rows, 3 * rows), bf16), (((POWERS + 1) * trace_rows, 3 * rows), bf16),
          (((POWERS + 1) * trace_rows, 3 * trace_rows), bf16), ((rows, 3 * faces * trace_rows), bf16), ((rows, 3 * trace_rows), bf16), ((1, LANES), f32)]
-        + [message] * messages, [face_stack])
+        + [prepared_message] * messages, [face_stack])
     advanced = []
     for level in range(LEVELS - 1):
         moved, extra, extra_trace, *sent = call(
@@ -616,7 +619,7 @@
         if level + 1 < LEVELS - 1:
             out, loaded, weights, new_trace, *rest = call(
                 beside, "between", 2 * 10 ** 9, operands + sent + advanced,
-                [table, own, weight, traced, whole] + [message] * messages, scratch)
+                [table, own, weight, traced, whole] + [prepared_message] * messages, scratch)
             advanced, prepared = rest[:1], rest[1:]
         else:
             loaded, weights, *advanced = call(

time: 34.7 us -> 34.7 us (level)
  no operation moved by 1% of the time
where the time goes in v9:
time: 34.7 us; the launch traced here: 34.6 us
  Pallas kernels  17.1 us (49%)
  starting transfers between devices  16.5 us (48%)
  waiting for transfers between devices  0.7 us (2%)
    pallas_call x9, Pallas kernels, call(): pl.pallas_call(kernel, out_shape=tuple((jax.ShapeDtypeStruct(shape, dtype...  17.1 us
    ppermute x12, starting transfers between devices, exchange(): lax.ppermute(one, swap[0], swap[1])  16.5 us
    ppermute x12, waiting for transfers between devices, exchange(): lax.ppermute(one, swap[0], swap[1])  0.7 us
  transfers between devices with their start and end apart: 12, of which 3 were waited for; matrix products, arithmetic and copies ran while one was open for 0% of the time, Pallas kernels for 32%

profile of v9, /device:TPU:0, one launch (start us, length us, event | category | flops | bytes accessed | tf_op | source)
XLA Modules:
  0.0 34.6 jit_solution(11006025130191865352)
XLA Ops:
  0.0 1.9 %first.1 = (f32[144,1024]{1,0:T(8,128)S(1)}, f32[64,1024]{1,0:T(8,128)S(1)}, f32[60,128]{1,0:T(8,128)S(1)}, f32[60,128]{1,0:T(8,128)S(1)}, f32[60,128]{1,0:T(8,1...) custom-call(f32[1120,128]{1,0:T(8,128)} %bitcast.9, ...), custom_call_target="tpu_custom_call" | custom-call | flops 100000000 | bytes 1048576 | tf_op jit(solution)/shard_map/first/pallas_call | solution.py:535
  1.9 5.5 %collective-permute-start = (f32[60,128]{1,0:T(8,128)S(1)}, f32[60,128]{1,0:T(8,128)S(1)}, u32[]{:S(2)}, u32[]{:S(2)}) collective-permute-start(f32[60,128]{1,0:T(8,128)S(1)} %get-tuple-element.86.refs_11_), channel_id=1, source_target_pairs={{0,30},{2,4},{4,2},{6,8},{8,6},{10,12},{12,10},{14,16},{16,14},{18... | collective-permute-start | bytes 92168 | tf_op jit(solution)/shard_map/ppermute | solution.py:583
  7.4 0.0 collective-permute-start.1
  7.4 1.5 %collective-permute-start.2 = (f32[60,128]{1,0:T(8,128)S(1)}, f32[60,128]{1,0:T(8,128)S(1)}, u32[]{:S(2)}, u32[]{:S(2)}) collective-permute-start(f32[60,128]{1,0:T(8,128)S(1)} %get-tuple-element.88.refs_13_), channel_id=1, source_target_pairs={{0,1},{1,0},{2,3},{3,2},{4,5},{5,4},{6,7},{7,6},{8,9},{9,8},{10,11... | collective-permute-start | bytes 92168 | tf_op jit(solution)/shard_map/ppermute | solution.py:583
  8.9 2.9 %plan.1 = (s32[8,1536]{1,0:T(8,128)S(1)}, s32[8,1536]{1,0:T(8,128)S(1)}, s32[8,128]{1,0:T(8,128)S(1)}, s32[8,128]{1,0:T(8,128)S(1)}, s32[8,128]{1,0:T(8,128)S(1)...) custom-call(f32[60,140]{1,0:T(8,128)S(1)} %get-tuple-element.75.refs, ...), custom_call_target="tpu_custom_call" | custom-call | flops 2000000000 | bytes 1048576 | tf_op jit(solution)/shard_map/plan/pallas_call | solution.py:535
  11.8 0.0 collective-permute-done.rest_0_
  11.8 0.0 collective-permute-done.1.rest_1_
  11.8 0.0 collective-permute-done.2.rest_2_
  11.8 0.5 %level.3 = (f32[64,384]{1,0:T(8,128)S(1)}, f32[144,384]{1,0:T(8,128)S(1)}, f32[64,384]{1,0:T(8,128)S(1)}, f32[60,128]{1,0:T(8,128)S(1)}, f32[60,128]{1,0:T(8,128)S(1)}, /*index=5*/f32[60,128]{1,0:T(8,128)S(1)}) custom-call(f32[4,128]{1,0:T(4,128)S(1)} %get-tuple-element.89.flags_ref, s32[8,1536]{1,0:T(8,128)S(1)} %get-tuple-element.90.joined_ref, ...), custom_call_target="tpu_custom_call" | custom-call | flops 100000000 | bytes 1048576 | tf_op jit(solution)/shard_map/level/pallas_call | solution.py:535
  12.3 1.7 %collective-permute-start.3 = (f32[60,128]{1,0:T(8,128)S(1)}, f32[60,128]{1,0:T(8,128)S(1)}, u32[]{:S(2)}, u32[]{:S(2)}) collective-permute-start(f32[60,128]{1,0:T(8,128)S(1)} %get-tuple-element.111.rest_3_), channel_id=1, source_target_pairs={{0,30},{2,4},{4,2},{6,8},{8,6},{10,12},{12,10},{14,16},{16,14},{18... | collective-permute-start | bytes 92168 | tf_op jit(solution)/shard_map/ppermute | solution.py:583
  14.0 0.0 collective-permute-start.4
  14.0 1.5 %collective-permute-start.5 = (f32[60,128]{1,0:T(8,128)S(1)}, f32[60,128]{1,0:T(8,128)S(1)}, u32[]{:S(2)}, u32[]{:S(2)}) collective-permute-start(f32[60,128]{1,0:T(8,128)S(1)} %get-tuple-element.113.rest_5_), channel_id=1, source_target_pairs={{0,1},{1,0},{2,3},{3,2},{4,5},{5,4},{6,7},{7,6},{8,9},{9,8},{10,11... | collective-permute-start | bytes 92168 | tf_op jit(solution)/shard_map/ppermute | solution.py:583
  15.5 2.8 %between.3 = (f32[64,1024]{1,0:T(8,128)S(1)}, f32[144,384]{1,0:T(8,128)S(1)}, f32[8,384]{1,0:T(8,128)S(1)}, f32[64,384]{1,0:T(8,128)S(1)}, f32[144,1024]{1,0:T(8...) custom-call(s32[8,1536]{1,0:T(8,128)S(1)} %get-tuple-element.91.members_ref, ...), custom_call_target="tpu_custom_call" | custom-call | flops 2000000000 | bytes 1048576 | tf_op jit(solution)/shard_map/between/pallas_call | solution.py:535
  18.3 0.1 collective-permute-done.3.rest_0_
  18.4 0.0 collective-permute-done.4.rest_1_
  18.4 0.0 collective-permute-done.5.rest_2_
  18.4 0.7 %level.4 = (f32[64,384]{1,0:T(8,128)S(1)}, f32[144,384]{1,0:T(8,128)S(1)}, f32[64,384]{1,0:T(8,128)S(1)}, f32[60,128]{1,0:T(8,128)S(1)}, f32[60,128]{1,0:T(8,128)S(1)}, /*index=5*/f32[60,128]{1,0:T(8,128)S(1)}) custom-call(f32[4,128]{1,0:T(4,128)S(1)} %get-tuple-element.89.flags_ref, s32[8,1536]{1,0:T(8,128)S(1)} %get-tuple-element.90.joined_ref, ...), custom_call_target="tpu_custom_call" | custom-call | flops 100000000 | bytes 1048576 | tf_op jit(solution)/shard_map/level/pallas_call | solution.py:535
  19.2 2.0 %collective-permute-start.6 = (f32[60,128]{1,0:T(8,128)S(1)}, f32[60,128]{1,0:T(8,128)S(1)}, u32[]{:S(2)}, u32[]{:S(2)}) collective-permute-start(f32[60,128]{1,0:T(8,128)S(1)} %get-tuple-element.124.rest_3_), channel_id=1, source_target_pairs={{0,30},{2,4},{4,2},{6,8},{8,6},{10,12},{12,10},{14,16},{16,14},{18... | collective-permute-start | bytes 92168 | tf_op jit(solution)/shard_map/ppermute | solution.py:583
  21.2 0.0 collective-permute-start.7
  21.2 1.2 %collective-permute-start.8 = (f32[60,128]{1,0:T(8,128)S(1)}, f32[60,128]{1,0:T(8,128)S(1)}, u32[]{:S(2)}, u32[]{:S(2)}) collective-permute-start(f32[60,128]{1,0:T(8,128)S(1)} %get-tuple-element.126.rest_5_), channel_id=1, source_target_pairs={{0,1},{1,0},{2,3},{3,2},{4,5},{5,4},{6,7},{7,6},{8,9},{9,8},{10,11... | collective-permute-start | bytes 92168 | tf_op jit(solution)/shard_map/ppermute | solution.py:583
  22.3 2.8 %between.4 = (f32[64,1024]{1,0:T(8,128)S(1)}, f32[144,384]{1,0:T(8,128)S(1)}, f32[8,384]{1,0:T(8,128)S(1)}, f32[64,384]{1,0:T(8,128)S(1)}, f32[144,1024]{1,0:T(8...) custom-call(s32[8,1536]{1,0:T(8,128)S(1)} %get-tuple-element.91.members_ref, ...), custom_call_target="tpu_custom_call" | custom-call | flops 2000000000 | bytes 1048576 | tf_op jit(solution)/shard_map/between/pallas_call | solution.py:535
  25.1 0.1 collective-permute-done.6.rest_0_
  25.3 0.0 collective-permute-done.7.rest_1_
  25.3 0.0 collective-permute-done.8.rest_2_
  25.3 0.5 %level.5 = (f32[64,384]{1,0:T(8,128)S(1)}, f32[144,384]{1,0:T(8,128)S(1)}, f32[64,384]{1,0:T(8,128)S(1)}, f32[60,128]{1,0:T(8,128)S(1)}, f32[60,128]{1,0:T(8,128)S(1)}, /*index=5*/f32[60,128]{1,0:T(8,128)S(1)}) custom-call(f32[4,128]{1,0:T(4,128)S(1)} %get-tuple-element.89.flags_ref, s32[8,1536]{1,0:T(8,128)S(1)} %get-tuple-element.90.joined_ref, ...), custom_call_target="tpu_custom_call" | custom-call | flops 100000000 | bytes 1048576 | tf_op jit(solution)/shard_map/level/pallas_call | solution.py:535
  25.8 2.0 %collective-permute-start.9 = (f32[60,128]{1,0:T(8,128)S(1)}, f32[60,128]{1,0:T(8,128)S(1)}, u32[]{:S(2)}, u32[]{:S(2)}) collective-permute-start(f32[60,128]{1,0:T(8,128)S(1)} %get-tuple-element.142), channel_id=1, source_target_pairs={{0,30},{2,4},{4,2},{6,8},{8,6},{10,12},{12,10},{14,16},{16,14},{18... | collective-permute-start | bytes 92168 | tf_op jit(solution)/shard_map/ppermute | solution.py:583
  27.8 0.0 collective-permute-start.10
  27.8 1.2 %collective-permute-start.11 = (f32[60,128]{1,0:T(8,128)S(1)}, f32[60,128]{1,0:T(8,128)S(1)}, u32[]{:S(2)}, u32[]{:S(2)}) collective-permute-start(f32[60,128]{1,0:T(8,128)S(1)} %get-tuple-element.144), channel_id=1, source_target_pairs={{0,1},{1,0},{2,3},{3,2},{4,5},{5,4},{6,7},{7,6},{8,9},{9,8},{10,11... | collective-permute-start | bytes 92168 | tf_op jit(solution)/shard_map/ppermute | solution.py:583
  29.0 2.5 %between.5 = (f32[144,384]{1,0:T(8,128)S(1)}, f32[8,384]{1,0:T(8,128)S(1)}, f32[144,1024]{1,0:T(8,128)S(1)}) custom-call(s32[8,1536]{1,0:T(8,128)S(1)} %get-tuple-element.91.members_ref, s32[8,1536]{1,0:T(8,128)S(1)} %get-tuple-element.90.joined_ref, s32[8,128]{1,0:T(8,128)S(1)} %get-tuple-element.92.places_ref, ...), custom_call_target="tpu_custom_call" | custom-call | flops 2000000000 | bytes 1048576 | tf_op jit(solution)/shard_map/between/pallas_call | solution.py:535
  31.5 0.4 %collective-permute-done.9.rest_0_ = f32[60,128]{1,0:T(8,128)S(1)} collective-permute-done((f32[60,128]{1,0:T(8,128)S(1)}, f32[60,128]{1,0:T(8,128)S(1)}, u32[]{:S(2)}, u32[]{:S(2)}) %collective-permute-start.9) | collective-permute-done | bytes 30752 | tf_op jit(solution)/shard_map/ppermute | solution.py:583
  31.9 0.0 collective-permute-done.10.rest_1_
  31.9 0.0 collective-permute-done.11.rest_2_
  31.9 2.5 %last.1 = f32[1120,128]{1,0:T(8,128)} custom-call(f32[4,128]{1,0:T(4,128)S(1)} %get-tuple-element.89.flags_ref, s32[8,1536]{1,0:T(8,128)S(1)} %get-tuple-element.90.joined_ref, f32[144,384]{1,0:T(8,128)S(1)} %get-tuple-element.139.local_ref, f32[8,384]{1,0:T(8,128)S(1)} %get-tuple-element.140.weights_ref, bf16[144,768]{1,0:T(8,128)(2,1)S(1)} %get-tuple-element.97.lift_ref, ...), custom_call_target="tpu_custom_call" | custom-call | flops 1000000000 | bytes 1048576 | tf_op jit(solution)/shard_map/last/pallas_call | solution.py:535
Async XLA Ops:
  1.9 9.9 %collective-permute-start = (f32[60,128]{1,0:T(8,128)S(1)}, f32[60,128]{1,0:T(8,128)S(1)}, u32[]{:S(2)}, u32[]{:S(2)}) collective-permute-start(f32[60,128]{1,0:T(8,128)S(1)} %get-tuple-element.86.refs_11_), channel_id=1, source_target_pairs={{0,30},{2,4},{4,2},{6,8},{8,6},{10,12},{12,10},{14,16},{16,14},{18... | collective-permute-start | bytes 92168 | tf_op jit(solution)/shard_map/ppermute | solution.py:583
  7.4 4.4 %collective-permute-start.1 = (f32[60,128]{1,0:T(8,128)S(1)}, f32[60,128]{1,0:T(8,128)S(1)}, u32[]{:S(2)}, u32[]{:S(2)}) collective-permute-start(f32[60,128]{1,0:T(8,128)S(1)} %get-tuple-element.87.refs_12_), channel_id=1, source_target_pairs={{0,2},{2,0},{4,6},{6,4},{8,10},{10,8},{12,14},{14,12},{16,18},{18,... | collective-permute-start | bytes 92168 | tf_op jit(solution)/shard_map/ppermute | solution.py:583
  7.4 4.4 %collective-permute-start.2 = (f32[60,128]{1,0:T(8,128)S(1)}, f32[60,128]{1,0:T(8,128)S(1)}, u32[]{:S(2)}, u32[]{:S(2)}) collective-permute-start(f32[60,128]{1,0:T(8,128)S(1)} %get-tuple-element.88.refs_13_), channel_id=1, source_target_pairs={{0,1},{1,0},{2,3},{3,2},{4,5},{5,4},{6,7},{7,6},{8,9},{9,8},{10,11... | collective-permute-start | bytes 92168 | tf_op jit(solution)/shard_map/ppermute | solution.py:583
  12.3 6.1 %collective-permute-start.3 = (f32[60,128]{1,0:T(8,128)S(1)}, f32[60,128]{1,0:T(8,128)S(1)}, u32[]{:S(2)}, u32[]{:S(2)}) collective-permute-start(f32[60,128]{1,0:T(8,128)S(1)} %get-tuple-element.111.rest_3_), channel_id=1, source_target_pairs={{0,30},{2,4},{4,2},{6,8},{8,6},{10,12},{12,10},{14,16},{16,14},{18... | collective-permute-start | bytes 92168 | tf_op jit(solution)/shard_map/ppermute | solution.py:583
  14.0 4.4 %collective-permute-start.4 = (f32[60,128]{1,0:T(8,128)S(1)}, f32[60,128]{1,0:T(8,128)S(1)}, u32[]{:S(2)}, u32[]{:S(2)}) collective-permute-start(f32[60,128]{1,0:T(8,128)S(1)} %get-tuple-element.112.rest_4_), channel_id=1, source_target_pairs={{0,2},{2,0},{4,6},{6,4},{8,10},{10,8},{12,14},{14,12},{16,18},{18,... | collective-permute-start | bytes 92168 | tf_op jit(solution)/shard_map/ppermute | solution.py:583
  14.0 4.4 %collective-permute-start.5 = (f32[60,128]{1,0:T(8,128)S(1)}, f32[60,128]{1,0:T(8,128)S(1)}, u32[]{:S(2)}, u32[]{:S(2)}) collective-permute-start(f32[60,128]{1,0:T(8,128)S(1)} %get-tuple-element.113.rest_5_), channel_id=1, source_target_pairs={{0,1},{1,0},{2,3},{3,2},{4,5},{5,4},{6,7},{7,6},{8,9},{9,8},{10,11... | collective-permute-start | bytes 92168 | tf_op jit(solution)/shard_map/ppermute | solution.py:583
  19.2 6.1 %collective-permute-start.6 = (f32[60,128]{1,0:T(8,128)S(1)}, f32[60,128]{1,0:T(8,128)S(1)}, u32[]{:S(2)}, u32[]{:S(2)}) collective-permute-start(f32[60,128]{1,0:T(8,128)S(1)} %get-tuple-element.124.rest_3_), channel_id=1, source_target_pairs={{0,30},{2,4},{4,2},{6,8},{8,6},{10,12},{12,10},{14,16},{16,14},{18... | collective-permute-start | bytes 92168 | tf_op jit(solution)/shard_map/ppermute | solution.py:583
  21.2 4.1 %collective-permute-start.7 = (f32[60,128]{1,0:T(8,128)S(1)}, f32[60,128]{1,0:T(8,128)S(1)}, u32[]{:S(2)}, u32[]{:S(2)}) collective-permute-start(f32[60,128]{1,0:T(8,128)S(1)} %get-tuple-element.125.rest_4_), channel_id=1, source_target_pairs={{0,2},{2,0},{4,6},{6,4},{8,10},{10,8},{12,14},{14,12},{16,18},{18,... | collective-permute-start | bytes 92168 | tf_op jit(solution)/shard_map/ppermute | solution.py:583
  21.2 4.1 %collective-permute-start.8 = (f32[60,128]{1,0:T(8,128)S(1)}, f32[60,128]{1,0:T(8,128)S(1)}, u32[]{:S(2)}, u32[]{:S(2)}) collective-permute-start(f32[60,128]{1,0:T(8,128)S(1)} %get-tuple-element.126.rest_5_), channel_id=1, source_target_pairs={{0,1},{1,0},{2,3},{3,2},{4,5},{5,4},{6,7},{7,6},{8,9},{9,8},{10,11... | collective-permute-start | bytes 92168 | tf_op jit(solution)/shard_map/ppermute | solution.py:583
  25.8 6.1 %collective-permute-start.9 = (f32[60,128]{1,0:T(8,128)S(1)}, f32[60,128]{1,0:T(8,128)S(1)}, u32[]{:S(2)}, u32[]{:S(2)}) collective-permute-start(f32[60,128]{1,0:T(8,128)S(1)} %get-tuple-element.142), channel_id=1, source_target_pairs={{0,30},{2,4},{4,2},{6,8},{8,6},{10,12},{12,10},{14,16},{16,14},{18... | collective-permute-start | bytes 92168 | tf_op jit(solution)/shard_map/ppermute | solution.py:583
  27.8 4.1 %collective-permute-start.10 = (f32[60,128]{1,0:T(8,128)S(1)}, f32[60,128]{1,0:T(8,128)S(1)}, u32[]{:S(2)}, u32[]{:S(2)}) collective-permute-start(f32[60,128]{1,0:T(8,128)S(1)} %get-tuple-element.143), channel_id=1, source_target_pairs={{0,2},{2,0},{4,6},{6,4},{8,10},{10,8},{12,14},{14,12},{16,18},{18,... | collective-permute-start | bytes 92168 | tf_op jit(solution)/shard_map/ppermute | solution.py:583
  27.8 4.1 %collective-permute-start.11 = (f32[60,128]{1,0:T(8,128)S(1)}, f32[60,128]{1,0:T(8,128)S(1)}, u32[]{:S(2)}, u32[]{:S(2)}) collective-permute-start(f32[60,128]{1,0:T(8,128)S(1)} %get-tuple-element.144), channel_id=1, source_target_pairs={{0,1},{1,0},{2,3},{3,2},{4,5},{5,4},{6,7},{7,6},{8,9},{9,8},{10,11... | collective-permute-start | bytes 92168 | tf_op jit(solution)/shard_map/ppermute | solution.py:583

commit v10 on v9

--- a/solution.py
+++ b/solution.py
@@ -366,9 +366,31 @@
     return jnp.concatenate(parts, axis=1)
 
 
-def other_traces(level, received, joined_ref, count):
-    parts = [received_traces(level, face, received, joined_ref, count) for face in range(1, faces_in(joined_ref))]
-    return jnp.concatenate([jnp.zeros_like(parts[0])] + parts, axis=0)
+def gather_received(level, low, received, joined_ref, count, traces_ref):
+    faces = faces_in(joined_ref)
+    rows = traces_ref.shape[0] // faces
+    if low:
+        traces_ref[:low * rows, :] = jnp.zeros((low * rows, traces_ref.shape[1]), f32)
+
+    def step(face, carry):
+        for block in range(BLOCK // LANES):
+            there = block_at(level * (BLOCK // LANES) + block)
+            index = joined_ref[low:low + 1, there]
+            for other in range(low + 1, faces):
+                index = jnp.where(face == other, joined_ref[other:other + 1, there], index)
+            traces_ref[pl.ds(pl.multiple_of(face * rows, rows), rows), block_at(block)] = pick(
+                received_blocks(received, count, rows), index, index >> 7, jnp.zeros((rows, LANES), f32))
+        return carry
+
+    lax.fori_loop(low, faces, step, 0)
+
+
+def for_blocks(body):
+    def step(block, carry):
+        body(pl.ds(pl.multiple_of(block * LANES, LANES), LANES))
+        return carry
+
+    lax.fori_loop(0, BLOCK // LANES, step, 0)
 
 
 def any_other(level, flags_ref):
@@ -448,7 +470,8 @@
                  trace_grow_ref, send_places_ref, send_codes_ref, *rest):
     received, rest = rest[:messages], rest[messages:]
     prepared, rest = rest[:messages], rest[messages:]
-    moved_ref, extra_ref, extra_trace_ref, sends = rest[0], rest[1], rest[2], rest[3:]
+    moved_ref, extra_ref, extra_trace_ref, sends = rest[0], rest[1], rest[2], rest[3:3 + messages]
+    traces_ref, = rest[3 + messages:]
     rows = moved_ref.shape[0]
     pieces = BLOCK // LANES
     other = any_other(level, flags_ref)
@@ -466,10 +489,14 @@
 
     @pl.when(other)
     def _():
-        others = other_traces(level, received, joined_ref, count)
-        extra = product(lift_ref[...], stacked_columns(others))
-        extra_ref[...] = extra
-        extra_trace_ref[...] = advanced_traces(extra, trace_grow_ref, weights_ref, rows)
+        gather_received(level, 1, received, joined_ref, count, traces_ref)
+
+        def add_block(here):
+            extra = product(lift_ref[...], stacked_columns(traces_ref[:, here]))
+            extra_ref[:, here] = extra
+            extra_trace_ref[:, here] = advanced_traces(extra, trace_grow_ref, weights_ref[:, here], rows)
+
+        for_blocks(add_block)
         for group, send in enumerate(sends):
             place = send_places_ref[group:group + 1, :]
             more = pick(
@@ -487,9 +514,9 @@
 
 def last_kernel(level, messages, flags_ref, joined_ref, local_ref, weights_ref, lift_ref, lift_first_ref, grow_ref,
                 places_ref, advanced_ref, *rest):
-    received, (final_hbm, final_ref, sent) = rest[:messages], rest[messages:]
+    received, (final_hbm, final_ref, traces_ref, whole_ref, sent) = rest[:messages], rest[messages:]
     count = places_ref.shape[0]
-    comp = final_ref.shape[0] // count
+    comp = final_hbm.shape[0] // count
 
     def finish(whole):
         stacked = stacked_columns(whole)
@@ -514,17 +541,36 @@
         for copy in copies:
             copy.wait()
 
-    def whole_of(others):
-        first = received_traces(level, 0, received, joined_ref, count)
-        whole = local_ref[...] + product(lift_first_ref[...], stacked_columns(first))
-        return whole if others is None else whole + product(lift_ref[...], stacked_columns(others))
-
     other = any_other(level, flags_ref)
-    finish(whole_of(None))
+    first = received_traces(level, 0, received, joined_ref, count)
+    finish(local_ref[...] + product(lift_first_ref[...], stacked_columns(first)))
 
     @pl.when(other)
     def _():
-        finish(whole_of(other_traces(level, received, joined_ref, count)))
+        gather_received(level, 0, received, joined_ref, count, traces_ref)
+
+        def load_block(here):
+            whole_ref[:, here] = local_ref[:, here] + product(lift_ref[...], stacked_columns(traces_ref[:, here]))
+
+        for_blocks(load_block)
+        rows, height = whole_ref.shape[0], 16
+
+        def step(number, carry):
+            start = pl.multiple_of(number * height, height)
+            matrix = jnp.concatenate(
+                [grow_ref[pl.ds(power * rows + start, height), :] for power in range(POWERS)], axis=0)
+            new = summed_powers(product(matrix, stacked_columns(whole_ref[...])), weights_ref, height,
+                                whole_ref[pl.ds(start, height), :])
+            for block in range(count):
+                before = advanced_ref[pl.ds(start, height), block_at(block)]
+                done = settle(level, value_blocks(new), places_ref, before, block)
+                final_ref[pl.ds(start * count + block, height, stride=count), :] = done
+            return carry
+
+        lax.fori_loop(0, rows // height, step, 0)
+        copy = pltpu.make_async_copy(final_ref.at[pl.ds(0, comp * count)], final_hbm, sent.at[0])
+        copy.start()
+        copy.wait()
 
 
 def call(kernel, name, flops, operands, outs, scratch=(), hbm=False, out_hbm=False):
@@ -610,7 +656,7 @@
         moved, extra, extra_trace, *sent = call(
             functools.partial(level_kernel, level, messages, count), "level", 10 ** 8,
             [flags, joined, weights, slot_weights, mix, lift, trace_grow, send_places, send_codes] + received + prepared,
-            [slots, own, traced] + [message] * messages)
+            [slots, own, traced] + [message] * messages, [face_stack])
         arrived, received = received, exchange(sent)
         beside = functools.partial(between_kernel, level + 1, messages)
         operands = [members, joined, places, columns, out, new_trace, moved, extra, extra_trace, heights, loaded,
@@ -627,7 +673,8 @@
     final, = call(
         functools.partial(last_kernel, LEVELS - 1, messages), "last", 10 ** 9,
         [flags, joined, loaded, weights, lift, lift_first, grow, places] + advanced + received,
-        [(flat, f32)], [(flat, f32), pltpu.SemaphoreType.DMA((len(last_chunks(rows)),))], out_hbm=True)
+        [(flat, f32)],
+        [((rows * count, LANES), f32), face_stack, own, pltpu.SemaphoreType.DMA((len(last_chunks(rows)),))], out_hbm=True)
     return final.reshape(1, 1, comp, elements)
 
 

time: 34.7 us -> 34.7 us (level)
  no operation moved by 1% of the time
where the time goes in v10:
time: 34.7 us; the launch traced here: 34.6 us
  Pallas kernels  17.1 us (49%)
  starting transfers between devices  16.5 us (48%)
  waiting for transfers between devices  0.71 us (2%)
    pallas_call x9, Pallas kernels, call(): pl.pallas_call(kernel, out_shape=tuple((jax.ShapeDtypeStruct(shape, dtype...  17.1 us
    ppermute x12, starting transfers between devices, exchange(): lax.ppermute(one, swap[0], swap[1])  16.5 us
    ppermute x12, waiting for transfers between devices, exchange(): lax.ppermute(one, swap[0], swap[1])  0.71 us
  transfers between devices with their start and end apart: 12, of which 3 were waited for; matrix products, arithmetic and copies ran while one was open for 0% of the time, Pallas kernels for 32%

profile of v10, /device:TPU:0, one launch (start us, length us, event | category | flops | bytes accessed | tf_op | source)
XLA Modules:
  0.0 34.6 jit_solution(537325970884491920)
XLA Ops:
  0.0 1.9 %first.1 = (f32[144,1024]{1,0:T(8,128)S(1)}, f32[64,1024]{1,0:T(8,128)S(1)}, f32[60,128]{1,0:T(8,128)S(1)}, f32[60,128]{1,0:T(8,128)S(1)}, f32[60,128]{1,0:T(8,1...) custom-call(f32[1120,128]{1,0:T(8,128)} %bitcast.9, ...), custom_call_target="tpu_custom_call" | custom-call | flops 100000000 | bytes 1048576 | tf_op jit(solution)/shard_map/first/pallas_call | solution.py:581
  1.9 5.5 %collective-permute-start = (f32[60,128]{1,0:T(8,128)S(1)}, f32[60,128]{1,0:T(8,128)S(1)}, u32[]{:S(2)}, u32[]{:S(2)}) collective-permute-start(f32[60,128]{1,0:T(8,128)S(1)} %get-tuple-element.86.refs_11_), channel_id=1, source_target_pairs={{0,30},{2,4},{4,2},{6,8},{8,6},{10,12},{12,10},{14,16},{16,14},{18... | collective-permute-start | bytes 92168 | tf_op jit(solution)/shard_map/ppermute | solution.py:629
  7.4 0.0 collective-permute-start.1
  7.4 1.5 %collective-permute-start.2 = (f32[60,128]{1,0:T(8,128)S(1)}, f32[60,128]{1,0:T(8,128)S(1)}, u32[]{:S(2)}, u32[]{:S(2)}) collective-permute-start(f32[60,128]{1,0:T(8,128)S(1)} %get-tuple-element.88.refs_13_), channel_id=1, source_target_pairs={{0,1},{1,0},{2,3},{3,2},{4,5},{5,4},{6,7},{7,6},{8,9},{9,8},{10,11... | collective-permute-start | bytes 92168 | tf_op jit(solution)/shard_map/ppermute | solution.py:629
  8.9 2.9 %plan.1 = (s32[8,1536]{1,0:T(8,128)S(1)}, s32[8,1536]{1,0:T(8,128)S(1)}, s32[8,128]{1,0:T(8,128)S(1)}, s32[8,128]{1,0:T(8,128)S(1)}, s32[8,128]{1,0:T(8,128)S(1)...) custom-call(f32[60,140]{1,0:T(8,128)S(1)} %get-tuple-element.75.refs, ...), custom_call_target="tpu_custom_call" | custom-call | flops 2000000000 | bytes 1048576 | tf_op jit(solution)/shard_map/plan/pallas_call | solution.py:581
  11.8 0.0 collective-permute-done.rest_0_
  11.8 0.0 collective-permute-done.1.rest_1_
  11.8 0.0 collective-permute-done.2.rest_2_
  11.8 0.5 %level.3 = (f32[64,384]{1,0:T(8,128)S(1)}, f32[144,384]{1,0:T(8,128)S(1)}, f32[64,384]{1,0:T(8,128)S(1)}, f32[60,128]{1,0:T(8,128)S(1)}, f32[60,128]{1,0:T(8,128)S(1)}, /*index=5*/f32[60,128]{1,0:T(8,128)S(1)}) custom-call(f32[4,128]{1,0:T(4,128)S(1)} %get-tuple-element.89.flags_ref, s32[8,1536]{1,0:T(8,128)S(1)} %get-tuple-element.90.joined_ref, ...), custom_call_target="tpu_custom_call" | custom-call | flops 100000000 | bytes 1048576 | tf_op jit(solution)/shard_map/level/pallas_call | solution.py:581
  12.3 1.7 %collective-permute-start.3 = (f32[60,128]{1,0:T(8,128)S(1)}, f32[60,128]{1,0:T(8,128)S(1)}, u32[]{:S(2)}, u32[]{:S(2)}) collective-permute-start(f32[60,128]{1,0:T(8,128)S(1)} %get-tuple-element.111.rest_3_), channel_id=1, source_target_pairs={{0,30},{2,4},{4,2},{6,8},{8,6},{10,12},{12,10},{14,16},{16,14},{18... | collective-permute-start | bytes 92168 | tf_op jit(solution)/shard_map/ppermute | solution.py:629
  14.0 0.0 collective-permute-start.4
  14.0 1.5 %collective-permute-start.5 = (f32[60,128]{1,0:T(8,128)S(1)}, f32[60,128]{1,0:T(8,128)S(1)}, u32[]{:S(2)}, u32[]{:S(2)}) collective-permute-start(f32[60,128]{1,0:T(8,128)S(1)} %get-tuple-element.113.rest_5_), channel_id=1, source_target_pairs={{0,1},{1,0},{2,3},{3,2},{4,5},{5,4},{6,7},{7,6},{8,9},{9,8},{10,11... | collective-permute-start | bytes 92168 | tf_op jit(solution)/shard_map/ppermute | solution.py:629
  15.5 2.8 %between.3 = (f32[64,1024]{1,0:T(8,128)S(1)}, f32[144,384]{1,0:T(8,128)S(1)}, f32[8,384]{1,0:T(8,128)S(1)}, f32[64,384]{1,0:T(8,128)S(1)}, f32[144,1024]{1,0:T(8...) custom-call(s32[8,1536]{1,0:T(8,128)S(1)} %get-tuple-element.91.members_ref, ...), custom_call_target="tpu_custom_call" | custom-call | flops 2000000000 | bytes 1048576 | tf_op jit(solution)/shard_map/between/pallas_call | solution.py:581
  18.3 0.1 collective-permute-done.3.rest_0_
  18.4 0.0 collective-permute-done.4.rest_1_
  18.4 0.0 collective-permute-done.5.rest_2_
  18.4 0.5 %level.4 = (f32[64,384]{1,0:T(8,128)S(1)}, f32[144,384]{1,0:T(8,128)S(1)}, f32[64,384]{1,0:T(8,128)S(1)}, f32[60,128]{1,0:T(8,128)S(1)}, f32[60,128]{1,0:T(8,128)S(1)}, /*index=5*/f32[60,128]{1,0:T(8,128)S(1)}) custom-call(f32[4,128]{1,0:T(4,128)S(1)} %get-tuple-element.89.flags_ref, s32[8,1536]{1,0:T(8,128)S(1)} %get-tuple-element.90.joined_ref, ...), custom_call_target="tpu_custom_call" | custom-call | flops 100000000 | bytes 1048576 | tf_op jit(solution)/shard_map/level/pallas_call | solution.py:581
  19.0 2.0 %collective-permute-start.6 = (f32[60,128]{1,0:T(8,128)S(1)}, f32[60,128]{1,0:T(8,128)S(1)}, u32[]{:S(2)}, u32[]{:S(2)}) collective-permute-start(f32[60,128]{1,0:T(8,128)S(1)} %get-tuple-element.124.rest_3_), channel_id=1, source_target_pairs={{0,30},{2,4},{4,2},{6,8},{8,6},{10,12},{12,10},{14,16},{16,14},{18... | collective-permute-start | bytes 92168 | tf_op jit(solution)/shard_map/ppermute | solution.py:629
  21.0 0.0 collective-permute-start.7
  21.0 1.2 %collective-permute-start.8 = (f32[60,128]{1,0:T(8,128)S(1)}, f32[60,128]{1,0:T(8,128)S(1)}, u32[]{:S(2)}, u32[]{:S(2)}) collective-permute-start(f32[60,128]{1,0:T(8,128)S(1)} %get-tuple-element.126.rest_5_), channel_id=1, source_target_pairs={{0,1},{1,0},{2,3},{3,2},{4,5},{5,4},{6,7},{7,6},{8,9},{9,8},{10,11... | collective-permute-start | bytes 92168 | tf_op jit(solution)/shard_map/ppermute | solution.py:629
  22.2 2.8 %between.4 = (f32[64,1024]{1,0:T(8,128)S(1)}, f32[144,384]{1,0:T(8,128)S(1)}, f32[8,384]{1,0:T(8,128)S(1)}, f32[64,384]{1,0:T(8,128)S(1)}, f32[144,1024]{1,0:T(8...) custom-call(s32[8,1536]{1,0:T(8,128)S(1)} %get-tuple-element.91.members_ref, ...), custom_call_target="tpu_custom_call" | custom-call | flops 2000000000 | bytes 1048576 | tf_op jit(solution)/shard_map/between/pallas_call | solution.py:581
  24.9 0.1 collective-permute-done.6.rest_0_
  25.1 0.0 collective-permute-done.7.rest_1_
  25.1 0.0 collective-permute-done.8.rest_2_
  25.1 0.7 %level.5 = (f32[64,384]{1,0:T(8,128)S(1)}, f32[144,384]{1,0:T(8,128)S(1)}, f32[64,384]{1,0:T(8,128)S(1)}, f32[60,128]{1,0:T(8,128)S(1)}, f32[60,128]{1,0:T(8,128)S(1)}, /*index=5*/f32[60,128]{1,0:T(8,128)S(1)}) custom-call(f32[4,128]{1,0:T(4,128)S(1)} %get-tuple-element.89.flags_ref, s32[8,1536]{1,0:T(8,128)S(1)} %get-tuple-element.90.joined_ref, ...), custom_call_target="tpu_custom_call" | custom-call | flops 100000000 | bytes 1048576 | tf_op jit(solution)/shard_map/level/pallas_call | solution.py:581
  25.8 2.0 %collective-permute-start.9 = (f32[60,128]{1,0:T(8,128)S(1)}, f32[60,128]{1,0:T(8,128)S(1)}, u32[]{:S(2)}, u32[]{:S(2)}) collective-permute-start(f32[60,128]{1,0:T(8,128)S(1)} %get-tuple-element.142), channel_id=1, source_target_pairs={{0,30},{2,4},{4,2},{6,8},{8,6},{10,12},{12,10},{14,16},{16,14},{18... | collective-permute-start | bytes 92168 | tf_op jit(solution)/shard_map/ppermute | solution.py:629
  27.8 0.0 collective-permute-start.10
  27.8 1.2 %collective-permute-start.11 = (f32[60,128]{1,0:T(8,128)S(1)}, f32[60,128]{1,0:T(8,128)S(1)}, u32[]{:S(2)}, u32[]{:S(2)}) collective-permute-start(f32[60,128]{1,0:T(8,128)S(1)} %get-tuple-element.144), channel_id=1, source_target_pairs={{0,1},{1,0},{2,3},{3,2},{4,5},{5,4},{6,7},{7,6},{8,9},{9,8},{10,11... | collective-permute-start | bytes 92168 | tf_op jit(solution)/shard_map/ppermute | solution.py:629
  29.0 2.5 %between.5 = (f32[144,384]{1,0:T(8,128)S(1)}, f32[8,384]{1,0:T(8,128)S(1)}, f32[144,1024]{1,0:T(8,128)S(1)}) custom-call(s32[8,1536]{1,0:T(8,128)S(1)} %get-tuple-element.91.members_ref, s32[8,1536]{1,0:T(8,128)S(1)} %get-tuple-element.90.joined_ref, s32[8,128]{1,0:T(8,128)S(1)} %get-tuple-element.92.places_ref, ...), custom_call_target="tpu_custom_call" | custom-call | flops 2000000000 | bytes 1048576 | tf_op jit(solution)/shard_map/between/pallas_call | solution.py:581
  31.5 0.4 %collective-permute-done.9.rest_0_ = f32[60,128]{1,0:T(8,128)S(1)} collective-permute-done((f32[60,128]{1,0:T(8,128)S(1)}, f32[60,128]{1,0:T(8,128)S(1)}, u32[]{:S(2)}, u32[]{:S(2)}) %collective-permute-start.9) | collective-permute-done | bytes 30752 | tf_op jit(solution)/shard_map/ppermute | solution.py:629
  31.9 0.0 collective-permute-done.10.rest_1_
  31.9 0.0 collective-permute-done.11.rest_2_
  31.9 2.5 %last.1 = f32[1120,128]{1,0:T(8,128)} custom-call(f32[4,128]{1,0:T(4,128)S(1)} %get-tuple-element.89.flags_ref, s32[8,1536]{1,0:T(8,128)S(1)} %get-tuple-element.90.joined_ref, f32[144,384]{1,0:T(8,128)S(1)} %get-tuple-element.139.local_ref, f32[8,384]{1,0:T(8,128)S(1)} %get-tuple-element.140.weights_ref, bf16[144,768]{1,0:T(8,128)(2,1)S(1)} %get-tuple-element.97.lift_ref, ...), custom_call_target="tpu_custom_call" | custom-call | flops 1000000000 | bytes 1048576 | tf_op jit(solution)/shard_map/last/pallas_call | solution.py:581
Async XLA Ops:
  1.9 9.9 %collective-permute-start = (f32[60,128]{1,0:T(8,128)S(1)}, f32[60,128]{1,0:T(8,128)S(1)}, u32[]{:S(2)}, u32[]{:S(2)}) collective-permute-start(f32[60,128]{1,0:T(8,128)S(1)} %get-tuple-element.86.refs_11_), channel_id=1, source_target_pairs={{0,30},{2,4},{4,2},{6,8},{8,6},{10,12},{12,10},{14,16},{16,14},{18... | collective-permute-start | bytes 92168 | tf_op jit(solution)/shard_map/ppermute | solution.py:629
  7.4 4.4 %collective-permute-start.1 = (f32[60,128]{1,0:T(8,128)S(1)}, f32[60,128]{1,0:T(8,128)S(1)}, u32[]{:S(2)}, u32[]{:S(2)}) collective-permute-start(f32[60,128]{1,0:T(8,128)S(1)} %get-tuple-element.87.refs_12_), channel_id=1, source_target_pairs={{0,2},{2,0},{4,6},{6,4},{8,10},{10,8},{12,14},{14,12},{16,18},{18,... | collective-permute-start | bytes 92168 | tf_op jit(solution)/shard_map/ppermute | solution.py:629
  7.4 4.4 %collective-permute-start.2 = (f32[60,128]{1,0:T(8,128)S(1)}, f32[60,128]{1,0:T(8,128)S(1)}, u32[]{:S(2)}, u32[]{:S(2)}) collective-permute-start(f32[60,128]{1,0:T(8,128)S(1)} %get-tuple-element.88.refs_13_), channel_id=1, source_target_pairs={{0,1},{1,0},{2,3},{3,2},{4,5},{5,4},{6,7},{7,6},{8,9},{9,8},{10,11... | collective-permute-start | bytes 92168 | tf_op jit(solution)/shard_map/ppermute | solution.py:629
  12.3 6.1 %collective-permute-start.3 = (f32[60,128]{1,0:T(8,128)S(1)}, f32[60,128]{1,0:T(8,128)S(1)}, u32[]{:S(2)}, u32[]{:S(2)}) collective-permute-start(f32[60,128]{1,0:T(8,128)S(1)} %get-tuple-element.111.rest_3_), channel_id=1, source_target_pairs={{0,30},{2,4},{4,2},{6,8},{8,6},{10,12},{12,10},{14,16},{16,14},{18... | collective-permute-start | bytes 92168 | tf_op jit(solution)/shard_map/ppermute | solution.py:629
  14.0 4.4 %collective-permute-start.4 = (f32[60,128]{1,0:T(8,128)S(1)}, f32[60,128]{1,0:T(8,128)S(1)}, u32[]{:S(2)}, u32[]{:S(2)}) collective-permute-start(f32[60,128]{1,0:T(8,128)S(1)} %get-tuple-element.112.rest_4_), channel_id=1, source_target_pairs={{0,2},{2,0},{4,6},{6,4},{8,10},{10,8},{12,14},{14,12},{16,18},{18,... | collective-permute-start | bytes 92168 | tf_op jit(solution)/shard_map/ppermute | solution.py:629
  14.0 4.4 %collective-permute-start.5 = (f32[60,128]{1,0:T(8,128)S(1)}, f32[60,128]{1,0:T(8,128)S(1)}, u32[]{:S(2)}, u32[]{:S(2)}) collective-permute-start(f32[60,128]{1,0:T(8,128)S(1)} %get-tuple-element.113.rest_5_), channel_id=1, source_target_pairs={{0,1},{1,0},{2,3},{3,2},{4,5},{5,4},{6,7},{7,6},{8,9},{9,8},{10,11... | collective-permute-start | bytes 92168 | tf_op jit(solution)/shard_map/ppermute | solution.py:629
  19.0 6.1 %collective-permute-start.6 = (f32[60,128]{1,0:T(8,128)S(1)}, f32[60,128]{1,0:T(8,128)S(1)}, u32[]{:S(2)}, u32[]{:S(2)}) collective-permute-start(f32[60,128]{1,0:T(8,128)S(1)} %get-tuple-element.124.rest_3_), channel_id=1, source_target_pairs={{0,30},{2,4},{4,2},{6,8},{8,6},{10,12},{12,10},{14,16},{16,14},{18... | collective-permute-start | bytes 92168 | tf_op jit(solution)/shard_map/ppermute | solution.py:629
  21.0 4.1 %collective-permute-start.7 = (f32[60,128]{1,0:T(8,128)S(1)}, f32[60,128]{1,0:T(8,128)S(1)}, u32[]{:S(2)}, u32[]{:S(2)}) collective-permute-start(f32[60,128]{1,0:T(8,128)S(1)} %get-tuple-element.125.rest_4_), channel_id=1, source_target_pairs={{0,2},{2,0},{4,6},{6,4},{8,10},{10,8},{12,14},{14,12},{16,18},{18,... | collective-permute-start | bytes 92168 | tf_op jit(solution)/shard_map/ppermute | solution.py:629
  21.0 4.1 %collective-permute-start.8 = (f32[60,128]{1,0:T(8,128)S(1)}, f32[60,128]{1,0:T(8,128)S(1)}, u32[]{:S(2)}, u32[]{:S(2)}) collective-permute-start(f32[60,128]{1,0:T(8,128)S(1)} %get-tuple-element.126.rest_5_), channel_id=1, source_target_pairs={{0,1},{1,0},{2,3},{3,2},{4,5},{5,4},{6,7},{7,6},{8,9},{9,8},{10,11... | collective-permute-start | bytes 92168 | tf_op jit(solution)/shard_map/ppermute | solution.py:629
  25.8 6.1 %collective-permute-start.9 = (f32[60,128]{1,0:T(8,128)S(1)}, f32[60,128]{1,0:T(8,128)S(1)}, u32[]{:S(2)}, u32[]{:S(2)}) collective-permute-start(f32[60,128]{1,0:T(8,128)S(1)} %get-tuple-element.142), channel_id=1, source_target_pairs={{0,30},{2,4},{4,2},{6,8},{8,6},{10,12},{12,10},{14,16},{16,14},{18... | collective-permute-start | bytes 92168 | tf_op jit(solution)/shard_map/ppermute | solution.py:629
  27.8 4.1 %collective-permute-start.10 = (f32[60,128]{1,0:T(8,128)S(1)}, f32[60,128]{1,0:T(8,128)S(1)}, u32[]{:S(2)}, u32[]{:S(2)}) collective-permute-start(f32[60,128]{1,0:T(8,128)S(1)} %get-tuple-element.143), channel_id=1, source_target_pairs={{0,2},{2,0},{4,6},{6,4},{8,10},{10,8},{12,14},{14,12},{16,18},{18,... | collective-permute-start | bytes 92168 | tf_op jit(solution)/shard_map/ppermute | solution.py:629
  27.8 4.1 %collective-permute-start.11 = (f32[60,128]{1,0:T(8,128)S(1)}, f32[60,128]{1,0:T(8,128)S(1)}, u32[]{:S(2)}, u32[]{:S(2)}) collective-permute-start(f32[60,128]{1,0:T(8,128)S(1)} %get-tuple-element.144), channel_id=1, source_target_pairs={{0,1},{1,0},{2,3},{3,2},{4,5},{5,4},{6,7},{7,6},{8,9},{9,8},{10,11... | collective-permute-start | bytes 92168 | tf_op jit(solution)/shard_map/ppermute | solution.py:629

commit v11 on v10

--- a/solution.py
+++ b/solution.py
@@ -145,14 +145,15 @@
     rows = out_ref.shape[0]
     elements = out_ref.shape[1]
     count = elements // LANES
-    comp = fields_ref.shape[0] // count
+    comp = fields_hbm.shape[0] // count
     cuts = [slice(0, rounded_up(comp // 2, 16)), slice(rounded_up(comp // 2, 16), comp)]
     parts = [pl.ds(cut.start * count, (cut.stop - cut.start) * count) for cut in cuts]
     trace_hbm, send_hbm, *others = given
     trace_ref, send_ref, *others_held = held
     pairs = [(fields_hbm.at[parts[0]], fields_ref.at[parts[0]]), (trace_hbm, trace_ref),
              (fields_hbm.at[parts[1]], fields_ref.at[parts[1]]), (send_hbm, send_ref)]
-    pairs += list(zip(others, others_held))
+    pairs += [(source, target if source.shape == target.shape else target.at[pl.ds(0, source.shape[0])])
+              for source, target in zip(others, others_held)]
     copies = [pltpu.make_async_copy(source, target, arrived.at[i]) for i, (source, target) in enumerate(pairs)]
     for copy in copies:
         copy.start()
@@ -236,14 +237,16 @@
 def matrix_powers(operator_ref, trace_ref, lift_ref, grow_ref, trace_grow_ref, mix_ref, lift_out_ref,
                   lift_first_ref):
     comp = operator_ref.shape[0]
-    trace_comp, faces, _ = lift_ref.shape
+    faces = lift_ref.shape[1]
+    trace_comp = trace_ref.shape[0]
     rows = lift_out_ref.shape[0]
     trace_rows = trace_grow_ref.shape[0] // (POWERS + 1)
     operator = pad_rows(operator_ref[...], rows)
     operator = jnp.concatenate([operator, jnp.zeros((rows, rows - comp), f32)], axis=1)
     traces = pad_rows(trace_ref[...], trace_rows)
     traces = jnp.concatenate([traces, jnp.zeros((trace_rows, rows - comp), f32)], axis=1)
-    lift = jnp.concatenate([pad_rows(lift_ref[:, face, :], trace_rows) for face in range(faces)], axis=0)
+    filled = lax.broadcasted_iota(i32, (trace_rows, comp), 0) < trace_comp
+    lift = jnp.concatenate([jnp.where(filled, lift_ref[:, face, :], 0.0) for face in range(faces)], axis=0)
     lift = pad_rows(jnp.transpose(lift), rows)
     lift_out_ref[...] = stacked_matrix(lift)
     lift_first_ref[...] = stacked_matrix(lift[:, :trace_rows])
@@ -628,7 +631,7 @@
     def exchange(sent):
         return [lax.ppermute(one, swap[0], swap[1]) for one, swap in zip(sent, swaps)]
 
-    message, prepared_message = ((trace, bnd), f32), ((trace_rows, bnd), f32)
+    message = ((trace_rows, bnd), f32)
     own, face_stack = ((rows, BLOCK), f32), ((faces * trace_rows, BLOCK), f32)
     weight, table, traced = ((POWERS, BLOCK), f32), ((trace_rows, elements), f32), ((trace_rows, BLOCK), f32)
     whole = ((rows, elements), f32)
@@ -638,8 +641,9 @@
                  jnp.transpose(lift_map, (2, 0, 1)), tent_height[None]]
     columns, out, *rest = call(
         functools.partial(first_kernel, swaps), "first", 10 ** 8, [fields.reshape(flat)] + arguments,
-        [whole, table] + [message] * messages + [(one.shape, one.dtype) for one in arguments],
-        [(flat, f32), pltpu.SemaphoreType.DMA((ARGUMENTS + 1,))], hbm=True)
+        [whole, table] + [message] * messages
+        + [((trace_rows,) + one.shape[1:] if one.ndim == 3 else one.shape, one.dtype) for one in arguments],
+        [((rows * count, LANES), f32), pltpu.SemaphoreType.DMA((ARGUMENTS + 1,))], hbm=True)
     sent, held = rest[:messages], rest[messages:]
     received = exchange(sent)
     slots = ((trace_rows, messages * LANES), f32)
@@ -650,7 +654,7 @@
          ((POWERS, messages * LANES), f32), ((LEVELS, LANES), f32), own, weight, traced,
          ((POWERS * rows, 3 * rows), bf16), (((POWERS + 1) * trace_rows, 3 * rows), bf16),
          (((POWERS + 1) * trace_rows, 3 * trace_rows), bf16), ((rows, 3 * faces * trace_rows), bf16), ((rows, 3 * trace_rows), bf16), ((1, LANES), f32)]
-        + [prepared_message] * messages, [face_stack])
+        + [message] * messages, [face_stack])
     advanced = []
     for level in range(LEVELS - 1):
         moved, extra, extra_trace, *sent = call(
@@ -665,7 +669,7 @@
         if level + 1 < LEVELS - 1:
             out, loaded, weights, new_trace, *rest = call(
                 beside, "between", 2 * 10 ** 9, operands + sent + advanced,
-                [table, own, weight, traced, whole] + [prepared_message] * messages, scratch)
+                [table, own, weight, traced, whole] + [message] * messages, scratch)
             advanced, prepared = rest[:1], rest[1:]
         else:
             loaded, weights, *advanced = call(

time: 34.7 us -> 34.7 us (level)
  no operation moved by 1% of the time
where the time goes in v11:
time: 34.7 us; the launch traced here: 34.6 us
  Pallas kernels  17.1 us (49%)
  starting transfers between devices  16.5 us (48%)
  waiting for transfers between devices  0.71 us (2%)
    pallas_call x9, Pallas kernels, call(): pl.pallas_call(kernel, out_shape=tuple((jax.ShapeDtypeStruct(shape, dtype...  17.1 us
    ppermute x12, starting transfers between devices, exchange(): lax.ppermute(one, swap[0], swap[1])  16.5 us
    ppermute x12, waiting for transfers between devices, exchange(): lax.ppermute(one, swap[0], swap[1])  0.71 us
  transfers between devices with their start and end apart: 12, of which 3 were waited for; matrix products, arithmetic and copies ran while one was open for 0% of the time, Pallas kernels for 32%

profile of v11, /device:TPU:0, one launch (start us, length us, event | category | flops | bytes accessed | tf_op | source)
XLA Modules:
  0.0 34.6 jit_solution(16486280810901316088)
XLA Ops:
  0.0 1.9 %first.1 = (f32[144,1024]{1,0:T(8,128)S(1)}, f32[64,1024]{1,0:T(8,128)S(1)}, f32[64,128]{1,0:T(8,128)S(1)}, f32[64,128]{1,0:T(8,128)S(1)}, f32[64,128]{1,0:T(8,1...) custom-call(f32[1120,128]{1,0:T(8,128)} %bitcast.9, ...), custom_call_target="tpu_custom_call" | custom-call | flops 100000000 | bytes 1048576 | tf_op jit(solution)/shard_map/first/pallas_call | solution.py:584
  1.9 5.5 %collective-permute-start = (f32[64,128]{1,0:T(8,128)S(1)}, f32[64,128]{1,0:T(8,128)S(1)}, u32[]{:S(2)}, u32[]{:S(2)}) collective-permute-start(f32[64,128]{1,0:T(8,128)S(1)} %get-tuple-element.86.refs_11_), channel_id=1, source_target_pairs={{0,30},{2,4},{4,2},{6,8},{8,6},{10,12},{12,10},{14,16},{16,14},{18... | collective-permute-start | bytes 98312 | tf_op jit(solution)/shard_map/ppermute | solution.py:632
  7.4 0.0 collective-permute-start.1
  7.4 1.5 %collective-permute-start.2 = (f32[64,128]{1,0:T(8,128)S(1)}, f32[64,128]{1,0:T(8,128)S(1)}, u32[]{:S(2)}, u32[]{:S(2)}) collective-permute-start(f32[64,128]{1,0:T(8,128)S(1)} %get-tuple-element.88.refs_13_), channel_id=1, source_target_pairs={{0,1},{1,0},{2,3},{3,2},{4,5},{5,4},{6,7},{7,6},{8,9},{9,8},{10,11... | collective-permute-start | bytes 98312 | tf_op jit(solution)/shard_map/ppermute | solution.py:632
  8.9 2.9 %plan.1 = (s32[8,1536]{1,0:T(8,128)S(1)}, s32[8,1536]{1,0:T(8,128)S(1)}, s32[8,128]{1,0:T(8,128)S(1)}, s32[8,128]{1,0:T(8,128)S(1)}, s32[8,128]{1,0:T(8,128)S(1)...) custom-call(f32[60,140]{1,0:T(8,128)S(1)} %get-tuple-element.75.refs, ...), custom_call_target="tpu_custom_call" | custom-call | flops 2000000000 | bytes 1048576 | tf_op jit(solution)/shard_map/plan/pallas_call | solution.py:584
  11.7 0.0 collective-permute-done.rest_0_
  11.8 0.0 collective-permute-done.1.rest_1_
  11.8 0.0 collective-permute-done.2.rest_2_
  11.8 0.5 %level.3 = (f32[64,384]{1,0:T(8,128)S(1)}, f32[144,384]{1,0:T(8,128)S(1)}, f32[64,384]{1,0:T(8,128)S(1)}, f32[64,128]{1,0:T(8,128)S(1)}, f32[64,128]{1,0:T(8,128)S(1)}, /*index=5*/f32[64,128]{1,0:T(8,128)S(1)}) custom-call(f32[4,128]{1,0:T(4,128)S(1)} %get-tuple-element.89.flags_ref, s32[8,1536]{1,0:T(8,128)S(1)} %get-tuple-element.90.joined_ref, ...), custom_call_target="tpu_custom_call" | custom-call | flops 100000000 | bytes 1048576 | tf_op jit(solution)/shard_map/level/pallas_call | solution.py:584
  12.3 1.7 %collective-permute-start.3 = (f32[64,128]{1,0:T(8,128)S(1)}, f32[64,128]{1,0:T(8,128)S(1)}, u32[]{:S(2)}, u32[]{:S(2)}) collective-permute-start(f32[64,128]{1,0:T(8,128)S(1)} %get-tuple-element.111.rest_3_), channel_id=1, source_target_pairs={{0,30},{2,4},{4,2},{6,8},{8,6},{10,12},{12,10},{14,16},{16,14},{18... | collective-permute-start | bytes 98312 | tf_op jit(solution)/shard_map/ppermute | solution.py:632
  14.0 0.0 collective-permute-start.4
  14.0 1.5 %collective-permute-start.5 = (f32[64,128]{1,0:T(8,128)S(1)}, f32[64,128]{1,0:T(8,128)S(1)}, u32[]{:S(2)}, u32[]{:S(2)}) collective-permute-start(f32[64,128]{1,0:T(8,128)S(1)} %get-tuple-element.113.rest_5_), channel_id=1, source_target_pairs={{0,1},{1,0},{2,3},{3,2},{4,5},{5,4},{6,7},{7,6},{8,9},{9,8},{10,11... | collective-permute-start | bytes 98312 | tf_op jit(solution)/shard_map/ppermute | solution.py:632
  15.5 2.8 %between.3 = (f32[64,1024]{1,0:T(8,128)S(1)}, f32[144,384]{1,0:T(8,128)S(1)}, f32[8,384]{1,0:T(8,128)S(1)}, f32[64,384]{1,0:T(8,128)S(1)}, f32[144,1024]{1,0:T(8...) custom-call(s32[8,1536]{1,0:T(8,128)S(1)} %get-tuple-element.91.members_ref, ...), custom_call_target="tpu_custom_call" | custom-call | flops 2000000000 | bytes 1048576 | tf_op jit(solution)/shard_map/between/pallas_call | solution.py:584
  18.3 0.1 collective-permute-done.3.rest_0_
  18.4 0.0 collective-permute-done.4.rest_1_
  18.4 0.0 collective-permute-done.5.rest_2_
  18.4 0.5 %level.4 = (f32[64,384]{1,0:T(8,128)S(1)}, f32[144,384]{1,0:T(8,128)S(1)}, f32[64,384]{1,0:T(8,128)S(1)}, f32[64,128]{1,0:T(8,128)S(1)}, f32[64,128]{1,0:T(8,128)S(1)}, /*index=5*/f32[64,128]{1,0:T(8,128)S(1)}) custom-call(f32[4,128]{1,0:T(4,128)S(1)} %get-tuple-element.89.flags_ref, s32[8,1536]{1,0:T(8,128)S(1)} %get-tuple-element.90.joined_ref, ...), custom_call_target="tpu_custom_call" | custom-call | flops 100000000 | bytes 1048576 | tf_op jit(solution)/shard_map/level/pallas_call | solution.py:584
  19.0 2.0 %collective-permute-start.6 = (f32[64,128]{1,0:T(8,128)S(1)}, f32[64,128]{1,0:T(8,128)S(1)}, u32[]{:S(2)}, u32[]{:S(2)}) collective-permute-start(f32[64,128]{1,0:T(8,128)S(1)} %get-tuple-element.124.rest_3_), channel_id=1, source_target_pairs={{0,30},{2,4},{4,2},{6,8},{8,6},{10,12},{12,10},{14,16},{16,14},{18... | collective-permute-start | bytes 98312 | tf_op jit(solution)/shard_map/ppermute | solution.py:632
  21.0 0.0 collective-permute-start.7
  21.0 1.2 %collective-permute-start.8 = (f32[64,128]{1,0:T(8,128)S(1)}, f32[64,128]{1,0:T(8,128)S(1)}, u32[]{:S(2)}, u32[]{:S(2)}) collective-permute-start(f32[64,128]{1,0:T(8,128)S(1)} %get-tuple-element.126.rest_5_), channel_id=1, source_target_pairs={{0,1},{1,0},{2,3},{3,2},{4,5},{5,4},{6,7},{7,6},{8,9},{9,8},{10,11... | collective-permute-start | bytes 98312 | tf_op jit(solution)/shard_map/ppermute | solution.py:632
  22.2 2.8 %between.4 = (f32[64,1024]{1,0:T(8,128)S(1)}, f32[144,384]{1,0:T(8,128)S(1)}, f32[8,384]{1,0:T(8,128)S(1)}, f32[64,384]{1,0:T(8,128)S(1)}, f32[144,1024]{1,0:T(8...) custom-call(s32[8,1536]{1,0:T(8,128)S(1)} %get-tuple-element.91.members_ref, ...), custom_call_target="tpu_custom_call" | custom-call | flops 2000000000 | bytes 1048576 | tf_op jit(solution)/shard_map/between/pallas_call | solution.py:584
  24.9 0.1 collective-permute-done.6.rest_0_
  25.1 0.0 collective-permute-done.7.rest_1_
  25.1 0.0 collective-permute-done.8.rest_2_
  25.1 0.7 %level.5 = (f32[64,384]{1,0:T(8,128)S(1)}, f32[144,384]{1,0:T(8,128)S(1)}, f32[64,384]{1,0:T(8,128)S(1)}, f32[64,128]{1,0:T(8,128)S(1)}, f32[64,128]{1,0:T(8,128)S(1)}, /*index=5*/f32[64,128]{1,0:T(8,128)S(1)}) custom-call(f32[4,128]{1,0:T(4,128)S(1)} %get-tuple-element.89.flags_ref, s32[8,1536]{1,0:T(8,128)S(1)} %get-tuple-element.90.joined_ref, ...), custom_call_target="tpu_custom_call" | custom-call | flops 100000000 | bytes 1048576 | tf_op jit(solution)/shard_map/level/pallas_call | solution.py:584
  25.8 2.0 %collective-permute-start.9 = (f32[64,128]{1,0:T(8,128)S(1)}, f32[64,128]{1,0:T(8,128)S(1)}, u32[]{:S(2)}, u32[]{:S(2)}) collective-permute-start(f32[64,128]{1,0:T(8,128)S(1)} %get-tuple-element.142), channel_id=1, source_target_pairs={{0,30},{2,4},{4,2},{6,8},{8,6},{10,12},{12,10},{14,16},{16,14},{18... | collective-permute-start | bytes 98312 | tf_op jit(solution)/shard_map/ppermute | solution.py:632
  27.8 0.0 collective-permute-start.10
  27.8 1.2 %collective-permute-start.11 = (f32[64,128]{1,0:T(8,128)S(1)}, f32[64,128]{1,0:T(8,128)S(1)}, u32[]{:S(2)}, u32[]{:S(2)}) collective-permute-start(f32[64,128]{1,0:T(8,128)S(1)} %get-tuple-element.144), channel_id=1, source_target_pairs={{0,1},{1,0},{2,3},{3,2},{4,5},{5,4},{6,7},{7,6},{8,9},{9,8},{10,11... | collective-permute-start | bytes 98312 | tf_op jit(solution)/shard_map/ppermute | solution.py:632
  29.0 2.5 %between.5 = (f32[144,384]{1,0:T(8,128)S(1)}, f32[8,384]{1,0:T(8,128)S(1)}, f32[144,1024]{1,0:T(8,128)S(1)}) custom-call(s32[8,1536]{1,0:T(8,128)S(1)} %get-tuple-element.91.members_ref, s32[8,1536]{1,0:T(8,128)S(1)} %get-tuple-element.90.joined_ref, s32[8,128]{1,0:T(8,128)S(1)} %get-tuple-element.92.places_ref, ...), custom_call_target="tpu_custom_call" | custom-call | flops 2000000000 | bytes 1048576 | tf_op jit(solution)/shard_map/between/pallas_call | solution.py:584
  31.5 0.4 %collective-permute-done.9.rest_0_ = f32[64,128]{1,0:T(8,128)S(1)} collective-permute-done((f32[64,128]{1,0:T(8,128)S(1)}, f32[64,128]{1,0:T(8,128)S(1)}, u32[]{:S(2)}, u32[]{:S(2)}) %collective-permute-start.9) | collective-permute-done | bytes 32800 | tf_op jit(solution)/shard_map/ppermute | solution.py:632
  31.9 0.0 collective-permute-done.10.rest_1_
  31.9 0.0 collective-permute-done.11.rest_2_
  31.9 2.5 %last.1 = f32[1120,128]{1,0:T(8,128)} custom-call(f32[4,128]{1,0:T(4,128)S(1)} %get-tuple-element.89.flags_ref, s32[8,1536]{1,0:T(8,128)S(1)} %get-tuple-element.90.joined_ref, f32[144,384]{1,0:T(8,128)S(1)} %get-tuple-element.139.local_ref, f32[8,384]{1,0:T(8,128)S(1)} %get-tuple-element.140.weights_ref, bf16[144,768]{1,0:T(8,128)(2,1)S(1)} %get-tuple-element.97.lift_ref, ...), custom_call_target="tpu_custom_call" | custom-call | flops 1000000000 | bytes 1048576 | tf_op jit(solution)/shard_map/last/pallas_call | solution.py:584
Async XLA Ops:
  1.9 9.9 %collective-permute-start = (f32[64,128]{1,0:T(8,128)S(1)}, f32[64,128]{1,0:T(8,128)S(1)}, u32[]{:S(2)}, u32[]{:S(2)}) collective-permute-start(f32[64,128]{1,0:T(8,128)S(1)} %get-tuple-element.86.refs_11_), channel_id=1, source_target_pairs={{0,30},{2,4},{4,2},{6,8},{8,6},{10,12},{12,10},{14,16},{16,14},{18... | collective-permute-start | bytes 98312 | tf_op jit(solution)/shard_map/ppermute | solution.py:632
  7.4 4.4 %collective-permute-start.1 = (f32[64,128]{1,0:T(8,128)S(1)}, f32[64,128]{1,0:T(8,128)S(1)}, u32[]{:S(2)}, u32[]{:S(2)}) collective-permute-start(f32[64,128]{1,0:T(8,128)S(1)} %get-tuple-element.87.refs_12_), channel_id=1, source_target_pairs={{0,2},{2,0},{4,6},{6,4},{8,10},{10,8},{12,14},{14,12},{16,18},{18,... | collective-permute-start | bytes 98312 | tf_op jit(solution)/shard_map/ppermute | solution.py:632
  7.4 4.4 %collective-permute-start.2 = (f32[64,128]{1,0:T(8,128)S(1)}, f32[64,128]{1,0:T(8,128)S(1)}, u32[]{:S(2)}, u32[]{:S(2)}) collective-permute-start(f32[64,128]{1,0:T(8,128)S(1)} %get-tuple-element.88.refs_13_), channel_id=1, source_target_pairs={{0,1},{1,0},{2,3},{3,2},{4,5},{5,4},{6,7},{7,6},{8,9},{9,8},{10,11... | collective-permute-start | bytes 98312 | tf_op jit(solution)/shard_map/ppermute | solution.py:632
  12.3 6.1 %collective-permute-start.3 = (f32[64,128]{1,0:T(8,128)S(1)}, f32[64,128]{1,0:T(8,128)S(1)}, u32[]{:S(2)}, u32[]{:S(2)}) collective-permute-start(f32[64,128]{1,0:T(8,128)S(1)} %get-tuple-element.111.rest_3_), channel_id=1, source_target_pairs={{0,30},{2,4},{4,2},{6,8},{8,6},{10,12},{12,10},{14,16},{16,14},{18... | collective-permute-start | bytes 98312 | tf_op jit(solution)/shard_map/ppermute | solution.py:632
  14.0 4.4 %collective-permute-start.4 = (f32[64,128]{1,0:T(8,128)S(1)}, f32[64,128]{1,0:T(8,128)S(1)}, u32[]{:S(2)}, u32[]{:S(2)}) collective-permute-start(f32[64,128]{1,0:T(8,128)S(1)} %get-tuple-element.112.rest_4_), channel_id=1, source_target_pairs={{0,2},{2,0},{4,6},{6,4},{8,10},{10,8},{12,14},{14,12},{16,18},{18,... | collective-permute-start | bytes 98312 | tf_op jit(solution)/shard_map/ppermute | solution.py:632
  14.0 4.4 %collective-permute-start.5 = (f32[64,128]{1,0:T(8,128)S(1)}, f32[64,128]{1,0:T(8,128)S(1)}, u32[]{:S(2)}, u32[]{:S(2)}) collective-permute-start(f32[64,128]{1,0:T(8,128)S(1)} %get-tuple-element.113.rest_5_), channel_id=1, source_target_pairs={{0,1},{1,0},{2,3},{3,2},{4,5},{5,4},{6,7},{7,6},{8,9},{9,8},{10,11... | collective-permute-start | bytes 98312 | tf_op jit(solution)/shard_map/ppermute | solution.py:632
  19.0 6.1 %collective-permute-start.6 = (f32[64,128]{1,0:T(8,128)S(1)}, f32[64,128]{1,0:T(8,128)S(1)}, u32[]{:S(2)}, u32[]{:S(2)}) collective-permute-start(f32[64,128]{1,0:T(8,128)S(1)} %get-tuple-element.124.rest_3_), channel_id=1, source_target_pairs={{0,30},{2,4},{4,2},{6,8},{8,6},{10,12},{12,10},{14,16},{16,14},{18... | collective-permute-start | bytes 98312 | tf_op jit(solution)/shard_map/ppermute | solution.py:632
  21.0 4.1 %collective-permute-start.7 = (f32[64,128]{1,0:T(8,128)S(1)}, f32[64,128]{1,0:T(8,128)S(1)}, u32[]{:S(2)}, u32[]{:S(2)}) collective-permute-start(f32[64,128]{1,0:T(8,128)S(1)} %get-tuple-element.125.rest_4_), channel_id=1, source_target_pairs={{0,2},{2,0},{4,6},{6,4},{8,10},{10,8},{12,14},{14,12},{16,18},{18,... | collective-permute-start | bytes 98312 | tf_op jit(solution)/shard_map/ppermute | solution.py:632
  21.0 4.1 %collective-permute-start.8 = (f32[64,128]{1,0:T(8,128)S(1)}, f32[64,128]{1,0:T(8,128)S(1)}, u32[]{:S(2)}, u32[]{:S(2)}) collective-permute-start(f32[64,128]{1,0:T(8,128)S(1)} %get-tuple-element.126.rest_5_), channel_id=1, source_target_pairs={{0,1},{1,0},{2,3},{3,2},{4,5},{5,4},{6,7},{7,6},{8,9},{9,8},{10,11... | collective-permute-start | bytes 98312 | tf_op jit(solution)/shard_map/ppermute | solution.py:632
  25.8 6.1 %collective-permute-start.9 = (f32[64,128]{1,0:T(8,128)S(1)}, f32[64,128]{1,0:T(8,128)S(1)}, u32[]{:S(2)}, u32[]{:S(2)}) collective-permute-start(f32[64,128]{1,0:T(8,128)S(1)} %get-tuple-element.142), channel_id=1, source_target_pairs={{0,30},{2,4},{4,2},{6,8},{8,6},{10,12},{12,10},{14,16},{16,14},{18... | collective-permute-start | bytes 98312 | tf_op jit(solution)/shard_map/ppermute | solution.py:632
  27.8 4.1 %collective-permute-start.10 = (f32[64,128]{1,0:T(8,128)S(1)}, f32[64,128]{1,0:T(8,128)S(1)}, u32[]{:S(2)}, u32[]{:S(2)}) collective-permute-start(f32[64,128]{1,0:T(8,128)S(1)} %get-tuple-element.143), channel_id=1, source_target_pairs={{0,2},{2,0},{4,6},{6,4},{8,10},{10,8},{12,14},{14,12},{16,18},{18,... | collective-permute-start | bytes 98312 | tf_op jit(solution)/shard_map/ppermute | solution.py:632
  27.8 4.1 %collective-permute-start.11 = (f32[64,128]{1,0:T(8,128)S(1)}, f32[64,128]{1,0:T(8,128)S(1)}, u32[]{:S(2)}, u32[]{:S(2)}) collective-permute-start(f32[64,128]{1,0:T(8,128)S(1)} %get-tuple-element.144), channel_id=1, source_target_pairs={{0,1},{1,0},{2,3},{3,2},{4,5},{5,4},{6,7},{7,6},{8,9},{9,8},{10,11... | collective-permute-start | bytes 98312 | tf_op jit(solution)/shard_map/ppermute | solution.py:632

commit v12 on v11

--- a/solution.py
+++ b/solution.py
@@ -146,40 +146,26 @@
     elements = out_ref.shape[1]
     count = elements // LANES
     comp = fields_hbm.shape[0] // count
-    cuts = [slice(0, rounded_up(comp // 2, 16)), slice(rounded_up(comp // 2, 16), comp)]
-    parts = [pl.ds(cut.start * count, (cut.stop - cut.start) * count) for cut in cuts]
     trace_hbm, send_hbm, *others = given
     trace_ref, send_ref, *others_held = held
-    pairs = [(fields_hbm.at[parts[0]], fields_ref.at[parts[0]]), (trace_hbm, trace_ref),
-             (fields_hbm.at[parts[1]], fields_ref.at[parts[1]]), (send_hbm, send_ref)]
+    pairs = [(fields_hbm, fields_ref.at[pl.ds(0, comp * count)]), (trace_hbm, trace_ref), (send_hbm, send_ref)]
+    needed = len(pairs)
     pairs += [(source, target if source.shape == target.shape else target.at[pl.ds(0, source.shape[0])])
               for source, target in zip(others, others_held)]
     copies = [pltpu.make_async_copy(source, target, arrived.at[i]) for i, (source, target) in enumerate(pairs)]
     for copy in copies:
         copy.start()
-    total = None
-    for number, cut in enumerate(cuts):
-        if number == 0:
-            copies[0].wait()
-            copies[1].wait()
-            trace = pad_rows(trace_ref[...], rows)
-        else:
-            copies[2].wait()
-        height = cut.stop - cut.start
-        fields = jnp.concatenate(
-            [fields_ref[pl.ds(cut.start * count + b, height, stride=count), :] for b in range(count)], axis=1)
-        trace_high, trace_low = split(trace[:, cut])
-        high, low = split(fields)
-        upper = product(jnp.concatenate([trace_high, trace_low], axis=0), high)
-        part = upper[:rows] + upper[rows:] + product(trace_high, low)
-        total = part if total is None else total + part
-        columns_ref[cut, :] = fields
-    out_ref[...] = total
-    copies[3].wait()
+    for copy in copies[:needed]:
+        copy.wait()
+    trace_high, trace_low = split(pad_rows(trace_ref[...], rows))
+    fields = jnp.concatenate([fields_ref[pl.ds(b, comp, stride=count), :] for b in range(count)], axis=1)
+    high, low = split(fields)
+    upper = product(jnp.concatenate([trace_high, trace_low], axis=0), high)
+    out_ref[...] = upper[:rows] + upper[rows:] + product(trace_high, low)
     for index, send in zip(sent_rows(send_ref, swaps), sends):
         send[...] = pick(ref_blocks(out_ref, count), index, index >> 7)[:send.shape[0]]
-    columns_ref[comp:, :] = jnp.zeros((columns_ref.shape[0] - comp, elements), f32)
-    for copy in copies[4:]:
+    columns_ref[...] = pad_rows(fields, columns_ref.shape[0])
+    for copy in copies[needed:]:
         copy.wait()
 
 
@@ -509,8 +495,8 @@
 
 def last_chunks(rows):
     units = rows // 16
-    first = -(-units * 4 // 9)
-    second = -(-(units - first) * 3 // 5)
+    first = -(-units * 5 // 9)
+    second = -(-(units - first) * 3 // 4)
     bounds = [0, first * 16, (first + second) * 16, rows]
     return [slice(low, high) for low, high in zip(bounds, bounds[1:]) if high > low]
 
@@ -643,7 +629,7 @@
         functools.partial(first_kernel, swaps), "first", 10 ** 8, [fields.reshape(flat)] + arguments,
         [whole, table] + [message] * messages
         + [((trace_rows,) + one.shape[1:] if one.ndim == 3 else one.shape, one.dtype) for one in arguments],
-        [((rows * count, LANES), f32), pltpu.SemaphoreType.DMA((ARGUMENTS + 1,))], hbm=True)
+        [((rows * count, LANES), f32), pltpu.SemaphoreType.DMA((ARGUMENTS,))], hbm=True)
     sent, held = rest[:messages], rest[messages:]
     received = exchange(sent)
     slots = ((trace_rows, messages * LANES), f32)

time: 34.7 us -> 34.7 us (level)
  no operation moved by 1% of the time
where the time goes in v12:
time: 34.7 us; the launch traced here: 34.6 us
  Pallas kernels  17.1 us (49%)
  starting transfers between devices  16.5 us (48%)
  waiting for transfers between devices  0.71 us (2%)
    pallas_call x9, Pallas kernels, call(): pl.pallas_call(kernel, out_shape=tuple((jax.ShapeDtypeStruct(shape, dtype...  17.1 us
    ppermute x12, starting transfers between devices, exchange(): lax.ppermute(one, swap[0], swap[1])  16.5 us
    ppermute x12, waiting for transfers between devices, exchange(): lax.ppermute(one, swap[0], swap[1])  0.71 us
  transfers between devices with their start and end apart: 12, of which 3 were waited for; matrix products, arithmetic and copies ran while one was open for 0% of the time, Pallas kernels for 32%

profile of v12, /device:TPU:0, one launch (start us, length us, event | category | flops | bytes accessed | tf_op | source)
XLA Modules:
  0.0 34.6 jit_solution(6044941557934474080)
XLA Ops:
  0.0 1.8 %first.1 = (f32[144,1024]{1,0:T(8,128)S(1)}, f32[64,1024]{1,0:T(8,128)S(1)}, f32[64,128]{1,0:T(8,128)S(1)}, f32[64,128]{1,0:T(8,128)S(1)}, f32[64,128]{1,0:T(8,1...) custom-call(f32[1120,128]{1,0:T(8,128)} %bitcast.9, ...), custom_call_target="tpu_custom_call" | custom-call | flops 100000000 | bytes 1048576 | tf_op jit(solution)/shard_map/first/pallas_call | solution.py:570
  1.8 5.5 %collective-permute-start = (f32[64,128]{1,0:T(8,128)S(1)}, f32[64,128]{1,0:T(8,128)S(1)}, u32[]{:S(2)}, u32[]{:S(2)}) collective-permute-start(f32[64,128]{1,0:T(8,128)S(1)} %get-tuple-element.86.refs_11_), channel_id=1, source_target_pairs={{0,30},{2,4},{4,2},{6,8},{8,6},{10,12},{12,10},{14,16},{16,14},{18... | collective-permute-start | bytes 98312 | tf_op jit(solution)/shard_map/ppermute | solution.py:618
  7.4 0.0 collective-permute-start.1
  7.4 1.5 %collective-permute-start.2 = (f32[64,128]{1,0:T(8,128)S(1)}, f32[64,128]{1,0:T(8,128)S(1)}, u32[]{:S(2)}, u32[]{:S(2)}) collective-permute-start(f32[64,128]{1,0:T(8,128)S(1)} %get-tuple-element.88.refs_13_), channel_id=1, source_target_pairs={{0,1},{1,0},{2,3},{3,2},{4,5},{5,4},{6,7},{7,6},{8,9},{9,8},{10,11... | collective-permute-start | bytes 98312 | tf_op jit(solution)/shard_map/ppermute | solution.py:618
  8.9 2.9 %plan.1 = (s32[8,1536]{1,0:T(8,128)S(1)}, s32[8,1536]{1,0:T(8,128)S(1)}, s32[8,128]{1,0:T(8,128)S(1)}, s32[8,128]{1,0:T(8,128)S(1)}, s32[8,128]{1,0:T(8,128)S(1)...) custom-call(f32[60,140]{1,0:T(8,128)S(1)} %get-tuple-element.75.refs, ...), custom_call_target="tpu_custom_call" | custom-call | flops 2000000000 | bytes 1048576 | tf_op jit(solution)/shard_map/plan/pallas_call | solution.py:570
  11.7 0.0 collective-permute-done.rest_0_
  11.8 0.0 collective-permute-done.1.rest_1_
  11.8 0.0 collective-permute-done.2.rest_2_
  11.8 0.5 %level.3 = (f32[64,384]{1,0:T(8,128)S(1)}, f32[144,384]{1,0:T(8,128)S(1)}, f32[64,384]{1,0:T(8,128)S(1)}, f32[64,128]{1,0:T(8,128)S(1)}, f32[64,128]{1,0:T(8,128)S(1)}, /*index=5*/f32[64,128]{1,0:T(8,128)S(1)}) custom-call(f32[4,128]{1,0:T(4,128)S(1)} %get-tuple-element.89.flags_ref, s32[8,1536]{1,0:T(8,128)S(1)} %get-tuple-element.90.joined_ref, ...), custom_call_target="tpu_custom_call" | custom-call | flops 100000000 | bytes 1048576 | tf_op jit(solution)/shard_map/level/pallas_call | solution.py:570
  12.3 1.7 %collective-permute-start.3 = (f32[64,128]{1,0:T(8,128)S(1)}, f32[64,128]{1,0:T(8,128)S(1)}, u32[]{:S(2)}, u32[]{:S(2)}) collective-permute-start(f32[64,128]{1,0:T(8,128)S(1)} %get-tuple-element.111.rest_3_), channel_id=1, source_target_pairs={{0,30},{2,4},{4,2},{6,8},{8,6},{10,12},{12,10},{14,16},{16,14},{18... | collective-permute-start | bytes 98312 | tf_op jit(solution)/shard_map/ppermute | solution.py:618
  14.0 0.0 collective-permute-start.4
  14.0 1.5 %collective-permute-start.5 = (f32[64,128]{1,0:T(8,128)S(1)}, f32[64,128]{1,0:T(8,128)S(1)}, u32[]{:S(2)}, u32[]{:S(2)}) collective-permute-start(f32[64,128]{1,0:T(8,128)S(1)} %get-tuple-element.113.rest_5_), channel_id=1, source_target_pairs={{0,1},{1,0},{2,3},{3,2},{4,5},{5,4},{6,7},{7,6},{8,9},{9,8},{10,11... | collective-permute-start | bytes 98312 | tf_op jit(solution)/shard_map/ppermute | solution.py:618
  15.5 2.8 %between.3 = (f32[64,1024]{1,0:T(8,128)S(1)}, f32[144,384]{1,0:T(8,128)S(1)}, f32[8,384]{1,0:T(8,128)S(1)}, f32[64,384]{1,0:T(8,128)S(1)}, f32[144,1024]{1,0:T(8...) custom-call(s32[8,1536]{1,0:T(8,128)S(1)} %get-tuple-element.91.members_ref, ...), custom_call_target="tpu_custom_call" | custom-call | flops 2000000000 | bytes 1048576 | tf_op jit(solution)/shard_map/between/pallas_call | solution.py:570
  18.3 0.1 collective-permute-done.3.rest_0_
  18.4 0.0 collective-permute-done.4.rest_1_
  18.4 0.0 collective-permute-done.5.rest_2_
  18.4 0.5 %level.4 = (f32[64,384]{1,0:T(8,128)S(1)}, f32[144,384]{1,0:T(8,128)S(1)}, f32[64,384]{1,0:T(8,128)S(1)}, f32[64,128]{1,0:T(8,128)S(1)}, f32[64,128]{1,0:T(8,128)S(1)}, /*index=5*/f32[64,128]{1,0:T(8,128)S(1)}) custom-call(f32[4,128]{1,0:T(4,128)S(1)} %get-tuple-element.89.flags_ref, s32[8,1536]{1,0:T(8,128)S(1)} %get-tuple-element.90.joined_ref, ...), custom_call_target="tpu_custom_call" | custom-call | flops 100000000 | bytes 1048576 | tf_op jit(solution)/shard_map/level/pallas_call | solution.py:570
  19.0 2.0 %collective-permute-start.6 = (f32[64,128]{1,0:T(8,128)S(1)}, f32[64,128]{1,0:T(8,128)S(1)}, u32[]{:S(2)}, u32[]{:S(2)}) collective-permute-start(f32[64,128]{1,0:T(8,128)S(1)} %get-tuple-element.124.rest_3_), channel_id=1, source_target_pairs={{0,30},{2,4},{4,2},{6,8},{8,6},{10,12},{12,10},{14,16},{16,14},{18... | collective-permute-start | bytes 98312 | tf_op jit(solution)/shard_map/ppermute | solution.py:618
  21.0 0.0 collective-permute-start.7
  21.0 1.2 %collective-permute-start.8 = (f32[64,128]{1,0:T(8,128)S(1)}, f32[64,128]{1,0:T(8,128)S(1)}, u32[]{:S(2)}, u32[]{:S(2)}) collective-permute-start(f32[64,128]{1,0:T(8,128)S(1)} %get-tuple-element.126.rest_5_), channel_id=1, source_target_pairs={{0,1},{1,0},{2,3},{3,2},{4,5},{5,4},{6,7},{7,6},{8,9},{9,8},{10,11... | collective-permute-start | bytes 98312 | tf_op jit(solution)/shard_map/ppermute | solution.py:618
  22.1 2.8 %between.4 = (f32[64,1024]{1,0:T(8,128)S(1)}, f32[144,384]{1,0:T(8,128)S(1)}, f32[8,384]{1,0:T(8,128)S(1)}, f32[64,384]{1,0:T(8,128)S(1)}, f32[144,1024]{1,0:T(8...) custom-call(s32[8,1536]{1,0:T(8,128)S(1)} %get-tuple-element.91.members_ref, ...), custom_call_target="tpu_custom_call" | custom-call | flops 2000000000 | bytes 1048576 | tf_op jit(solution)/shard_map/between/pallas_call | solution.py:570
  24.9 0.1 collective-permute-done.6.rest_0_
  25.1 0.0 collective-permute-done.7.rest_1_
  25.1 0.0 collective-permute-done.8.rest_2_
  25.1 0.7 %level.5 = (f32[64,384]{1,0:T(8,128)S(1)}, f32[144,384]{1,0:T(8,128)S(1)}, f32[64,384]{1,0:T(8,128)S(1)}, f32[64,128]{1,0:T(8,128)S(1)}, f32[64,128]{1,0:T(8,128)S(1)}, /*index=5*/f32[64,128]{1,0:T(8,128)S(1)}) custom-call(f32[4,128]{1,0:T(4,128)S(1)} %get-tuple-element.89.flags_ref, s32[8,1536]{1,0:T(8,128)S(1)} %get-tuple-element.90.joined_ref, ...), custom_call_target="tpu_custom_call" | custom-call | flops 100000000 | bytes 1048576 | tf_op jit(solution)/shard_map/level/pallas_call | solution.py:570
  25.8 2.0 %collective-permute-start.9 = (f32[64,128]{1,0:T(8,128)S(1)}, f32[64,128]{1,0:T(8,128)S(1)}, u32[]{:S(2)}, u32[]{:S(2)}) collective-permute-start(f32[64,128]{1,0:T(8,128)S(1)} %get-tuple-element.142), channel_id=1, source_target_pairs={{0,30},{2,4},{4,2},{6,8},{8,6},{10,12},{12,10},{14,16},{16,14},{18... | collective-permute-start | bytes 98312 | tf_op jit(solution)/shard_map/ppermute | solution.py:618
  27.8 0.0 collective-permute-start.10
  27.8 1.2 %collective-permute-start.11 = (f32[64,128]{1,0:T(8,128)S(1)}, f32[64,128]{1,0:T(8,128)S(1)}, u32[]{:S(2)}, u32[]{:S(2)}) collective-permute-start(f32[64,128]{1,0:T(8,128)S(1)} %get-tuple-element.144), channel_id=1, source_target_pairs={{0,1},{1,0},{2,3},{3,2},{4,5},{5,4},{6,7},{7,6},{8,9},{9,8},{10,11... | collective-permute-start | bytes 98312 | tf_op jit(solution)/shard_map/ppermute | solution.py:618
  29.0 2.5 %between.5 = (f32[144,384]{1,0:T(8,128)S(1)}, f32[8,384]{1,0:T(8,128)S(1)}, f32[144,1024]{1,0:T(8,128)S(1)}) custom-call(s32[8,1536]{1,0:T(8,128)S(1)} %get-tuple-element.91.members_ref, s32[8,1536]{1,0:T(8,128)S(1)} %get-tuple-element.90.joined_ref, s32[8,128]{1,0:T(8,128)S(1)} %get-tuple-element.92.places_ref, ...), custom_call_target="tpu_custom_call" | custom-call | flops 2000000000 | bytes 1048576 | tf_op jit(solution)/shard_map/between/pallas_call | solution.py:570
  31.5 0.4 %collective-permute-done.9.rest_0_ = f32[64,128]{1,0:T(8,128)S(1)} collective-permute-done((f32[64,128]{1,0:T(8,128)S(1)}, f32[64,128]{1,0:T(8,128)S(1)}, u32[]{:S(2)}, u32[]{:S(2)}) %collective-permute-start.9) | collective-permute-done | bytes 32800 | tf_op jit(solution)/shard_map/ppermute | solution.py:618
  31.9 0.0 collective-permute-done.10.rest_1_
  31.9 0.0 collective-permute-done.11.rest_2_
  31.9 2.5 %last.1 = f32[1120,128]{1,0:T(8,128)} custom-call(f32[4,128]{1,0:T(4,128)S(1)} %get-tuple-element.89.flags_ref, s32[8,1536]{1,0:T(8,128)S(1)} %get-tuple-element.90.joined_ref, f32[144,384]{1,0:T(8,128)S(1)} %get-tuple-element.139.local_ref, f32[8,384]{1,0:T(8,128)S(1)} %get-tuple-element.140.weights_ref, bf16[144,768]{1,0:T(8,128)(2,1)S(1)} %get-tuple-element.97.lift_ref, ...), custom_call_target="tpu_custom_call" | custom-call | flops 1000000000 | bytes 1048576 | tf_op jit(solution)/shard_map/last/pallas_call | solution.py:570
Async XLA Ops:
  1.8 9.9 %collective-permute-start = (f32[64,128]{1,0:T(8,128)S(1)}, f32[64,128]{1,0:T(8,128)S(1)}, u32[]{:S(2)}, u32[]{:S(2)}) collective-permute-start(f32[64,128]{1,0:T(8,128)S(1)} %get-tuple-element.86.refs_11_), channel_id=1, source_target_pairs={{0,30},{2,4},{4,2},{6,8},{8,6},{10,12},{12,10},{14,16},{16,14},{18... | collective-permute-start | bytes 98312 | tf_op jit(solution)/shard_map/ppermute | solution.py:618
  7.4 4.4 %collective-permute-start.1 = (f32[64,128]{1,0:T(8,128)S(1)}, f32[64,128]{1,0:T(8,128)S(1)}, u32[]{:S(2)}, u32[]{:S(2)}) collective-permute-start(f32[64,128]{1,0:T(8,128)S(1)} %get-tuple-element.87.refs_12_), channel_id=1, source_target_pairs={{0,2},{2,0},{4,6},{6,4},{8,10},{10,8},{12,14},{14,12},{16,18},{18,... | collective-permute-start | bytes 98312 | tf_op jit(solution)/shard_map/ppermute | solution.py:618
  7.4 4.4 %collective-permute-start.2 = (f32[64,128]{1,0:T(8,128)S(1)}, f32[64,128]{1,0:T(8,128)S(1)}, u32[]{:S(2)}, u32[]{:S(2)}) collective-permute-start(f32[64,128]{1,0:T(8,128)S(1)} %get-tuple-element.88.refs_13_), channel_id=1, source_target_pairs={{0,1},{1,0},{2,3},{3,2},{4,5},{5,4},{6,7},{7,6},{8,9},{9,8},{10,11... | collective-permute-start | bytes 98312 | tf_op jit(solution)/shard_map/ppermute | solution.py:618
  12.3 6.1 %collective-permute-start.3 = (f32[64,128]{1,0:T(8,128)S(1)}, f32[64,128]{1,0:T(8,128)S(1)}, u32[]{:S(2)}, u32[]{:S(2)}) collective-permute-start(f32[64,128]{1,0:T(8,128)S(1)} %get-tuple-element.111.rest_3_), channel_id=1, source_target_pairs={{0,30},{2,4},{4,2},{6,8},{8,6},{10,12},{12,10},{14,16},{16,14},{18... | collective-permute-start | bytes 98312 | tf_op jit(solution)/shard_map/ppermute | solution.py:618
  14.0 4.4 %collective-permute-start.4 = (f32[64,128]{1,0:T(8,128)S(1)}, f32[64,128]{1,0:T(8,128)S(1)}, u32[]{:S(2)}, u32[]{:S(2)}) collective-permute-start(f32[64,128]{1,0:T(8,128)S(1)} %get-tuple-element.112.rest_4_), channel_id=1, source_target_pairs={{0,2},{2,0},{4,6},{6,4},{8,10},{10,8},{12,14},{14,12},{16,18},{18,... | collective-permute-start | bytes 98312 | tf_op jit(solution)/shard_map/ppermute | solution.py:618
  14.0 4.4 %collective-permute-start.5 = (f32[64,128]{1,0:T(8,128)S(1)}, f32[64,128]{1,0:T(8,128)S(1)}, u32[]{:S(2)}, u32[]{:S(2)}) collective-permute-start(f32[64,128]{1,0:T(8,128)S(1)} %get-tuple-element.113.rest_5_), channel_id=1, source_target_pairs={{0,1},{1,0},{2,3},{3,2},{4,5},{5,4},{6,7},{7,6},{8,9},{9,8},{10,11... | collective-permute-start | bytes 98312 | tf_op jit(solution)/shard_map/ppermute | solution.py:618
  19.0 6.1 %collective-permute-start.6 = (f32[64,128]{1,0:T(8,128)S(1)}, f32[64,128]{1,0:T(8,128)S(1)}, u32[]{:S(2)}, u32[]{:S(2)}) collective-permute-start(f32[64,128]{1,0:T(8,128)S(1)} %get-tuple-element.124.rest_3_), channel_id=1, source_target_pairs={{0,30},{2,4},{4,2},{6,8},{8,6},{10,12},{12,10},{14,16},{16,14},{18... | collective-permute-start | bytes 98312 | tf_op jit(solution)/shard_map/ppermute | solution.py:618
  21.0 4.1 %collective-permute-start.7 = (f32[64,128]{1,0:T(8,128)S(1)}, f32[64,128]{1,0:T(8,128)S(1)}, u32[]{:S(2)}, u32[]{:S(2)}) collective-permute-start(f32[64,128]{1,0:T(8,128)S(1)} %get-tuple-element.125.rest_4_), channel_id=1, source_target_pairs={{0,2},{2,0},{4,6},{6,4},{8,10},{10,8},{12,14},{14,12},{16,18},{18,... | collective-permute-start | bytes 98312 | tf_op jit(solution)/shard_map/ppermute | solution.py:618
  21.0 4.1 %collective-permute-start.8 = (f32[64,128]{1,0:T(8,128)S(1)}, f32[64,128]{1,0:T(8,128)S(1)}, u32[]{:S(2)}, u32[]{:S(2)}) collective-permute-start(f32[64,128]{1,0:T(8,128)S(1)} %get-tuple-element.126.rest_5_), channel_id=1, source_target_pairs={{0,1},{1,0},{2,3},{3,2},{4,5},{5,4},{6,7},{7,6},{8,9},{9,8},{10,11... | collective-permute-start | bytes 98312 | tf_op jit(solution)/shard_map/ppermute | solution.py:618
  25.8 6.1 %collective-permute-start.9 = (f32[64,128]{1,0:T(8,128)S(1)}, f32[64,128]{1,0:T(8,128)S(1)}, u32[]{:S(2)}, u32[]{:S(2)}) collective-permute-start(f32[64,128]{1,0:T(8,128)S(1)} %get-tuple-element.142), channel_id=1, source_target_pairs={{0,30},{2,4},{4,2},{6,8},{8,6},{10,12},{12,10},{14,16},{16,14},{18... | collective-permute-start | bytes 98312 | tf_op jit(solution)/shard_map/ppermute | solution.py:618
  27.8 4.1 %collective-permute-start.10 = (f32[64,128]{1,0:T(8,128)S(1)}, f32[64,128]{1,0:T(8,128)S(1)}, u32[]{:S(2)}, u32[]{:S(2)}) collective-permute-start(f32[64,128]{1,0:T(8,128)S(1)} %get-tuple-element.143), channel_id=1, source_target_pairs={{0,2},{2,0},{4,6},{6,4},{8,10},{10,8},{12,14},{14,12},{16,18},{18,... | collective-permute-start | bytes 98312 | tf_op jit(solution)/shard_map/ppermute | solution.py:618
  27.8 4.1 %collective-permute-start.11 = (f32[64,128]{1,0:T(8,128)S(1)}, f32[64,128]{1,0:T(8,128)S(1)}, u32[]{:S(2)}, u32[]{:S(2)}) collective-permute-start(f32[64,128]{1,0:T(8,128)S(1)} %get-tuple-element.144), channel_id=1, source_target_pairs={{0,1},{1,0},{2,3},{3,2},{4,5},{5,4},{6,7},{7,6},{8,9},{9,8},{10,11... | collective-permute-start | bytes 98312 | tf_op jit(solution)/shard_map/ppermute | solution.py:618

commit v13 on v12

--- a/solution.py
+++ b/solution.py
@@ -387,7 +387,7 @@
 
 
 def between_kernel(level, messages, members_ref, joined_ref, places_ref, columns_ref, old_out_ref, old_trace_ref,
-                   moved_ref, extra_ref, extra_trace_ref, heights_ref, local_ref, old_weights_ref, lift_ref,
+                   moved_ref, heights_ref, local_ref, old_weights_ref, lift_ref,
                    lift_first_ref, grow_ref, trace_grow_ref, send_places_ref, *rest):
     received, rest = rest[:messages], rest[messages:]
     final = level == LEVELS - 1
@@ -408,9 +408,9 @@
         here = block_at(block)
         index = joined_ref[0:1, block_at(done * (BLOCK // LANES) + block)]
         moved = [(count + i, read) for i, read in ref_blocks(moved_ref, messages)]
-        trace_ref[:, here] = old_trace_ref[:, here] + extra_trace_ref[:, here] + pick(
+        trace_ref[:, here] = old_trace_ref[:, here] + pick(
             moved, index, index >> 7, jnp.zeros((old_trace_ref.shape[0], LANES), f32))
-    whole = local_ref[...] + inflow + extra_ref[...]
+    whole = local_ref[...] + inflow
     stacked = stacked_columns(whole)
     chunks = row_chunks(whole.shape[0])
     pieces = BLOCK // LANES
@@ -459,16 +459,15 @@
                  trace_grow_ref, send_places_ref, send_codes_ref, *rest):
     received, rest = rest[:messages], rest[messages:]
     prepared, rest = rest[:messages], rest[messages:]
-    moved_ref, extra_ref, extra_trace_ref, sends = rest[0], rest[1], rest[2], rest[3:3 + messages]
-    traces_ref, = rest[3 + messages:]
+    (_, _), rest = rest[:2], rest[2:]
+    moved_ref, loaded_any, trace_any, sends = rest[0], rest[1], rest[2], rest[3:3 + messages]
+    traces_ref, extra_ref, extra_trace_ref, before_ref, before_trace_ref, moving = rest[3 + messages:]
     rows = moved_ref.shape[0]
     pieces = BLOCK // LANES
     other = any_other(level, flags_ref)
     arrived = jnp.concatenate([pad_rows(ref[...], rows) for ref in received], axis=1)
     stacked = product(mix_ref[...], stacked_columns(arrived))
     moved_ref[...] = summed_powers(stacked[rows:], slot_weights_ref, rows, stacked[:rows])
-    extra_ref[...] = jnp.zeros(extra_ref.shape, f32)
-    extra_trace_ref[...] = jnp.zeros(extra_trace_ref.shape, f32)
     moved = [(count + i, read) for i, read in ref_blocks(moved_ref, messages)]
     for group, (before, send) in enumerate(zip(prepared, sends)):
         place, code = send_places_ref[group:group + 1, :], send_codes_ref[group:group + 1, :]
@@ -486,6 +485,14 @@
             extra_trace_ref[:, here] = advanced_traces(extra, trace_grow_ref, weights_ref[:, here], rows)
 
         for_blocks(add_block)
+        for part, whole, before in ((extra_ref, loaded_any, before_ref), (extra_trace_ref, trace_any, before_trace_ref)):
+            copy = pltpu.make_async_copy(whole, before, moving)
+            copy.start()
+            copy.wait()
+            before[...] = before[...] + part[...]
+            copy = pltpu.make_async_copy(before, whole, moving)
+            copy.start()
+            copy.wait()
         for group, send in enumerate(sends):
             place = send_places_ref[group:group + 1, :]
             more = pick(
@@ -562,7 +569,7 @@
         copy.wait()
 
 
-def call(kernel, name, flops, operands, outs, scratch=(), hbm=False, out_hbm=False):
+def call(kernel, name, flops, operands, outs, scratch=(), hbm=False, out_hbm=False, through=()):
     vmem = pl.BlockSpec(memory_space=pltpu.VMEM)
     given = pl.BlockSpec(memory_space=pltpu.HBM) if hbm else vmem
     if hbm:
@@ -570,8 +577,11 @@
     return pl.pallas_call(
         kernel,
         out_shape=tuple(jax.ShapeDtypeStruct(shape, dtype) for shape, dtype in outs),
-        in_specs=[given] * len(operands),
-        out_specs=tuple([pl.BlockSpec(memory_space=pltpu.HBM) if out_hbm else vmem] * len(outs)),
+        in_specs=[pl.BlockSpec(memory_space=pl.ANY) if i in dict(through) else given for i in range(len(operands))],
+        out_specs=tuple(
+            pl.BlockSpec(memory_space=pltpu.HBM) if out_hbm else
+            pl.BlockSpec(memory_space=pl.ANY) if i in dict(through).values() else vmem for i in range(len(outs))),
+        input_output_aliases=dict(through),
         scratch_shapes=[one if not isinstance(one, tuple) else pltpu.VMEM(*one) for one in scratch],
         compiler_params=pltpu.CompilerParams(vmem_limit_bytes=16 * 1024 * 1024),
         cost_estimate=pl.CostEstimate(flops=flops, bytes_accessed=1 << 20, transcendentals=0),
@@ -643,13 +653,16 @@
         + [message] * messages, [face_stack])
     advanced = []
     for level in range(LEVELS - 1):
-        moved, extra, extra_trace, *sent = call(
+        operands = [flags, joined, weights, slot_weights, mix, lift, trace_grow, send_places, send_codes]
+        operands += received + prepared + [loaded, new_trace]
+        moved, loaded, new_trace, *sent = call(
             functools.partial(level_kernel, level, messages, count), "level", 10 ** 8,
-            [flags, joined, weights, slot_weights, mix, lift, trace_grow, send_places, send_codes] + received + prepared,
-            [slots, own, traced] + [message] * messages, [face_stack])
+            operands, [slots, own, traced] + [message] * messages,
+            [face_stack, own, traced, own, traced, pltpu.SemaphoreType.DMA(())],
+            through=[(len(operands) - 2, 1), (len(operands) - 1, 2)])
         arrived, received = received, exchange(sent)
         beside = functools.partial(between_kernel, level + 1, messages)
-        operands = [members, joined, places, columns, out, new_trace, moved, extra, extra_trace, heights, loaded,
+        operands = [members, joined, places, columns, out, new_trace, moved, heights, loaded,
                     weights, lift, lift_first, grow, trace_grow, send_places] + arrived
         scratch = [face_stack, traced, own]
         if level + 1 < LEVELS - 1:

time: 34.7 us -> 34.8 us (level)
  no operation moved by 1% of the time
where the time goes in v13:
time: 34.8 us; the launch traced here: 34.7 us
  Pallas kernels  17.2 us (49%)
  starting transfers between devices  16.4 us (47%)
  waiting for transfers between devices  0.84 us (2%)
    pallas_call x9, Pallas kernels, call(): pl.pallas_call(kernel, out_shape=tuple((jax.ShapeDtypeStruct(shape, dtype...  17.2 us
    ppermute x12, starting transfers between devices, exchange(): lax.ppermute(one, swap[0], swap[1])  16.4 us
    ppermute x12, waiting for transfers between devices, exchange(): lax.ppermute(one, swap[0], swap[1])  0.84 us
  transfers between devices with their start and end apart: 12, of which 3 were waited for; matrix products, arithmetic and copies ran while one was open for 0% of the time, Pallas kernels for 32%

profile of v13, /device:TPU:0, one launch (start us, length us, event | category | flops | bytes accessed | tf_op | source)
XLA Modules:
  0.0 34.7 jit_solution(12915886814857139115)
XLA Ops:
  0.0 1.8 %first.1 = (f32[144,1024]{1,0:T(8,128)S(1)}, f32[64,1024]{1,0:T(8,128)S(1)}, f32[64,128]{1,0:T(8,128)S(1)}, f32[64,128]{1,0:T(8,128)S(1)}, f32[64,128]{1,0:T(8,1...) custom-call(f32[1120,128]{1,0:T(8,128)} %bitcast.9, ...), custom_call_target="tpu_custom_call" | custom-call | flops 100000000 | bytes 1048576 | tf_op jit(solution)/shard_map/first/pallas_call | solution.py:577
  1.8 5.5 %collective-permute-start = (f32[64,128]{1,0:T(8,128)S(1)}, f32[64,128]{1,0:T(8,128)S(1)}, u32[]{:S(2)}, u32[]{:S(2)}) collective-permute-start(f32[64,128]{1,0:T(8,128)S(1)} %get-tuple-element.86.refs_11_), channel_id=1, source_target_pairs={{0,30},{2,4},{4,2},{6,8},{8,6},{10,12},{12,10},{14,16},{16,14},{18... | collective-permute-start | bytes 98312 | tf_op jit(solution)/shard_map/ppermute | solution.py:628
  7.4 0.0 collective-permute-start.1
  7.4 1.5 %collective-permute-start.2 = (f32[64,128]{1,0:T(8,128)S(1)}, f32[64,128]{1,0:T(8,128)S(1)}, u32[]{:S(2)}, u32[]{:S(2)}) collective-permute-start(f32[64,128]{1,0:T(8,128)S(1)} %get-tuple-element.88.refs_13_), channel_id=1, source_target_pairs={{0,1},{1,0},{2,3},{3,2},{4,5},{5,4},{6,7},{7,6},{8,9},{9,8},{10,11... | collective-permute-start | bytes 98312 | tf_op jit(solution)/shard_map/ppermute | solution.py:628
  8.9 2.9 %plan.1 = (s32[8,1536]{1,0:T(8,128)S(1)}, s32[8,1536]{1,0:T(8,128)S(1)}, s32[8,128]{1,0:T(8,128)S(1)}, s32[8,128]{1,0:T(8,128)S(1)}, s32[8,128]{1,0:T(8,128)S(1)...) custom-call(f32[60,140]{1,0:T(8,128)S(1)} %get-tuple-element.75.refs, ...), custom_call_target="tpu_custom_call" | custom-call | flops 2000000000 | bytes 1048576 | tf_op jit(solution)/shard_map/plan/pallas_call | solution.py:577
  11.8 0.0 collective-permute-done.rest_0_
  11.8 0.0 collective-permute-done.1.rest_1_
  11.8 0.0 collective-permute-done.2.rest_2_
  11.8 0.6 %level.3 = (f32[64,384]{1,0:T(8,128)S(1)}, f32[144,384]{1,0:T(8,128)S(1)}, f32[64,384]{1,0:T(8,128)S(1)}, f32[64,128]{1,0:T(8,128)S(1)}, f32[64,128]{1,0:T(8,128)S(1)}, /*index=5*/f32[64,128]{1,0:T(8,128)S(1)}) custom-call(f32[4,128]{1,0:T(4,128)S(1)} %get-tuple-element.89.flags_ref, ...), custom_call_target="tpu_custom_call", output_to_operand_aliasing={{1}: (15, {}), {2}: (16, {})} | custom-call | flops 100000000 | bytes 1048576 | tf_op jit(solution)/shard_map/level/pallas_call | solution.py:577
  12.4 1.7 %collective-permute-start.3 = (f32[64,128]{1,0:T(8,128)S(1)}, f32[64,128]{1,0:T(8,128)S(1)}, u32[]{:S(2)}, u32[]{:S(2)}) collective-permute-start(f32[64,128]{1,0:T(8,128)S(1)} %get-tuple-element.111.rest_3_), channel_id=1, source_target_pairs={{0,30},{2,4},{4,2},{6,8},{8,6},{10,12},{12,10},{14,16},{16,14},{18... | collective-permute-start | bytes 98312 | tf_op jit(solution)/shard_map/ppermute | solution.py:628
  14.0 0.0 collective-permute-start.4
  14.0 1.5 %collective-permute-start.5 = (f32[64,128]{1,0:T(8,128)S(1)}, f32[64,128]{1,0:T(8,128)S(1)}, u32[]{:S(2)}, u32[]{:S(2)}) collective-permute-start(f32[64,128]{1,0:T(8,128)S(1)} %get-tuple-element.113.rest_5_), channel_id=1, source_target_pairs={{0,1},{1,0},{2,3},{3,2},{4,5},{5,4},{6,7},{7,6},{8,9},{9,8},{10,11... | collective-permute-start | bytes 98312 | tf_op jit(solution)/shard_map/ppermute | solution.py:628
  15.5 2.8 %between.3 = (f32[64,1024]{1,0:T(8,128)S(1)}, f32[144,384]{1,0:T(8,128)S(1)}, f32[8,384]{1,0:T(8,128)S(1)}, f32[64,384]{1,0:T(8,128)S(1)}, f32[144,1024]{1,0:T(8...) custom-call(s32[8,1536]{1,0:T(8,128)S(1)} %get-tuple-element.91.members_ref, ...), custom_call_target="tpu_custom_call" | custom-call | flops 2000000000 | bytes 1048576 | tf_op jit(solution)/shard_map/between/pallas_call | solution.py:577
  18.3 0.2 collective-permute-done.3.rest_0_
  18.5 0.0 collective-permute-done.4.rest_1_
  18.5 0.0 collective-permute-done.5.rest_2_
  18.5 0.6 %level.4 = (f32[64,384]{1,0:T(8,128)S(1)}, f32[144,384]{1,0:T(8,128)S(1)}, f32[64,384]{1,0:T(8,128)S(1)}, f32[64,128]{1,0:T(8,128)S(1)}, f32[64,128]{1,0:T(8,128)S(1)}, /*index=5*/f32[64,128]{1,0:T(8,128)S(1)}) custom-call(f32[4,128]{1,0:T(4,128)S(1)} %get-tuple-element.89.flags_ref, ...), custom_call_target="tpu_custom_call", output_to_operand_aliasing={{1}: (15, {}), {2}: (16, {})} | custom-call | flops 100000000 | bytes 1048576 | tf_op jit(solution)/shard_map/level/pallas_call | solution.py:577
  19.0 2.0 %collective-permute-start.6 = (f32[64,128]{1,0:T(8,128)S(1)}, f32[64,128]{1,0:T(8,128)S(1)}, u32[]{:S(2)}, u32[]{:S(2)}) collective-permute-start(f32[64,128]{1,0:T(8,128)S(1)} %get-tuple-element.124.rest_3_), channel_id=1, source_target_pairs={{0,30},{2,4},{4,2},{6,8},{8,6},{10,12},{12,10},{14,16},{16,14},{18... | collective-permute-start | bytes 98312 | tf_op jit(solution)/shard_map/ppermute | solution.py:628
  21.0 0.0 collective-permute-start.7
  21.0 1.2 %collective-permute-start.8 = (f32[64,128]{1,0:T(8,128)S(1)}, f32[64,128]{1,0:T(8,128)S(1)}, u32[]{:S(2)}, u32[]{:S(2)}) collective-permute-start(f32[64,128]{1,0:T(8,128)S(1)} %get-tuple-element.126.rest_5_), channel_id=1, source_target_pairs={{0,1},{1,0},{2,3},{3,2},{4,5},{5,4},{6,7},{7,6},{8,9},{9,8},{10,11... | collective-permute-start | bytes 98312 | tf_op jit(solution)/shard_map/ppermute | solution.py:628
  22.2 2.8 %between.4 = (f32[64,1024]{1,0:T(8,128)S(1)}, f32[144,384]{1,0:T(8,128)S(1)}, f32[8,384]{1,0:T(8,128)S(1)}, f32[64,384]{1,0:T(8,128)S(1)}, f32[144,1024]{1,0:T(8...) custom-call(s32[8,1536]{1,0:T(8,128)S(1)} %get-tuple-element.91.members_ref, ...), custom_call_target="tpu_custom_call" | custom-call | flops 2000000000 | bytes 1048576 | tf_op jit(solution)/shard_map/between/pallas_call | solution.py:577
  25.0 0.2 collective-permute-done.6.rest_0_
  25.1 0.0 collective-permute-done.7.rest_1_
  25.2 0.0 collective-permute-done.8.rest_2_
  25.2 0.7 %level.5 = (f32[64,384]{1,0:T(8,128)S(1)}, f32[144,384]{1,0:T(8,128)S(1)}, f32[64,384]{1,0:T(8,128)S(1)}, f32[64,128]{1,0:T(8,128)S(1)}, f32[64,128]{1,0:T(8,128)S(1)}, /*index=5*/f32[64,128]{1,0:T(8,128)S(1)}) custom-call(f32[4,128]{1,0:T(4,128)S(1)} %get-tuple-element.89.flags_ref, ...), custom_call_target="tpu_custom_call", output_to_operand_aliasing={{1}: (15, {}), {2}: (16, {})} | custom-call | flops 100000000 | bytes 1048576 | tf_op jit(solution)/shard_map/level/pallas_call | solution.py:577
  25.9 2.0 %collective-permute-start.9 = (f32[64,128]{1,0:T(8,128)S(1)}, f32[64,128]{1,0:T(8,128)S(1)}, u32[]{:S(2)}, u32[]{:S(2)}) collective-permute-start(f32[64,128]{1,0:T(8,128)S(1)} %get-tuple-element.142), channel_id=1, source_target_pairs={{0,30},{2,4},{4,2},{6,8},{8,6},{10,12},{12,10},{14,16},{16,14},{18... | collective-permute-start | bytes 98312 | tf_op jit(solution)/shard_map/ppermute | solution.py:628
  27.8 0.0 collective-permute-start.10
  27.8 1.2 %collective-permute-start.11 = (f32[64,128]{1,0:T(8,128)S(1)}, f32[64,128]{1,0:T(8,128)S(1)}, u32[]{:S(2)}, u32[]{:S(2)}) collective-permute-start(f32[64,128]{1,0:T(8,128)S(1)} %get-tuple-element.144), channel_id=1, source_target_pairs={{0,1},{1,0},{2,3},{3,2},{4,5},{5,4},{6,7},{7,6},{8,9},{9,8},{10,11... | collective-permute-start | bytes 98312 | tf_op jit(solution)/shard_map/ppermute | solution.py:628
  29.0 2.5 %between.5 = (f32[144,384]{1,0:T(8,128)S(1)}, f32[8,384]{1,0:T(8,128)S(1)}, f32[144,1024]{1,0:T(8,128)S(1)}) custom-call(s32[8,1536]{1,0:T(8,128)S(1)} %get-tuple-element.91.members_ref, s32[8,1536]{1,0:T(8,128)S(1)} %get-tuple-element.90.joined_ref, s32[8,128]{1,0:T(8,128)S(1)} %get-tuple-element.92.places_ref, ...), custom_call_target="tpu_custom_call" | custom-call | flops 2000000000 | bytes 1048576 | tf_op jit(solution)/shard_map/between/pallas_call | solution.py:577
  31.5 0.5 %collective-permute-done.9.rest_0_ = f32[64,128]{1,0:T(8,128)S(1)} collective-permute-done((f32[64,128]{1,0:T(8,128)S(1)}, f32[64,128]{1,0:T(8,128)S(1)}, u32[]{:S(2)}, u32[]{:S(2)}) %collective-permute-start.9) | collective-permute-done | bytes 32800 | tf_op jit(solution)/shard_map/ppermute | solution.py:628
  32.0 0.0 collective-permute-done.10.rest_1_
  32.0 0.0 collective-permute-done.11.rest_2_
  32.0 2.5 %last.1 = f32[1120,128]{1,0:T(8,128)} custom-call(f32[4,128]{1,0:T(4,128)S(1)} %get-tuple-element.89.flags_ref, s32[8,1536]{1,0:T(8,128)S(1)} %get-tuple-element.90.joined_ref, f32[144,384]{1,0:T(8,128)S(1)} %get-tuple-element.139.local_ref, f32[8,384]{1,0:T(8,128)S(1)} %get-tuple-element.140.weights_ref, bf16[144,768]{1,0:T(8,128)(2,1)S(1)} %get-tuple-element.96.lift_ref, ...), custom_call_target="tpu_custom_call" | custom-call | flops 1000000000 | bytes 1048576 | tf_op jit(solution)/shard_map/last/pallas_call | solution.py:577
Async XLA Ops:
  1.8 9.9 %collective-permute-start = (f32[64,128]{1,0:T(8,128)S(1)}, f32[64,128]{1,0:T(8,128)S(1)}, u32[]{:S(2)}, u32[]{:S(2)}) collective-permute-start(f32[64,128]{1,0:T(8,128)S(1)} %get-tuple-element.86.refs_11_), channel_id=1, source_target_pairs={{0,30},{2,4},{4,2},{6,8},{8,6},{10,12},{12,10},{14,16},{16,14},{18... | collective-permute-start | bytes 98312 | tf_op jit(solution)/shard_map/ppermute | solution.py:628
  7.4 4.4 %collective-permute-start.1 = (f32[64,128]{1,0:T(8,128)S(1)}, f32[64,128]{1,0:T(8,128)S(1)}, u32[]{:S(2)}, u32[]{:S(2)}) collective-permute-start(f32[64,128]{1,0:T(8,128)S(1)} %get-tuple-element.87.refs_12_), channel_id=1, source_target_pairs={{0,2},{2,0},{4,6},{6,4},{8,10},{10,8},{12,14},{14,12},{16,18},{18,... | collective-permute-start | bytes 98312 | tf_op jit(solution)/shard_map/ppermute | solution.py:628
  7.4 4.4 %collective-permute-start.2 = (f32[64,128]{1,0:T(8,128)S(1)}, f32[64,128]{1,0:T(8,128)S(1)}, u32[]{:S(2)}, u32[]{:S(2)}) collective-permute-start(f32[64,128]{1,0:T(8,128)S(1)} %get-tuple-element.88.refs_13_), channel_id=1, source_target_pairs={{0,1},{1,0},{2,3},{3,2},{4,5},{5,4},{6,7},{7,6},{8,9},{9,8},{10,11... | collective-permute-start | bytes 98312 | tf_op jit(solution)/shard_map/ppermute | solution.py:628
  12.4 6.1 %collective-permute-start.3 = (f32[64,128]{1,0:T(8,128)S(1)}, f32[64,128]{1,0:T(8,128)S(1)}, u32[]{:S(2)}, u32[]{:S(2)}) collective-permute-start(f32[64,128]{1,0:T(8,128)S(1)} %get-tuple-element.111.rest_3_), channel_id=1, source_target_pairs={{0,30},{2,4},{4,2},{6,8},{8,6},{10,12},{12,10},{14,16},{16,14},{18... | collective-permute-start | bytes 98312 | tf_op jit(solution)/shard_map/ppermute | solution.py:628
  14.0 4.5 %collective-permute-start.4 = (f32[64,128]{1,0:T(8,128)S(1)}, f32[64,128]{1,0:T(8,128)S(1)}, u32[]{:S(2)}, u32[]{:S(2)}) collective-permute-start(f32[64,128]{1,0:T(8,128)S(1)} %get-tuple-element.112.rest_4_), channel_id=1, source_target_pairs={{0,2},{2,0},{4,6},{6,4},{8,10},{10,8},{12,14},{14,12},{16,18},{18,... | collective-permute-start | bytes 98312 | tf_op jit(solution)/shard_map/ppermute | solution.py:628
  14.0 4.5 %collective-permute-start.5 = (f32[64,128]{1,0:T(8,128)S(1)}, f32[64,128]{1,0:T(8,128)S(1)}, u32[]{:S(2)}, u32[]{:S(2)}) collective-permute-start(f32[64,128]{1,0:T(8,128)S(1)} %get-tuple-element.113.rest_5_), channel_id=1, source_target_pairs={{0,1},{1,0},{2,3},{3,2},{4,5},{5,4},{6,7},{7,6},{8,9},{9,8},{10,11... | collective-permute-start | bytes 98312 | tf_op jit(solution)/shard_map/ppermute | solution.py:628
  19.0 6.1 %collective-permute-start.6 = (f32[64,128]{1,0:T(8,128)S(1)}, f32[64,128]{1,0:T(8,128)S(1)}, u32[]{:S(2)}, u32[]{:S(2)}) collective-permute-start(f32[64,128]{1,0:T(8,128)S(1)} %get-tuple-element.124.rest_3_), channel_id=1, source_target_pairs={{0,30},{2,4},{4,2},{6,8},{8,6},{10,12},{12,10},{14,16},{16,14},{18... | collective-permute-start | bytes 98312 | tf_op jit(solution)/shard_map/ppermute | solution.py:628
  21.0 4.2 %collective-permute-start.7 = (f32[64,128]{1,0:T(8,128)S(1)}, f32[64,128]{1,0:T(8,128)S(1)}, u32[]{:S(2)}, u32[]{:S(2)}) collective-permute-start(f32[64,128]{1,0:T(8,128)S(1)} %get-tuple-element.125.rest_4_), channel_id=1, source_target_pairs={{0,2},{2,0},{4,6},{6,4},{8,10},{10,8},{12,14},{14,12},{16,18},{18,... | collective-permute-start | bytes 98312 | tf_op jit(solution)/shard_map/ppermute | solution.py:628
  21.0 4.2 %collective-permute-start.8 = (f32[64,128]{1,0:T(8,128)S(1)}, f32[64,128]{1,0:T(8,128)S(1)}, u32[]{:S(2)}, u32[]{:S(2)}) collective-permute-start(f32[64,128]{1,0:T(8,128)S(1)} %get-tuple-element.126.rest_5_), channel_id=1, source_target_pairs={{0,1},{1,0},{2,3},{3,2},{4,5},{5,4},{6,7},{7,6},{8,9},{9,8},{10,11... | collective-permute-start | bytes 98312 | tf_op jit(solution)/shard_map/ppermute | solution.py:628
  25.9 6.1 %collective-permute-start.9 = (f32[64,128]{1,0:T(8,128)S(1)}, f32[64,128]{1,0:T(8,128)S(1)}, u32[]{:S(2)}, u32[]{:S(2)}) collective-permute-start(f32[64,128]{1,0:T(8,128)S(1)} %get-tuple-element.142), channel_id=1, source_target_pairs={{0,30},{2,4},{4,2},{6,8},{8,6},{10,12},{12,10},{14,16},{16,14},{18... | collective-permute-start | bytes 98312 | tf_op jit(solution)/shard_map/ppermute | solution.py:628
  27.8 4.1 %collective-permute-start.10 = (f32[64,128]{1,0:T(8,128)S(1)}, f32[64,128]{1,0:T(8,128)S(1)}, u32[]{:S(2)}, u32[]{:S(2)}) collective-permute-start(f32[64,128]{1,0:T(8,128)S(1)} %get-tuple-element.143), channel_id=1, source_target_pairs={{0,2},{2,0},{4,6},{6,4},{8,10},{10,8},{12,14},{14,12},{16,18},{18,... | collective-permute-start | bytes 98312 | tf_op jit(solution)/shard_map/ppermute | solution.py:628
  27.8 4.1 %collective-permute-start.11 = (f32[64,128]{1,0:T(8,128)S(1)}, f32[64,128]{1,0:T(8,128)S(1)}, u32[]{:S(2)}, u32[]{:S(2)}) collective-permute-start(f32[64,128]{1,0:T(8,128)S(1)} %get-tuple-element.144), channel_id=1, source_target_pairs={{0,1},{1,0},{2,3},{3,2},{4,5},{5,4},{6,7},{7,6},{8,9},{9,8},{10,11... | collective-permute-start | bytes 98312 | tf_op jit(solution)/shard_map/ppermute | solution.py:628

commit v14 on v12

--- a/solution.py
+++ b/solution.py
@@ -15,7 +15,7 @@
 LANES = 128
 NO_GROUP = 1 << 20
 ARGUMENTS = 10
-ROW_CHUNK = 48
+ROW_CHUNK = 144
 
 f32, bf16, i32 = jnp.float32, jnp.bfloat16, jnp.int32
 precise = lax.Precision.HIGHEST

time: 34.7 us -> 34.7 us (level)
  no operation moved by 1% of the time
where the time goes in v14:
time: 34.7 us; the launch traced here: 34.6 us
  Pallas kernels  17.2 us (50%)
  starting transfers between devices  16.5 us (48%)
  waiting for transfers between devices  0.63 us (2%)
    pallas_call x9, Pallas kernels, call(): pl.pallas_call(kernel, out_shape=tuple((jax.ShapeDtypeStruct(shape, dtype...  17.2 us
    ppermute x12, starting transfers between devices, exchange(): lax.ppermute(one, swap[0], swap[1])  16.5 us
  transfers between devices with their start and end apart: 12, of which 3 were waited for; matrix products, arithmetic and copies ran while one was open for 0% of the time, Pallas kernels for 32%

profile of v14, /device:TPU:0, one launch (start us, length us, event | category | flops | bytes accessed | tf_op | source)
XLA Modules:
  0.0 34.6 jit_solution(13797958340817850041)
XLA Ops:
  0.0 1.8 %first.1 = (f32[144,1024]{1,0:T(8,128)S(1)}, f32[64,1024]{1,0:T(8,128)S(1)}, f32[64,128]{1,0:T(8,128)S(1)}, f32[64,128]{1,0:T(8,128)S(1)}, f32[64,128]{1,0:T(8,1...) custom-call(f32[1120,128]{1,0:T(8,128)} %bitcast.9, ...), custom_call_target="tpu_custom_call" | custom-call | flops 100000000 | bytes 1048576 | tf_op jit(solution)/shard_map/first/pallas_call | solution.py:570
  1.8 5.5 %collective-permute-start = (f32[64,128]{1,0:T(8,128)S(1)}, f32[64,128]{1,0:T(8,128)S(1)}, u32[]{:S(2)}, u32[]{:S(2)}) collective-permute-start(f32[64,128]{1,0:T(8,128)S(1)} %get-tuple-element.86.refs_11_), channel_id=1, source_target_pairs={{0,30},{2,4},{4,2},{6,8},{8,6},{10,12},{12,10},{14,16},{16,14},{18... | collective-permute-start | bytes 98312 | tf_op jit(solution)/shard_map/ppermute | solution.py:618
  7.4 0.0 collective-permute-start.1
  7.4 1.5 %collective-permute-start.2 = (f32[64,128]{1,0:T(8,128)S(1)}, f32[64,128]{1,0:T(8,128)S(1)}, u32[]{:S(2)}, u32[]{:S(2)}) collective-permute-start(f32[64,128]{1,0:T(8,128)S(1)} %get-tuple-element.88.refs_13_), channel_id=1, source_target_pairs={{0,1},{1,0},{2,3},{3,2},{4,5},{5,4},{6,7},{7,6},{8,9},{9,8},{10,11... | collective-permute-start | bytes 98312 | tf_op jit(solution)/shard_map/ppermute | solution.py:618
  8.9 2.9 %plan.1 = (s32[8,1536]{1,0:T(8,128)S(1)}, s32[8,1536]{1,0:T(8,128)S(1)}, s32[8,128]{1,0:T(8,128)S(1)}, s32[8,128]{1,0:T(8,128)S(1)}, s32[8,128]{1,0:T(8,128)S(1)...) custom-call(f32[60,140]{1,0:T(8,128)S(1)} %get-tuple-element.75.refs, ...), custom_call_target="tpu_custom_call" | custom-call | flops 2000000000 | bytes 1048576 | tf_op jit(solution)/shard_map/plan/pallas_call | solution.py:570
  11.7 0.0 collective-permute-done.rest_0_
  11.8 0.0 collective-permute-done.1.rest_1_
  11.8 0.0 collective-permute-done.2.rest_2_
  11.8 0.5 %level.3 = (f32[64,384]{1,0:T(8,128)S(1)}, f32[144,384]{1,0:T(8,128)S(1)}, f32[64,384]{1,0:T(8,128)S(1)}, f32[64,128]{1,0:T(8,128)S(1)}, f32[64,128]{1,0:T(8,128)S(1)}, /*index=5*/f32[64,128]{1,0:T(8,128)S(1)}) custom-call(f32[4,128]{1,0:T(4,128)S(1)} %get-tuple-element.89.flags_ref, s32[8,1536]{1,0:T(8,128)S(1)} %get-tuple-element.90.joined_ref, ...), custom_call_target="tpu_custom_call" | custom-call | flops 100000000 | bytes 1048576 | tf_op jit(solution)/shard_map/level/pallas_call | solution.py:570
  12.3 1.7 %collective-permute-start.3 = (f32[64,128]{1,0:T(8,128)S(1)}, f32[64,128]{1,0:T(8,128)S(1)}, u32[]{:S(2)}, u32[]{:S(2)}) collective-permute-start(f32[64,128]{1,0:T(8,128)S(1)} %get-tuple-element.111.rest_3_), channel_id=1, source_target_pairs={{0,30},{2,4},{4,2},{6,8},{8,6},{10,12},{12,10},{14,16},{16,14},{18... | collective-permute-start | bytes 98312 | tf_op jit(solution)/shard_map/ppermute | solution.py:618
  14.0 0.0 collective-permute-start.4
  14.0 1.5 %collective-permute-start.5 = (f32[64,128]{1,0:T(8,128)S(1)}, f32[64,128]{1,0:T(8,128)S(1)}, u32[]{:S(2)}, u32[]{:S(2)}) collective-permute-start(f32[64,128]{1,0:T(8,128)S(1)} %get-tuple-element.113.rest_5_), channel_id=1, source_target_pairs={{0,1},{1,0},{2,3},{3,2},{4,5},{5,4},{6,7},{7,6},{8,9},{9,8},{10,11... | collective-permute-start | bytes 98312 | tf_op jit(solution)/shard_map/ppermute | solution.py:618
  15.5 2.8 %between.3 = (f32[64,1024]{1,0:T(8,128)S(1)}, f32[144,384]{1,0:T(8,128)S(1)}, f32[8,384]{1,0:T(8,128)S(1)}, f32[64,384]{1,0:T(8,128)S(1)}, f32[144,1024]{1,0:T(8...) custom-call(s32[8,1536]{1,0:T(8,128)S(1)} %get-tuple-element.91.members_ref, ...), custom_call_target="tpu_custom_call" | custom-call | flops 2000000000 | bytes 1048576 | tf_op jit(solution)/shard_map/between/pallas_call | solution.py:570
  18.3 0.1 collective-permute-done.3.rest_0_
  18.4 0.0 collective-permute-done.4.rest_1_
  18.4 0.0 collective-permute-done.5.rest_2_
  18.4 0.5 %level.4 = (f32[64,384]{1,0:T(8,128)S(1)}, f32[144,384]{1,0:T(8,128)S(1)}, f32[64,384]{1,0:T(8,128)S(1)}, f32[64,128]{1,0:T(8,128)S(1)}, f32[64,128]{1,0:T(8,128)S(1)}, /*index=5*/f32[64,128]{1,0:T(8,128)S(1)}) custom-call(f32[4,128]{1,0:T(4,128)S(1)} %get-tuple-element.89.flags_ref, s32[8,1536]{1,0:T(8,128)S(1)} %get-tuple-element.90.joined_ref, ...), custom_call_target="tpu_custom_call" | custom-call | flops 100000000 | bytes 1048576 | tf_op jit(solution)/shard_map/level/pallas_call | solution.py:570
  19.0 2.0 %collective-permute-start.6 = (f32[64,128]{1,0:T(8,128)S(1)}, f32[64,128]{1,0:T(8,128)S(1)}, u32[]{:S(2)}, u32[]{:S(2)}) collective-permute-start(f32[64,128]{1,0:T(8,128)S(1)} %get-tuple-element.124.rest_3_), channel_id=1, source_target_pairs={{0,30},{2,4},{4,2},{6,8},{8,6},{10,12},{12,10},{14,16},{16,14},{18... | collective-permute-start | bytes 98312 | tf_op jit(solution)/shard_map/ppermute | solution.py:618
  21.0 0.0 collective-permute-start.7
  21.0 1.1 %collective-permute-start.8 = (f32[64,128]{1,0:T(8,128)S(1)}, f32[64,128]{1,0:T(8,128)S(1)}, u32[]{:S(2)}, u32[]{:S(2)}) collective-permute-start(f32[64,128]{1,0:T(8,128)S(1)} %get-tuple-element.126.rest_5_), channel_id=1, source_target_pairs={{0,1},{1,0},{2,3},{3,2},{4,5},{5,4},{6,7},{7,6},{8,9},{9,8},{10,11... | collective-permute-start | bytes 98312 | tf_op jit(solution)/shard_map/ppermute | solution.py:618
  22.1 2.9 %between.4 = (f32[64,1024]{1,0:T(8,128)S(1)}, f32[144,384]{1,0:T(8,128)S(1)}, f32[8,384]{1,0:T(8,128)S(1)}, f32[64,384]{1,0:T(8,128)S(1)}, f32[144,1024]{1,0:T(8...) custom-call(s32[8,1536]{1,0:T(8,128)S(1)} %get-tuple-element.91.members_ref, ...), custom_call_target="tpu_custom_call" | custom-call | flops 2000000000 | bytes 1048576 | tf_op jit(solution)/shard_map/between/pallas_call | solution.py:570
  25.0 0.1 collective-permute-done.6.rest_0_
  25.1 0.0 collective-permute-done.7.rest_1_
  25.1 0.0 collective-permute-done.8.rest_2_
  25.1 0.7 %level.5 = (f32[64,384]{1,0:T(8,128)S(1)}, f32[144,384]{1,0:T(8,128)S(1)}, f32[64,384]{1,0:T(8,128)S(1)}, f32[64,128]{1,0:T(8,128)S(1)}, f32[64,128]{1,0:T(8,128)S(1)}, /*index=5*/f32[64,128]{1,0:T(8,128)S(1)}) custom-call(f32[4,128]{1,0:T(4,128)S(1)} %get-tuple-element.89.flags_ref, s32[8,1536]{1,0:T(8,128)S(1)} %get-tuple-element.90.joined_ref, ...), custom_call_target="tpu_custom_call" | custom-call | flops 100000000 | bytes 1048576 | tf_op jit(solution)/shard_map/level/pallas_call | solution.py:570
  25.8 2.1 %collective-permute-start.9 = (f32[64,128]{1,0:T(8,128)S(1)}, f32[64,128]{1,0:T(8,128)S(1)}, u32[]{:S(2)}, u32[]{:S(2)}) collective-permute-start(f32[64,128]{1,0:T(8,128)S(1)} %get-tuple-element.142), channel_id=1, source_target_pairs={{0,30},{2,4},{4,2},{6,8},{8,6},{10,12},{12,10},{14,16},{16,14},{18... | collective-permute-start | bytes 98312 | tf_op jit(solution)/shard_map/ppermute | solution.py:618
  27.9 0.0 collective-permute-start.10
  27.9 1.1 %collective-permute-start.11 = (f32[64,128]{1,0:T(8,128)S(1)}, f32[64,128]{1,0:T(8,128)S(1)}, u32[]{:S(2)}, u32[]{:S(2)}) collective-permute-start(f32[64,128]{1,0:T(8,128)S(1)} %get-tuple-element.144), channel_id=1, source_target_pairs={{0,1},{1,0},{2,3},{3,2},{4,5},{5,4},{6,7},{7,6},{8,9},{9,8},{10,11... | collective-permute-start | bytes 98312 | tf_op jit(solution)/shard_map/ppermute | solution.py:618
  29.0 2.5 %between.5 = (f32[144,384]{1,0:T(8,128)S(1)}, f32[8,384]{1,0:T(8,128)S(1)}, f32[144,1024]{1,0:T(8,128)S(1)}) custom-call(s32[8,1536]{1,0:T(8,128)S(1)} %get-tuple-element.91.members_ref, s32[8,1536]{1,0:T(8,128)S(1)} %get-tuple-element.90.joined_ref, s32[8,128]{1,0:T(8,128)S(1)} %get-tuple-element.92.places_ref, ...), custom_call_target="tpu_custom_call" | custom-call | flops 2000000000 | bytes 1048576 | tf_op jit(solution)/shard_map/between/pallas_call | solution.py:570
  31.4 0.5 %collective-permute-done.9.rest_0_ = f32[64,128]{1,0:T(8,128)S(1)} collective-permute-done((f32[64,128]{1,0:T(8,128)S(1)}, f32[64,128]{1,0:T(8,128)S(1)}, u32[]{:S(2)}, u32[]{:S(2)}) %collective-permute-start.9) | collective-permute-done | bytes 32800 | tf_op jit(solution)/shard_map/ppermute | solution.py:618
  31.9 0.0 collective-permute-done.10.rest_1_
  31.9 0.0 collective-permute-done.11.rest_2_
  31.9 2.5 %last.1 = f32[1120,128]{1,0:T(8,128)} custom-call(f32[4,128]{1,0:T(4,128)S(1)} %get-tuple-element.89.flags_ref, s32[8,1536]{1,0:T(8,128)S(1)} %get-tuple-element.90.joined_ref, f32[144,384]{1,0:T(8,128)S(1)} %get-tuple-element.139.local_ref, f32[8,384]{1,0:T(8,128)S(1)} %get-tuple-element.140.weights_ref, bf16[144,768]{1,0:T(8,128)(2,1)S(1)} %get-tuple-element.97.lift_ref, ...), custom_call_target="tpu_custom_call" | custom-call | flops 1000000000 | bytes 1048576 | tf_op jit(solution)/shard_map/last/pallas_call | solution.py:570
Async XLA Ops:
  1.8 9.9 %collective-permute-start = (f32[64,128]{1,0:T(8,128)S(1)}, f32[64,128]{1,0:T(8,128)S(1)}, u32[]{:S(2)}, u32[]{:S(2)}) collective-permute-start(f32[64,128]{1,0:T(8,128)S(1)} %get-tuple-element.86.refs_11_), channel_id=1, source_target_pairs={{0,30},{2,4},{4,2},{6,8},{8,6},{10,12},{12,10},{14,16},{16,14},{18... | collective-permute-start | bytes 98312 | tf_op jit(solution)/shard_map/ppermute | solution.py:618
  7.4 4.4 %collective-permute-start.1 = (f32[64,128]{1,0:T(8,128)S(1)}, f32[64,128]{1,0:T(8,128)S(1)}, u32[]{:S(2)}, u32[]{:S(2)}) collective-permute-start(f32[64,128]{1,0:T(8,128)S(1)} %get-tuple-element.87.refs_12_), channel_id=1, source_target_pairs={{0,2},{2,0},{4,6},{6,4},{8,10},{10,8},{12,14},{14,12},{16,18},{18,... | collective-permute-start | bytes 98312 | tf_op jit(solution)/shard_map/ppermute | solution.py:618
  7.4 4.4 %collective-permute-start.2 = (f32[64,128]{1,0:T(8,128)S(1)}, f32[64,128]{1,0:T(8,128)S(1)}, u32[]{:S(2)}, u32[]{:S(2)}) collective-permute-start(f32[64,128]{1,0:T(8,128)S(1)} %get-tuple-element.88.refs_13_), channel_id=1, source_target_pairs={{0,1},{1,0},{2,3},{3,2},{4,5},{5,4},{6,7},{7,6},{8,9},{9,8},{10,11... | collective-permute-start | bytes 98312 | tf_op jit(solution)/shard_map/ppermute | solution.py:618
  12.3 6.1 %collective-permute-start.3 = (f32[64,128]{1,0:T(8,128)S(1)}, f32[64,128]{1,0:T(8,128)S(1)}, u32[]{:S(2)}, u32[]{:S(2)}) collective-permute-start(f32[64,128]{1,0:T(8,128)S(1)} %get-tuple-element.111.rest_3_), channel_id=1, source_target_pairs={{0,30},{2,4},{4,2},{6,8},{8,6},{10,12},{12,10},{14,16},{16,14},{18... | collective-permute-start | bytes 98312 | tf_op jit(solution)/shard_map/ppermute | solution.py:618
  14.0 4.4 %collective-permute-start.4 = (f32[64,128]{1,0:T(8,128)S(1)}, f32[64,128]{1,0:T(8,128)S(1)}, u32[]{:S(2)}, u32[]{:S(2)}) collective-permute-start(f32[64,128]{1,0:T(8,128)S(1)} %get-tuple-element.112.rest_4_), channel_id=1, source_target_pairs={{0,2},{2,0},{4,6},{6,4},{8,10},{10,8},{12,14},{14,12},{16,18},{18,... | collective-permute-start | bytes 98312 | tf_op jit(solution)/shard_map/ppermute | solution.py:618
  14.0 4.4 %collective-permute-start.5 = (f32[64,128]{1,0:T(8,128)S(1)}, f32[64,128]{1,0:T(8,128)S(1)}, u32[]{:S(2)}, u32[]{:S(2)}) collective-permute-start(f32[64,128]{1,0:T(8,128)S(1)} %get-tuple-element.113.rest_5_), channel_id=1, source_target_pairs={{0,1},{1,0},{2,3},{3,2},{4,5},{5,4},{6,7},{7,6},{8,9},{9,8},{10,11... | collective-permute-start | bytes 98312 | tf_op jit(solution)/shard_map/ppermute | solution.py:618
  19.0 6.1 %collective-permute-start.6 = (f32[64,128]{1,0:T(8,128)S(1)}, f32[64,128]{1,0:T(8,128)S(1)}, u32[]{:S(2)}, u32[]{:S(2)}) collective-permute-start(f32[64,128]{1,0:T(8,128)S(1)} %get-tuple-element.124.rest_3_), channel_id=1, source_target_pairs={{0,30},{2,4},{4,2},{6,8},{8,6},{10,12},{12,10},{14,16},{16,14},{18... | collective-permute-start | bytes 98312 | tf_op jit(solution)/shard_map/ppermute | solution.py:618
  21.0 4.1 %collective-permute-start.7 = (f32[64,128]{1,0:T(8,128)S(1)}, f32[64,128]{1,0:T(8,128)S(1)}, u32[]{:S(2)}, u32[]{:S(2)}) collective-permute-start(f32[64,128]{1,0:T(8,128)S(1)} %get-tuple-element.125.rest_4_), channel_id=1, source_target_pairs={{0,2},{2,0},{4,6},{6,4},{8,10},{10,8},{12,14},{14,12},{16,18},{18,... | collective-permute-start | bytes 98312 | tf_op jit(solution)/shard_map/ppermute | solution.py:618
  21.0 4.1 %collective-permute-start.8 = (f32[64,128]{1,0:T(8,128)S(1)}, f32[64,128]{1,0:T(8,128)S(1)}, u32[]{:S(2)}, u32[]{:S(2)}) collective-permute-start(f32[64,128]{1,0:T(8,128)S(1)} %get-tuple-element.126.rest_5_), channel_id=1, source_target_pairs={{0,1},{1,0},{2,3},{3,2},{4,5},{5,4},{6,7},{7,6},{8,9},{9,8},{10,11... | collective-permute-start | bytes 98312 | tf_op jit(solution)/shard_map/ppermute | solution.py:618
  25.8 6.1 %collective-permute-start.9 = (f32[64,128]{1,0:T(8,128)S(1)}, f32[64,128]{1,0:T(8,128)S(1)}, u32[]{:S(2)}, u32[]{:S(2)}) collective-permute-start(f32[64,128]{1,0:T(8,128)S(1)} %get-tuple-element.142), channel_id=1, source_target_pairs={{0,30},{2,4},{4,2},{6,8},{8,6},{10,12},{12,10},{14,16},{16,14},{18... | collective-permute-start | bytes 98312 | tf_op jit(solution)/shard_map/ppermute | solution.py:618
  27.9 4.0 %collective-permute-start.10 = (f32[64,128]{1,0:T(8,128)S(1)}, f32[64,128]{1,0:T(8,128)S(1)}, u32[]{:S(2)}, u32[]{:S(2)}) collective-permute-start(f32[64,128]{1,0:T(8,128)S(1)} %get-tuple-element.143), channel_id=1, source_target_pairs={{0,2},{2,0},{4,6},{6,4},{8,10},{10,8},{12,14},{14,12},{16,18},{18,... | collective-permute-start | bytes 98312 | tf_op jit(solution)/shard_map/ppermute | solution.py:618
  27.9 4.0 %collective-permute-start.11 = (f32[64,128]{1,0:T(8,128)S(1)}, f32[64,128]{1,0:T(8,128)S(1)}, u32[]{:S(2)}, u32[]{:S(2)}) collective-permute-start(f32[64,128]{1,0:T(8,128)S(1)} %get-tuple-element.144), channel_id=1, source_target_pairs={{0,1},{1,0},{2,3},{3,2},{4,5},{5,4},{6,7},{7,6},{8,9},{9,8},{10,11... | collective-permute-start | bytes 98312 | tf_op jit(solution)/shard_map/ppermute | solution.py:618
